TPU v7x, 32 devices: a whole 2x2x4 slice. The times are simulated.
32 devices in a mesh: stream: 4 (over z), cy: 4 (over y, x), cz: 2 (over core).
Axes of the slice: x: 2, y: 2, z: 4, core: 2. Of those that a mesh axis runs over, the one named last changes fastest.
Arguments:
- populations: float32 [384, 19, 4096], P(('stream', 'cy', 'cz')), may hold values from 0.2 to 1
- solid_cells: int32 [384, 4096], P(('stream', 'cy', 'cz')), may hold values 0 or 1
- block_pos: int32 [384, 3], P(('stream', 'cy', 'cz')), may hold values from -1 to 7, as said below
Outputs:
- populations_out: float32 [19, 128, 64, 128], P(None, 'stream', 'cy', 'cz')
Inputs may be any that keep to these rules, and one draw needn't show every extreme that they name: `block_pos`: row r belongs to device r // 12 in mesh order. A device's rows hold, in order, a run of its (cy, cz) group's block list followed by rows of -1. The list names once every block with by in the group's 1 block and bz in its 4 blocks, ordered by bx, blocks of one bx in any order. The device at index s of stream holds the entries from s * 8 + d_s up to (s + 1) * 8 + d_(s+1), where d is 0 at both ends of the axis and |d_s| <= 2; so its rows name at most 2 blocks with bx // 2 equal to each of s - 1 and s + 1, no other foreign ones, and at most 4 of its own blocks lie on other devices.
All inputs are finite; a program needn't handle non-finite values. No bound on the sum of `solid_cells` on one device may be relied on, other than what follows from the above.
Results may differ from a plain program's by a relative error of at most 0.0001.
Values sent between devices are 32-bit elements; how exact they have to be, the bound alone decides.
No kernel may reach another device: no remote copies, remote signals or barrier semaphores. Data moves between devices by JAX's collectives and lax.ppermute only.
A program may use at most 128 MiB of HBM per device.

v0:
```python
import jax
import jax.numpy as jnp
from jax import lax
from jax.sharding import PartitionSpec as P

EDGE = 16
BXD = 2
BYD = 1
BZD = 4
STEPS = 2
MOVE_CAP = 2


VELOCITIES = (
    (0, 0, 0),
    (1, 0, 0),
    (-1, 0, 0),
    (0, 1, 0),
    (0, -1, 0),
    (0, 0, 1),
    (0, 0, -1),
    (1, 1, 0),
    (-1, -1, 0),
    (1, -1, 0),
    (-1, 1, 0),
    (1, 0, 1),
    (-1, 0, -1),
    (1, 0, -1),
    (-1, 0, 1),
    (0, 1, 1),
    (0, -1, -1),
    (0, 1, -1),
    (0, -1, 1),
)
WEIGHTS = (1.0 / 3.0,) + (1.0 / 18.0,) * 6 + (1.0 / 36.0,) * 12
OPPOSITE = (0, 2, 1, 4, 3, 6, 5, 8, 7, 10, 9, 12, 11, 14, 13, 16, 15, 18, 17)
OMEGA_EVEN = 1.25
OMEGA_ODD = 1.0 / 1.125


def shifted(value, axis, steps):
    count = lax.axis_size(axis)
    first, last = (max(0, -steps), min(count, count - steps))
    return lax.ppermute(value, axis, [(source, source + steps) for source in range(first, last)])


def with_halo(shard, sides, width):
    for axis, dim in sides:
        count, length = (lax.axis_size(axis), shard.shape[dim])
        up = [(i, (i + 1) % count) for i in range(count - 1)]
        down = [(j, i) for i, j in up]
        last = lax.slice_in_dim(shard, length - width, length, axis=dim)
        first = lax.slice_in_dim(shard, 0, width, axis=dim)
        before = lax.ppermute(last, axis, up)
        after = lax.ppermute(first, axis, down)
        shard = jnp.concatenate([before, shard, after], axis=dim)
    return shard


def moment(lattice, component):
    summed = jnp.zeros_like(lattice[0])
    for member in range(19):
        factor = VELOCITIES[member][component]
        if factor == 1:
            summed = summed + lattice[member]
        elif factor == -1:
            summed = summed - lattice[member]
    return summed


def collide(lattice):
    density = jnp.sum(lattice, axis=0)
    velocity = [moment(lattice, component) / density for component in range(3)]
    square = velocity[0] * velocity[0] + velocity[1] * velocity[1] + velocity[2] * velocity[2]
    outputs = []
    for member in range(19):
        step_x, step_y, step_z = VELOCITIES[member]
        projected = step_x * velocity[0] + step_y * velocity[1] + step_z * velocity[2]
        even_eq = WEIGHTS[member] * density * (1.0 + 4.5 * projected * projected - 1.5 * square)
        odd_eq = WEIGHTS[member] * density * 3.0 * projected
        mirror = lattice[OPPOSITE[member]]
        even_part = 0.5 * (lattice[member] + mirror)
        odd_part = 0.5 * (lattice[member] - mirror)
        outputs.append(
            lattice[member] - OMEGA_EVEN * (even_part - even_eq) - OMEGA_ODD * (odd_part - odd_eq)
        )
    return (jnp.stack(outputs), density)


def propagate(lattice, widened, wall_ext, drift_y, drift_z, density, rotor_here):
    size_x, size_y, size_z = lattice.shape[1:]
    outputs = []
    for member in range(19):
        step_x, step_y, step_z = VELOCITIES[member]
        window = (
            slice(1 - step_x, 1 - step_x + size_x),
            slice(1 - step_y, 1 - step_y + size_y),
            slice(1 - step_z, 1 - step_z + size_z),
        )
        pulled = widened[member][window]
        blocked = wall_ext[window]
        wall_push = (
            6.0 * WEIGHTS[member] * density * (step_y * drift_y[window] + step_z * drift_z[window])
        )
        bounced = (
            widened[OPPOSITE[member]][1 : 1 + size_x, 1 : 1 + size_y, 1 : 1 + size_z] + wall_push
        )
        read = jnp.where(blocked, bounced, pulled)
        outputs.append(jnp.where(rotor_here, lattice[member], read))
    return jnp.stack(outputs)


def into_lanes(values, bucket_lane, lanes, filler):
    buffer_shape = (lanes + 1,) + values.shape[1:]
    return jnp.full(buffer_shape, filler, values.dtype).at[bucket_lane].set(values)[:lanes]


def shards(populations, solid_cells, block_pos):
    slots = BXD * BYD * BZD
    block_cells = EDGE**3
    layer_here = lax.axis_index("stream")
    column_y = lax.axis_index("cy")
    column_z = lax.axis_index("cz")
    size_x = lax.axis_size("stream")
    size_y = lax.axis_size("cy")
    size_z = lax.axis_size("cz")
    occupied = block_pos[:, 0] >= 0
    home_layer = jnp.where(occupied, block_pos[:, 0] // BXD, -1)
    coded = jnp.where(occupied[:, None], block_pos + 1, 0)
    arrivals = []
    downward = occupied & (home_layer == layer_here - 1)
    upward = occupied & (home_layer == layer_here + 1)
    down_lane = jnp.where(downward, jnp.cumsum(downward.astype(jnp.int32)) - 1, MOVE_CAP)
    up_lane = jnp.where(upward, jnp.cumsum(upward.astype(jnp.int32)) - 1, MOVE_CAP)
    going_down = (
        into_lanes(populations, down_lane, MOVE_CAP, 0.0),
        into_lanes(solid_cells, down_lane, MOVE_CAP, 0),
        into_lanes(coded, down_lane, MOVE_CAP, 0),
    )
    going_up = (
        into_lanes(populations, up_lane, MOVE_CAP, 0.0),
        into_lanes(solid_cells, up_lane, MOVE_CAP, 0),
        into_lanes(coded, up_lane, MOVE_CAP, 0),
    )
    arrivals.append(shifted((going_down[0], going_down[1], going_down[2]), "stream", -1))
    arrivals.append(shifted((going_up[0], going_up[1], going_up[2]), "stream", 1))

    def home_spot(coords, valid):
        spot_here = (
            (coords[:, 0] - layer_here * BXD) * BYD + (coords[:, 1] - column_y * BYD)
        ) * BZD
        spot_here = spot_here + (coords[:, 2] - column_z * BZD)
        mine = valid & (coords[:, 0] // BXD == layer_here)
        return jnp.where(mine, spot_here, slots)

    settled = jnp.zeros((slots + 1, 19, block_cells), jnp.float32)
    settled_marks = jnp.zeros((slots + 1, block_cells), jnp.int32)
    spots = home_spot(block_pos, occupied)
    settled = settled.at[spots].set(populations)
    settled_marks = settled_marks.at[spots].set(solid_cells)
    for parcel in arrivals:
        incoming = parcel[2] - 1
        spots = home_spot(incoming, incoming[:, 0] >= 0)
        settled = settled.at[spots].set(parcel[0])
        settled_marks = settled_marks.at[spots].set(parcel[1])
    span_x = BXD * EDGE
    span_y = BYD * EDGE
    span_z = BZD * EDGE
    lattice = settled[:slots].reshape(BXD, BYD, BZD, 19, EDGE, EDGE, EDGE)
    lattice = lattice.transpose(3, 0, 4, 1, 5, 2, 6).reshape(19, span_x, span_y, span_z)
    marks = settled_marks[:slots].reshape(BXD, BYD, BZD, EDGE, EDGE, EDGE)
    marks = marks.transpose(0, 3, 1, 4, 2, 5).reshape(span_x, span_y, span_z)
    rotor_here = marks == 1
    marks_ext = with_halo(marks, (("stream", 0), ("cy", 1), ("cz", 2)), 1)
    total_x = span_x * size_x
    total_y = span_y * size_y
    total_z = span_z * size_z
    index_x = layer_here * span_x - 1 + jnp.arange(span_x + 2)
    index_y = column_y * span_y - 1 + jnp.arange(span_y + 2)
    index_z = column_z * span_z - 1 + jnp.arange(span_z + 2)
    inside = ((index_x >= 0) & (index_x < total_x))[:, None, None]
    inside = inside & ((index_y >= 0) & (index_y < total_y))[None, :, None]
    inside = inside & ((index_z >= 0) & (index_z < total_z))[None, None, :]
    rotor_ext = marks_ext == 1
    wall_ext = rotor_ext | jnp.logical_not(inside)
    spin = 0.2 / (total_y + total_z)
    centre_y = (total_y - 1) / 2.0
    centre_z = (total_z - 1) / 2.0
    coord_y = index_y.astype(jnp.float32)
    coord_z = index_z.astype(jnp.float32)
    drift_y = jnp.where(rotor_ext, -spin * (coord_z - centre_z)[None, None, :], 0.0)
    drift_z = jnp.where(rotor_ext, spin * (coord_y - centre_y)[None, :, None], 0.0)
    for sweep in range(STEPS):
        post, density = collide(lattice)
        widened = with_halo(post, (("stream", 1), ("cy", 2), ("cz", 3)), 1)
        lattice = propagate(lattice, widened, wall_ext, drift_y, drift_z, density, rotor_here)
    return lattice


def solution(mesh):
    in_specs = (
        P(("stream", "cy", "cz"), None, None),
        P(("stream", "cy", "cz"), None),
        P(("stream", "cy", "cz"), None),
    )
    out_specs = P(None, "stream", "cy", "cz")
    return jax.shard_map(shards, mesh=mesh, in_specs=in_specs, out_specs=out_specs, check_vma=False)
```

profile of v0, /device:TPU:1, one launch (start us, length us, event | category | flops | bytes accessed | tf_op | source)
XLA Modules:
  0.0 468.8 jit_solution(9927872190265813333)
XLA Ops:
  17.7 5.3 %scatter_fusion.3 = f32[3,19,4096]{2,1,0:T(8,128)S(1)} fusion(f32[3,19,4096]{2,1,0:T(8,128)S(1)} %broadcast.1568.clone, s32[12]{0:T(128)S(1)} %fusion.426, f32[12,19,4096]{2,1,0:T(8,128)} %param.3), kind=kCustom, calls=%fused_computation.8 | custom fusion | bytes 11206704 | tf_op jit(solution)/shard_map/scatter | solution.py:115
  26.2 5.3 %scatter_fusion.5 = f32[3,19,4096]{2,1,0:T(8,128)S(1)} fusion(f32[3,19,4096]{2,1,0:T(8,128)S(1)} %broadcast.1568.clone.1, s32[12]{0:T(128)S(1)} %fusion.427, f32[12,19,4096]{2,1,0:T(8,128)} %param.3), kind=kCustom, calls=%fused_computation.10 | custom fusion | bytes 11206704 | tf_op jit(solution)/shard_map/scatter | solution.py:115
  58.2 6.9 %collective-permute-start.11 = (s32[34,18,1]{2,1,0:T(8,128)S(1)}, s32[34,18,1]{2,1,0:T(8,128)S(1)}, u32[]{:S(2)}, u32[]{:S(2)}) collective-permute-start(s32[34,18,1]{2,1,0:T(8,128)S(1)} %get-tuple-element.114), channel_id=1, source_target_pairs={{1,0},{3,2},{5,4},{7,6},{9,8},{11,10},{13,12},{15,14},{17,16},{19,... | collective-permute-start | bytes 7352 | tf_op jit(solution)/shard_map/ppermute | solution.py:55
  67.3 9.7 %scatter_fusion.2 = f32[9,19,4096]{2,1,0:T(8,128)} fusion(f32[9,19,4096]{2,1,0:T(8,128)} %broadcast_in_dim.78, s32[12]{0:T(128)S(1)} %fusion.425, f32[12,19,4096]{2,1,0:T(8,128)} %param.3), kind=kCustom, calls=%fused_computation.7 | custom fusion | bytes 11206704 | tf_op jit(solution)/shard_map/scatter | solution.py:159
  89.1 13.2 %reshape.4211 = f32[2,1,4,19,16,16,16]{6,5,4,2,0,3,1:T(8,128)} reshape(f32[8,19,4096]{2,0,1:T(8,128)S(1)} %copy.110) | data formatting | bytes 4980736 | tf_op jit(solution)/shard_map/reshape | solution.py:169
  102.3 9.0 %bitcast_reduce_fusion = f32[2,16,16,4,16]{4,2,1,3,0:T(8,128)S(1)} fusion(f32[2,1,4,19,16,16,16]{6,5,4,2,0,3,1:T(8,128)} %reshape.4211), kind=kLoop, calls=%fused_computation.719 | loop fusion | flops 589824 | bytes 2621440 | tf_op jit(solution)/shard_map/reduce_sum | solution.py:72
  113.5 14.1 %fusion.450 = (f32[1,2,16,1,16,4,16]{6,4,2,5,1,0,3:T(8,128)S(1)}, f32[1,2,16,1,16,4,16]{6,4,2,5,1,0,3:T(8,128)}, f32[1,2,16,1,16,4,16]{6,4,2,5,1,0,3:T(8,128)}, ...) fusion(f32[19,2,16,1,16,4,16]{6,4,2,5,1,0,3:T(8,128)} %bitcast.331), kind=kLoop, calls=%fused_computation.722 | loop fusion | bytes 4980736 | tf_op jit(solution)/shard_map/slice | solution.py:67
  246.8 5.1 %collective-permute-done.14 = f32[19,34,1,64]{3,2,1,0:T(1,128)S(1)} collective-permute-done((f32[19,34,1,64]{3,2,1,0:T(1,128)S(1)}, f32[19,34,1,64]{3,2,1,0:T(1,128)S(1)}, u32[]{:S(2)}, u32[]{:S(2)}) %collective-permute-start.14) | collective-permute-done | bytes 165408 | tf_op jit(solution)/shard_map/ppermute | solution.py:54
  251.9 8.1 %collective-permute-done.15 = f32[19,34,1,64]{3,2,1,0:T(1,128)S(1)} collective-permute-done((f32[19,34,1,64]{3,2,1,0:T(1,128)S(1)}, f32[19,34,1,64]{3,2,1,0:T(1,128)S(1)}, u32[]{:S(2)}, u32[]{:S(2)}) %collective-permute-start.15) | collective-permute-done | bytes 165408 | tf_op jit(solution)/shard_map/ppermute | solution.py:55
  263.2 6.7 %fusion.452 = (f32[19,34,18,1]{3,2,1,0:T(8,128)}, f32[19,34,18,1]{3,2,1,0:T(8,128)}) fusion(f32[19,34,18,64]{3,2,1,0:T(8,128)S(1)} %pad_maximum_fusion), kind=kLoop, calls=%fused_computation.724 | loop fusion | bytes 186048 | tf_op jit(solution)/shard_map/slice | solution.py:52
  270.0 6.0 %copy.132 = f32[19,34,18,1]{1,3,2,0:T(1,128)} copy(f32[19,34,18,1]{3,2,1,0:T(8,128)} %get-tuple-element.100) | data formatting | bytes 93024 | tf_op jit(solution)/shard_map/slice | solution.py:52
  276.0 5.5 %copy.133 = f32[19,34,18,1]{1,3,2,0:T(1,128)S(1)} copy(f32[19,34,18,1]{3,2,1,0:T(8,128)} %get-tuple-element.101) | data formatting | bytes 93024 | tf_op jit(solution)/shard_map/slice | solution.py:53
  334.5 6.3 %copy.134 = f32[19,34,18,1]{3,2,1,0:T(8,128)} copy(f32[19,34,18,1]{1,3,2,0:T(1,128)} %collective-permute-done.16) | data formatting | bytes 93024 | tf_op jit(solution)/shard_map/ppermute | solution.py:54
  340.7 6.2 %copy.135 = f32[19,34,18,1]{3,2,1,0:T(8,128)} copy(f32[19,34,18,1]{1,3,2,0:T(1,128)} %collective-permute-done.17) | data formatting | bytes 93024 | tf_op jit(solution)/shard_map/ppermute | solution.py:55
  347.0 12.6 %pad_maximum_fusion.1 = f32[19,34,18,66]{3,2,1,0:T(8,128)S(1)} fusion(f32[19,34,18,1]{3,2,1,0:T(8,128)} %copy.135, f32[19,34,1,64]{3,2,1,0:T(1,128)S(1)} %copy-done.52, f32[19,1,16,64]{3,2,1,0:T(8,128)S(1)} %collective-permute-done.13, f32[19,32,16,64]{3,2,1,0:T(8,128)} %copy-done.1, f32[19,1,16,64]{3,2,1,0:T(8,128)S(1)} %collective-permute-done.12, ...), kind=kLoop, calls=%fused_computation.13 | loop fusion | flops 4604688 | bytes 6139584 | tf_op jit(solution)/shard_map/concatenate | solution.py:56
  362.2 9.7 %fusion.161 = (f32[19,32,16,64]{3,2,1,0:T(8,128)S(1)}, f32[32,16,64]{2,1,0:T(8,128)S(1)}, f32[32,16,64]{2,1,0:T(8,128)S(1)}, f32[32,16,64]{2,1,0:T(8,128)S(1)}, ...) fusion(f32[32,16,64]{2,1,0:T(8,128)} %squeeze.173, ...), kind=kLoop, calls=%fused_computation.267 | loop fusion | flops 6422527 | bytes 19693568
  392.9 8.2 %collective-permute-done.21 = f32[19,34,1,64]{3,2,1,0:T(1,128)S(1)} collective-permute-done((f32[19,34,1,64]{3,2,1,0:T(1,128)S(1)}, f32[19,34,1,64]{3,2,1,0:T(1,128)S(1)}, u32[]{:S(2)}, u32[]{:S(2)}) %collective-permute-start.21) | collective-permute-done | bytes 165408 | tf_op jit(solution)/shard_map/ppermute | solution.py:55
  404.4 6.8 %fusion.451 = (f32[19,34,18,1]{3,2,1,0:T(8,128)}, f32[19,34,18,1]{3,2,1,0:T(8,128)}) fusion(f32[19,34,18,64]{3,2,1,0:T(8,128)S(1)} %pad_maximum_fusion.2), kind=kLoop, calls=%fused_computation.723 | loop fusion | bytes 186048 | tf_op jit(solution)/shard_map/slice | solution.py:52
  411.2 6.0 %copy.157 = f32[19,34,18,1]{1,3,2,0:T(1,128)} copy(f32[19,34,18,1]{3,2,1,0:T(8,128)} %get-tuple-element.79) | data formatting | bytes 93024 | tf_op jit(solution)/shard_map/slice | solution.py:52
  418.5 6.0 %copy.158 = f32[19,34,18,1]{1,3,2,0:T(1,128)} copy(f32[19,34,18,1]{3,2,1,0:T(8,128)} %get-tuple-element.80) | data formatting | bytes 93024 | tf_op jit(solution)/shard_map/slice | solution.py:53
  424.5 6.8 %collective-permute-start.23 = (f32[19,34,18,1]{1,3,2,0:T(1,128)}, f32[19,34,18,1]{1,3,2,0:T(1,128)}, u32[]{:S(2)}, u32[]{:S(2)}) collective-permute-start(f32[19,34,18,1]{1,3,2,0:T(1,128)} %copy.158), channel_id=1, source_target_pairs={{1,0},{3,2},{5,4},{7,6},{9,8},{11,10},{13,12},{15,14},{17,16},{19,... | collective-permute-start | bytes 139544 | tf_op jit(solution)/shard_map/ppermute | solution.py:55
  431.3 6.5 %copy.159 = f32[19,34,18,1]{3,2,1,0:T(8,128)} copy(f32[19,34,18,1]{1,3,2,0:T(1,128)} %collective-permute-done.22) | data formatting | bytes 93024 | tf_op jit(solution)/shard_map/ppermute | solution.py:54
  437.8 6.2 %copy.160 = f32[19,34,18,1]{3,2,1,0:T(8,128)} copy(f32[19,34,18,1]{1,3,2,0:T(1,128)} %collective-permute-done.23) | data formatting | bytes 93024 | tf_op jit(solution)/shard_map/ppermute | solution.py:55
  444.0 13.0 %pad_maximum_fusion.3 = f32[19,34,18,66]{3,2,1,0:T(8,128)S(1)} fusion(f32[19,34,18,1]{3,2,1,0:T(8,128)} %copy.160, f32[19,34,1,64]{3,2,1,0:T(1,128)} %copy-done.54, f32[19,1,16,64]{3,2,1,0:T(8,128)} %copy-done.48, f32[19,32,16,64]{3,2,1,0:T(8,128)} %copy-done, f32[19,1,16,64]{3,2,1,0:T(8,128)S(1)} %collective-permute-done.18, ...), kind=kLoop, calls=%fused_computation.15 | loop fusion | flops 4604688 | bytes 6139584 | tf_op jit(solution)/shard_map/concatenate | solution.py:56
  (348 shorter events, 277.2 us)
Async XLA Ops:
  3.0 30.1 %collective-permute-start.2 = (s32[2,3]{1,0:T(2,128)S(1)}, s32[2,3]{1,0:T(2,128)S(1)}, u32[]{:S(2)}, u32[]{:S(2)}) collective-permute-start(s32[2,3]{1,0:T(2,128)S(1)} %slice.906), channel_id=1, source_target_pairs={{0,8},{8,16},{16,24},{1,9},{9,17},{17,25},{2,10},{10,18},{18,26},{... | collective-permute-start | bytes 80 | tf_op jit(solution)/shard_map/ppermute | solution.py:44
  7.8 30.2 %collective-permute-start = (s32[2,3]{1,0:T(2,128)S(1)}, s32[2,3]{1,0:T(2,128)S(1)}, u32[]{:S(2)}, u32[]{:S(2)}) collective-permute-start(s32[2,3]{1,0:T(2,128)S(1)} %slice.901), channel_id=1, source_target_pairs={{8,0},{16,8},{24,16},{9,1},{17,9},{25,17},{10,2},{18,10},{26,18},{... | collective-permute-start | bytes 80 | tf_op jit(solution)/shard_map/ppermute | solution.py:44
  10.4 27.8 %collective-permute-start.1 = (s32[2,4096]{1,0:T(2,128)S(1)}, s32[2,4096]{1,0:T(2,128)S(1)}, u32[]{:S(2)}, u32[]{:S(2)}) collective-permute-start(s32[2,4096]{1,0:T(2,128)S(1)} %slice.1121), channel_id=1, source_target_pairs={{8,0},{16,8},{24,16},{9,1},{17,9},{25,17},{10,2},{18,10},{26,18},{... | collective-permute-start | bytes 98312 | tf_op jit(solution)/shard_map/ppermute | solution.py:44
  13.0 26.0 %collective-permute-start.3 = (s32[2,4096]{1,0:T(2,128)S(1)}, s32[2,4096]{1,0:T(2,128)S(1)}, u32[]{:S(2)}, u32[]{:S(2)}) collective-permute-start(s32[2,4096]{1,0:T(2,128)S(1)} %slice.1122), channel_id=1, source_target_pairs={{0,8},{8,16},{16,24},{1,9},{9,17},{17,25},{2,10},{10,18},{18,26},{... | collective-permute-start | bytes 98312 | tf_op jit(solution)/shard_map/ppermute | solution.py:44
  23.6 53.9 %collective-permute-start.4 = (f32[2,19,4096]{2,0,1:T(2,128)S(1)}, f32[2,19,4096]{2,0,1:T(2,128)}, u32[]{:S(2)}, u32[]{:S(2)}) collective-permute-start(f32[2,19,4096]{2,0,1:T(2,128)S(1)} %copy.106), channel_id=1, source_target_pairs={{8,0},{16,8},{24,16},{9,1},{17,9},{25,17},{10,2},{18,10},{26,18},{... | collective-permute-start | bytes 1867784 | tf_op jit(solution)/shard_map/ppermute | solution.py:44
  33.0 48.4 %collective-permute-start.5 = (f32[2,19,4096]{2,0,1:T(2,128)}, f32[2,19,4096]{2,0,1:T(2,128)}, u32[]{:S(2)}, u32[]{:S(2)}) collective-permute-start(f32[2,19,4096]{2,0,1:T(2,128)} %copy.108), channel_id=1, source_target_pairs={{0,8},{8,16},{16,24},{1,9},{9,17},{17,25},{2,10},{10,18},{18,26},{... | collective-permute-start | bytes 1867784 | tf_op jit(solution)/shard_map/ppermute | solution.py:44
  41.4 7.5 %collective-permute-start.6 = (s32[1,16,64]{2,1,0:T(8,128)S(1)}, s32[1,16,64]{2,1,0:T(8,128)S(1)}, u32[]{:S(2)}, u32[]{:S(2)}) collective-permute-start(s32[1,16,64]{2,1,0:T(8,128)S(1)} %get-tuple-element.118), channel_id=1, source_target_pairs={{0,8},{8,16},{16,24},{1,9},{9,17},{17,25},{2,10},{10,18},{18,26},{... | collective-permute-start | bytes 12296 | tf_op jit(solution)/shard_map/ppermute | solution.py:54
  43.9 5.1 %collective-permute-start.7 = (s32[1,16,64]{2,1,0:T(8,128)S(1)}, s32[1,16,64]{2,1,0:T(8,128)S(1)}, u32[]{:S(2)}, u32[]{:S(2)}) collective-permute-start(s32[1,16,64]{2,1,0:T(8,128)S(1)} %get-tuple-element.117), channel_id=1, source_target_pairs={{8,0},{16,8},{24,16},{9,1},{17,9},{25,17},{10,2},{18,10},{26,18},{... | collective-permute-start | bytes 12296 | tf_op jit(solution)/shard_map/ppermute | solution.py:55
  49.0 4.4 collective-permute-start.8
  52.2 4.5 collective-permute-start.9
  56.9 20.1 %collective-permute-start.10 = (s32[34,18,1]{2,1,0:T(8,128)S(1)}, s32[34,18,1]{2,1,0:T(8,128)S(1)}, u32[]{:S(2)}, u32[]{:S(2)}) collective-permute-start(s32[34,18,1]{2,1,0:T(8,128)S(1)} %get-tuple-element.113), channel_id=1, source_target_pairs={{0,1},{2,3},{4,5},{6,7},{8,9},{10,11},{12,13},{14,15},{16,17},{18,... | collective-permute-start | bytes 7352 | tf_op jit(solution)/shard_map/ppermute | solution.py:54
  58.2 18.8 %collective-permute-start.11 = (s32[34,18,1]{2,1,0:T(8,128)S(1)}, s32[34,18,1]{2,1,0:T(8,128)S(1)}, u32[]{:S(2)}, u32[]{:S(2)}) collective-permute-start(s32[34,18,1]{2,1,0:T(8,128)S(1)} %get-tuple-element.114), channel_id=1, source_target_pairs={{1,0},{3,2},{5,4},{7,6},{9,8},{11,10},{13,12},{15,14},{17,16},{19,... | collective-permute-start | bytes 7352 | tf_op jit(solution)/shard_map/ppermute | solution.py:55
  229.3 7.2 %collective-permute-start.12 = (f32[19,1,16,64]{3,2,1,0:T(8,128)S(1)}, f32[19,1,16,64]{3,2,1,0:T(8,128)S(1)}, u32[]{:S(2)}, u32[]{:S(2)}) collective-permute-start(f32[19,1,16,64]{3,2,1,0:T(8,128)S(1)} %get-tuple-element.108), channel_id=1, source_target_pairs={{0,8},{8,16},{16,24},{1,9},{9,17},{17,25},{2,10},{10,18},{18,26},{... | collective-permute-start | bytes 233480 | tf_op jit(solution)/shard_map/ppermute | solution.py:54
  232.8 7.8 %collective-permute-start.13 = (f32[19,1,16,64]{3,2,1,0:T(8,128)S(1)}, f32[19,1,16,64]{3,2,1,0:T(8,128)S(1)}, u32[]{:S(2)}, u32[]{:S(2)}) collective-permute-start(f32[19,1,16,64]{3,2,1,0:T(8,128)S(1)} %get-tuple-element.109), channel_id=1, source_target_pairs={{8,0},{16,8},{24,16},{9,1},{17,9},{25,17},{10,2},{18,10},{26,18},{... | collective-permute-start | bytes 233480 | tf_op jit(solution)/shard_map/ppermute | solution.py:55
  241.3 10.6 %collective-permute-start.14 = (f32[19,34,1,64]{3,2,1,0:T(1,128)S(1)}, f32[19,34,1,64]{3,2,1,0:T(1,128)S(1)}, u32[]{:S(2)}, u32[]{:S(2)}) collective-permute-start(f32[19,34,1,64]{3,2,1,0:T(1,128)S(1)} %get-tuple-element.104), channel_id=1, source_target_pairs={{0,2},{2,4},{4,6},{1,3},{3,5},{5,7},{8,10},{10,12},{12,14},{9,11},... | collective-permute-start | bytes 496136 | tf_op jit(solution)/shard_map/ppermute | solution.py:54
  245.3 14.7 %collective-permute-start.15 = (f32[19,34,1,64]{3,2,1,0:T(1,128)S(1)}, f32[19,34,1,64]{3,2,1,0:T(1,128)S(1)}, u32[]{:S(2)}, u32[]{:S(2)}) collective-permute-start(f32[19,34,1,64]{3,2,1,0:T(1,128)S(1)} %get-tuple-element.105), channel_id=1, source_target_pairs={{2,0},{4,2},{6,4},{3,1},{5,3},{7,5},{10,8},{12,10},{14,12},{11,9},... | collective-permute-start | bytes 496136 | tf_op jit(solution)/shard_map/ppermute | solution.py:55
  281.5 59.2 %collective-permute-start.17 = (f32[19,34,18,1]{1,3,2,0:T(1,128)S(1)}, f32[19,34,18,1]{1,3,2,0:T(1,128)}, u32[]{:S(2)}, u32[]{:S(2)}) collective-permute-start(f32[19,34,18,1]{1,3,2,0:T(1,128)S(1)} %copy.133), channel_id=1, source_target_pairs={{1,0},{3,2},{5,4},{7,6},{9,8},{11,10},{13,12},{15,14},{17,16},{19,... | collective-permute-start | bytes 139544 | tf_op jit(solution)/shard_map/ppermute | solution.py:55
  285.4 49.0 %collective-permute-start.16 = (f32[19,34,18,1]{1,3,2,0:T(1,128)}, f32[19,34,18,1]{1,3,2,0:T(1,128)}, u32[]{:S(2)}, u32[]{:S(2)}) collective-permute-start(f32[19,34,18,1]{1,3,2,0:T(1,128)} %copy.132), channel_id=1, source_target_pairs={{0,1},{2,3},{4,5},{6,7},{8,9},{10,11},{12,13},{14,15},{16,17},{18,... | collective-permute-start | bytes 139544 | tf_op jit(solution)/shard_map/ppermute | solution.py:54
  376.7 5.6 %collective-permute-start.18 = (f32[19,1,16,64]{3,2,1,0:T(8,128)S(1)}, f32[19,1,16,64]{3,2,1,0:T(8,128)S(1)}, u32[]{:S(2)}, u32[]{:S(2)}) collective-permute-start(f32[19,1,16,64]{3,2,1,0:T(8,128)S(1)} %get-tuple-element.106), channel_id=1, source_target_pairs={{0,8},{8,16},{16,24},{1,9},{9,17},{17,25},{2,10},{10,18},{18,26},{... | collective-permute-start | bytes 233480 | tf_op jit(solution)/shard_map/ppermute | solution.py:54
  380.2 6.2 %collective-permute-start.19 = (f32[19,1,16,64]{3,2,1,0:T(8,128)S(1)}, f32[19,1,16,64]{3,2,1,0:T(8,128)S(1)}, u32[]{:S(2)}, u32[]{:S(2)}) collective-permute-start(f32[19,1,16,64]{3,2,1,0:T(8,128)S(1)} %get-tuple-element.107), channel_id=1, source_target_pairs={{8,0},{16,8},{24,16},{9,1},{17,9},{25,17},{10,2},{18,10},{26,18},{... | collective-permute-start | bytes 233480 | tf_op jit(solution)/shard_map/ppermute | solution.py:55
  387.0 6.0 %collective-permute-start.20 = (f32[19,34,1,64]{3,2,1,0:T(1,128)S(1)}, f32[19,34,1,64]{3,2,1,0:T(1,128)S(1)}, u32[]{:S(2)}, u32[]{:S(2)}) collective-permute-start(f32[19,34,1,64]{3,2,1,0:T(1,128)S(1)} %get-tuple-element.102), channel_id=1, source_target_pairs={{0,2},{2,4},{4,6},{1,3},{3,5},{5,7},{8,10},{10,12},{12,14},{9,11},... | collective-permute-start | bytes 496136 | tf_op jit(solution)/shard_map/ppermute | solution.py:54
  388.9 12.2 %collective-permute-start.21 = (f32[19,34,1,64]{3,2,1,0:T(1,128)S(1)}, f32[19,34,1,64]{3,2,1,0:T(1,128)S(1)}, u32[]{:S(2)}, u32[]{:S(2)}) collective-permute-start(f32[19,34,1,64]{3,2,1,0:T(1,128)S(1)} %get-tuple-element.103), channel_id=1, source_target_pairs={{2,0},{4,2},{6,4},{3,1},{5,3},{7,5},{10,8},{12,10},{14,12},{11,9},... | collective-permute-start | bytes 496136 | tf_op jit(solution)/shard_map/ppermute | solution.py:55
  417.2 14.1 %collective-permute-start.22 = (f32[19,34,18,1]{1,3,2,0:T(1,128)}, f32[19,34,18,1]{1,3,2,0:T(1,128)}, u32[]{:S(2)}, u32[]{:S(2)}) collective-permute-start(f32[19,34,18,1]{1,3,2,0:T(1,128)} %copy.157), channel_id=1, source_target_pairs={{0,1},{2,3},{4,5},{6,7},{8,9},{10,11},{12,13},{14,15},{16,17},{18,... | collective-permute-start | bytes 139544 | tf_op jit(solution)/shard_map/ppermute | solution.py:54
  424.5 13.3 %collective-permute-start.23 = (f32[19,34,18,1]{1,3,2,0:T(1,128)}, f32[19,34,18,1]{1,3,2,0:T(1,128)}, u32[]{:S(2)}, u32[]{:S(2)}) collective-permute-start(f32[19,34,18,1]{1,3,2,0:T(1,128)} %copy.158), channel_id=1, source_target_pairs={{1,0},{3,2},{5,4},{7,6},{9,8},{11,10},{13,12},{15,14},{17,16},{19,... | collective-permute-start | bytes 139544 | tf_op jit(solution)/shard_map/ppermute | solution.py:55
  (59 other events, 280.1 us)
where the time goes:
time: 478 us; the launch traced here: 469 us
  local copies, waits for them, and re-layouts  280 us (59%)
  other arithmetic  78.5 us (16%)
  starting transfers between devices  65.6 us (14%)
  waiting for transfers between devices  42.4 us (9%)
    slice x10, local copies, waits for them, and re-layouts, moment(): summed = summed - lattice[member]  38 us
    squeeze x18, local copies, waits for them, and re-layouts, moment(): summed = summed + lattice[member]  36.6 us
    squeeze x18, local copies, waits for them, and re-layouts, moment(): summed = summed - lattice[member]  36.5 us
    concatenate x5, other arithmetic, with_halo(): shard = jnp.concatenate([before, shard, after], axis=dim)  32 us
    unnamed x54, other arithmetic  28.2 us
    ppermute x9, waiting for transfers between devices, with_halo(): after = lax.ppermute(first, axis, down)  27.8 us
    slice x8, local copies, waits for them, and re-layouts, with_halo(): last = lax.slice_in_dim(shard, length - width, length, axis=dim)  25.8 us
    ppermute x9, starting transfers between devices, with_halo(): after = lax.ppermute(first, axis, down)  25.4 us
  transfers between devices with their start and end apart: 24, of which 11 were waited for; matrix products, arithmetic and copies ran while one was open for 22% of the time, Pallas kernels for 0%

commit v1 on v0

v1 whole, which is shorter than its diff:
```python
import functools

import jax
import jax.numpy as jnp
from jax import lax
from jax.experimental import pallas as pl
from jax.experimental.pallas import tpu as pltpu
from jax.sharding import PartitionSpec as P

EDGE = 16
BXD = 2
BYD = 1
BZD = 4
MOVE_CAP = 2

VELOCITIES = (
    (0, 0, 0),
    (1, 0, 0),
    (-1, 0, 0),
    (0, 1, 0),
    (0, -1, 0),
    (0, 0, 1),
    (0, 0, -1),
    (1, 1, 0),
    (-1, -1, 0),
    (1, -1, 0),
    (-1, 1, 0),
    (1, 0, 1),
    (-1, 0, -1),
    (1, 0, -1),
    (-1, 0, 1),
    (0, 1, 1),
    (0, -1, -1),
    (0, 1, -1),
    (0, -1, 1),
)
WEIGHTS = (1.0 / 3.0,) + (1.0 / 18.0,) * 6 + (1.0 / 36.0,) * 12
OPPOSITE = (0, 2, 1, 4, 3, 6, 5, 8, 7, 10, 9, 12, 11, 14, 13, 16, 15, 18, 17)
OMEGA_EVEN = 1.25
OMEGA_ODD = 1.0 / 1.125

POPS = 19
PLANES = 20
LANE = 128
TILES = EDGE**3 // LANE
BLOCK = PLANES * TILES
YLO = LANE // EDGE
SLAB = 4
SENT_SLABS = MOVE_CAP * BLOCK
SENT_META = SENT_SLABS + BZD * PLANES * SLAB
SENT_ROWS = SENT_META + 8
LAYERS = BXD + 2
ZGROUPS = 3
ZROWS = ZGROUPS * TILES
ZMETA = LAYERS * ZROWS
DIAG = ZROWS + ZGROUPS * SLAB

SPAN_X = BXD * EDGE
SPAN_Y = BYD * EDGE
SPAN_Z = BZD * EDGE
PITCH = SPAN_Y + 8
FIRST = 8
FIELD = (SPAN_X + 4) * PITCH + 16
EXT_X = SPAN_X + 4
EXT_Z = SPAN_Z + 2
RIM_UP = tuple(i for i in range(POPS) if VELOCITIES[i][1] == 1)
RIM_DOWN = tuple(i for i in range(POPS) if VELOCITIES[i][1] == -1)
RIM = POPS + len(RIM_UP)
RIM_BLOCKS = -(-RIM * EXT_Z // LANE)
RIM_ROWS = RIM_BLOCKS * EXT_X + 4
GRID_X = 48

ROTOR = -1.0e30
OUTSIDE = -2.0e30
WALL_BELOW = -1.0e20
OUT_BELOW = -1.5e30

VMEM = pltpu.VMEM
SMEM = pltpu.SMEM


def lanes():
    return lax.broadcasted_iota(jnp.int32, (8, LANE), 1)


def collide(f):
    even = [None] * POPS
    odd = [None] * POPS
    for i in range(1, POPS, 2):
        even[i] = f[i] + f[i + 1]
        odd[i] = f[i] - f[i + 1]
    density = f[0]
    for i in range(1, POPS, 2):
        density = density + even[i]
    flow = []
    for axis in range(3):
        total = None
        for i in range(1, POPS, 2):
            sign = VELOCITIES[i][axis]
            if sign == 0:
                continue
            if total is None:
                total = odd[i] if sign == 1 else -odd[i]
            else:
                total = total + odd[i] if sign == 1 else total - odd[i]
        flow.append(total)
    inverse = 1.0 / density
    velocity = [part * inverse for part in flow]
    square = velocity[0] * velocity[0] + velocity[1] * velocity[1] + velocity[2] * velocity[2]
    base = density * (1.0 - 1.5 * square)
    post = [None] * POPS
    post[0] = (1.0 - OMEGA_EVEN) * f[0] + (OMEGA_EVEN * WEIGHTS[0]) * base
    shared = {}
    for weight in (WEIGHTS[1], WEIGHTS[7]):
        shared[weight] = ((OMEGA_EVEN * weight) * base, (OMEGA_EVEN * weight * 4.5) * density,
                          (OMEGA_ODD * weight * 3.0) * density)
    for i in range(1, POPS, 2):
        projected = None
        for axis in range(3):
            sign = VELOCITIES[i][axis]
            if sign == 0:
                continue
            if projected is None:
                projected = velocity[axis] if sign == 1 else -velocity[axis]
            else:
                projected = projected + velocity[axis] if sign == 1 else projected - velocity[axis]
        low, curve, slope = shared[WEIGHTS[i]]
        even_part = (0.5 - 0.5 * OMEGA_EVEN) * even[i] + (low + curve * (projected * projected))
        odd_part = (0.5 - 0.5 * OMEGA_ODD) * odd[i] + slope * projected
        post[i] = even_part + odd_part
        post[i + 1] = even_part - odd_part
    return post, density


def pushes(density, drift_y, drift_z):
    along_y = density * drift_y
    along_z = density * drift_z
    out = [None] * POPS
    for i in range(1, POPS):
        _, step_y, step_z = VELOCITIES[i]
        total = None
        for sign, part in ((step_y, along_y), (step_z, along_z)):
            if sign == 0:
                continue
            if total is None:
                total = part if sign == 1 else -part
            else:
                total = total + part if sign == 1 else total - part
        if total is not None:
            out[i] = (6.0 * WEIGHTS[i]) * total
    return out


def streamed(pull, own, density, drift_y, drift_z):
    push = pushes(density, drift_y, drift_z)
    out = [own(0)]
    for i in range(1, POPS):
        pulled = pull(i)
        bounced = own(OPPOSITE[i])
        blocked = pulled < WALL_BELOW
        if push[i] is not None:
            bounced = jnp.where(pulled < OUT_BELOW, bounced, bounced + push[i])
        out.append(jnp.where(blocked, bounced, pulled))
    return out


def place():
    return lax.axis_index("stream"), lax.axis_index("cy"), lax.axis_index("cz")


def slot_of(pos, row, layer, column_z):
    slot = (pos[row, 0] - (layer * BXD - 1)) * BZD + (pos[row, 2] - column_z * BZD)
    return jnp.clip(slot, 0, LAYERS * BZD - 1)


def fill_table(pos, table):
    layer, _, column_z = place()
    for entry in range(LAYERS * BZD):
        table[entry] = -1
    for row in range(pos.shape[0]):

        @pl.when(pos[row, 0] >= 0)
        def _(row=row):
            table[slot_of(pos, row, layer, column_z)] = row


def spread_marks(marks, dense):
    rows = marks.shape[0]
    for first in range(0, rows, 8):
        size = min(8, rows - first)
        for tile in range(TILES):
            value = marks[first : first + size, tile * LANE : (tile + 1) * LANE].astype(jnp.float32)
            dense[pl.ds(first * TILES + tile, size, stride=TILES), :] = value


def pack_stream(pos, marks, pops, up, down, table, dense, blocks, slabs, sems):
    fill_table(pos, table)
    count = 0
    for row in range(pos.shape[0]):
        count = count + jnp.where(pos[row, 0] >= 0, 1, 0)
    last = jnp.clip(count - MOVE_CAP, 0, pos.shape[0] - MOVE_CAP)
    sources = [last, last + 1, 0, 1]
    copies = []
    for n, row in enumerate(sources):
        copies.append(pltpu.make_async_copy(pops.at[row], blocks.at[n], sems.at[n]))
    slab_rows = []
    for side in range(2):
        for bz in range(BZD):
            row = jnp.maximum(table[(2 - side) * BZD + bz], 0)
            n = side * BZD + bz
            first = (TILES - SLAB) * LANE if side == 0 else 0
            slab_rows.append(row)
            copies.append(
                pltpu.make_async_copy(
                    pops.at[row, :, pl.ds(first, SLAB * LANE)], slabs.at[n], sems.at[4 + n]
                )
            )
    for copy in copies:
        copy.start()
    spread_marks(marks, dense)
    for side, out in enumerate((up, down)):
        for j in range(MOVE_CAP):
            row = sources[side * MOVE_CAP + j]
            out[pl.ds(j * BLOCK + POPS * TILES, TILES), :] = dense[pl.ds(row * TILES, TILES), :]
            for part, column in ((0, 0), (1, 2)):
                value = jnp.full((1, LANE), pos[row, column], jnp.int32).astype(jnp.float32)
                out[pl.ds(SENT_META + 2 * j + part, 1), :] = value
        for bz in range(BZD):
            row = slab_rows[side * BZD + bz]
            first = TILES - SLAB if side == 0 else 0
            target = SENT_SLABS + (bz * PLANES + POPS) * SLAB
            out[pl.ds(target, SLAB), :] = dense[pl.ds(row * TILES + first, SLAB), :]
    for side, out in enumerate((up, down)):
        for j in range(MOVE_CAP):
            copies[side * MOVE_CAP + j].wait()
            for group, size in ((0, 8), (8, 8), (16, 3)):
                for tile in range(TILES):
                    value = blocks[side * MOVE_CAP + j, group : group + size, tile * LANE : (tile + 1) * LANE]
                    out[pl.ds(j * BLOCK + group * TILES + tile, size, stride=TILES), :] = value
        for bz in range(BZD):
            n = side * BZD + bz
            copies[4 + n].wait()
            for group, size in ((0, 8), (8, 8), (16, 3)):
                for q in range(SLAB):
                    value = slabs[n, group : group + size, q * LANE : (q + 1) * LANE]
                    target = SENT_SLABS + (bz * PLANES + group) * SLAB + q
                    out[pl.ds(target, size, stride=SLAB), :] = value


def pack_own(pos, marks, pops, own, zpack, zup, zdown, dense, stage, sems):
    layer, _, column_z = place()
    rows = pos.shape[0]
    copies = [pltpu.make_async_copy(pops.at[r], stage.at[r], sems.at[r]) for r in range(rows)]
    for copy in copies:
        copy.start()
    spread_marks(marks, dense)

    def settle(row, carry):
        pltpu.make_async_copy(pops.at[row], stage.at[row], sems.at[row]).wait()

        @pl.when(pos[row, 0] >= 0)
        def _():
            base = slot_of(pos, row, layer, column_z) * BLOCK
            for tile in range(TILES):
                for group, size in ((0, 8), (8, 8), (16, 3)):
                    value = stage[row, group : group + size, tile * LANE : (tile + 1) * LANE]
                    own[pl.ds(base + group * TILES + tile, size, stride=TILES), :] = value
            own[pl.ds(base + POPS * TILES, TILES), :] = dense[pl.ds(row * TILES, TILES), :]

        return carry

    lax.fori_loop(0, rows, settle, 0)
    edge_bz = jnp.where(column_z == 0, BZD - 1, 0)
    first_c = jnp.where(column_z == 0, EDGE - 2, 0)
    spot = (lanes() % EDGE) // 2
    for held in range(LAYERS):
        base = (held * BZD + edge_bz) * BLOCK
        for group in range(ZGROUPS):
            for part in range(TILES // 8):
                total = jnp.zeros((8, LANE), jnp.float32)
                for k in range(min(8, PLANES - group * 8)):
                    value = own[pl.ds(base + (group * 8 + k) * TILES + part * 8, 8), :]
                    value = pltpu.roll(value, (2 * k - first_c + LANE) % LANE, 1)
                    total = jnp.where(spot == k, value, total)
                zpack[pl.ds(held * ZROWS + group * TILES + part * 8, 8), :] = total
    present = [jnp.int32(0)] * LAYERS
    for row in range(rows):
        slot = slot_of(pos, row, layer, column_z)
        for held in range(LAYERS):
            hit = (pos[row, 0] >= 0) & (slot == held * BZD + edge_bz)
            present[held] = jnp.where(hit, 1, present[held])
    sublane = lax.broadcasted_iota(jnp.int32, (8, LANE), 0)
    flags = jnp.zeros((8, LANE), jnp.int32)
    for held in range(LAYERS):
        flags = jnp.where(sublane == held, present[held], flags)
    zpack[pl.ds(ZMETA, 8), :] = flags.astype(jnp.float32)
    zup[pl.ds(0, ZROWS), :] = zpack[pl.ds(3 * ZROWS, ZROWS), :]
    zdown[pl.ds(0, ZROWS), :] = zpack[pl.ds(0, ZROWS), :]
    for group in range(ZGROUPS):
        target = pl.ds(ZROWS + group * SLAB, SLAB)
        zup[target, :] = zpack[pl.ds(2 * ZROWS + group * TILES + TILES - SLAB, SLAB), :]
        zdown[target, :] = zpack[pl.ds(ZROWS + group * TILES, SLAB), :]


def gathered(load, zload, ylo, column_z):
    lane = lanes()
    parts = [load(bz) for bz in range(BZD)]
    rows = parts[0].shape[0]
    lane = lane[:rows]
    total = None
    for bz in range(BZD):
        shift = (bz * EDGE - ylo * EDGE) % LANE
        value = pltpu.roll(parts[bz], shift, 1) if shift else parts[bz]
        total = value if total is None else jnp.where(lane // EDGE == bz, value, total)
    zvalue, spot = zload
    goal = jnp.where(column_z == 0, SPAN_Z, LANE - 2)
    zvalue = pltpu.roll(zvalue, (goal - (ylo * EDGE + 2 * spot) + LANE) % LANE, 1)
    return jnp.where(lane >= SPAN_Z, zvalue, total)


def inside_lanes(rows, column_z):
    lane = lanes()[:rows]
    low = (column_z == 0) & (lane >= SPAN_Z) & (lane < SPAN_Z + 2)
    high = (column_z != 0) & (lane >= LANE - 2)
    return (lane < SPAN_Z) | low | high


def marked(post, mark, inside):
    flag = jnp.where(inside, jnp.where(mark > 0.5, ROTOR, 0.0), OUTSIDE)
    wall = flag < WALL_BELOW
    return [jnp.where(wall, flag, value) for value in post]


def chunk_values(own, edge, zall, zedge, chunk, yhi, ylo, column_z):
    out = []
    for plane in range(PLANES):
        group, spot = plane // 8, plane % 8
        if chunk is None:

            def load(bz):
                return edge[pl.ds((bz * PLANES + plane) * 8 + yhi, 4, stride=2), :]

            zvalue = zedge[pl.ds(group * 8 + yhi, 4, stride=2), :]
        else:
            held, half = 1 + chunk // 2, chunk % 2

            def load(bz):
                base = (held * BZD + bz) * BLOCK + plane * TILES + half * EDGE + yhi
                return own[pl.ds(base, 8, stride=2), :]

            zvalue = zall[pl.ds(held * ZROWS + group * TILES + half * EDGE + yhi, 8, stride=2), :]
        out.append(gathered(load, (zvalue, spot), ylo, column_z))
    return out


def halo_x_inside(layer, layers):
    row = lax.broadcasted_iota(jnp.int32, (4, LANE), 0)
    low = (row < 2) & (layer > 0)
    high = (row >= 2) & (layer < layers - 1)
    return low | high


def settle_rim(layers, pos, up, down, zin, zup, zdown, own_in, own, edge, zall, zedge, rim_up, rim_down, post_up, post_down):
    del own_in
    layer, _, column_z = place()
    for arrived in (up, down):
        for j in range(MOVE_CAP):
            bx = arrived[pl.ds(SENT_META + 2 * j, 1), :].astype(jnp.int32)
            bz = arrived[pl.ds(SENT_META + 2 * j + 1, 1), :].astype(jnp.int32)
            code = (bx - layer * BXD) * BZD + (bz - column_z * BZD)
            mine = (bx >= layer * BXD) & (bx < (layer + 1) * BXD)
            first = layer == 0 if arrived is up else layer == layers - 1
            code = jnp.max(jnp.where(mine, code, -1))

            @pl.when((code >= 0) & jnp.logical_not(first))
            def _(arrived=arrived, j=j, code=code):
                base = (jnp.clip(code, 0, BXD * BZD - 1) + BZD) * BLOCK

                def move(n, carry):
                    for k in range(4):
                        rows = n * 32 + 8 * k
                        own[pl.ds(base + rows, 8), :] = arrived[pl.ds(j * BLOCK + rows, 8), :]
                    return carry

                lax.fori_loop(0, BLOCK // 32, move, 0)

    for side, arrived in enumerate((up, down)):
        for bz in range(BZD):
            here = jnp.int32(0)
            goal = (0 if side == 0 else LAYERS - 1) * BZD + bz
            for row in range(pos.shape[0]):
                hit = (pos[row, 0] >= 0) & (slot_of(pos, row, layer, column_z) == goal)
                here = jnp.where(hit, 1, here)
            first = TILES - SLAB if side == 0 else 0
            for plane in range(PLANES):
                mine = own[pl.ds(goal * BLOCK + plane * TILES + first, SLAB), :]
                other = arrived[pl.ds(SENT_SLABS + (bz * PLANES + plane) * SLAB, SLAB), :]
                edge[pl.ds((bz * PLANES + plane) * 8 + side * SLAB, SLAB), :] = jnp.where(here == 1, mine, other)
    for held in range(LAYERS):
        flag = zin[pl.ds(ZMETA + held, 1), :] > 0.5
        for group in range(ZGROUPS):
            if held == 1 or held == 2:
                for part in range(TILES // 8):
                    rows = pl.ds(held * ZROWS + group * TILES + part * 8, 8)
                    source = zup if held == 1 else zdown
                    other = source[pl.ds(group * TILES + part * 8, 8), :]
                    zall[rows, :] = jnp.where(flag, zin[rows, :], other)
            else:
                side = 0 if held == 0 else 1
                source = zup if held == 0 else zdown
                first = TILES - SLAB if held == 0 else 0
                mine = zin[pl.ds(held * ZROWS + group * TILES + first, SLAB), :]
                other = source[pl.ds(ZROWS + group * SLAB, SLAB), :]
                zedge[pl.ds(group * 8 + side * SLAB, SLAB), :] = jnp.where(flag, mine, other)
    for chunk in (0, 1, 2, 3, None):
        for y in (0, 1, SPAN_Y - 2, SPAN_Y - 1):
            values = chunk_values(own, edge, zall, zedge, chunk, y // YLO, y % YLO, column_z)
            post, _ = collide(values[:POPS])
            rows = values[0].shape[0]
            inside = inside_lanes(rows, column_z)
            if chunk is None:
                inside = inside & halo_x_inside(layer, layers)
            post = marked(post, values[POPS], inside)
            target = post_down if y < 2 else post_up
            rim = RIM_DOWN if y < 2 else RIM_UP
            if y in (0, SPAN_Y - 1):
                pairs = [(i, i) for i in range(POPS)]
            else:
                pairs = [(POPS + n, i) for n, i in enumerate(rim)]
            for plane, i in pairs:
                if chunk is None:
                    target[pl.ds(plane * GRID_X, 2), :] = post[i][:2]
                    target[pl.ds(plane * GRID_X + EXT_X - 2, 2), :] = post[i][2:]
                else:
                    target[pl.ds(plane * GRID_X + 2 + 8 * chunk, 8), :] = post[i]
    lane = lanes()
    for source, target in ((post_up, rim_up), (post_down, rim_down)):
        for chunk in range(5):
            size = min(8, EXT_X - 8 * chunk)
            for block in range(RIM_BLOCKS):
                total = jnp.zeros((8, LANE), jnp.float32)
                for plane in range(RIM):
                    begin = plane * EXT_Z - block * LANE
                    if begin >= LANE or begin + EXT_Z <= 0:
                        continue
                    value = source[pl.ds(plane * GRID_X + 8 * chunk, 8), :]
                    value = pltpu.roll(value, (begin + LANE + 2 * column_z) % LANE, 1)
                    total = jnp.where((lane >= begin) & (lane < begin + EXT_Z), value, total)
                target[pl.ds(block * EXT_X + 8 * chunk, size), :] = total[:size]


def settle_all(layers, own, edge, zall, zedge, field, start, density):
    layer, _, column_z = place()

    def halves(yhi, carry):
        def chunks(chunk, carry):
            held = 1 + chunk // 2
            half = chunk % 2
            for ylo in range(YLO):
                values = []
                for plane in range(PLANES):
                    group, spot = plane // 8, plane % 8

                    def load(bz):
                        base = (held * BZD + bz) * BLOCK + plane * TILES + half * EDGE + yhi
                        return own[pl.ds(base, 8, stride=2), :]

                    zrow = held * ZROWS + group * TILES + half * EDGE + yhi
                    zvalue = zall[pl.ds(zrow, 8, stride=2), :]
                    values.append(gathered(load, (zvalue, spot), ylo, column_z))
                post, rho = collide(values[:POPS])
                post = marked(post, values[POPS], inside_lanes(8, column_z))
                row = (8 * chunk + 2) * PITCH + FIRST + YLO * yhi + ylo
                for i in range(POPS):
                    field[pl.ds(i * FIELD + row, 8, stride=PITCH), :] = post[i]
                    start[pl.ds((i * SPAN_X + 8 * chunk) * SPAN_Y + YLO * yhi + ylo, 8, stride=SPAN_Y), :] = values[i]
                density[pl.ds(row, 8, stride=PITCH), :] = rho
            return carry

        lax.fori_loop(0, SPAN_X // 8, chunks, 0)
        for ylo in range(YLO):
            values = []
            for plane in range(PLANES):
                group, spot = plane // 8, plane % 8

                def load(bz):
                    return edge[pl.ds((bz * PLANES + plane) * 8 + yhi, 4, stride=2), :]

                zvalue = zedge[pl.ds(group * 8 + yhi, 4, stride=2), :]
                values.append(gathered(load, (zvalue, spot), ylo, column_z))
            post, rho = collide(values[:POPS])
            inside = inside_lanes(4, column_z) & halo_x_inside(layer, layers)
            post = marked(post, values[POPS], inside)
            for first, side in ((0, 0), (EXT_X - 2, 2)):
                row = first * PITCH + FIRST + YLO * yhi + ylo
                for i in range(POPS):
                    field[pl.ds(i * FIELD + row, 2, stride=PITCH), :] = post[i][side : side + 2]
                density[pl.ds(row, 2, stride=PITCH), :] = rho[side : side + 2]
        return carry

    lax.fori_loop(0, SPAN_Y // YLO, halves, 0)


def finish(columns, depth, rim_low, rim_high, field_in, start, density, out, field, later, thick, low, high):
    del field_in
    _, column_y, column_z = place()
    lane = lanes()
    total_y = SPAN_Y * columns
    total_z = SPAN_Z * depth
    spin = 0.2 / (total_y + total_z)
    centre_y = (total_y - 1) / 2.0
    centre_z = (total_z - 1) / 2.0
    here_z = jnp.where(lane < SPAN_Z + 8, lane, lane - LANE) + column_z * SPAN_Z
    drift_y = -spin * (here_z.astype(jnp.float32) - centre_z)
    flat = (lane + 2 * column_z) % LANE
    for source, target, there in ((rim_low, low, column_y > 0), (rim_high, high, column_y < columns - 1)):
        for chunk in range(5):
            size = min(8, EXT_X - 8 * chunk)
            blocks = [source[pl.ds(block * EXT_X + 8 * chunk, 8), :] for block in range(RIM_BLOCKS)]
            for plane in range(RIM):
                block, begin = divmod(plane * EXT_Z, LANE)
                shift = (2 * LANE - begin - 2 * column_z) % LANE
                value = pltpu.roll(blocks[block], shift, 1)
                if begin + EXT_Z > LANE:
                    value = jnp.where(flat < LANE - begin, value, pltpu.roll(blocks[block + 1], shift, 1))
                value = jnp.where((flat < EXT_Z) & there, value, OUTSIDE)
                target[pl.ds(plane * GRID_X + 8 * chunk, 8), :] = value
    for source, y, rim in ((low, -1, RIM_UP), (high, SPAN_Y, RIM_DOWN)):
        for i in rim:
            for chunk in range(5):
                size = min(8, EXT_X - 8 * chunk)
                row = i * FIELD + 8 * chunk * PITCH + FIRST + y
                field[pl.ds(row, size, stride=PITCH), :] = source[pl.ds(i * GRID_X + 8 * chunk, size), :]

    def turned(value, step_z):
        return pltpu.roll(value, step_z % LANE, 1) if step_z else value

    for source, y, rim in ((low, -1, RIM_UP), (high, SPAN_Y, RIM_DOWN)):
        outer = {i: POPS + n for n, i in enumerate(rim)}
        toward = VELOCITIES[rim[0]][1]
        drift_z = spin * ((column_y * SPAN_Y + y).astype(jnp.float32) - centre_y)
        for chunk in range(5):
            first = 1 + 8 * chunk
            size = min(8, EXT_X - 1 - first)

            def pull(i):
                step_x, step_y, step_z = VELOCITIES[i]
                if step_y == toward:
                    value = source[pl.ds(outer[i] * GRID_X + first - step_x, 8), :]
                elif step_y == 0:
                    value = source[pl.ds(i * GRID_X + first - step_x, 8), :]
                else:
                    row = i * FIELD + (first - step_x) * PITCH + FIRST + y - step_y
                    if size == 8:
                        value = field[pl.ds(row, 8, stride=PITCH), :]
                    else:
                        value = field[pl.ds(row, size, stride=PITCH), :]
                if size < 8 and value.shape[0] == 8:
                    value = value[:size]
                return turned(value, step_z)

            posts = [source[pl.ds(i * GRID_X + first, 8), :][:size] for i in range(POPS)]
            rho = posts[0]
            for i in range(1, POPS):
                rho = rho + posts[i]
            values = streamed(pull, lambda i: posts[i], rho, drift_y[:size], drift_z)
            post, _ = collide(values)
            wall = posts[0] < WALL_BELOW
            for i in rim:
                row = i * FIELD + first * PITCH + FIRST + y
                later[pl.ds(row, size, stride=PITCH), :] = jnp.where(wall, posts[0], post[i])

    sublane = lax.broadcasted_iota(jnp.int32, (8, LANE), 0)
    drifts = []
    for half in range(SPAN_Y // 8):
        here_y = sublane + (column_y * SPAN_Y + 8 * half)
        drifts.append(spin * (here_y.astype(jnp.float32) - centre_y))

    def first_step(x, carry):
        for half in range(SPAN_Y // 8):
            base = x * PITCH + FIRST + 8 * half

            def pull(i):
                step_x, step_y, step_z = VELOCITIES[i]
                return turned(field[pl.ds(i * FIELD + base - step_x * PITCH - step_y, 8), :], step_z)

            def own(i):
                return field[pl.ds(i * FIELD + base, 8), :]

            rho = density[pl.ds(base, 8), :]
            values = streamed(pull, own, rho, drift_y, drifts[half])
            post, rho = collide(values)
            flag = own(0)
            wall = flag < WALL_BELOW
            for i in range(POPS):
                later[pl.ds(i * FIELD + base, 8), :] = jnp.where(wall, flag, post[i])
            thick[pl.ds(base, 8), :] = rho
        return carry

    lax.fori_loop(1, EXT_X - 1, first_step, 0)

    def second_step(x, carry):
        for half in range(SPAN_Y // 8):
            base = (x + 2) * PITCH + FIRST + 8 * half

            def pull(i):
                step_x, step_y, step_z = VELOCITIES[i]
                return turned(later[pl.ds(i * FIELD + base - step_x * PITCH - step_y, 8), :], step_z)

            def own(i):
                return later[pl.ds(i * FIELD + base, 8), :]

            values = streamed(pull, own, thick[pl.ds(base, 8), :], drift_y, drifts[half])
            wall = own(0) < WALL_BELOW
            for i in range(POPS):
                first = start[pl.ds((i * SPAN_X + x) * SPAN_Y + 8 * half, 8), :]
                value = jnp.where(wall, first, values[i])
                out[i, x, pl.ds(8 * half, 8), :] = value[:, :SPAN_Z]
        return carry

    lax.fori_loop(0, SPAN_X, second_step, 0)


def rows_of(count):
    return jax.ShapeDtypeStruct((count, LANE), jnp.float32)


def kept(count):
    return VMEM((count, LANE), jnp.float32)


def params(mib):
    return pltpu.CompilerParams(vmem_limit_bytes=mib * 2**20)


def shards(populations, solid_cells, block_pos):
    layers = lax.axis_size("stream")
    columns = lax.axis_size("cy")
    depth = lax.axis_size("cz")
    rows = block_pos.shape[0]
    smem = pl.BlockSpec(memory_space=SMEM)
    vmem = pl.BlockSpec(memory_space=VMEM)
    anywhere = pl.BlockSpec(memory_space=pl.ANY)

    send_up, send_down = pl.pallas_call(
        pack_stream,
        out_shape=(rows_of(SENT_ROWS), rows_of(SENT_ROWS)),
        in_specs=[smem, vmem, anywhere],
        out_specs=(vmem, vmem),
        scratch_shapes=[
            SMEM((LAYERS * BZD,), jnp.int32),
            VMEM((rows * TILES, LANE), jnp.float32),
            VMEM((2 * MOVE_CAP, POPS, EDGE**3), jnp.float32),
            VMEM((2 * BZD, POPS, SLAB * LANE), jnp.float32),
            pltpu.SemaphoreType.DMA((2 * MOVE_CAP + 2 * BZD,)),
        ],
        compiler_params=params(24),
        name="pack_stream",
    )(block_pos, solid_cells, populations)
    up = [(i, i + 1) for i in range(layers - 1)]
    down = [(i + 1, i) for i in range(layers - 1)]
    from_low = lax.ppermute(send_up, "stream", up)
    from_high = lax.ppermute(send_down, "stream", down)

    own, zpack, zsend_up, zsend_down = pl.pallas_call(
        pack_own,
        out_shape=(kept(LAYERS * BZD * BLOCK), rows_of(ZMETA + 8), rows_of(DIAG), rows_of(DIAG)),
        in_specs=[smem, vmem, anywhere],
        out_specs=(vmem,) * 4,
        scratch_shapes=[
            VMEM((rows * TILES, LANE), jnp.float32),
            VMEM((rows, POPS, EDGE**3), jnp.float32),
            pltpu.SemaphoreType.DMA((rows,)),
        ],
        compiler_params=params(24),
        name="pack_own",
    )(block_pos, solid_cells, populations)
    swap = [(i, depth - 1 - i) for i in range(depth)]
    zin = lax.ppermute(zpack, "cz", swap)
    zup_pairs = [(s * depth + c, t * depth + d) for s, t in up for c, d in swap]
    zdown_pairs = [(s * depth + c, t * depth + d) for s, t in down for c, d in swap]
    z_low = lax.ppermute(zsend_up, ("stream", "cz"), zup_pairs)
    z_high = lax.ppermute(zsend_down, ("stream", "cz"), zdown_pairs)

    own, edge, zall, zedge, rim_up, rim_down = pl.pallas_call(
        functools.partial(settle_rim, layers),
        out_shape=(
            kept(LAYERS * BZD * BLOCK),
            kept(BZD * PLANES * 8),
            kept(LAYERS * ZROWS),
            kept(ZGROUPS * 8),
            rows_of(RIM_ROWS),
            rows_of(RIM_ROWS),
        ),
        in_specs=[smem] + [vmem] * 6,
        out_specs=(vmem,) * 6,
        scratch_shapes=[
            VMEM((RIM * GRID_X, LANE), jnp.float32),
            VMEM((RIM * GRID_X, LANE), jnp.float32),
        ],
        input_output_aliases={6: 0},
        compiler_params=params(24),
        name="settle_rim",
    )(block_pos, from_low, from_high, zin, z_low, z_high, own)
    cy_up = [(i, i + 1) for i in range(columns - 1)]
    cy_down = [(i + 1, i) for i in range(columns - 1)]
    rim_low = lax.ppermute(rim_up, "cy", cy_up)
    rim_high = lax.ppermute(rim_down, "cy", cy_down)

    field, start, density = pl.pallas_call(
        functools.partial(settle_all, layers),
        out_shape=(kept(POPS * FIELD), kept(POPS * SPAN_X * SPAN_Y), kept(FIELD)),
        in_specs=[vmem] * 4,
        out_specs=(vmem,) * 3,
        compiler_params=params(24),
        name="settle_all",
    )(own, edge, zall, zedge)

    out, _ = pl.pallas_call(
        functools.partial(finish, columns, depth),
        out_shape=(
            jax.ShapeDtypeStruct((POPS, SPAN_X, SPAN_Y, SPAN_Z), jnp.float32),
            kept(POPS * FIELD),
        ),
        in_specs=[vmem] * 5,
        out_specs=(vmem, vmem),
        scratch_shapes=[
            VMEM((POPS * FIELD, LANE), jnp.float32),
            VMEM((FIELD, LANE), jnp.float32),
            VMEM((RIM * GRID_X, LANE), jnp.float32),
            VMEM((RIM * GRID_X, LANE), jnp.float32),
        ],
        input_output_aliases={2: 1},
        compiler_params=params(32),
        name="finish",
    )(rim_low, rim_high, field, start, density)
    return out


def solution(mesh):
    in_specs = (
        P(("stream", "cy", "cz"), None, None),
        P(("stream", "cy", "cz"), None),
        P(("stream", "cy", "cz"), None),
    )
    out_specs = P(None, "stream", "cy", "cz")
    return jax.shard_map(shards, mesh=mesh, in_specs=in_specs, out_specs=out_specs, check_vma=False)
```

time: 478 us -> 65.5 us (0.14)
  the two profiles are of different devices: /device:TPU:1 before, /device:TPU:0 now
where the time goes in v1:
time: 65.5 us; the launch traced here: 65.2 us
  Pallas kernels  33.8 us (52%)
  starting transfers between devices  15.4 us (24%)
  waiting for transfers between devices  11.8 us (18%)
  local copies, waits for them, and re-layouts  4.05 us (6%)
    pallas_call x1, Pallas kernels, shards(): pl.pallas_call(functools.partial(finish, columns, depth), out_shape=(jax....  10.7 us
    pallas_call x1, Pallas kernels, shards(): pl.pallas_call(functools.partial(settle_all, layers), out_shape=(kept(POP...  9.86 us
    ppermute x1, waiting for transfers between devices, shards(): z_low = lax.ppermute(zsend_up, ('stream', 'cz'), zup_pairs)  6.6 us
    pallas_call x1, Pallas kernels, shards(): pl.pallas_call(pack_own, out_shape=(kept(LAYERS * BZD * BLOCK), rows_of(Z...  6.4 us
    ppermute x1, starting transfers between devices, shards(): from_low = lax.ppermute(send_up, 'stream', up)  4.98 us
    pallas_call x1, Pallas kernels, shards(): pl.pallas_call(functools.partial(settle_rim, layers), out_shape=(kept(LAY...  4.1 us
    unnamed x5, local copies, waits for them, and re-layouts  4.05 us
    ppermute x1, starting transfers between devices, shards(): rim_low = lax.ppermute(rim_up, 'cy', cy_up)  3.41 us
  transfers between devices with their start and end apart: 7, of which 4 were waited for; matrix products, arithmetic and copies ran while one was open for 0% of the time, Pallas kernels for 25%

profile of v1, /device:TPU:0, one launch (start us, length us, event | category | flops | bytes accessed | tf_op | source)
XLA Modules:
  0.0 65.2 jit_solution(12757659755440172906)
XLA Ops:
  0.0 0.8 %copy.8.pos = s32[12,3]{1,0:T(8,128)S(1)} copy(s32[12,3]{0,1:T(4,128)} %param.5) | data formatting | bytes 288 | tf_op args[2]
  0.8 0.0 copy-start
  0.8 2.3 %copy-done = f32[12,19,4096]{2,1,0:T(8,128)S(1)} copy-done((f32[12,19,4096]{2,1,0:T(8,128)S(1)}, f32[12,19,4096]{2,1,0:T(8,128)}, u32[]{:S(2)}) %copy-start) | copy-done | bytes 3735576
  3.1 0.0 copy-start.1
  3.1 0.9 %copy-done.1 = s32[12,4096]{1,0:T(8,128)S(1)} copy-done((s32[12,4096]{1,0:T(8,128)S(1)}, s32[12,4096]{1,0:T(8,128)}, u32[]{:S(2)}) %copy-start.1) | copy-done | bytes 196632
  4.1 2.7 %pack_stream.1 = (f32[1608,128]{1,0:T(8,128)S(1)}, f32[1608,128]{1,0:T(8,128)S(1)}) custom-call(s32[12,3]{1,0:T(8,128)S(1)} %copy.8.pos, s32[12,4096]{1,0:T(8,128)S(1)} %copy-done.1, f32[12,19,4096]{2,1,0:T(8,128)S(1)} %copy-done), custom_call_target="tpu_custom_call" | custom-call | tf_op jit(solution)/shard_map/pack_stream/pallas_call | solution.py:645
  6.8 5.0 %collective-permute-start = (f32[1608,128]{1,0:T(8,128)S(1)}, f32[1608,128]{1,0:T(8,128)S(1)}, u32[]{:S(2)}, u32[]{:S(2)}) collective-permute-start(f32[1608,128]{1,0:T(8,128)S(1)} %get-tuple-element.21), channel_id=1, source_target_pairs={{0,8},{8,16},{16,24},{1,9},{9,17},{17,25},{2,10},{10,18},{18,26},{... | collective-permute-start | bytes 2469896 | tf_op jit(solution)/shard_map/ppermute | solution.py:662
  11.8 1.3 %collective-permute-start.1 = (f32[1608,128]{1,0:T(8,128)S(1)}, f32[1608,128]{1,0:T(8,128)S(1)}, u32[]{:S(2)}, u32[]{:S(2)}) collective-permute-start(f32[1608,128]{1,0:T(8,128)S(1)} %get-tuple-element.22), channel_id=1, source_target_pairs={{8,0},{16,8},{24,16},{9,1},{17,9},{25,17},{10,2},{18,10},{26,18},{... | collective-permute-start | bytes 2469896 | tf_op jit(solution)/shard_map/ppermute | solution.py:663
  13.1 6.4 %pack_own.1 = (f32[10240,128]{1,0:T(8,128)S(1)}, f32[392,128]{1,0:T(8,128)S(1)}, f32[108,128]{1,0:T(8,128)S(1)}, f32[108,128]{1,0:T(8,128)S(1)}) custom-call(s32[12,3]{1,0:T(8,128)S(1)} %copy.8.pos, s32[12,4096]{1,0:T(8,128)S(1)} %copy-done.1, f32[12,19,4096]{2,1,0:T(8,128)S(1)} %copy-done), custom_call_target="tpu_custom_call" | custom-call | tf_op jit(solution)/shard_map/pack_own/pallas_call | solution.py:665
  19.5 0.1 collective-permute-start.2
  19.5 3.0 %collective-permute-start.3 = (f32[108,128]{1,0:T(8,128)S(1)}, f32[108,128]{1,0:T(8,128)S(1)}, u32[]{:S(2)}, u32[]{:S(2)}) collective-permute-start(f32[108,128]{1,0:T(8,128)S(1)} %get-tuple-element.24), channel_id=1, source_target_pairs={{0,9},{1,8},{8,17},{9,16},{16,25},{17,24},{2,11},{3,10},{10,19},{1... | collective-permute-start | bytes 165896 | tf_op jit(solution)/shard_map/ppermute | solution.py:682
  22.6 1.3 %collective-permute-start.4 = (f32[108,128]{1,0:T(8,128)S(1)}, f32[108,128]{1,0:T(8,128)S(1)}, u32[]{:S(2)}, u32[]{:S(2)}) collective-permute-start(f32[108,128]{1,0:T(8,128)S(1)} %get-tuple-element.25), channel_id=1, source_target_pairs={{8,1},{9,0},{16,9},{17,8},{24,17},{25,16},{10,3},{11,2},{18,11},{1... | collective-permute-start | bytes 165896 | tf_op jit(solution)/shard_map/ppermute | solution.py:683
  23.9 6.6 %collective-permute-done.3.zup = f32[108,128]{1,0:T(8,128)S(1)} collective-permute-done((f32[108,128]{1,0:T(8,128)S(1)}, f32[108,128]{1,0:T(8,128)S(1)}, u32[]{:S(2)}, u32[]{:S(2)}) %collective-permute-start.3) | collective-permute-done | bytes 55328 | tf_op jit(solution)/shard_map/ppermute | solution.py:682
  30.5 2.7 %collective-permute-done.4.zdown = f32[108,128]{1,0:T(8,128)S(1)} collective-permute-done((f32[108,128]{1,0:T(8,128)S(1)}, f32[108,128]{1,0:T(8,128)S(1)}, u32[]{:S(2)}, u32[]{:S(2)}) %collective-permute-start.4) | collective-permute-done | bytes 55328 | tf_op jit(solution)/shard_map/ppermute | solution.py:683
  33.2 0.0 collective-permute-done.2.zin
  33.2 0.0 collective-permute-done.up
  33.2 0.8 %collective-permute-done.1.down = f32[1608,128]{1,0:T(8,128)S(1)} collective-permute-done((f32[1608,128]{1,0:T(8,128)S(1)}, f32[1608,128]{1,0:T(8,128)S(1)}, u32[]{:S(2)}, u32[]{:S(2)}) %collective-permute-start.1) | collective-permute-done | bytes 823328 | tf_op jit(solution)/shard_map/ppermute | solution.py:663
  34.1 4.1 %settle_rim.1 = (f32[10240,128]{1,0:T(8,128)S(1)}, f32[640,128]{1,0:T(8,128)S(1)}, f32[384,128]{1,0:T(8,128)S(1)}, f32[24,128]{1,0:T(8,128)S(1)}, f32[472,128]{1,0:T(8,128)S(1)}, /*index=5*/f32[472,128]{1,0:T(8,128)S(1)}) custom-call(s32[12,3]{1,0:T(8,128)S(1)} %copy.8.pos, ...), custom_call_target="tpu_custom_call", output_to_operand_aliasing={{0}: (6, {})} | custom-call | tf_op jit(solution)/shard_map/settle_rim/pallas_call | solution.py:685
  38.2 3.4 %collective-permute-start.5 = (f32[472,128]{1,0:T(8,128)S(1)}, f32[472,128]{1,0:T(8,128)S(1)}, u32[]{:S(2)}, u32[]{:S(2)}) collective-permute-start(f32[472,128]{1,0:T(8,128)S(1)} %get-tuple-element.27), channel_id=1, source_target_pairs={{0,2},{2,4},{4,6},{1,3},{3,5},{5,7},{8,10},{10,12},{12,14},{9,11},... | collective-permute-start | bytes 725000 | tf_op jit(solution)/shard_map/ppermute | solution.py:707
  41.6 1.3 %collective-permute-start.6 = (f32[472,128]{1,0:T(8,128)S(1)}, f32[472,128]{1,0:T(8,128)S(1)}, u32[]{:S(2)}, u32[]{:S(2)}) collective-permute-start(f32[472,128]{1,0:T(8,128)S(1)} %get-tuple-element.28), channel_id=1, source_target_pairs={{2,0},{4,2},{6,4},{3,1},{5,3},{7,5},{10,8},{12,10},{14,12},{11,9},... | collective-permute-start | bytes 725000 | tf_op jit(solution)/shard_map/ppermute | solution.py:708
  42.9 9.9 %settle_all.1 = (f32[16720,128]{1,0:T(8,128)S(1)}, f32[9728,128]{1,0:T(8,128)S(1)}, f32[880,128]{1,0:T(8,128)S(1)}) custom-call(f32[10240,128]{1,0:T(8,128)S(1)} %get-tuple-element.29.own, f32[640,128]{1,0:T(8,128)S(1)} %get-tuple-element.30.edge, f32[384,128]{1,0:T(8,128)S(1)} %get-tuple-element.31.zall, f32[24,128]{1,0:T(8,128)S(1)} %get-tuple-element.32.zedge), custom_call_target="tpu_custom_call" | custom-call | tf_op jit(solution)/shard_map/settle_all/pallas_call | solution.py:710
  52.7 0.0 collective-permute-done.5.rim_low
  52.8 1.7 %collective-permute-done.6.rim_high = f32[472,128]{1,0:T(8,128)S(1)} collective-permute-done((f32[472,128]{1,0:T(8,128)S(1)}, f32[472,128]{1,0:T(8,128)S(1)}, u32[]{:S(2)}, u32[]{:S(2)}) %collective-permute-start.6) | collective-permute-done | bytes 241696 | tf_op jit(solution)/shard_map/ppermute | solution.py:708
  54.4 10.7 %finish.1 = (f32[19,32,16,64]{3,2,1,0:T(8,128)}, f32[16720,128]{1,0:T(8,128)S(1)}) custom-call(f32[472,128]{1,0:T(8,128)S(1)} %collective-permute-done.5.rim_low, f32[472,128]{1,0:T(8,128)S(1)} %collective-permute-done.6.rim_high, f32[16720,128]{1,0:T(8,128)S(1)} %get-tuple-element.33.field_in, ...), custom_call_target="tpu_custom_call", output_to_operand_aliasing={{1}: (2, {})} | custom-call | tf_op jit(solution)/shard_map/finish/pallas_call | solution.py:719
Async XLA Ops:
  0.8 2.3 %copy-start = (f32[12,19,4096]{2,1,0:T(8,128)S(1)}, f32[12,19,4096]{2,1,0:T(8,128)}, u32[]{:S(2)}) copy-start(f32[12,19,4096]{2,1,0:T(8,128)} %pops.3) | copy-start | bytes 11206660
  3.1 0.9 %copy-start.1 = (s32[12,4096]{1,0:T(8,128)S(1)}, s32[12,4096]{1,0:T(8,128)}, u32[]{:S(2)}) copy-start(s32[12,4096]{1,0:T(8,128)} %marks.3) | copy-start | bytes 589828
  6.8 26.4 %collective-permute-start = (f32[1608,128]{1,0:T(8,128)S(1)}, f32[1608,128]{1,0:T(8,128)S(1)}, u32[]{:S(2)}, u32[]{:S(2)}) collective-permute-start(f32[1608,128]{1,0:T(8,128)S(1)} %get-tuple-element.21), channel_id=1, source_target_pairs={{0,8},{8,16},{16,24},{1,9},{9,17},{17,25},{2,10},{10,18},{18,26},{... | collective-permute-start | bytes 2469896 | tf_op jit(solution)/shard_map/ppermute | solution.py:662
  11.8 22.3 %collective-permute-start.1 = (f32[1608,128]{1,0:T(8,128)S(1)}, f32[1608,128]{1,0:T(8,128)S(1)}, u32[]{:S(2)}, u32[]{:S(2)}) collective-permute-start(f32[1608,128]{1,0:T(8,128)S(1)} %get-tuple-element.22), channel_id=1, source_target_pairs={{8,0},{16,8},{24,16},{9,1},{17,9},{25,17},{10,2},{18,10},{26,18},{... | collective-permute-start | bytes 2469896 | tf_op jit(solution)/shard_map/ppermute | solution.py:663
  19.5 13.7 %collective-permute-start.2 = (f32[392,128]{1,0:T(8,128)S(1)}, f32[392,128]{1,0:T(8,128)S(1)}, u32[]{:S(2)}, u32[]{:S(2)}) collective-permute-start(f32[392,128]{1,0:T(8,128)S(1)} %get-tuple-element.23), channel_id=1, source_target_pairs={{0,1},{1,0},{2,3},{3,2},{4,5},{5,4},{6,7},{7,6},{8,9},{9,8},{10,11... | collective-permute-start | bytes 602120 | tf_op jit(solution)/shard_map/ppermute | solution.py:679
  19.5 11.0 %collective-permute-start.3 = (f32[108,128]{1,0:T(8,128)S(1)}, f32[108,128]{1,0:T(8,128)S(1)}, u32[]{:S(2)}, u32[]{:S(2)}) collective-permute-start(f32[108,128]{1,0:T(8,128)S(1)} %get-tuple-element.24), channel_id=1, source_target_pairs={{0,9},{1,8},{8,17},{9,16},{16,25},{17,24},{2,11},{3,10},{10,19},{1... | collective-permute-start | bytes 165896 | tf_op jit(solution)/shard_map/ppermute | solution.py:682
  22.6 10.6 %collective-permute-start.4 = (f32[108,128]{1,0:T(8,128)S(1)}, f32[108,128]{1,0:T(8,128)S(1)}, u32[]{:S(2)}, u32[]{:S(2)}) collective-permute-start(f32[108,128]{1,0:T(8,128)S(1)} %get-tuple-element.25), channel_id=1, source_target_pairs={{8,1},{9,0},{16,9},{17,8},{24,17},{25,16},{10,3},{11,2},{18,11},{1... | collective-permute-start | bytes 165896 | tf_op jit(solution)/shard_map/ppermute | solution.py:683
  38.2 14.6 %collective-permute-start.5 = (f32[472,128]{1,0:T(8,128)S(1)}, f32[472,128]{1,0:T(8,128)S(1)}, u32[]{:S(2)}, u32[]{:S(2)}) collective-permute-start(f32[472,128]{1,0:T(8,128)S(1)} %get-tuple-element.27), channel_id=1, source_target_pairs={{0,2},{2,4},{4,6},{1,3},{3,5},{5,7},{8,10},{10,12},{12,14},{9,11},... | collective-permute-start | bytes 725000 | tf_op jit(solution)/shard_map/ppermute | solution.py:707
  41.6 12.8 %collective-permute-start.6 = (f32[472,128]{1,0:T(8,128)S(1)}, f32[472,128]{1,0:T(8,128)S(1)}, u32[]{:S(2)}, u32[]{:S(2)}) collective-permute-start(f32[472,128]{1,0:T(8,128)S(1)} %get-tuple-element.28), channel_id=1, source_target_pairs={{2,0},{4,2},{6,4},{3,1},{5,3},{7,5},{10,8},{12,10},{14,12},{11,9},... | collective-permute-start | bytes 725000 | tf_op jit(solution)/shard_map/ppermute | solution.py:708

commit v2 on v1

v2 whole, which is shorter than its diff:
```python
import functools

import jax
import jax.numpy as jnp
from jax import lax
from jax.experimental import pallas as pl
from jax.experimental.pallas import tpu as pltpu
from jax.sharding import PartitionSpec as P

EDGE = 16
BXD = 2
BYD = 1
BZD = 4
MOVE_CAP = 2

VELOCITIES = (
    (0, 0, 0),
    (1, 0, 0),
    (-1, 0, 0),
    (0, 1, 0),
    (0, -1, 0),
    (0, 0, 1),
    (0, 0, -1),
    (1, 1, 0),
    (-1, -1, 0),
    (1, -1, 0),
    (-1, 1, 0),
    (1, 0, 1),
    (-1, 0, -1),
    (1, 0, -1),
    (-1, 0, 1),
    (0, 1, 1),
    (0, -1, -1),
    (0, 1, -1),
    (0, -1, 1),
)
WEIGHTS = (1.0 / 3.0,) + (1.0 / 18.0,) * 6 + (1.0 / 36.0,) * 12
OPPOSITE = (0, 2, 1, 4, 3, 6, 5, 8, 7, 10, 9, 12, 11, 14, 13, 16, 15, 18, 17)
OMEGA_EVEN = 1.25
OMEGA_ODD = 1.0 / 1.125

POPS = 19
PLANES = 20
LANE = 128
TILES = EDGE**3 // LANE
BLOCK = PLANES * TILES
YLO = LANE // EDGE
SLAB = 4
SENT_SLABS = MOVE_CAP * BLOCK
LAYERS = BXD + 2
ZGROUPS = 3
ZROWS = ZGROUPS * TILES
ZMETA = LAYERS * ZROWS
DIAG = ZROWS + ZGROUPS * SLAB

SPAN_X = BXD * EDGE
SPAN_Y = BYD * EDGE
SPAN_Z = BZD * EDGE
PITCH = SPAN_Y + 8
FIRST = 8
FIELD = (SPAN_X + 4) * PITCH + 16
EXT_X = SPAN_X + 4
EXT_Z = SPAN_Z + 2
RIM_UP = tuple(i for i in range(POPS) if VELOCITIES[i][1] == 1)
RIM_DOWN = tuple(i for i in range(POPS) if VELOCITIES[i][1] == -1)
RIM = POPS + len(RIM_UP)
AHEAD = tuple(i for i in range(POPS) if VELOCITIES[i][0] == 1)
BACK = tuple(i for i in range(POPS) if VELOCITIES[i][0] == -1)
FACE = 2 * BZD
SENT_META = SENT_SLABS + RIM * FACE
SENT_ROWS = SENT_META + 8
RIM_BLOCKS = -(-RIM * EXT_Z // LANE)
RIM_ROWS = RIM_BLOCKS * EXT_X + 4
GRID_X = 48

ROTOR = -1.0e30
OUTSIDE = -2.0e30
WALL_BELOW = -1.0e20
OUT_BELOW = -1.5e30

VMEM = pltpu.VMEM
SMEM = pltpu.SMEM


def lanes():
    return lax.broadcasted_iota(jnp.int32, (8, LANE), 1)


def collide(f):
    even = [None] * POPS
    odd = [None] * POPS
    for i in range(1, POPS, 2):
        even[i] = f[i] + f[i + 1]
        odd[i] = f[i] - f[i + 1]
    density = f[0]
    for i in range(1, POPS, 2):
        density = density + even[i]
    flow = []
    for axis in range(3):
        total = None
        for i in range(1, POPS, 2):
            sign = VELOCITIES[i][axis]
            if sign == 0:
                continue
            if total is None:
                total = odd[i] if sign == 1 else -odd[i]
            else:
                total = total + odd[i] if sign == 1 else total - odd[i]
        flow.append(total)
    inverse = 1.0 / density
    velocity = [part * inverse for part in flow]
    square = velocity[0] * velocity[0] + velocity[1] * velocity[1] + velocity[2] * velocity[2]
    base = density * (1.0 - 1.5 * square)
    post = [None] * POPS
    post[0] = (1.0 - OMEGA_EVEN) * f[0] + (OMEGA_EVEN * WEIGHTS[0]) * base
    shared = {}
    for weight in (WEIGHTS[1], WEIGHTS[7]):
        shared[weight] = ((OMEGA_EVEN * weight) * base, (OMEGA_EVEN * weight * 4.5) * density,
                          (OMEGA_ODD * weight * 3.0) * density)
    for i in range(1, POPS, 2):
        projected = None
        for axis in range(3):
            sign = VELOCITIES[i][axis]
            if sign == 0:
                continue
            if projected is None:
                projected = velocity[axis] if sign == 1 else -velocity[axis]
            else:
                projected = projected + velocity[axis] if sign == 1 else projected - velocity[axis]
        low, curve, slope = shared[WEIGHTS[i]]
        even_part = (0.5 - 0.5 * OMEGA_EVEN) * even[i] + (low + curve * (projected * projected))
        odd_part = (0.5 - 0.5 * OMEGA_ODD) * odd[i] + slope * projected
        post[i] = even_part + odd_part
        post[i + 1] = even_part - odd_part
    return post, density


def pushes(density, drift_y, drift_z):
    along_y = density * drift_y
    along_z = density * drift_z
    out = [None] * POPS
    for i in range(1, POPS):
        _, step_y, step_z = VELOCITIES[i]
        total = None
        for sign, part in ((step_y, along_y), (step_z, along_z)):
            if sign == 0:
                continue
            if total is None:
                total = part if sign == 1 else -part
            else:
                total = total + part if sign == 1 else total - part
        if total is not None:
            out[i] = (6.0 * WEIGHTS[i]) * total
    return out


def total_of(parts):
    parts = list(parts)
    while len(parts) > 1:
        pairs = [parts[n] + parts[n + 1] for n in range(0, len(parts) - 1, 2)]
        parts = pairs + parts[len(parts) - len(parts) % 2 :]
    return parts[0]


def streamed(pull, own, drift_y, drift_z):
    push = pushes(total_of(own), drift_y, drift_z)
    out = [own[0]]
    for i in range(1, POPS):
        pulled = pull(i)
        bounced = own[OPPOSITE[i]]
        blocked = pulled < WALL_BELOW
        if push[i] is not None:
            bounced = jnp.where(pulled < OUT_BELOW, bounced, bounced + push[i])
        out.append(jnp.where(blocked, bounced, pulled))
    return out


def place():
    return lax.axis_index("stream"), lax.axis_index("cy"), lax.axis_index("cz")


def slot_of(pos, row, layer, column_z):
    slot = (pos[0, row] - (layer * BXD - 1)) * BZD + (pos[2, row] - column_z * BZD)
    return jnp.clip(slot, 0, LAYERS * BZD - 1)


def fill_table(pos, table):
    layer, _, column_z = place()
    for entry in range(LAYERS * BZD):
        table[entry] = -1
    for row in range(pos.shape[1]):

        @pl.when(pos[0, row] >= 0)
        def _(row=row):
            table[slot_of(pos, row, layer, column_z)] = row


def spread_marks(marks, dense):
    rows = marks.shape[0]
    for first in range(0, rows, 8):
        size = min(8, rows - first)
        for tile in range(TILES):
            value = marks[first : first + size, tile * LANE : (tile + 1) * LANE].astype(jnp.float32)
            dense[pl.ds(first * TILES + tile, size, stride=TILES), :] = value


def collide_block(ref, base):
    for part in range(TILES // 8):
        old = [ref[pl.ds(base + i * TILES + 8 * part, 8), :] for i in range(POPS)]
        mark = ref[pl.ds(base + POPS * TILES + 8 * part, 8), :] > 0.5
        post, _ = collide(old)
        for i in range(POPS):
            ref[pl.ds(base + i * TILES + 8 * part, 8), :] = jnp.where(mark, old[i], post[i])


def pack_stream(places, marks_in, pops, up, down, pos, table, marks, dense, blocks, slabs, strip, sems):
    mark_copy = pltpu.make_async_copy(marks_in, marks, sems.at[2 * MOVE_CAP + 2 * BZD])
    mark_copy.start()
    place_copy = pltpu.make_async_copy(places, pos, sems.at[2 * MOVE_CAP + 2 * BZD + 1])
    place_copy.start()
    place_copy.wait()
    fill_table(pos, table)
    rows = pos.shape[1]
    count = 0
    for row in range(rows):
        count = count + jnp.where(pos[0, row] >= 0, 1, 0)
    last = jnp.clip(count - MOVE_CAP, 0, rows - MOVE_CAP)
    sources = [last, last + 1, 0, 1]
    copies = []
    for n, row in enumerate(sources):
        copies.append(pltpu.make_async_copy(pops.at[row], blocks.at[n], sems.at[n]))
    slab_rows = []
    for side in range(2):
        for bz in range(BZD):
            row = jnp.maximum(table[(2 - side) * BZD + bz], 0)
            n = side * BZD + bz
            first = (TILES - SLAB) * LANE if side == 0 else 0
            slab_rows.append(row)
            copies.append(
                pltpu.make_async_copy(
                    pops.at[row, :, pl.ds(first, SLAB * LANE)], slabs.at[n], sems.at[4 + n]
                )
            )
    for copy in copies:
        copy.start()
    mark_copy.wait()
    spread_marks(marks, dense)
    groups = ((0, 8), (8, 8), (16, 3))
    for side, out in enumerate((up, down)):
        for j in range(MOVE_CAP):
            row = sources[side * MOVE_CAP + j]
            out[pl.ds(j * BLOCK + POPS * TILES, TILES), :] = dense[pl.ds(row * TILES, TILES), :]
            for part, axis in ((0, 0), (1, 2)):
                value = jnp.full((1, LANE), pos[axis, row], jnp.int32).astype(jnp.float32)
                out[pl.ds(SENT_META + 2 * j + part, 1), :] = value
            copies[side * MOVE_CAP + j].wait()
            for group, size in groups:
                for tile in range(TILES):
                    value = blocks[side * MOVE_CAP + j, group : group + size, tile * LANE : (tile + 1) * LANE]
                    out[pl.ds(j * BLOCK + group * TILES + tile, size, stride=TILES), :] = value
            collide_block(out, j * BLOCK)
        for bz in range(BZD):
            n = side * BZD + bz
            first = slab_rows[n] * TILES + (TILES - SLAB if side == 0 else 0)
            copies[4 + n].wait()
            for x in range(2):
                for yhi in range(2):
                    q = 2 * x + yhi
                    row = x * FACE + 2 * bz + yhi
                    for group, size in groups:
                        value = slabs[n, group : group + size, q * LANE : (q + 1) * LANE]
                        strip[pl.ds(group * 2 * FACE + row, size, stride=2 * FACE), :] = value
                row = POPS * 2 * FACE + x * FACE + 2 * bz
                strip[pl.ds(row, 2), :] = dense[pl.ds(first + 2 * x, 2), :]
        inner = 1 if side == 0 else 0
        for x in range(2):
            old = [strip[pl.ds(i * 2 * FACE + x * FACE, FACE), :] for i in range(POPS)]
            mark = strip[pl.ds(POPS * 2 * FACE + x * FACE, FACE), :] > 0.5
            post, _ = collide(old)
            if x == inner:
                pairs = [(i, i) for i in range(POPS)]
            else:
                pairs = [(POPS + n, i) for n, i in enumerate(AHEAD if side == 0 else BACK)]
            for plane, i in pairs:
                out[pl.ds(SENT_SLABS + plane * FACE, FACE), :] = jnp.where(mark, ROTOR, post[i])


def pack_own(places, marks_in, pops, own, zpack, zup, zdown, pos, marks, dense, stage, sems):
    layer, _, column_z = place()
    rows = pos.shape[1]
    mark_copy = pltpu.make_async_copy(marks_in, marks, sems.at[rows])
    mark_copy.start()
    place_copy = pltpu.make_async_copy(places, pos, sems.at[rows + 1])
    place_copy.start()
    copies = [pltpu.make_async_copy(pops.at[r], stage.at[r], sems.at[r]) for r in range(rows)]
    for copy in copies:
        copy.start()
    mark_copy.wait()
    spread_marks(marks, dense)
    place_copy.wait()

    def settle(row, carry):
        pltpu.make_async_copy(pops.at[row], stage.at[row], sems.at[row]).wait()

        @pl.when(pos[0, row] >= 0)
        def _():
            base = pl.multiple_of(slot_of(pos, row, layer, column_z) * BLOCK, 8)
            for tile in range(TILES):
                for group, size in ((0, 8), (8, 8), (16, 3)):
                    value = stage[row, group : group + size, tile * LANE : (tile + 1) * LANE]
                    own[pl.ds(base + group * TILES + tile, size, stride=TILES), :] = value
            from_row = pl.multiple_of(row * TILES, 8)
            own[pl.ds(base + POPS * TILES, TILES), :] = dense[pl.ds(from_row, TILES), :]
            collide_block(own, base)

        return carry

    lax.fori_loop(0, rows, settle, 0)
    edge_bz = jnp.where(column_z == 0, BZD - 1, 0)
    first_c = jnp.where(column_z == 0, EDGE - 2, 0)
    spot = (lanes() % EDGE) // 2
    for held in range(LAYERS):
        base = pl.multiple_of((held * BZD + edge_bz) * BLOCK, 8)
        for group in range(ZGROUPS):
            for part in range(TILES // 8):
                total = jnp.zeros((8, LANE), jnp.float32)
                for k in range(min(8, PLANES - group * 8)):
                    value = own[pl.ds(base + (group * 8 + k) * TILES + part * 8, 8), :]
                    value = pltpu.roll(value, (2 * k - first_c + LANE) % LANE, 1)
                    total = jnp.where(spot == k, value, total)
                zpack[pl.ds(held * ZROWS + group * TILES + part * 8, 8), :] = total
    present = [jnp.int32(0)] * LAYERS
    for row in range(rows):
        slot = slot_of(pos, row, layer, column_z)
        for held in range(LAYERS):
            hit = (pos[0, row] >= 0) & (slot == held * BZD + edge_bz)
            present[held] = jnp.where(hit, 1, present[held])
    sublane = lax.broadcasted_iota(jnp.int32, (8, LANE), 0)
    flags = jnp.zeros((8, LANE), jnp.int32)
    for held in range(LAYERS):
        flags = jnp.where(sublane == held, present[held], flags)
    zpack[pl.ds(ZMETA, 8), :] = flags.astype(jnp.float32)
    zup[pl.ds(0, ZROWS), :] = zpack[pl.ds(3 * ZROWS, ZROWS), :]
    zdown[pl.ds(0, ZROWS), :] = zpack[pl.ds(0, ZROWS), :]
    for group in range(ZGROUPS):
        target = pl.ds(ZROWS + group * SLAB, SLAB)
        zup[target, :] = zpack[pl.ds(2 * ZROWS + group * TILES + TILES - SLAB, SLAB), :]
        zdown[target, :] = zpack[pl.ds(ZROWS + group * TILES, SLAB), :]


def gathered(load, zload, ylo, column_z):
    lane = lanes()
    parts = [load(bz) for bz in range(BZD)]
    rows = parts[0].shape[0]
    lane = lane[:rows]
    total = None
    for bz in range(BZD):
        shift = (bz * EDGE - ylo * EDGE) % LANE
        value = pltpu.roll(parts[bz], shift, 1) if shift else parts[bz]
        total = value if total is None else jnp.where(lane // EDGE == bz, value, total)
    zvalue, spot = zload
    goal = jnp.where(column_z == 0, SPAN_Z, LANE - 2)
    zvalue = pltpu.roll(zvalue, (goal - (ylo * EDGE + 2 * spot) + LANE) % LANE, 1)
    return jnp.where(lane >= SPAN_Z, zvalue, total)


def inside_lanes(rows, column_z):
    lane = lanes()[:rows]
    low = (column_z == 0) & (lane >= SPAN_Z) & (lane < SPAN_Z + 2)
    high = (column_z != 0) & (lane >= LANE - 2)
    return (lane < SPAN_Z) | low | high


def marked(post, mark, inside):
    flag = jnp.where(inside, jnp.where(mark > 0.5, ROTOR, 0.0), OUTSIDE)
    wall = flag < WALL_BELOW
    return [jnp.where(wall, flag, value) for value in post]


def chunk_values(own, edge, zall, zedge, chunk, yhi, ylo, column_z):
    out = []
    for plane in range(PLANES):
        group, spot = plane // 8, plane % 8
        if chunk is None:

            def load(bz):
                if plane == POPS:
                    return jnp.zeros((4, LANE), jnp.float32)
                return edge[pl.ds(plane * 4 * FACE + 2 * bz + yhi, 4, stride=FACE), :]

            zvalue = zedge[pl.ds(group * 8 + yhi, 4, stride=2), :]
        else:
            held, half = 1 + chunk // 2, chunk % 2

            def load(bz):
                base = (held * BZD + bz) * BLOCK + plane * TILES + half * EDGE + yhi
                return own[pl.ds(base, 8, stride=2), :]

            zvalue = zall[pl.ds(held * ZROWS + group * TILES + half * EDGE + yhi, 8, stride=2), :]
        out.append(gathered(load, (zvalue, spot), ylo, column_z))
    return out


def halo_x_inside(layer, layers):
    row = lax.broadcasted_iota(jnp.int32, (4, LANE), 0)
    low = (row < 2) & (layer > 0)
    high = (row >= 2) & (layer < layers - 1)
    return low | high


def settle_rim(layers, places, up, down, zin, zup, zdown, own_in, own, edge, zall, zedge, rim_up, rim_down, pos, post_up, post_down, sem):
    del own_in
    layer, _, column_z = place()
    place_copy = pltpu.make_async_copy(places, pos, sem)
    place_copy.start()
    for arrived in (up, down):
        for j in range(MOVE_CAP):
            bx = arrived[pl.ds(SENT_META + 2 * j, 1), :].astype(jnp.int32)
            bz = arrived[pl.ds(SENT_META + 2 * j + 1, 1), :].astype(jnp.int32)
            code = (bx - layer * BXD) * BZD + (bz - column_z * BZD)
            mine = (bx >= layer * BXD) & (bx < (layer + 1) * BXD)
            first = layer == 0 if arrived is up else layer == layers - 1
            code = jnp.max(jnp.where(mine, code, -1))

            @pl.when((code >= 0) & jnp.logical_not(first))
            def _(arrived=arrived, j=j, code=code):
                base = pl.multiple_of((jnp.clip(code, 0, BXD * BZD - 1) + BZD) * BLOCK, 8)
                for n in range(BLOCK // 8):
                    own[pl.ds(base + 8 * n, 8), :] = arrived[pl.ds(j * BLOCK + 8 * n, 8), :]

    place_copy.wait()
    for side, arrived in enumerate((up, down)):
        inner, outer = (1, 0) if side == 0 else (2, 3)
        pairs = [(i, i, inner) for i in range(POPS)]
        pairs += [(POPS + n, i, outer) for n, i in enumerate(AHEAD if side == 0 else BACK)]
        for plane, i, x in pairs:
            edge[pl.ds((i * 4 + x) * FACE, FACE), :] = arrived[pl.ds(SENT_SLABS + plane * FACE, FACE), :]
        for bz in range(BZD):
            here = jnp.int32(0)
            goal = (0 if side == 0 else LAYERS - 1) * BZD + bz
            for row in range(pos.shape[1]):
                hit = (pos[0, row] >= 0) & (slot_of(pos, row, layer, column_z) == goal)
                here = jnp.where(hit, 1, here)

            @pl.when(here == 1)
            def _(side=side, pairs=pairs, goal=goal, bz=bz):
                first = goal * BLOCK + (TILES - SLAB if side == 0 else 0)
                for _, i, x in pairs:
                    shift = 2 * (x if side == 0 else x - 2)
                    mark = own[pl.ds(first + POPS * TILES + shift, 2), :] > 0.5
                    value = own[pl.ds(first + i * TILES + shift, 2), :]
                    edge[pl.ds((i * 4 + x) * FACE + 2 * bz, 2), :] = jnp.where(mark, ROTOR, value)

    for held in range(LAYERS):
        flag = zin[pl.ds(ZMETA + held, 1), :] > 0.5
        for group in range(ZGROUPS):
            if held == 1 or held == 2:
                for part in range(TILES // 8):
                    rows = pl.ds(held * ZROWS + group * TILES + part * 8, 8)
                    source = zup if held == 1 else zdown
                    other = source[pl.ds(group * TILES + part * 8, 8), :]
                    zall[rows, :] = jnp.where(flag, zin[rows, :], other)
            else:
                side = 0 if held == 0 else 1
                source = zup if held == 0 else zdown
                first = TILES - SLAB if held == 0 else 0
                mine = zin[pl.ds(held * ZROWS + group * TILES + first, SLAB), :]
                other = source[pl.ds(ZROWS + group * SLAB, SLAB), :]
                zedge[pl.ds(group * 8 + side * SLAB, SLAB), :] = jnp.where(flag, mine, other)
    for chunk in (0, 1, 2, 3, None):
        for y in (0, 1, SPAN_Y - 2, SPAN_Y - 1):
            values = chunk_values(own, edge, zall, zedge, chunk, y // YLO, y % YLO, column_z)
            inside = inside_lanes(values[0].shape[0], column_z)
            if chunk is None:
                inside = inside & halo_x_inside(layer, layers)
            post = marked(values[:POPS], values[POPS], inside)
            target = post_down if y < 2 else post_up
            rim = RIM_DOWN if y < 2 else RIM_UP
            if y in (0, SPAN_Y - 1):
                pairs = [(i, i) for i in range(POPS)]
            else:
                pairs = [(POPS + n, i) for n, i in enumerate(rim)]
            for plane, i in pairs:
                if chunk is None:
                    target[pl.ds(plane * GRID_X, 2), :] = post[i][:2]
                    target[pl.ds(plane * GRID_X + EXT_X - 2, 2), :] = post[i][2:]
                else:
                    target[pl.ds(plane * GRID_X + 2 + 8 * chunk, 8), :] = post[i]
    lane = lanes()
    for source, target in ((post_up, rim_up), (post_down, rim_down)):
        for chunk in range(5):
            size = min(8, EXT_X - 8 * chunk)
            for block in range(RIM_BLOCKS):
                total = jnp.zeros((8, LANE), jnp.float32)
                for plane in range(RIM):
                    begin = plane * EXT_Z - block * LANE
                    if begin >= LANE or begin + EXT_Z <= 0:
                        continue
                    value = source[pl.ds(plane * GRID_X + 8 * chunk, 8), :]
                    value = pltpu.roll(value, (begin + LANE + 2 * column_z) % LANE, 1)
                    total = jnp.where((lane >= begin) & (lane < begin + EXT_Z), value, total)
                target[pl.ds(block * EXT_X + 8 * chunk, size), :] = total[:size]


def turned(value, step_z):
    return pltpu.roll(value, step_z % LANE, 1) if step_z else value


def drifts_of(columns, depth):
    _, _, column_z = place()
    lane = lanes()
    total_y = SPAN_Y * columns
    total_z = SPAN_Z * depth
    spin = 0.2 / (total_y + total_z)
    here_z = jnp.where(lane < SPAN_Z + 8, lane, lane - LANE) + column_z * SPAN_Z
    drift_y = -spin * (here_z.astype(jnp.float32) - (total_z - 1) / 2.0)
    return drift_y, spin, (total_y - 1) / 2.0


def drifts_by_half(columns, depth):
    _, column_y, _ = place()
    drift_y, spin, centre_y = drifts_of(columns, depth)
    sublane = lax.broadcasted_iota(jnp.int32, (8, LANE), 0)
    halves = []
    for half in range(SPAN_Y // 8):
        here_y = sublane + (column_y * SPAN_Y + 8 * half)
        halves.append(spin * (here_y.astype(jnp.float32) - centre_y))
    return drift_y, halves


def pull_from(field, base):
    def pull(i):
        step_x, step_y, step_z = VELOCITIES[i]
        return turned(field[pl.ds(i * FIELD + base - step_x * PITCH - step_y, 8), :], step_z)

    return pull


def settle_all(layers, columns, depth, own, edge, zall, zedge, field, start, later):
    layer, _, column_z = place()

    def halves(yhi, carry):
        def chunks(chunk, carry):
            for ylo in range(YLO):
                values = chunk_values(own, edge, zall, zedge, chunk, yhi, ylo, column_z)
                post = marked(values[:POPS], values[POPS], inside_lanes(8, column_z))
                row = (8 * chunk + 2) * PITCH + FIRST + YLO * yhi + ylo
                for i in range(POPS):
                    field[pl.ds(i * FIELD + row, 8, stride=PITCH), :] = post[i]
                    target = (i * SPAN_X + 8 * chunk) * SPAN_Y + YLO * yhi + ylo
                    start[pl.ds(target, 8, stride=SPAN_Y), :] = values[i]
            return carry

        lax.fori_loop(0, SPAN_X // 8, chunks, 0)
        for ylo in range(YLO):
            values = chunk_values(own, edge, zall, zedge, None, yhi, ylo, column_z)
            inside = inside_lanes(4, column_z) & halo_x_inside(layer, layers)
            post = marked(values[:POPS], values[POPS], inside)
            for first, side in ((0, 0), (EXT_X - 2, 2)):
                row = first * PITCH + FIRST + YLO * yhi + ylo
                for i in range(POPS):
                    field[pl.ds(i * FIELD + row, 2, stride=PITCH), :] = post[i][side : side + 2]
        return carry

    lax.fori_loop(0, SPAN_Y // YLO, halves, 0)
    drift_y, drifts = drifts_by_half(columns, depth)

    def first_step(x, carry):
        for half in range(SPAN_Y // 8):
            base = pl.multiple_of(x * PITCH + FIRST + 8 * half, 8)
            old = [field[pl.ds(i * FIELD + base, 8), :] for i in range(POPS)]
            values = streamed(pull_from(field, base), old, drift_y, drifts[half])
            post, _ = collide(values)
            wall = old[0] < WALL_BELOW
            for i in range(POPS):
                later[pl.ds(i * FIELD + base, 8), :] = jnp.where(wall, old[0], post[i])
        return carry

    lax.fori_loop(1, EXT_X - 1, first_step, 0)


def finish(columns, depth, rim_low, rim_high, field, start, later_in, out, later, low, high, result, sems):
    del later_in
    _, column_y, column_z = place()
    flat = (lanes() + 2 * column_z) % LANE
    for source, target, there in ((rim_low, low, column_y > 0), (rim_high, high, column_y < columns - 1)):
        for chunk in range(5):
            blocks = [source[pl.ds(block * EXT_X + 8 * chunk, 8), :] for block in range(RIM_BLOCKS)]
            for plane in range(RIM):
                block, begin = divmod(plane * EXT_Z, LANE)
                shift = (2 * LANE - begin - 2 * column_z) % LANE
                value = pltpu.roll(blocks[block], shift, 1)
                if begin + EXT_Z > LANE:
                    value = jnp.where(flat < LANE - begin, value, pltpu.roll(blocks[block + 1], shift, 1))
                value = jnp.where((flat < EXT_Z) & there, value, OUTSIDE)
                target[pl.ds(plane * GRID_X + 8 * chunk, 8), :] = value

    drift_y, spin, centre_y = drifts_of(columns, depth)
    for source, face, rim in ((low, 0, RIM_UP), (high, SPAN_Y - 1, RIM_DOWN)):
        outer = {i: POPS + n for n, i in enumerate(rim)}
        toward = VELOCITIES[rim[0]][1]
        for y in (face - toward, face):
            drift_z = spin * ((column_y * SPAN_Y + y).astype(jnp.float32) - centre_y)
            for chunk in range(5):
                first = 1 + 8 * chunk
                size = min(8, EXT_X - 1 - first)

                def value_at(i, x, y):
                    if y == face - 2 * toward:
                        return source[pl.ds(outer[i] * GRID_X + x, size), :]
                    if y == face - toward:
                        return source[pl.ds(i * GRID_X + x, size), :]
                    return field[pl.ds(i * FIELD + x * PITCH + FIRST + y, size, stride=PITCH), :]

                def pull(i):
                    step_x, step_y, step_z = VELOCITIES[i]
                    return turned(value_at(i, first - step_x, y - step_y), step_z)

                old = [value_at(i, first, y) for i in range(POPS)]
                values = streamed(pull, old, drift_y[:size], drift_z)
                post, _ = collide(values)
                wall = old[0] < WALL_BELOW
                for i in range(POPS) if y == face else rim:
                    row = i * FIELD + first * PITCH + FIRST + y
                    later[pl.ds(row, size, stride=PITCH), :] = jnp.where(wall, old[0], post[i])

    drift_y, drifts = drifts_by_half(columns, depth)
    quarter = SPAN_X // 4

    def leave(n):
        part = pl.ds(n * quarter, quarter)
        return pltpu.make_async_copy(result.at[:, part], out.at[:, part], sems.at[n])

    def second_step(x, carry):
        for half in range(SPAN_Y // 8):
            base = pl.multiple_of((x + 2) * PITCH + FIRST + 8 * half, 8)
            old = [later[pl.ds(i * FIELD + base, 8), :] for i in range(POPS)]
            values = streamed(pull_from(later, base), old, drift_y, drifts[half])
            wall = old[0] < WALL_BELOW
            for i in range(POPS):
                first = pl.multiple_of((i * SPAN_X + x) * SPAN_Y + 8 * half, 8)
                value = jnp.where(wall, start[pl.ds(first, 8), :], values[i])
                result[i, x, pl.ds(8 * half, 8), :] = value[:, :SPAN_Z]
        return carry

    for n in range(4):
        lax.fori_loop(n * quarter, (n + 1) * quarter, second_step, 0)
        leave(n).start()
    for n in range(4):
        leave(n).wait()


def rows_of(count):
    return jax.ShapeDtypeStruct((count, LANE), jnp.float32)


def kept(count):
    return VMEM((count, LANE), jnp.float32)


def params(mib):
    return pltpu.CompilerParams(vmem_limit_bytes=mib * 2**20)


def shards(populations, solid_cells, block_pos):
    layers = lax.axis_size("stream")
    columns = lax.axis_size("cy")
    depth = lax.axis_size("cz")
    rows = block_pos.shape[0]
    vmem = pl.BlockSpec(memory_space=VMEM)
    hbm = pl.BlockSpec(memory_space=pltpu.HBM)
    populations = pltpu.with_memory_space_constraint(populations, pltpu.HBM)
    solid_cells = pltpu.with_memory_space_constraint(solid_cells, pltpu.HBM)
    places = pltpu.with_memory_space_constraint(block_pos.T, pltpu.HBM)
    place_scratch = SMEM((3, rows), jnp.int32)
    mark_scratch = [VMEM((rows, EDGE**3), jnp.int32), VMEM((rows * TILES, LANE), jnp.float32)]

    send_up, send_down = pl.pallas_call(
        pack_stream,
        out_shape=(kept(SENT_ROWS), kept(SENT_ROWS)),
        in_specs=[hbm, hbm, hbm],
        out_specs=(vmem, vmem),
        scratch_shapes=[place_scratch, SMEM((LAYERS * BZD,), jnp.int32)]
        + mark_scratch
        + [
            VMEM((2 * MOVE_CAP, POPS, EDGE**3), jnp.float32),
            VMEM((2 * BZD, POPS, SLAB * LANE), jnp.float32),
            VMEM((PLANES * 2 * FACE, LANE), jnp.float32),
            pltpu.SemaphoreType.DMA((2 * MOVE_CAP + 2 * BZD + 2,)),
        ],
        compiler_params=params(16),
        name="pack_stream",
    )(places, solid_cells, populations)
    up = [(i, i + 1) for i in range(layers - 1)]
    down = [(i + 1, i) for i in range(layers - 1)]
    from_low = lax.ppermute(send_up, "stream", up)
    from_high = lax.ppermute(send_down, "stream", down)

    own, zpack, zsend_up, zsend_down = pl.pallas_call(
        pack_own,
        out_shape=(kept(LAYERS * BZD * BLOCK), kept(ZMETA + 8), kept(DIAG), kept(DIAG)),
        in_specs=[hbm, hbm, hbm],
        out_specs=(vmem,) * 4,
        scratch_shapes=[place_scratch]
        + mark_scratch
        + [
            VMEM((rows, POPS, EDGE**3), jnp.float32),
            pltpu.SemaphoreType.DMA((rows + 2,)),
        ],
        compiler_params=params(16),
        name="pack_own",
    )(places, solid_cells, populations)
    swap = [(i, depth - 1 - i) for i in range(depth)]
    zin = lax.ppermute(zpack, "cz", swap)
    zup_pairs = [(s * depth + c, t * depth + d) for s, t in up for c, d in swap]
    zdown_pairs = [(s * depth + c, t * depth + d) for s, t in down for c, d in swap]
    z_low = lax.ppermute(zsend_up, ("stream", "cz"), zup_pairs)
    z_high = lax.ppermute(zsend_down, ("stream", "cz"), zdown_pairs)

    own, edge, zall, zedge, rim_up, rim_down = pl.pallas_call(
        functools.partial(settle_rim, layers),
        out_shape=(
            kept(LAYERS * BZD * BLOCK),
            kept(POPS * 4 * FACE),
            kept(LAYERS * ZROWS),
            kept(ZGROUPS * 8),
            kept(RIM_ROWS),
            kept(RIM_ROWS),
        ),
        in_specs=[hbm] + [vmem] * 6,
        out_specs=(vmem,) * 6,
        scratch_shapes=[
            place_scratch,
            VMEM((RIM * GRID_X, LANE), jnp.float32),
            VMEM((RIM * GRID_X, LANE), jnp.float32),
            pltpu.SemaphoreType.DMA,
        ],
        input_output_aliases={6: 0},
        compiler_params=params(16),
        name="settle_rim",
    )(places, from_low, from_high, zin, z_low, z_high, own)
    cy_up = [(i, i + 1) for i in range(columns - 1)]
    cy_down = [(i + 1, i) for i in range(columns - 1)]
    rim_low = lax.ppermute(rim_up, "cy", cy_up)
    rim_high = lax.ppermute(rim_down, "cy", cy_down)

    field, start, later = pl.pallas_call(
        functools.partial(settle_all, layers, columns, depth),
        out_shape=(kept(POPS * FIELD), kept(POPS * SPAN_X * SPAN_Y), kept(POPS * FIELD)),
        in_specs=[vmem] * 4,
        out_specs=(vmem,) * 3,
        compiler_params=params(16),
        name="settle_all",
    )(own, edge, zall, zedge)

    out, _ = pl.pallas_call(
        functools.partial(finish, columns, depth),
        out_shape=(
            jax.ShapeDtypeStruct((POPS, SPAN_X, SPAN_Y, SPAN_Z), jnp.float32),
            kept(POPS * FIELD),
        ),
        in_specs=[vmem] * 5,
        out_specs=(hbm, vmem),
        scratch_shapes=[
            VMEM((RIM * GRID_X, LANE), jnp.float32),
            VMEM((RIM * GRID_X, LANE), jnp.float32),
            VMEM((POPS, SPAN_X, SPAN_Y, SPAN_Z), jnp.float32),
            pltpu.SemaphoreType.DMA((4,)),
        ],
        input_output_aliases={4: 1},
        compiler_params=params(16),
        name="finish",
    )(rim_low, rim_high, field, start, later)
    return out


def solution(mesh):
    in_specs = (
        P(("stream", "cy", "cz"), None, None),
        P(("stream", "cy", "cz"), None),
        P(("stream", "cy", "cz"), None),
    )
    out_specs = P(None, "stream", "cy", "cz")
    return jax.shard_map(shards, mesh=mesh, in_specs=in_specs, out_specs=out_specs, check_vma=False)
```

time: 65.5 us -> 57.3 us (0.87)
  local copies, waits for them, and re-layouts: 4.05 us -> 0 us
  Pallas kernels: 33.8 us -> 31.5 us
  waiting for transfers between devices: 11.8 us -> 10.2 us
  starting transfers between devices: 15.4 us -> 14.6 us
    pallas_call x1, Pallas kernels: 10.7 us -> 5.41 us  [shards(): pl.pallas_call(functools.partial(finish, columns, depth), out_shape=(jax....]
    unnamed x5 -> x0, local copies, waits for them, and re-layouts: 4.05 us -> none
    pallas_call x3, Pallas kernels: 19 us -> 23 us  [the longest x1 13.7 us: shards(): pl.pallas_call(functools.partial(settle_all, layers, columns, depth), out...]
    ppermute x1, waiting for transfers between devices: 1.67 us -> 0.01 us  [shards(): rim_high = lax.ppermute(rim_down, 'cy', cy_down)]
    pallas_call x1, Pallas kernels: 4.1 us -> 3.07 us  [shards(): pl.pallas_call(functools.partial(settle_rim, layers), out_shape=(kept(LAY...]
    ppermute x1, starting transfers between devices: 3.05 us -> 2.26 us  [shards(): z_low = lax.ppermute(zsend_up, ('stream', 'cz'), zup_pairs)]
  transfers between devices with their start and end apart: 7 -> 7, of which waited for: 4 -> 3; matrix products, arithmetic and copies ran while one was open for 0% -> 0% of each run, Pallas kernels for 25% -> 35%
where the time goes in v2:
time: 57.3 us; the launch traced here: 56.3 us
  Pallas kernels  31.5 us (55%)
  starting transfers between devices  14.6 us (25%)
  waiting for transfers between devices  10.2 us (18%)
    pallas_call x1, Pallas kernels, shards(): pl.pallas_call(functools.partial(settle_all, layers, columns, depth), out...  13.7 us
    ppermute x1, waiting for transfers between devices, shards(): z_low = lax.ppermute(zsend_up, ('stream', 'cz'), zup_pairs)  6.62 us
    pallas_call x1, Pallas kernels, shards(): pl.pallas_call(pack_own, out_shape=(kept(LAYERS * BZD * BLOCK), kept(ZMET...  5.77 us
    pallas_call x1, Pallas kernels, shards(): pl.pallas_call(functools.partial(finish, columns, depth), out_shape=(jax....  5.41 us
    ppermute x1, starting transfers between devices, shards(): from_low = lax.ppermute(send_up, 'stream', up)  4.98 us
    pallas_call x1, Pallas kernels, shards(): pl.pallas_call(pack_stream, out_shape=(kept(SENT_ROWS), kept(SENT_ROWS)),...  3.48 us
    ppermute x1, starting transfers between devices, shards(): rim_low = lax.ppermute(rim_up, 'cy', cy_up)  3.41 us
    pallas_call x1, Pallas kernels, shards(): pl.pallas_call(functools.partial(settle_rim, layers), out_shape=(kept(LAY...  3.07 us
  transfers between devices with their start and end apart: 7, of which 3 were waited for; matrix products, arithmetic and copies ran while one was open for 0% of the time, Pallas kernels for 35%

profile of v2, /device:TPU:0, one launch (start us, length us, event | category | flops | bytes accessed | tf_op | source)
XLA Modules:
  0.0 56.3 jit_solution(10071071195871494315)
XLA Ops:
  0.0 3.5 %pack_stream.1 = (f32[1480,128]{1,0:T(8,128)S(1)}, f32[1480,128]{1,0:T(8,128)S(1)}) custom-call(s32[3,12]{1,0:T(4,128)} %bitcast.1, s32[12,4096]{1,0:T(8,128)} %marks_in.3, f32[12,19,4096]{2,1,0:T(8,128)} %pops.3), custom_call_target="tpu_custom_call" | custom-call | tf_op jit(solution)/shard_map/pack_stream/pallas_call | solution.py:678
  3.5 5.0 %collective-permute-start = (f32[1480,128]{1,0:T(8,128)S(1)}, f32[1480,128]{1,0:T(8,128)S(1)}, u32[]{:S(2)}, u32[]{:S(2)}) collective-permute-start(f32[1480,128]{1,0:T(8,128)S(1)} %get-tuple-element.21), channel_id=1, source_target_pairs={{0,8},{8,16},{16,24},{1,9},{9,17},{17,25},{2,10},{10,18},{18,26},{... | collective-permute-start | bytes 2273288 | tf_op jit(solution)/shard_map/ppermute | solution.py:696
  8.5 1.3 %collective-permute-start.1 = (f32[1480,128]{1,0:T(8,128)S(1)}, f32[1480,128]{1,0:T(8,128)S(1)}, u32[]{:S(2)}, u32[]{:S(2)}) collective-permute-start(f32[1480,128]{1,0:T(8,128)S(1)} %get-tuple-element.22), channel_id=1, source_target_pairs={{8,0},{16,8},{24,16},{9,1},{17,9},{25,17},{10,2},{18,10},{26,18},{... | collective-permute-start | bytes 2273288 | tf_op jit(solution)/shard_map/ppermute | solution.py:697
  9.8 5.8 %pack_own.1 = (f32[10240,128]{1,0:T(8,128)S(1)}, f32[392,128]{1,0:T(8,128)S(1)}, f32[108,128]{1,0:T(8,128)S(1)}, f32[108,128]{1,0:T(8,128)S(1)}) custom-call(s32[3,12]{1,0:T(4,128)} %bitcast.2, s32[12,4096]{1,0:T(8,128)} %marks_in.3, f32[12,19,4096]{2,1,0:T(8,128)} %pops.3), custom_call_target="tpu_custom_call" | custom-call | tf_op jit(solution)/shard_map/pack_own/pallas_call | solution.py:699
  15.6 0.1 collective-permute-start.2
  15.6 2.3 %collective-permute-start.3 = (f32[108,128]{1,0:T(8,128)S(1)}, f32[108,128]{1,0:T(8,128)S(1)}, u32[]{:S(2)}, u32[]{:S(2)}) collective-permute-start(f32[108,128]{1,0:T(8,128)S(1)} %get-tuple-element.24), channel_id=1, source_target_pairs={{0,9},{1,8},{8,17},{9,16},{16,25},{17,24},{2,11},{3,10},{10,19},{1... | collective-permute-start | bytes 165896 | tf_op jit(solution)/shard_map/ppermute | solution.py:717
  17.9 1.3 %collective-permute-start.4 = (f32[108,128]{1,0:T(8,128)S(1)}, f32[108,128]{1,0:T(8,128)S(1)}, u32[]{:S(2)}, u32[]{:S(2)}) collective-permute-start(f32[108,128]{1,0:T(8,128)S(1)} %get-tuple-element.25), channel_id=1, source_target_pairs={{8,1},{9,0},{16,9},{17,8},{24,17},{25,16},{10,3},{11,2},{18,11},{1... | collective-permute-start | bytes 165896 | tf_op jit(solution)/shard_map/ppermute | solution.py:718
  19.2 6.6 %collective-permute-done.3.zup = f32[108,128]{1,0:T(8,128)S(1)} collective-permute-done((f32[108,128]{1,0:T(8,128)S(1)}, f32[108,128]{1,0:T(8,128)S(1)}, u32[]{:S(2)}, u32[]{:S(2)}) %collective-permute-start.3) | collective-permute-done | bytes 55328 | tf_op jit(solution)/shard_map/ppermute | solution.py:717
  25.8 2.7 %collective-permute-done.4.zdown = f32[108,128]{1,0:T(8,128)S(1)} collective-permute-done((f32[108,128]{1,0:T(8,128)S(1)}, f32[108,128]{1,0:T(8,128)S(1)}, u32[]{:S(2)}, u32[]{:S(2)}) %collective-permute-start.4) | collective-permute-done | bytes 55328 | tf_op jit(solution)/shard_map/ppermute | solution.py:718
  28.5 0.0 collective-permute-done.2.zin
  28.5 0.0 collective-permute-done.up
  28.5 0.8 %collective-permute-done.1.down = f32[1480,128]{1,0:T(8,128)S(1)} collective-permute-done((f32[1480,128]{1,0:T(8,128)S(1)}, f32[1480,128]{1,0:T(8,128)S(1)}, u32[]{:S(2)}, u32[]{:S(2)}) %collective-permute-start.1) | collective-permute-done | bytes 757792 | tf_op jit(solution)/shard_map/ppermute | solution.py:697
  29.4 3.1 %settle_rim.1 = (f32[10240,128]{1,0:T(8,128)S(1)}, f32[608,128]{1,0:T(8,128)S(1)}, f32[384,128]{1,0:T(8,128)S(1)}, f32[24,128]{1,0:T(8,128)S(1)}, f32[472,128]{1,0:T(8,128)S(1)}, /*index=5*/f32[472,128]{1,0:T(8,128)S(1)}) custom-call(s32[3,12]{1,0:T(4,128)} %bitcast.3, f32[1480,128]{1,0:T(8,128)S(1)} %collective-permute-done.up, ...), custom_call_target="tpu_custom_call", output_to_operand_aliasing={{0}: (6, {})} | custom-call | tf_op jit(solution)/shard_map/settle_rim/pallas_call | solution.py:720
  32.4 3.4 %collective-permute-start.5 = (f32[472,128]{1,0:T(8,128)S(1)}, f32[472,128]{1,0:T(8,128)S(1)}, u32[]{:S(2)}, u32[]{:S(2)}) collective-permute-start(f32[472,128]{1,0:T(8,128)S(1)} %get-tuple-element.27), channel_id=1, source_target_pairs={{0,2},{2,4},{4,6},{1,3},{3,5},{5,7},{8,10},{10,12},{12,14},{9,11},... | collective-permute-start | bytes 725000 | tf_op jit(solution)/shard_map/ppermute | solution.py:744
  35.9 1.3 %collective-permute-start.6 = (f32[472,128]{1,0:T(8,128)S(1)}, f32[472,128]{1,0:T(8,128)S(1)}, u32[]{:S(2)}, u32[]{:S(2)}) collective-permute-start(f32[472,128]{1,0:T(8,128)S(1)} %get-tuple-element.28), channel_id=1, source_target_pairs={{2,0},{4,2},{6,4},{3,1},{5,3},{7,5},{10,8},{12,10},{14,12},{11,9},... | collective-permute-start | bytes 725000 | tf_op jit(solution)/shard_map/ppermute | solution.py:745
  37.2 13.7 %settle_all.1 = (f32[16720,128]{1,0:T(8,128)S(1)}, f32[9728,128]{1,0:T(8,128)S(1)}, f32[16720,128]{1,0:T(8,128)S(1)}) custom-call(f32[10240,128]{1,0:T(8,128)S(1)} %get-tuple-element.29.own, f32[608,128]{1,0:T(8,128)S(1)} %get-tuple-element.30.edge, f32[384,128]{1,0:T(8,128)S(1)} %get-tuple-element.31.zall, f32[24,128]{1,0:T(8,128)S(1)} %get-tuple-element.32.zedge), custom_call_target="tpu_custom_call" | custom-call | tf_op jit(solution)/shard_map/settle_all/pallas_call | solution.py:747
  50.9 0.0 collective-permute-done.5.rim_low
  50.9 0.0 collective-permute-done.6.rim_high
  50.9 5.4 %finish.1 = (f32[19,32,16,64]{3,2,1,0:T(8,128)}, f32[16720,128]{1,0:T(8,128)S(1)}) custom-call(f32[472,128]{1,0:T(8,128)S(1)} %collective-permute-done.5.rim_low, f32[472,128]{1,0:T(8,128)S(1)} %collective-permute-done.6.rim_high, f32[16720,128]{1,0:T(8,128)S(1)} %get-tuple-element.33.field, ...), custom_call_target="tpu_custom_call", output_to_operand_aliasing={{1}: (4, {})} | custom-call | tf_op jit(solution)/shard_map/finish/pallas_call | solution.py:756
Async XLA Ops:
  3.5 25.0 %collective-permute-start = (f32[1480,128]{1,0:T(8,128)S(1)}, f32[1480,128]{1,0:T(8,128)S(1)}, u32[]{:S(2)}, u32[]{:S(2)}) collective-permute-start(f32[1480,128]{1,0:T(8,128)S(1)} %get-tuple-element.21), channel_id=1, source_target_pairs={{0,8},{8,16},{16,24},{1,9},{9,17},{17,25},{2,10},{10,18},{18,26},{... | collective-permute-start | bytes 2273288 | tf_op jit(solution)/shard_map/ppermute | solution.py:696
  8.5 20.9 %collective-permute-start.1 = (f32[1480,128]{1,0:T(8,128)S(1)}, f32[1480,128]{1,0:T(8,128)S(1)}, u32[]{:S(2)}, u32[]{:S(2)}) collective-permute-start(f32[1480,128]{1,0:T(8,128)S(1)} %get-tuple-element.22), channel_id=1, source_target_pairs={{8,0},{16,8},{24,16},{9,1},{17,9},{25,17},{10,2},{18,10},{26,18},{... | collective-permute-start | bytes 2273288 | tf_op jit(solution)/shard_map/ppermute | solution.py:697
  15.6 13.0 %collective-permute-start.2 = (f32[392,128]{1,0:T(8,128)S(1)}, f32[392,128]{1,0:T(8,128)S(1)}, u32[]{:S(2)}, u32[]{:S(2)}) collective-permute-start(f32[392,128]{1,0:T(8,128)S(1)} %get-tuple-element.23), channel_id=1, source_target_pairs={{0,1},{1,0},{2,3},{3,2},{4,5},{5,4},{6,7},{7,6},{8,9},{9,8},{10,11... | collective-permute-start | bytes 602120 | tf_op jit(solution)/shard_map/ppermute | solution.py:714
  15.6 10.2 %collective-permute-start.3 = (f32[108,128]{1,0:T(8,128)S(1)}, f32[108,128]{1,0:T(8,128)S(1)}, u32[]{:S(2)}, u32[]{:S(2)}) collective-permute-start(f32[108,128]{1,0:T(8,128)S(1)} %get-tuple-element.24), channel_id=1, source_target_pairs={{0,9},{1,8},{8,17},{9,16},{16,25},{17,24},{2,11},{3,10},{10,19},{1... | collective-permute-start | bytes 165896 | tf_op jit(solution)/shard_map/ppermute | solution.py:717
  17.9 10.6 %collective-permute-start.4 = (f32[108,128]{1,0:T(8,128)S(1)}, f32[108,128]{1,0:T(8,128)S(1)}, u32[]{:S(2)}, u32[]{:S(2)}) collective-permute-start(f32[108,128]{1,0:T(8,128)S(1)} %get-tuple-element.25), channel_id=1, source_target_pairs={{8,1},{9,0},{16,9},{17,8},{24,17},{25,16},{10,3},{11,2},{18,11},{1... | collective-permute-start | bytes 165896 | tf_op jit(solution)/shard_map/ppermute | solution.py:718
  32.4 18.5 %collective-permute-start.5 = (f32[472,128]{1,0:T(8,128)S(1)}, f32[472,128]{1,0:T(8,128)S(1)}, u32[]{:S(2)}, u32[]{:S(2)}) collective-permute-start(f32[472,128]{1,0:T(8,128)S(1)} %get-tuple-element.27), channel_id=1, source_target_pairs={{0,2},{2,4},{4,6},{1,3},{3,5},{5,7},{8,10},{10,12},{12,14},{9,11},... | collective-permute-start | bytes 725000 | tf_op jit(solution)/shard_map/ppermute | solution.py:744
  35.9 15.1 %collective-permute-start.6 = (f32[472,128]{1,0:T(8,128)S(1)}, f32[472,128]{1,0:T(8,128)S(1)}, u32[]{:S(2)}, u32[]{:S(2)}) collective-permute-start(f32[472,128]{1,0:T(8,128)S(1)} %get-tuple-element.28), channel_id=1, source_target_pairs={{2,0},{4,2},{6,4},{3,1},{5,3},{7,5},{10,8},{12,10},{14,12},{11,9},... | collective-permute-start | bytes 725000 | tf_op jit(solution)/shard_map/ppermute | solution.py:745

commit v3 on v2

--- a/solution.py
+++ b/solution.py
@@ -46,7 +46,8 @@
 BLOCK = PLANES * TILES
 YLO = LANE // EDGE
 SLAB = 4
-SENT_SLABS = MOVE_CAP * BLOCK
+GROUPS = ((0, 8), (8, 8), (16, 3))
+SENT_SLABS = BLOCK + 8
 LAYERS = BXD + 2
 ZGROUPS = 3
 ZROWS = ZGROUPS * TILES
@@ -67,8 +68,7 @@
 AHEAD = tuple(i for i in range(POPS) if VELOCITIES[i][0] == 1)
 BACK = tuple(i for i in range(POPS) if VELOCITIES[i][0] == -1)
 FACE = 2 * BZD
-SENT_META = SENT_SLABS + RIM * FACE
-SENT_ROWS = SENT_META + 8
+SENT_ROWS = SENT_SLABS + RIM * FACE
 RIM_BLOCKS = -(-RIM * EXT_Z // LANE)
 RIM_ROWS = RIM_BLOCKS * EXT_X + 4
 GRID_X = 48
@@ -213,61 +213,67 @@
             ref[pl.ds(base + i * TILES + 8 * part, 8), :] = jnp.where(mark, old[i], post[i])
 
 
-def pack_stream(places, marks_in, pops, up, down, pos, table, marks, dense, blocks, slabs, strip, sems):
-    mark_copy = pltpu.make_async_copy(marks_in, marks, sems.at[2 * MOVE_CAP + 2 * BZD])
+def pack_block(out, base, stage, dense, row):
+    out[pl.ds(base + POPS * TILES, TILES), :] = dense[pl.ds(pl.multiple_of(row * TILES, 8), TILES), :]
+    for tile in range(TILES):
+        for group, size in GROUPS:
+            value = stage[group : group + size, tile * LANE : (tile + 1) * LANE]
+            out[pl.ds(base + group * TILES + tile, size, stride=TILES), :] = value
+    collide_block(out, base)
+
+
+def pack_stream(part, places, marks_in, pops, up, down, pos, table, marks, dense, blocks, slabs, strip, sems):
+    mark_copy = pltpu.make_async_copy(marks_in, marks, sems.at[0])
     mark_copy.start()
-    place_copy = pltpu.make_async_copy(places, pos, sems.at[2 * MOVE_CAP + 2 * BZD + 1])
+    place_copy = pltpu.make_async_copy(places, pos, sems.at[1])
     place_copy.start()
+    down_copy = pltpu.make_async_copy(pops.at[part], blocks.at[1], sems.at[3])
+    down_copy.start()
     place_copy.wait()
-    fill_table(pos, table)
     rows = pos.shape[1]
     count = 0
     for row in range(rows):
         count = count + jnp.where(pos[0, row] >= 0, 1, 0)
-    last = jnp.clip(count - MOVE_CAP, 0, rows - MOVE_CAP)
-    sources = [last, last + 1, 0, 1]
-    copies = []
-    for n, row in enumerate(sources):
-        copies.append(pltpu.make_async_copy(pops.at[row], blocks.at[n], sems.at[n]))
+    last = jnp.clip(count - MOVE_CAP, 0, rows - MOVE_CAP) + part
+    up_copy = pltpu.make_async_copy(pops.at[last], blocks.at[0], sems.at[2])
+    up_copy.start()
     slab_rows = []
-    for side in range(2):
-        for bz in range(BZD):
-            row = jnp.maximum(table[(2 - side) * BZD + bz], 0)
-            n = side * BZD + bz
-            first = (TILES - SLAB) * LANE if side == 0 else 0
-            slab_rows.append(row)
-            copies.append(
-                pltpu.make_async_copy(
-                    pops.at[row, :, pl.ds(first, SLAB * LANE)], slabs.at[n], sems.at[4 + n]
+    slab_copies = []
+    if part == MOVE_CAP - 1:
+        fill_table(pos, table)
+        for side in range(2):
+            for bz in range(BZD):
+                row = jnp.maximum(table[(2 - side) * BZD + bz], 0)
+                n = side * BZD + bz
+                first = (TILES - SLAB) * LANE if side == 0 else 0
+                slab_rows.append(row)
+                slab_copies.append(
+                    pltpu.make_async_copy(
+                        pops.at[row, :, pl.ds(first, SLAB * LANE)], slabs.at[n], sems.at[4 + n]
+                    )
                 )
-            )
-    for copy in copies:
-        copy.start()
+        for copy in slab_copies:
+            copy.start()
     mark_copy.wait()
     spread_marks(marks, dense)
-    groups = ((0, 8), (8, 8), (16, 3))
+    for n, (out, row, copy) in ((1, (down, part, down_copy)), (0, (up, last, up_copy))):
+        for k, axis in ((0, 0), (1, 2)):
+            value = jnp.full((1, LANE), pos[axis, row], jnp.int32).astype(jnp.float32)
+            out[pl.ds(BLOCK + k, 1), :] = value
+        copy.wait()
+        pack_block(out, 0, blocks.at[n], dense, row)
+    if part < MOVE_CAP - 1:
+        return
     for side, out in enumerate((up, down)):
-        for j in range(MOVE_CAP):
-            row = sources[side * MOVE_CAP + j]
-            out[pl.ds(j * BLOCK + POPS * TILES, TILES), :] = dense[pl.ds(row * TILES, TILES), :]
-            for part, axis in ((0, 0), (1, 2)):
-                value = jnp.full((1, LANE), pos[axis, row], jnp.int32).astype(jnp.float32)
-                out[pl.ds(SENT_META + 2 * j + part, 1), :] = value
-            copies[side * MOVE_CAP + j].wait()
-            for group, size in groups:
-                for tile in range(TILES):
-                    value = blocks[side * MOVE_CAP + j, group : group + size, tile * LANE : (tile + 1) * LANE]
-                    out[pl.ds(j * BLOCK + group * TILES + tile, size, stride=TILES), :] = value
-            collide_block(out, j * BLOCK)
         for bz in range(BZD):
             n = side * BZD + bz
             first = slab_rows[n] * TILES + (TILES - SLAB if side == 0 else 0)
-            copies[4 + n].wait()
+            slab_copies[n].wait()
             for x in range(2):
                 for yhi in range(2):
                     q = 2 * x + yhi
                     row = x * FACE + 2 * bz + yhi
-                    for group, size in groups:
+                    for group, size in GROUPS:
                         value = slabs[n, group : group + size, q * LANE : (q + 1) * LANE]
                         strip[pl.ds(group * 2 * FACE + row, size, stride=2 * FACE), :] = value
                 row = POPS * 2 * FACE + x * FACE + 2 * bz
@@ -305,13 +311,7 @@
         @pl.when(pos[0, row] >= 0)
         def _():
             base = pl.multiple_of(slot_of(pos, row, layer, column_z) * BLOCK, 8)
-            for tile in range(TILES):
-                for group, size in ((0, 8), (8, 8), (16, 3)):
-                    value = stage[row, group : group + size, tile * LANE : (tile + 1) * LANE]
-                    own[pl.ds(base + group * TILES + tile, size, stride=TILES), :] = value
-            from_row = pl.multiple_of(row * TILES, 8)
-            own[pl.ds(base + POPS * TILES, TILES), :] = dense[pl.ds(from_row, TILES), :]
-            collide_block(own, base)
+            pack_block(own, base, stage.at[row], dense, row)
 
         return carry
 
@@ -348,9 +348,8 @@
         zdown[target, :] = zpack[pl.ds(ZROWS + group * TILES, SLAB), :]
 
 
-def gathered(load, zload, ylo, column_z):
+def gathered(parts, zvalue, spot, ylo, column_z):
     lane = lanes()
-    parts = [load(bz) for bz in range(BZD)]
     rows = parts[0].shape[0]
     lane = lane[:rows]
     total = None
@@ -358,10 +357,33 @@
         shift = (bz * EDGE - ylo * EDGE) % LANE
         value = pltpu.roll(parts[bz], shift, 1) if shift else parts[bz]
         total = value if total is None else jnp.where(lane // EDGE == bz, value, total)
-    zvalue, spot = zload
     goal = jnp.where(column_z == 0, SPAN_Z, LANE - 2)
     zvalue = pltpu.roll(zvalue, (goal - (ylo * EDGE + 2 * spot) + LANE) % LANE, 1)
     return jnp.where(lane >= SPAN_Z, zvalue, total)
+
+
+def gathered_rows(parts, zvalue, spot, column_z):
+    lane = lanes()[: parts[0].shape[0]]
+    single = (lane // EDGE) % 2 == 1
+    double = (lane // (2 * EDGE)) % 2 == 1
+    main = lane < SPAN_Z
+    pairs = []
+    for n in (0, 2):
+        even = jnp.where(single, pltpu.roll(parts[n + 1], EDGE, 1), parts[n])
+        odd = jnp.where(single, parts[n + 1], pltpu.roll(parts[n], LANE - EDGE, 1))
+        pairs.append((even, odd))
+    goal = jnp.where(column_z == 0, SPAN_Z, LANE - 2)
+    out = [None] * YLO
+    for r in range(4):
+        low, high = pairs[0][r % 2], pairs[1][r % 2]
+        if r < 2:
+            both = jnp.where(double, pltpu.roll(high, 2 * EDGE, 1), low)
+        else:
+            both = jnp.where(double, high, pltpu.roll(low, LANE - 2 * EDGE, 1))
+        beyond = pltpu.roll(zvalue, (goal - (r * EDGE + 2 * spot) + LANE) % LANE, 1)
+        out[r] = jnp.where(main, both, beyond)
+        out[r + 4] = pltpu.roll(jnp.where(main, beyond, both), SPAN_Z, 1)
+    return out
 
 
 def inside_lanes(rows, column_z):
@@ -377,27 +399,27 @@
     return [jnp.where(wall, flag, value) for value in post]
 
 
+def plane_parts(own, edge, zall, zedge, chunk, yhi, plane):
+    group = plane // 8
+    if chunk is None:
+        if plane == POPS:
+            parts = [jnp.zeros((4, LANE), jnp.float32)] * BZD
+        else:
+            parts = [edge[pl.ds(plane * 4 * FACE + 2 * bz + yhi, 4, stride=FACE), :] for bz in range(BZD)]
+        return parts, zedge[pl.ds(group * 8 + yhi, 4, stride=2), :]
+    held, half = 1 + chunk // 2, chunk % 2
+    parts = []
+    for bz in range(BZD):
+        base = (held * BZD + bz) * BLOCK + plane * TILES + half * EDGE + yhi
+        parts.append(own[pl.ds(base, 8, stride=2), :])
+    return parts, zall[pl.ds(held * ZROWS + group * TILES + half * EDGE + yhi, 8, stride=2), :]
+
+
 def chunk_values(own, edge, zall, zedge, chunk, yhi, ylo, column_z):
     out = []
     for plane in range(PLANES):
-        group, spot = plane // 8, plane % 8
-        if chunk is None:
-
-            def load(bz):
-                if plane == POPS:
-                    return jnp.zeros((4, LANE), jnp.float32)
-                return edge[pl.ds(plane * 4 * FACE + 2 * bz + yhi, 4, stride=FACE), :]
-
-            zvalue = zedge[pl.ds(group * 8 + yhi, 4, stride=2), :]
-        else:
-            held, half = 1 + chunk // 2, chunk % 2
-
-            def load(bz):
-                base = (held * BZD + bz) * BLOCK + plane * TILES + half * EDGE + yhi
-                return own[pl.ds(base, 8, stride=2), :]
-
-            zvalue = zall[pl.ds(held * ZROWS + group * TILES + half * EDGE + yhi, 8, stride=2), :]
-        out.append(gathered(load, (zvalue, spot), ylo, column_z))
+        parts, zvalue = plane_parts(own, edge, zall, zedge, chunk, yhi, plane)
+        out.append(gathered(parts, zvalue, plane % 8, ylo, column_z))
     return out
 
 
@@ -408,25 +430,24 @@
     return low | high
 
 
-def settle_rim(layers, places, up, down, zin, zup, zdown, own_in, own, edge, zall, zedge, rim_up, rim_down, pos, post_up, post_down, sem):
+def settle_rim(layers, places, up_first, down_first, up, down, zin, zup, zdown, own_in, own, edge, zall, zedge, rim_up, rim_down, pos, post_up, post_down, sem):
     del own_in
     layer, _, column_z = place()
     place_copy = pltpu.make_async_copy(places, pos, sem)
     place_copy.start()
-    for arrived in (up, down):
-        for j in range(MOVE_CAP):
-            bx = arrived[pl.ds(SENT_META + 2 * j, 1), :].astype(jnp.int32)
-            bz = arrived[pl.ds(SENT_META + 2 * j + 1, 1), :].astype(jnp.int32)
-            code = (bx - layer * BXD) * BZD + (bz - column_z * BZD)
-            mine = (bx >= layer * BXD) & (bx < (layer + 1) * BXD)
-            first = layer == 0 if arrived is up else layer == layers - 1
-            code = jnp.max(jnp.where(mine, code, -1))
-
-            @pl.when((code >= 0) & jnp.logical_not(first))
-            def _(arrived=arrived, j=j, code=code):
-                base = pl.multiple_of((jnp.clip(code, 0, BXD * BZD - 1) + BZD) * BLOCK, 8)
-                for n in range(BLOCK // 8):
-                    own[pl.ds(base + 8 * n, 8), :] = arrived[pl.ds(j * BLOCK + 8 * n, 8), :]
+    for n, arrived in enumerate((up_first, down_first, up, down)):
+        bx = arrived[pl.ds(BLOCK, 1), :].astype(jnp.int32)
+        bz = arrived[pl.ds(BLOCK + 1, 1), :].astype(jnp.int32)
+        code = (bx - layer * BXD) * BZD + (bz - column_z * BZD)
+        mine = (bx >= layer * BXD) & (bx < (layer + 1) * BXD)
+        first = layer == 0 if n % 2 == 0 else layer == layers - 1
+        code = jnp.max(jnp.where(mine, code, -1))
+
+        @pl.when((code >= 0) & jnp.logical_not(first))
+        def _(arrived=arrived, code=code):
+            base = pl.multiple_of((jnp.clip(code, 0, BXD * BZD - 1) + BZD) * BLOCK, 8)
+            for k in range(BLOCK // 8):
+                own[pl.ds(base + 8 * k, 8), :] = arrived[pl.ds(8 * k, 8), :]
 
     place_copy.wait()
     for side, arrived in enumerate((up, down)):
@@ -539,27 +560,36 @@
 def settle_all(layers, columns, depth, own, edge, zall, zedge, field, start, later):
     layer, _, column_z = place()
 
+    def flags_of(mark, inside):
+        return [jnp.where(inside, jnp.where(value > 0.5, ROTOR, 0.0), OUTSIDE) for value in mark]
+
     def halves(yhi, carry):
+        def rows_of_plane(chunk, plane):
+            parts, zvalue = plane_parts(own, edge, zall, zedge, chunk, yhi, plane)
+            return gathered_rows(parts, zvalue, plane % 8, column_z)
+
         def chunks(chunk, carry):
+            flags = flags_of(rows_of_plane(chunk, POPS), inside_lanes(8, column_z))
+            for i in range(POPS):
+                values = rows_of_plane(chunk, i)
+                for ylo in range(YLO):
+                    row = i * FIELD + (8 * chunk + 2) * PITCH + FIRST + YLO * yhi + ylo
+                    value = jnp.where(flags[ylo] < WALL_BELOW, flags[ylo], values[ylo])
+                    field[pl.ds(row, 8, stride=PITCH), :] = value
+                    target = (i * SPAN_X + 8 * chunk) * SPAN_Y + YLO * yhi + ylo
+                    start[pl.ds(target, 8, stride=SPAN_Y), :] = values[ylo]
+            return carry
+
+        lax.fori_loop(0, SPAN_X // 8, chunks, 0)
+        inside = inside_lanes(4, column_z) & halo_x_inside(layer, layers)
+        flags = flags_of(rows_of_plane(None, POPS), inside)
+        for i in range(POPS):
+            values = rows_of_plane(None, i)
             for ylo in range(YLO):
-                values = chunk_values(own, edge, zall, zedge, chunk, yhi, ylo, column_z)
-                post = marked(values[:POPS], values[POPS], inside_lanes(8, column_z))
-                row = (8 * chunk + 2) * PITCH + FIRST + YLO * yhi + ylo
-                for i in range(POPS):
-                    field[pl.ds(i * FIELD + row, 8, stride=PITCH), :] = post[i]
-                    target = (i * SPAN_X + 8 * chunk) * SPAN_Y + YLO * yhi + ylo
-                    start[pl.ds(target, 8, stride=SPAN_Y), :] = values[i]
-            return carry
-
-        lax.fori_loop(0, SPAN_X // 8, chunks, 0)
-        for ylo in range(YLO):
-            values = chunk_values(own, edge, zall, zedge, None, yhi, ylo, column_z)
-            inside = inside_lanes(4, column_z) & halo_x_inside(layer, layers)
-            post = marked(values[:POPS], values[POPS], inside)
-            for first, side in ((0, 0), (EXT_X - 2, 2)):
-                row = first * PITCH + FIRST + YLO * yhi + ylo
-                for i in range(POPS):
-                    field[pl.ds(i * FIELD + row, 2, stride=PITCH), :] = post[i][side : side + 2]
+                value = jnp.where(flags[ylo] < WALL_BELOW, flags[ylo], values[ylo])
+                for first, side in ((0, 0), (EXT_X - 2, 2)):
+                    row = i * FIELD + first * PITCH + FIRST + YLO * yhi + ylo
+                    field[pl.ds(row, 2, stride=PITCH), :] = value[side : side + 2]
         return carry
 
     lax.fori_loop(0, SPAN_Y // YLO, halves, 0)
@@ -675,26 +705,33 @@
     place_scratch = SMEM((3, rows), jnp.int32)
     mark_scratch = [VMEM((rows, EDGE**3), jnp.int32), VMEM((rows * TILES, LANE), jnp.float32)]
 
-    send_up, send_down = pl.pallas_call(
-        pack_stream,
-        out_shape=(kept(SENT_ROWS), kept(SENT_ROWS)),
-        in_specs=[hbm, hbm, hbm],
-        out_specs=(vmem, vmem),
-        scratch_shapes=[place_scratch, SMEM((LAYERS * BZD,), jnp.int32)]
-        + mark_scratch
-        + [
-            VMEM((2 * MOVE_CAP, POPS, EDGE**3), jnp.float32),
-            VMEM((2 * BZD, POPS, SLAB * LANE), jnp.float32),
-            VMEM((PLANES * 2 * FACE, LANE), jnp.float32),
-            pltpu.SemaphoreType.DMA((2 * MOVE_CAP + 2 * BZD + 2,)),
-        ],
-        compiler_params=params(16),
-        name="pack_stream",
-    )(places, solid_cells, populations)
     up = [(i, i + 1) for i in range(layers - 1)]
     down = [(i + 1, i) for i in range(layers - 1)]
-    from_low = lax.ppermute(send_up, "stream", up)
-    from_high = lax.ppermute(send_down, "stream", down)
+    from_low = []
+    from_high = []
+    for part in range(MOVE_CAP):
+        sent = BLOCK + 8 if part < MOVE_CAP - 1 else SENT_ROWS
+        send_up, send_down = pl.pallas_call(
+            functools.partial(pack_stream, part),
+            out_shape=(kept(sent), kept(sent)),
+            in_specs=[hbm, hbm, hbm],
+            out_specs=(vmem, vmem),
+            scratch_shapes=[place_scratch, SMEM((LAYERS * BZD,), jnp.int32)]
+            + mark_scratch
+            + [
+                VMEM((2, POPS, EDGE**3), jnp.float32),
+                VMEM((2 * BZD, POPS, SLAB * LANE), jnp.float32),
+                VMEM((PLANES * 2 * FACE, LANE), jnp.float32),
+                pltpu.SemaphoreType.DMA((4 + 2 * BZD,)),
+            ],
+            compiler_params=params(16),
+            name="pack_stream",
+        )(places, solid_cells, populations)
+        if part < MOVE_CAP - 1:
+            send_up, send_down, places = lax.optimization_barrier((send_up, send_down, places))
+            places = pltpu.with_memory_space_constraint(places, pltpu.HBM)
+        from_low.append(lax.ppermute(send_up, "stream", up))
+        from_high.append(lax.ppermute(send_down, "stream", down))
 
     own, zpack, zsend_up, zsend_down = pl.pallas_call(
         pack_own,
@@ -710,6 +747,9 @@
         compiler_params=params(16),
         name="pack_own",
     )(places, solid_cells, populations)
+    zpack, zsend_up, zsend_down, from_low[0], from_high[0] = lax.optimization_barrier(
+        (zpack, zsend_up, zsend_down, from_low[0], from_high[0])
+    )
     swap = [(i, depth - 1 - i) for i in range(depth)]
     zin = lax.ppermute(zpack, "cz", swap)
     zup_pairs = [(s * depth + c, t * depth + d) for s, t in up for c, d in swap]
@@ -727,7 +767,7 @@
             kept(RIM_ROWS),
             kept(RIM_ROWS),
         ),
-        in_specs=[hbm] + [vmem] * 6,
+        in_specs=[hbm] + [vmem] * 8,
         out_specs=(vmem,) * 6,
         scratch_shapes=[
             place_scratch,
@@ -735,10 +775,10 @@
             VMEM((RIM * GRID_X, LANE), jnp.float32),
             pltpu.SemaphoreType.DMA,
         ],
-        input_output_aliases={6: 0},
+        input_output_aliases={8: 0},
         compiler_params=params(16),
         name="settle_rim",
-    )(places, from_low, from_high, zin, z_low, z_high, own)
+    )(places, from_low[0], from_high[0], from_low[1], from_high[1], zin, z_low, z_high, own)
     cy_up = [(i, i + 1) for i in range(columns - 1)]
     cy_down = [(i + 1, i) for i in range(columns - 1)]
     rim_low = lax.ppermute(rim_up, "cy", cy_up)

time: 57.3 us -> 75.4 us (1.32)
  the two profiles are of different devices: /device:TPU:0 before, /device:TPU:12 now
where the time goes in v3:
time: 75.4 us; the launch traced here: 75.1 us
  Pallas kernels  43.8 us (58%)
  starting transfers between devices  27.1 us (36%)
  waiting for transfers between devices  3.98 us (5%)
    pallas_call x1, Pallas kernels, shards(): pl.pallas_call(functools.partial(settle_all, layers, columns, depth), out...  26.9 us
    ppermute x2, starting transfers between devices, shards(): from_low.append(lax.ppermute(send_up, 'stream', up))  6.95 us
    ppermute x1, starting transfers between devices, shards(): z_low = lax.ppermute(zsend_up, ('stream', 'cz'), zup_pairs)  6.65 us
    pallas_call x1, Pallas kernels, shards(): pl.pallas_call(functools.partial(finish, columns, depth), out_shape=(jax....  5.41 us
    pallas_call x2, Pallas kernels, shards(): pl.pallas_call(functools.partial(pack_stream, part), out_shape=(kept(sent...  4.99 us
    ppermute x2, starting transfers between devices, shards(): from_high.append(lax.ppermute(send_down, 'stream', down))  4.77 us
    ppermute x1, waiting for transfers between devices, shards(): z_high = lax.ppermute(zsend_down, ('stream', 'cz'), zdown_pairs)  3.96 us
    ppermute x1, starting transfers between devices, shards(): rim_low = lax.ppermute(rim_up, 'cy', cy_up)  3.4 us
  transfers between devices with their start and end apart: 9, of which 1 were waited for; matrix products, arithmetic and copies ran while one was open for 0% of the time, Pallas kernels for 44%

profile of v3, /device:TPU:12, one launch (start us, length us, event | category | flops | bytes accessed | tf_op | source)
XLA Modules:
  0.0 75.1 jit_solution(2123859949161247145)
XLA Ops:
  0.0 2.4 %pack_stream.2 = (f32[648,128]{1,0:T(8,128)S(1)}, f32[648,128]{1,0:T(8,128)S(1)}) custom-call(s32[3,12]{1,0:T(4,128)} %bitcast.1, s32[12,4096]{1,0:T(8,128)} %marks_in.5, f32[12,19,4096]{2,1,0:T(8,128)} %pops.5), custom_call_target="tpu_custom_call" | custom-call | tf_op jit(solution)/shard_map/pack_stream/pallas_call | solution.py:714
  2.4 3.5 %collective-permute-start = (f32[648,128]{1,0:T(8,128)S(1)}, f32[648,128]{1,0:T(8,128)S(1)}, u32[]{:S(2)}, u32[]{:S(2)}) collective-permute-start(f32[648,128]{1,0:T(8,128)S(1)} %get-tuple-element.37), channel_id=1, source_target_pairs={{0,8},{8,16},{16,24},{1,9},{9,17},{17,25},{2,10},{10,18},{18,26},{... | collective-permute-start | bytes 995336 | tf_op jit(solution)/shard_map/ppermute | solution.py:733
  5.9 2.4 %collective-permute-start.1 = (f32[648,128]{1,0:T(8,128)S(1)}, f32[648,128]{1,0:T(8,128)S(1)}, u32[]{:S(2)}, u32[]{:S(2)}) collective-permute-start(f32[648,128]{1,0:T(8,128)S(1)} %get-tuple-element.38), channel_id=1, source_target_pairs={{8,0},{16,8},{24,16},{9,1},{17,9},{25,17},{10,2},{18,10},{26,18},{... | collective-permute-start | bytes 995336 | tf_op jit(solution)/shard_map/ppermute | solution.py:734
  8.3 2.6 %pack_stream.3 = (f32[840,128]{1,0:T(8,128)S(1)}, f32[840,128]{1,0:T(8,128)S(1)}) custom-call(s32[3,12]{1,0:T(4,128)} %bitcast.2, s32[12,4096]{1,0:T(8,128)} %marks_in.5, f32[12,19,4096]{2,1,0:T(8,128)} %pops.5), custom_call_target="tpu_custom_call" | custom-call | tf_op jit(solution)/shard_map/pack_stream/pallas_call | solution.py:714
  10.9 3.5 %collective-permute-start.2 = (f32[840,128]{1,0:T(8,128)S(1)}, f32[840,128]{1,0:T(8,128)S(1)}, u32[]{:S(2)}, u32[]{:S(2)}) collective-permute-start(f32[840,128]{1,0:T(8,128)S(1)} %get-tuple-element.41), channel_id=1, source_target_pairs={{0,8},{8,16},{16,24},{1,9},{9,17},{17,25},{2,10},{10,18},{18,26},{... | collective-permute-start | bytes 1290248 | tf_op jit(solution)/shard_map/ppermute | solution.py:733
  14.4 2.4 %collective-permute-start.3 = (f32[840,128]{1,0:T(8,128)S(1)}, f32[840,128]{1,0:T(8,128)S(1)}, u32[]{:S(2)}, u32[]{:S(2)}) collective-permute-start(f32[840,128]{1,0:T(8,128)S(1)} %get-tuple-element.42), channel_id=1, source_target_pairs={{8,0},{16,8},{24,16},{9,1},{17,9},{25,17},{10,2},{18,10},{26,18},{... | collective-permute-start | bytes 1290248 | tf_op jit(solution)/shard_map/ppermute | solution.py:734
  16.8 3.4 %pack_own.1 = (f32[10240,128]{1,0:T(8,128)S(1)}, f32[392,128]{1,0:T(8,128)S(1)}, f32[108,128]{1,0:T(8,128)S(1)}, f32[108,128]{1,0:T(8,128)S(1)}) custom-call(s32[3,12]{1,0:T(4,128)} %bitcast.3, s32[12,4096]{1,0:T(8,128)} %marks_in.5, f32[12,19,4096]{2,1,0:T(8,128)} %pops.5), custom_call_target="tpu_custom_call" | custom-call | tf_op jit(solution)/shard_map/pack_own/pallas_call | solution.py:736
  20.2 0.0 collective-permute-done.up_first
  20.2 0.0 collective-permute-done.1.down_first
  20.2 0.1 collective-permute-start.4
  20.3 6.7 %collective-permute-start.5 = (f32[108,128]{1,0:T(8,128)S(1)}, f32[108,128]{1,0:T(8,128)S(1)}, u32[]{:S(2)}, u32[]{:S(2)}) collective-permute-start(f32[108,128]{1,0:T(8,128)S(1)} %get-tuple-element.44), channel_id=1, source_target_pairs={{0,9},{1,8},{8,17},{9,16},{16,25},{17,24},{2,11},{3,10},{10,19},{1... | collective-permute-start | bytes 165896 | tf_op jit(solution)/shard_map/ppermute | solution.py:757
  26.9 1.9 %collective-permute-start.6 = (f32[108,128]{1,0:T(8,128)S(1)}, f32[108,128]{1,0:T(8,128)S(1)}, u32[]{:S(2)}, u32[]{:S(2)}) collective-permute-start(f32[108,128]{1,0:T(8,128)S(1)} %get-tuple-element.45), channel_id=1, source_target_pairs={{8,1},{9,0},{16,9},{17,8},{24,17},{25,16},{10,3},{11,2},{18,11},{1... | collective-permute-start | bytes 165896 | tf_op jit(solution)/shard_map/ppermute | solution.py:758
  28.8 0.0 collective-permute-done.5.zup
  28.9 4.0 %collective-permute-done.6.zdown = f32[108,128]{1,0:T(8,128)S(1)} collective-permute-done((f32[108,128]{1,0:T(8,128)S(1)}, f32[108,128]{1,0:T(8,128)S(1)}, u32[]{:S(2)}, u32[]{:S(2)}) %collective-permute-start.6) | collective-permute-done | bytes 55328 | tf_op jit(solution)/shard_map/ppermute | solution.py:758
  32.8 0.0 collective-permute-done.2.up
  32.8 0.0 collective-permute-done.3.down
  32.8 0.0 collective-permute-done.4.zin
  32.8 3.2 %settle_rim.1 = (f32[10240,128]{1,0:T(8,128)S(1)}, f32[608,128]{1,0:T(8,128)S(1)}, f32[384,128]{1,0:T(8,128)S(1)}, f32[24,128]{1,0:T(8,128)S(1)}, f32[472,128]{1,0:T(8,128)S(1)}, /*index=5*/f32[472,128]{1,0:T(8,128)S(1)}) custom-call(s32[3,12]{1,0:T(4,128)} %bitcast.4, ...), custom_call_target="tpu_custom_call", output_to_operand_aliasing={{0}: (8, {})} | custom-call | tf_op jit(solution)/shard_map/settle_rim/pallas_call | solution.py:760
  36.0 3.4 %collective-permute-start.7 = (f32[472,128]{1,0:T(8,128)S(1)}, f32[472,128]{1,0:T(8,128)S(1)}, u32[]{:S(2)}, u32[]{:S(2)}) collective-permute-start(f32[472,128]{1,0:T(8,128)S(1)} %get-tuple-element.47), channel_id=1, source_target_pairs={{0,2},{2,4},{4,6},{1,3},{3,5},{5,7},{8,10},{10,12},{12,14},{9,11},... | collective-permute-start | bytes 725000 | tf_op jit(solution)/shard_map/ppermute | solution.py:784
  39.4 3.3 %collective-permute-start.8 = (f32[472,128]{1,0:T(8,128)S(1)}, f32[472,128]{1,0:T(8,128)S(1)}, u32[]{:S(2)}, u32[]{:S(2)}) collective-permute-start(f32[472,128]{1,0:T(8,128)S(1)} %get-tuple-element.48), channel_id=1, source_target_pairs={{2,0},{4,2},{6,4},{3,1},{5,3},{7,5},{10,8},{12,10},{14,12},{11,9},... | collective-permute-start | bytes 725000 | tf_op jit(solution)/shard_map/ppermute | solution.py:785
  42.8 26.9 %settle_all.1 = (f32[16720,128]{1,0:T(8,128)S(1)}, f32[9728,128]{1,0:T(8,128)S(1)}, f32[16720,128]{1,0:T(8,128)S(1)}) custom-call(f32[10240,128]{1,0:T(8,128)S(1)} %get-tuple-element.49.own, f32[608,128]{1,0:T(8,128)S(1)} %get-tuple-element.50.edge, f32[384,128]{1,0:T(8,128)S(1)} %get-tuple-element.51.zall, f32[24,128]{1,0:T(8,128)S(1)} %get-tuple-element.52.zedge), custom_call_target="tpu_custom_call" | custom-call | tf_op jit(solution)/shard_map/settle_all/pallas_call | solution.py:787
  69.6 0.0 collective-permute-done.7.rim_low
  69.6 0.0 collective-permute-done.8.rim_high
  69.7 5.4 %finish.1 = (f32[19,32,16,64]{3,2,1,0:T(8,128)}, f32[16720,128]{1,0:T(8,128)S(1)}) custom-call(f32[472,128]{1,0:T(8,128)S(1)} %collective-permute-done.7.rim_low, f32[472,128]{1,0:T(8,128)S(1)} %collective-permute-done.8.rim_high, f32[16720,128]{1,0:T(8,128)S(1)} %get-tuple-element.53.field, ...), custom_call_target="tpu_custom_call", output_to_operand_aliasing={{1}: (4, {})} | custom-call | tf_op jit(solution)/shard_map/finish/pallas_call | solution.py:796
Async XLA Ops:
  2.4 17.8 %collective-permute-start = (f32[648,128]{1,0:T(8,128)S(1)}, f32[648,128]{1,0:T(8,128)S(1)}, u32[]{:S(2)}, u32[]{:S(2)}) collective-permute-start(f32[648,128]{1,0:T(8,128)S(1)} %get-tuple-element.37), channel_id=1, source_target_pairs={{0,8},{8,16},{16,24},{1,9},{9,17},{17,25},{2,10},{10,18},{18,26},{... | collective-permute-start | bytes 995336 | tf_op jit(solution)/shard_map/ppermute | solution.py:733
  5.9 14.3 %collective-permute-start.1 = (f32[648,128]{1,0:T(8,128)S(1)}, f32[648,128]{1,0:T(8,128)S(1)}, u32[]{:S(2)}, u32[]{:S(2)}) collective-permute-start(f32[648,128]{1,0:T(8,128)S(1)} %get-tuple-element.38), channel_id=1, source_target_pairs={{8,0},{16,8},{24,16},{9,1},{17,9},{25,17},{10,2},{18,10},{26,18},{... | collective-permute-start | bytes 995336 | tf_op jit(solution)/shard_map/ppermute | solution.py:734
  10.9 21.9 %collective-permute-start.2 = (f32[840,128]{1,0:T(8,128)S(1)}, f32[840,128]{1,0:T(8,128)S(1)}, u32[]{:S(2)}, u32[]{:S(2)}) collective-permute-start(f32[840,128]{1,0:T(8,128)S(1)} %get-tuple-element.41), channel_id=1, source_target_pairs={{0,8},{8,16},{16,24},{1,9},{9,17},{17,25},{2,10},{10,18},{18,26},{... | collective-permute-start | bytes 1290248 | tf_op jit(solution)/shard_map/ppermute | solution.py:733
  14.4 18.5 %collective-permute-start.3 = (f32[840,128]{1,0:T(8,128)S(1)}, f32[840,128]{1,0:T(8,128)S(1)}, u32[]{:S(2)}, u32[]{:S(2)}) collective-permute-start(f32[840,128]{1,0:T(8,128)S(1)} %get-tuple-element.42), channel_id=1, source_target_pairs={{8,0},{16,8},{24,16},{9,1},{17,9},{25,17},{10,2},{18,10},{26,18},{... | collective-permute-start | bytes 1290248 | tf_op jit(solution)/shard_map/ppermute | solution.py:734
  20.2 12.7 %collective-permute-start.4 = (f32[392,128]{1,0:T(8,128)S(1)}, f32[392,128]{1,0:T(8,128)S(1)}, u32[]{:S(2)}, u32[]{:S(2)}) collective-permute-start(f32[392,128]{1,0:T(8,128)S(1)} %get-tuple-element.43), channel_id=1, source_target_pairs={{0,1},{1,0},{2,3},{3,2},{4,5},{5,4},{6,7},{7,6},{8,9},{9,8},{10,11... | collective-permute-start | bytes 602120 | tf_op jit(solution)/shard_map/ppermute | solution.py:754
  20.3 8.6 %collective-permute-start.5 = (f32[108,128]{1,0:T(8,128)S(1)}, f32[108,128]{1,0:T(8,128)S(1)}, u32[]{:S(2)}, u32[]{:S(2)}) collective-permute-start(f32[108,128]{1,0:T(8,128)S(1)} %get-tuple-element.44), channel_id=1, source_target_pairs={{0,9},{1,8},{8,17},{9,16},{16,25},{17,24},{2,11},{3,10},{10,19},{1... | collective-permute-start | bytes 165896 | tf_op jit(solution)/shard_map/ppermute | solution.py:757
  26.9 5.9 %collective-permute-start.6 = (f32[108,128]{1,0:T(8,128)S(1)}, f32[108,128]{1,0:T(8,128)S(1)}, u32[]{:S(2)}, u32[]{:S(2)}) collective-permute-start(f32[108,128]{1,0:T(8,128)S(1)} %get-tuple-element.45), channel_id=1, source_target_pairs={{8,1},{9,0},{16,9},{17,8},{24,17},{25,16},{10,3},{11,2},{18,11},{1... | collective-permute-start | bytes 165896 | tf_op jit(solution)/shard_map/ppermute | solution.py:758
  36.0 33.6 %collective-permute-start.7 = (f32[472,128]{1,0:T(8,128)S(1)}, f32[472,128]{1,0:T(8,128)S(1)}, u32[]{:S(2)}, u32[]{:S(2)}) collective-permute-start(f32[472,128]{1,0:T(8,128)S(1)} %get-tuple-element.47), channel_id=1, source_target_pairs={{0,2},{2,4},{4,6},{1,3},{3,5},{5,7},{8,10},{10,12},{12,14},{9,11},... | collective-permute-start | bytes 725000 | tf_op jit(solution)/shard_map/ppermute | solution.py:784
  39.4 30.2 %collective-permute-start.8 = (f32[472,128]{1,0:T(8,128)S(1)}, f32[472,128]{1,0:T(8,128)S(1)}, u32[]{:S(2)}, u32[]{:S(2)}) collective-permute-start(f32[472,128]{1,0:T(8,128)S(1)} %get-tuple-element.48), channel_id=1, source_target_pairs={{2,0},{4,2},{6,4},{3,1},{5,3},{7,5},{10,8},{12,10},{14,12},{11,9},... | collective-permute-start | bytes 725000 | tf_op jit(solution)/shard_map/ppermute | solution.py:785

commit v4 on v3

--- a/solution.py
+++ b/solution.py
@@ -47,7 +47,7 @@
 YLO = LANE // EDGE
 SLAB = 4
 GROUPS = ((0, 8), (8, 8), (16, 3))
-SENT_SLABS = BLOCK + 8
+SENT_SLABS = MOVE_CAP * BLOCK
 LAYERS = BXD + 2
 ZGROUPS = 3
 ZROWS = ZGROUPS * TILES
@@ -68,7 +68,8 @@
 AHEAD = tuple(i for i in range(POPS) if VELOCITIES[i][0] == 1)
 BACK = tuple(i for i in range(POPS) if VELOCITIES[i][0] == -1)
 FACE = 2 * BZD
-SENT_ROWS = SENT_SLABS + RIM * FACE
+SENT_META = SENT_SLABS + RIM * FACE
+SENT_ROWS = SENT_META + 8
 RIM_BLOCKS = -(-RIM * EXT_Z // LANE)
 RIM_ROWS = RIM_BLOCKS * EXT_X + 4
 GRID_X = 48
@@ -175,6 +176,16 @@
     return out
 
 
+def ahead(items, take, leave, depth):
+    waiting = []
+    for n in items:
+        waiting.append((n, take(n)))
+        if len(waiting) > depth:
+            leave(*waiting.pop(0))
+    for pair in waiting:
+        leave(*pair)
+
+
 def place():
     return lax.axis_index("stream"), lax.axis_index("cy"), lax.axis_index("cz")
 
@@ -199,9 +210,10 @@
     rows = marks.shape[0]
     for first in range(0, rows, 8):
         size = min(8, rows - first)
-        for tile in range(TILES):
-            value = marks[first : first + size, tile * LANE : (tile + 1) * LANE].astype(jnp.float32)
-            dense[pl.ds(first * TILES + tile, size, stride=TILES), :] = value
+        for begin in range(0, TILES, 8):
+            values = [marks[first : first + size, t * LANE : (t + 1) * LANE] for t in range(begin, begin + 8)]
+            for k, value in enumerate(values):
+                dense[pl.ds(first * TILES + begin + k, size, stride=TILES), :] = value.astype(jnp.float32)
 
 
 def collide_block(ref, base):
@@ -215,69 +227,78 @@
 
 def pack_block(out, base, stage, dense, row):
     out[pl.ds(base + POPS * TILES, TILES), :] = dense[pl.ds(pl.multiple_of(row * TILES, 8), TILES), :]
-    for tile in range(TILES):
-        for group, size in GROUPS:
-            value = stage[group : group + size, tile * LANE : (tile + 1) * LANE]
-            out[pl.ds(base + group * TILES + tile, size, stride=TILES), :] = value
+    for first in range(0, TILES, 4):
+        moves = []
+        for tile in range(first, first + 4):
+            for group, size in GROUPS:
+                value = stage[group : group + size, tile * LANE : (tile + 1) * LANE]
+                moves.append((pl.ds(base + group * TILES + tile, size, stride=TILES), value))
+        for target, value in moves:
+            out[target, :] = value
     collide_block(out, base)
 
 
-def pack_stream(part, places, marks_in, pops, up, down, pos, table, marks, dense, blocks, slabs, strip, sems):
+def pack_stream(places, marks_in, pops, up, down, pos, table, marks, dense, blocks, slabs, strip, sems):
     mark_copy = pltpu.make_async_copy(marks_in, marks, sems.at[0])
     mark_copy.start()
     place_copy = pltpu.make_async_copy(places, pos, sems.at[1])
     place_copy.start()
-    down_copy = pltpu.make_async_copy(pops.at[part], blocks.at[1], sems.at[3])
-    down_copy.start()
+    rows = pos.shape[1]
+    copies = [None] * 4
+    for j in range(MOVE_CAP):
+        copies[MOVE_CAP + j] = pltpu.make_async_copy(pops.at[j], blocks.at[MOVE_CAP + j], sems.at[2 + MOVE_CAP + j])
+        copies[MOVE_CAP + j].start()
     place_copy.wait()
-    rows = pos.shape[1]
     count = 0
     for row in range(rows):
         count = count + jnp.where(pos[0, row] >= 0, 1, 0)
-    last = jnp.clip(count - MOVE_CAP, 0, rows - MOVE_CAP) + part
-    up_copy = pltpu.make_async_copy(pops.at[last], blocks.at[0], sems.at[2])
-    up_copy.start()
+    last = jnp.clip(count - MOVE_CAP, 0, rows - MOVE_CAP)
+    for j in range(MOVE_CAP):
+        copies[j] = pltpu.make_async_copy(pops.at[last + j], blocks.at[j], sems.at[2 + j])
+        copies[j].start()
+    fill_table(pos, table)
     slab_rows = []
     slab_copies = []
-    if part == MOVE_CAP - 1:
-        fill_table(pos, table)
-        for side in range(2):
-            for bz in range(BZD):
-                row = jnp.maximum(table[(2 - side) * BZD + bz], 0)
-                n = side * BZD + bz
-                first = (TILES - SLAB) * LANE if side == 0 else 0
-                slab_rows.append(row)
-                slab_copies.append(
-                    pltpu.make_async_copy(
-                        pops.at[row, :, pl.ds(first, SLAB * LANE)], slabs.at[n], sems.at[4 + n]
-                    )
+    for side in range(2):
+        for bz in range(BZD):
+            row = jnp.maximum(table[(2 - side) * BZD + bz], 0)
+            n = side * BZD + bz
+            first = (TILES - SLAB) * LANE if side == 0 else 0
+            slab_rows.append(row)
+            slab_copies.append(
+                pltpu.make_async_copy(
+                    pops.at[row, :, pl.ds(first, SLAB * LANE)], slabs.at[n], sems.at[2 + 2 * MOVE_CAP + n]
                 )
-        for copy in slab_copies:
-            copy.start()
+            )
+            slab_copies[n].start()
     mark_copy.wait()
     spread_marks(marks, dense)
-    for n, (out, row, copy) in ((1, (down, part, down_copy)), (0, (up, last, up_copy))):
-        for k, axis in ((0, 0), (1, 2)):
-            value = jnp.full((1, LANE), pos[axis, row], jnp.int32).astype(jnp.float32)
-            out[pl.ds(BLOCK + k, 1), :] = value
-        copy.wait()
-        pack_block(out, 0, blocks.at[n], dense, row)
-    if part < MOVE_CAP - 1:
-        return
+    for side, out in ((1, down), (0, up)):
+        for j in range(MOVE_CAP):
+            row = j if side == 1 else last + j
+            for k, axis in ((0, 0), (1, 2)):
+                value = jnp.full((1, LANE), pos[axis, row], jnp.int32).astype(jnp.float32)
+                out[pl.ds(SENT_META + 2 * j + k, 1), :] = value
+            n = side * MOVE_CAP + j
+            copies[n].wait()
+            pack_block(out, j * BLOCK, blocks.at[n], dense, row)
     for side, out in enumerate((up, down)):
         for bz in range(BZD):
             n = side * BZD + bz
             first = slab_rows[n] * TILES + (TILES - SLAB if side == 0 else 0)
             slab_copies[n].wait()
+            moves = []
             for x in range(2):
                 for yhi in range(2):
                     q = 2 * x + yhi
                     row = x * FACE + 2 * bz + yhi
                     for group, size in GROUPS:
                         value = slabs[n, group : group + size, q * LANE : (q + 1) * LANE]
-                        strip[pl.ds(group * 2 * FACE + row, size, stride=2 * FACE), :] = value
+                        moves.append((pl.ds(group * 2 * FACE + row, size, stride=2 * FACE), value))
                 row = POPS * 2 * FACE + x * FACE + 2 * bz
-                strip[pl.ds(row, 2), :] = dense[pl.ds(first + 2 * x, 2), :]
+                moves.append((pl.ds(row, 2), dense[pl.ds(first + 2 * x, 2), :]))
+            for target, value in moves:
+                strip[target, :] = value
         inner = 1 if side == 0 else 0
         for x in range(2):
             old = [strip[pl.ds(i * 2 * FACE + x * FACE, FACE), :] for i in range(POPS)]
@@ -291,8 +312,60 @@
                 out[pl.ds(SENT_SLABS + plane * FACE, FACE), :] = jnp.where(mark, ROTOR, post[i])
 
 
-def pack_own(places, marks_in, pops, own, zpack, zup, zdown, pos, marks, dense, stage, sems):
+def pack_edge(places, marks_in, pops, own, zpack, zup, zdown, pos, table, marks, dense, stage, sems):
+    column_z = lax.axis_index("cz")
+    mark_copy = pltpu.make_async_copy(marks_in, marks, sems.at[LAYERS])
+    mark_copy.start()
+    place_copy = pltpu.make_async_copy(places, pos, sems.at[LAYERS + 1])
+    place_copy.start()
+    place_copy.wait()
+    fill_table(pos, table)
+    edge_bz = jnp.where(column_z == 0, BZD - 1, 0)
+    first_c = jnp.where(column_z == 0, EDGE - 2, 0)
+    found = [table[held * BZD + edge_bz] for held in range(LAYERS)]
+    row_of = [jnp.maximum(row, 0) for row in found]
+    copies = []
+    for held in range(LAYERS):
+        copies.append(pltpu.make_async_copy(pops.at[row_of[held]], stage.at[held], sems.at[held]))
+        copies[held].start()
+    mark_copy.wait()
+    spread_marks(marks, dense)
+    spot = (lanes() % EDGE) // 2
+    sublane = lax.broadcasted_iota(jnp.int32, (8, LANE), 0)
+    flags = jnp.zeros((8, LANE), jnp.int32)
+    for held in range(LAYERS):
+        copies[held].wait()
+        base = pl.multiple_of((held * BZD + edge_bz) * BLOCK, 8)
+
+        @pl.when(found[held] >= 0)
+        def _(held=held, base=base):
+            pack_block(own, base, stage.at[held], dense, row_of[held])
+            totals = []
+            for group in range(ZGROUPS):
+                for part in range(TILES // 8):
+                    total = jnp.zeros((8, LANE), jnp.float32)
+                    for k in range(min(8, PLANES - group * 8)):
+                        value = own[pl.ds(base + (group * 8 + k) * TILES + part * 8, 8), :]
+                        value = pltpu.roll(value, (2 * k - first_c + LANE) % LANE, 1)
+                        total = jnp.where(spot == k, value, total)
+                    totals.append((held * ZROWS + group * TILES + part * 8, total))
+            for row, total in totals:
+                zpack[pl.ds(row, 8), :] = total
+
+        flags = jnp.where((sublane == held) & (found[held] >= 0), 1, flags)
+    zpack[pl.ds(ZMETA, 8), :] = flags.astype(jnp.float32)
+    zup[pl.ds(0, ZROWS), :] = zpack[pl.ds(3 * ZROWS, ZROWS), :]
+    zdown[pl.ds(0, ZROWS), :] = zpack[pl.ds(0, ZROWS), :]
+    for group in range(ZGROUPS):
+        target = pl.ds(ZROWS + group * SLAB, SLAB)
+        zup[target, :] = zpack[pl.ds(2 * ZROWS + group * TILES + TILES - SLAB, SLAB), :]
+        zdown[target, :] = zpack[pl.ds(ZROWS + group * TILES, SLAB), :]
+
+
+def pack_own(places, marks_in, pops, own_in, own, pos, marks, dense, stage, sems):
+    del own_in
     layer, _, column_z = place()
+    edge_bz = jnp.where(column_z == 0, BZD - 1, 0)
     rows = pos.shape[1]
     mark_copy = pltpu.make_async_copy(marks_in, marks, sems.at[rows])
     mark_copy.start()
@@ -307,45 +380,15 @@
 
     def settle(row, carry):
         pltpu.make_async_copy(pops.at[row], stage.at[row], sems.at[row]).wait()
-
-        @pl.when(pos[0, row] >= 0)
+        slot = slot_of(pos, row, layer, column_z)
+
+        @pl.when((pos[0, row] >= 0) & (slot % BZD != edge_bz))
         def _():
-            base = pl.multiple_of(slot_of(pos, row, layer, column_z) * BLOCK, 8)
-            pack_block(own, base, stage.at[row], dense, row)
+            pack_block(own, pl.multiple_of(slot * BLOCK, 8), stage.at[row], dense, row)
 
         return carry
 
     lax.fori_loop(0, rows, settle, 0)
-    edge_bz = jnp.where(column_z == 0, BZD - 1, 0)
-    first_c = jnp.where(column_z == 0, EDGE - 2, 0)
-    spot = (lanes() % EDGE) // 2
-    for held in range(LAYERS):
-        base = pl.multiple_of((held * BZD + edge_bz) * BLOCK, 8)
-        for group in range(ZGROUPS):
-            for part in range(TILES // 8):
-                total = jnp.zeros((8, LANE), jnp.float32)
-                for k in range(min(8, PLANES - group * 8)):
-                    value = own[pl.ds(base + (group * 8 + k) * TILES + part * 8, 8), :]
-                    value = pltpu.roll(value, (2 * k - first_c + LANE) % LANE, 1)
-                    total = jnp.where(spot == k, value, total)
-                zpack[pl.ds(held * ZROWS + group * TILES + part * 8, 8), :] = total
-    present = [jnp.int32(0)] * LAYERS
-    for row in range(rows):
-        slot = slot_of(pos, row, layer, column_z)
-        for held in range(LAYERS):
-            hit = (pos[0, row] >= 0) & (slot == held * BZD + edge_bz)
-            present[held] = jnp.where(hit, 1, present[held])
-    sublane = lax.broadcasted_iota(jnp.int32, (8, LANE), 0)
-    flags = jnp.zeros((8, LANE), jnp.int32)
-    for held in range(LAYERS):
-        flags = jnp.where(sublane == held, present[held], flags)
-    zpack[pl.ds(ZMETA, 8), :] = flags.astype(jnp.float32)
-    zup[pl.ds(0, ZROWS), :] = zpack[pl.ds(3 * ZROWS, ZROWS), :]
-    zdown[pl.ds(0, ZROWS), :] = zpack[pl.ds(0, ZROWS), :]
-    for group in range(ZGROUPS):
-        target = pl.ds(ZROWS + group * SLAB, SLAB)
-        zup[target, :] = zpack[pl.ds(2 * ZROWS + group * TILES + TILES - SLAB, SLAB), :]
-        zdown[target, :] = zpack[pl.ds(ZROWS + group * TILES, SLAB), :]
 
 
 def gathered(parts, zvalue, spot, ylo, column_z):
@@ -430,32 +473,36 @@
     return low | high
 
 
-def settle_rim(layers, places, up_first, down_first, up, down, zin, zup, zdown, own_in, own, edge, zall, zedge, rim_up, rim_down, pos, post_up, post_down, sem):
+def settle_rim(layers, places, up, down, zin, zup, zdown, own_in, own, edge, zall, zedge, rim_up, rim_down, pos, post_up, post_down, sem):
     del own_in
     layer, _, column_z = place()
     place_copy = pltpu.make_async_copy(places, pos, sem)
     place_copy.start()
-    for n, arrived in enumerate((up_first, down_first, up, down)):
-        bx = arrived[pl.ds(BLOCK, 1), :].astype(jnp.int32)
-        bz = arrived[pl.ds(BLOCK + 1, 1), :].astype(jnp.int32)
-        code = (bx - layer * BXD) * BZD + (bz - column_z * BZD)
-        mine = (bx >= layer * BXD) & (bx < (layer + 1) * BXD)
-        first = layer == 0 if n % 2 == 0 else layer == layers - 1
-        code = jnp.max(jnp.where(mine, code, -1))
-
-        @pl.when((code >= 0) & jnp.logical_not(first))
-        def _(arrived=arrived, code=code):
-            base = pl.multiple_of((jnp.clip(code, 0, BXD * BZD - 1) + BZD) * BLOCK, 8)
-            for k in range(BLOCK // 8):
-                own[pl.ds(base + 8 * k, 8), :] = arrived[pl.ds(8 * k, 8), :]
+    for arrived in (up, down):
+        for j in range(MOVE_CAP):
+            bx = arrived[pl.ds(SENT_META + 2 * j, 1), :].astype(jnp.int32)
+            bz = arrived[pl.ds(SENT_META + 2 * j + 1, 1), :].astype(jnp.int32)
+            code = (bx - layer * BXD) * BZD + (bz - column_z * BZD)
+            mine = (bx >= layer * BXD) & (bx < (layer + 1) * BXD)
+            first = layer == 0 if arrived is up else layer == layers - 1
+            code = jnp.max(jnp.where(mine, code, -1))
+
+            @pl.when((code >= 0) & jnp.logical_not(first))
+            def _(arrived=arrived, j=j, code=code):
+                base = pl.multiple_of((jnp.clip(code, 0, BXD * BZD - 1) + BZD) * BLOCK, 8)
+                for k in range(0, BLOCK, 128):
+                    values = [arrived[pl.ds(j * BLOCK + k + 8 * n, 8), :] for n in range(16)]
+                    for n, value in enumerate(values):
+                        own[pl.ds(base + k + 8 * n, 8), :] = value
 
     place_copy.wait()
     for side, arrived in enumerate((up, down)):
         inner, outer = (1, 0) if side == 0 else (2, 3)
         pairs = [(i, i, inner) for i in range(POPS)]
         pairs += [(POPS + n, i, outer) for n, i in enumerate(AHEAD if side == 0 else BACK)]
-        for plane, i, x in pairs:
-            edge[pl.ds((i * 4 + x) * FACE, FACE), :] = arrived[pl.ds(SENT_SLABS + plane * FACE, FACE), :]
+        values = [arrived[pl.ds(SENT_SLABS + plane * FACE, FACE), :] for plane, _, _ in pairs]
+        for (_, i, x), value in zip(pairs, values):
+            edge[pl.ds((i * 4 + x) * FACE, FACE), :] = value
         for bz in range(BZD):
             here = jnp.int32(0)
             goal = (0 if side == 0 else LAYERS - 1) * BZD + bz
@@ -466,12 +513,15 @@
             @pl.when(here == 1)
             def _(side=side, pairs=pairs, goal=goal, bz=bz):
                 first = goal * BLOCK + (TILES - SLAB if side == 0 else 0)
+                values = []
                 for _, i, x in pairs:
                     shift = 2 * (x if side == 0 else x - 2)
                     mark = own[pl.ds(first + POPS * TILES + shift, 2), :] > 0.5
-                    value = own[pl.ds(first + i * TILES + shift, 2), :]
-                    edge[pl.ds((i * 4 + x) * FACE + 2 * bz, 2), :] = jnp.where(mark, ROTOR, value)
-
+                    values.append(jnp.where(mark, ROTOR, own[pl.ds(first + i * TILES + shift, 2), :]))
+                for (_, i, x), value in zip(pairs, values):
+                    edge[pl.ds((i * 4 + x) * FACE + 2 * bz, 2), :] = value
+
+    moves = []
     for held in range(LAYERS):
         flag = zin[pl.ds(ZMETA + held, 1), :] > 0.5
         for group in range(ZGROUPS):
@@ -480,14 +530,16 @@
                     rows = pl.ds(held * ZROWS + group * TILES + part * 8, 8)
                     source = zup if held == 1 else zdown
                     other = source[pl.ds(group * TILES + part * 8, 8), :]
-                    zall[rows, :] = jnp.where(flag, zin[rows, :], other)
+                    moves.append((zall, rows, jnp.where(flag, zin[rows, :], other)))
             else:
                 side = 0 if held == 0 else 1
                 source = zup if held == 0 else zdown
                 first = TILES - SLAB if held == 0 else 0
                 mine = zin[pl.ds(held * ZROWS + group * TILES + first, SLAB), :]
                 other = source[pl.ds(ZROWS + group * SLAB, SLAB), :]
-                zedge[pl.ds(group * 8 + side * SLAB, SLAB), :] = jnp.where(flag, mine, other)
+                moves.append((zedge, pl.ds(group * 8 + side * SLAB, SLAB), jnp.where(flag, mine, other)))
+    for target, rows, value in moves:
+        target[rows, :] = value
     for chunk in (0, 1, 2, 3, None):
         for y in (0, 1, SPAN_Y - 2, SPAN_Y - 1):
             values = chunk_values(own, edge, zall, zedge, chunk, y // YLO, y % YLO, column_z)
@@ -511,16 +563,21 @@
     for source, target in ((post_up, rim_up), (post_down, rim_down)):
         for chunk in range(5):
             size = min(8, EXT_X - 8 * chunk)
+            values = []
+            for plane in range(RIM):
+                value = source[pl.ds(plane * GRID_X + 8 * chunk, 8), :]
+                values.append(pltpu.roll(value, (plane * EXT_Z + 2 * column_z) % LANE, 1))
+            totals = []
             for block in range(RIM_BLOCKS):
                 total = jnp.zeros((8, LANE), jnp.float32)
                 for plane in range(RIM):
                     begin = plane * EXT_Z - block * LANE
                     if begin >= LANE or begin + EXT_Z <= 0:
                         continue
-                    value = source[pl.ds(plane * GRID_X + 8 * chunk, 8), :]
-                    value = pltpu.roll(value, (begin + LANE + 2 * column_z) % LANE, 1)
-                    total = jnp.where((lane >= begin) & (lane < begin + EXT_Z), value, total)
-                target[pl.ds(block * EXT_X + 8 * chunk, size), :] = total[:size]
+                    total = jnp.where((lane >= begin) & (lane < begin + EXT_Z), values[plane], total)
+                totals.append(total)
+            for block in range(RIM_BLOCKS):
+                target[pl.ds(block * EXT_X + 8 * chunk, size), :] = totals[block][:size]
 
 
 def turned(value, step_z):
@@ -570,26 +627,30 @@
 
         def chunks(chunk, carry):
             flags = flags_of(rows_of_plane(chunk, POPS), inside_lanes(8, column_z))
-            for i in range(POPS):
-                values = rows_of_plane(chunk, i)
+
+            def leave(i, values):
                 for ylo in range(YLO):
                     row = i * FIELD + (8 * chunk + 2) * PITCH + FIRST + YLO * yhi + ylo
                     value = jnp.where(flags[ylo] < WALL_BELOW, flags[ylo], values[ylo])
                     field[pl.ds(row, 8, stride=PITCH), :] = value
                     target = (i * SPAN_X + 8 * chunk) * SPAN_Y + YLO * yhi + ylo
                     start[pl.ds(target, 8, stride=SPAN_Y), :] = values[ylo]
+
+            ahead(range(POPS), lambda i: rows_of_plane(chunk, i), leave, 3)
             return carry
 
         lax.fori_loop(0, SPAN_X // 8, chunks, 0)
         inside = inside_lanes(4, column_z) & halo_x_inside(layer, layers)
         flags = flags_of(rows_of_plane(None, POPS), inside)
-        for i in range(POPS):
-            values = rows_of_plane(None, i)
+
+        def leave(i, values):
             for ylo in range(YLO):
                 value = jnp.where(flags[ylo] < WALL_BELOW, flags[ylo], values[ylo])
                 for first, side in ((0, 0), (EXT_X - 2, 2)):
                     row = i * FIELD + first * PITCH + FIRST + YLO * yhi + ylo
                     field[pl.ds(row, 2, stride=PITCH), :] = value[side : side + 2]
+
+        ahead(range(POPS), lambda i: rows_of_plane(None, i), leave, 3)
         return carry
 
     lax.fori_loop(0, SPAN_Y // YLO, halves, 0)
@@ -703,59 +764,66 @@
     solid_cells = pltpu.with_memory_space_constraint(solid_cells, pltpu.HBM)
     places = pltpu.with_memory_space_constraint(block_pos.T, pltpu.HBM)
     place_scratch = SMEM((3, rows), jnp.int32)
+    table_scratch = SMEM((LAYERS * BZD,), jnp.int32)
     mark_scratch = [VMEM((rows, EDGE**3), jnp.int32), VMEM((rows * TILES, LANE), jnp.float32)]
 
     up = [(i, i + 1) for i in range(layers - 1)]
     down = [(i + 1, i) for i in range(layers - 1)]
-    from_low = []
-    from_high = []
-    for part in range(MOVE_CAP):
-        sent = BLOCK + 8 if part < MOVE_CAP - 1 else SENT_ROWS
-        send_up, send_down = pl.pallas_call(
-            functools.partial(pack_stream, part),
-            out_shape=(kept(sent), kept(sent)),
-            in_specs=[hbm, hbm, hbm],
-            out_specs=(vmem, vmem),
-            scratch_shapes=[place_scratch, SMEM((LAYERS * BZD,), jnp.int32)]
-            + mark_scratch
-            + [
-                VMEM((2, POPS, EDGE**3), jnp.float32),
-                VMEM((2 * BZD, POPS, SLAB * LANE), jnp.float32),
-                VMEM((PLANES * 2 * FACE, LANE), jnp.float32),
-                pltpu.SemaphoreType.DMA((4 + 2 * BZD,)),
-            ],
-            compiler_params=params(16),
-            name="pack_stream",
-        )(places, solid_cells, populations)
-        if part < MOVE_CAP - 1:
-            send_up, send_down, places = lax.optimization_barrier((send_up, send_down, places))
-            places = pltpu.with_memory_space_constraint(places, pltpu.HBM)
-        from_low.append(lax.ppermute(send_up, "stream", up))
-        from_high.append(lax.ppermute(send_down, "stream", down))
+    send_up, send_down = pl.pallas_call(
+        pack_stream,
+        out_shape=(kept(SENT_ROWS), kept(SENT_ROWS)),
+        in_specs=[hbm, hbm, hbm],
+        out_specs=(vmem, vmem),
+        scratch_shapes=[place_scratch, table_scratch]
+        + mark_scratch
+        + [
+            VMEM((2 * MOVE_CAP, POPS, EDGE**3), jnp.float32),
+            VMEM((2 * BZD, POPS, SLAB * LANE), jnp.float32),
+            VMEM((PLANES * 2 * FACE, LANE), jnp.float32),
+            pltpu.SemaphoreType.DMA((2 + 2 * MOVE_CAP + 2 * BZD,)),
+        ],
+        compiler_params=params(16),
+        name="pack_stream",
+    )(places, solid_cells, populations)
+    from_low = lax.ppermute(send_up, "stream", up)
+    from_high = lax.ppermute(send_down, "stream", down)
 
     own, zpack, zsend_up, zsend_down = pl.pallas_call(
-        pack_own,
+        pack_edge,
         out_shape=(kept(LAYERS * BZD * BLOCK), kept(ZMETA + 8), kept(DIAG), kept(DIAG)),
         in_specs=[hbm, hbm, hbm],
         out_specs=(vmem,) * 4,
+        scratch_shapes=[place_scratch, table_scratch]
+        + mark_scratch
+        + [
+            VMEM((LAYERS, POPS, EDGE**3), jnp.float32),
+            pltpu.SemaphoreType.DMA((LAYERS + 2,)),
+        ],
+        compiler_params=params(16),
+        name="pack_edge",
+    )(places, solid_cells, populations)
+    swap = [(i, depth - 1 - i) for i in range(depth)]
+    zin = lax.ppermute(zpack, "cz", swap)
+    zup_pairs = [(s * depth + c, t * depth + d) for s, t in up for c, d in swap]
+    zdown_pairs = [(s * depth + c, t * depth + d) for s, t in down for c, d in swap]
+    z_low = lax.ppermute(zsend_up, ("stream", "cz"), zup_pairs)
+    z_high = lax.ppermute(zsend_down, ("stream", "cz"), zdown_pairs)
+
+    own = pl.pallas_call(
+        pack_own,
+        out_shape=kept(LAYERS * BZD * BLOCK),
+        in_specs=[hbm, hbm, hbm, vmem],
+        out_specs=vmem,
         scratch_shapes=[place_scratch]
         + mark_scratch
         + [
             VMEM((rows, POPS, EDGE**3), jnp.float32),
             pltpu.SemaphoreType.DMA((rows + 2,)),
         ],
+        input_output_aliases={3: 0},
         compiler_params=params(16),
         name="pack_own",
-    )(places, solid_cells, populations)
-    zpack, zsend_up, zsend_down, from_low[0], from_high[0] = lax.optimization_barrier(
-        (zpack, zsend_up, zsend_down, from_low[0], from_high[0])
-    )
-    swap = [(i, depth - 1 - i) for i in range(depth)]
-    zin = lax.ppermute(zpack, "cz", swap)
-    zup_pairs = [(s * depth + c, t * depth + d) for s, t in up for c, d in swap]
-    zdown_pairs = [(s * depth + c, t * depth + d) for s, t in down for c, d in swap]
-    z_low = lax.ppermute(zsend_up, ("stream", "cz"), zup_pairs)
-    z_high = lax.ppermute(zsend_down, ("stream", "cz"), zdown_pairs)
+    )(places, solid_cells, populations, own)
 
     own, edge, zall, zedge, rim_up, rim_down = pl.pallas_call(
         functools.partial(settle_rim, layers),
@@ -767,7 +835,7 @@
             kept(RIM_ROWS),
             kept(RIM_ROWS),
         ),
-        in_specs=[hbm] + [vmem] * 8,
+        in_specs=[hbm] + [vmem] * 6,
         out_specs=(vmem,) * 6,
         scratch_shapes=[
             place_scratch,
@@ -775,10 +843,10 @@
             VMEM((RIM * GRID_X, LANE), jnp.float32),
             pltpu.SemaphoreType.DMA,
         ],
-        input_output_aliases={8: 0},
+        input_output_aliases={6: 0},
         compiler_params=params(16),
         name="settle_rim",
-    )(places, from_low[0], from_high[0], from_low[1], from_high[1], zin, z_low, z_high, own)
+    )(places, from_low, from_high, zin, z_low, z_high, own)
     cy_up = [(i, i + 1) for i in range(columns - 1)]
     cy_down = [(i + 1, i) for i in range(columns - 1)]
     rim_low = lax.ppermute(rim_up, "cy", cy_up)

time: 75.4 us -> 69.9 us (0.927)
  the two profiles are of different devices: /device:TPU:12 before, /device:TPU:0 now
where the time goes in v4:
time: 69.9 us; the launch traced here: 68.9 us
  Pallas kernels  46.3 us (66%)
  starting transfers between devices  15.8 us (23%)
  waiting for transfers between devices  6.77 us (10%)
    pallas_call x1, Pallas kernels, shards(): pl.pallas_call(functools.partial(settle_all, layers, columns, depth), out...  26.9 us
    pallas_call x1, Pallas kernels, shards(): pl.pallas_call(functools.partial(finish, columns, depth), out_shape=(jax....  5.41 us
    ppermute x1, starting transfers between devices, shards(): from_low = lax.ppermute(send_up, 'stream', up)  4.98 us
    pallas_call x1, Pallas kernels, shards(): pl.pallas_call(pack_own, out_shape=kept(LAYERS * BZD * BLOCK), in_specs=[...  4.31 us
    pallas_call x1, Pallas kernels, shards(): pl.pallas_call(pack_edge, out_shape=(kept(LAYERS * BZD * BLOCK), kept(ZME...  3.68 us
    ppermute x1, starting transfers between devices, shards(): z_low = lax.ppermute(zsend_up, ('stream', 'cz'), zup_pairs)  3.44 us
    ppermute x1, starting transfers between devices, shards(): rim_low = lax.ppermute(rim_up, 'cy', cy_up)  3.41 us
    ppermute x1, waiting for transfers between devices, shards(): z_low = lax.ppermute(zsend_up, ('stream', 'cz'), zup_pairs)  3.22 us
  transfers between devices with their start and end apart: 7, of which 3 were waited for; matrix products, arithmetic and copies ran while one was open for 0% of the time, Pallas kernels for 51%

profile of v4, /device:TPU:0, one launch (start us, length us, event | category | flops | bytes accessed | tf_op | source)
XLA Modules:
  0.0 68.9 jit_solution(7492308656742255730)
XLA Ops:
  0.0 3.1 %pack_stream.1 = (f32[1480,128]{1,0:T(8,128)S(1)}, f32[1480,128]{1,0:T(8,128)S(1)}) custom-call(s32[3,12]{1,0:T(4,128)} %bitcast.1, s32[12,4096]{1,0:T(8,128)} %marks_in.5, f32[12,19,4096]{2,1,0:T(8,128)} %pops.5), custom_call_target="tpu_custom_call" | custom-call | tf_op jit(solution)/shard_map/pack_stream/pallas_call | solution.py:772
  3.1 5.0 %collective-permute-start = (f32[1480,128]{1,0:T(8,128)S(1)}, f32[1480,128]{1,0:T(8,128)S(1)}, u32[]{:S(2)}, u32[]{:S(2)}) collective-permute-start(f32[1480,128]{1,0:T(8,128)S(1)} %get-tuple-element.21), channel_id=1, source_target_pairs={{0,8},{8,16},{16,24},{1,9},{9,17},{17,25},{2,10},{10,18},{18,26},{... | collective-permute-start | bytes 2273288 | tf_op jit(solution)/shard_map/ppermute | solution.py:788
  8.1 1.3 %collective-permute-start.1 = (f32[1480,128]{1,0:T(8,128)S(1)}, f32[1480,128]{1,0:T(8,128)S(1)}, u32[]{:S(2)}, u32[]{:S(2)}) collective-permute-start(f32[1480,128]{1,0:T(8,128)S(1)} %get-tuple-element.22), channel_id=1, source_target_pairs={{8,0},{16,8},{24,16},{9,1},{17,9},{25,17},{10,2},{18,10},{26,18},{... | collective-permute-start | bytes 2273288 | tf_op jit(solution)/shard_map/ppermute | solution.py:789
  9.4 3.7 %pack_edge.1 = (f32[10240,128]{1,0:T(8,128)S(1)}, f32[392,128]{1,0:T(8,128)S(1)}, f32[108,128]{1,0:T(8,128)S(1)}, f32[108,128]{1,0:T(8,128)S(1)}) custom-call(s32[3,12]{1,0:T(4,128)} %bitcast.2, s32[12,4096]{1,0:T(8,128)} %marks_in.5, f32[12,19,4096]{2,1,0:T(8,128)} %pops.5), custom_call_target="tpu_custom_call" | custom-call | tf_op jit(solution)/shard_map/pack_edge/pallas_call | solution.py:791
  13.1 0.1 collective-permute-start.2
  13.1 3.4 %collective-permute-start.3 = (f32[108,128]{1,0:T(8,128)S(1)}, f32[108,128]{1,0:T(8,128)S(1)}, u32[]{:S(2)}, u32[]{:S(2)}) collective-permute-start(f32[108,128]{1,0:T(8,128)S(1)} %get-tuple-element.24), channel_id=1, source_target_pairs={{0,9},{1,8},{8,17},{9,16},{16,25},{17,24},{2,11},{3,10},{10,19},{1... | collective-permute-start | bytes 165896 | tf_op jit(solution)/shard_map/ppermute | solution.py:809
  16.6 1.3 %collective-permute-start.4 = (f32[108,128]{1,0:T(8,128)S(1)}, f32[108,128]{1,0:T(8,128)S(1)}, u32[]{:S(2)}, u32[]{:S(2)}) collective-permute-start(f32[108,128]{1,0:T(8,128)S(1)} %get-tuple-element.25), channel_id=1, source_target_pairs={{8,1},{9,0},{16,9},{17,8},{24,17},{25,16},{10,3},{11,2},{18,11},{1... | collective-permute-start | bytes 165896 | tf_op jit(solution)/shard_map/ppermute | solution.py:810
  17.9 4.3 %pack_own.1.own_in = f32[10240,128]{1,0:T(8,128)S(1)} custom-call(s32[3,12]{1,0:T(4,128)} %bitcast.3, s32[12,4096]{1,0:T(8,128)} %marks_in.5, f32[12,19,4096]{2,1,0:T(8,128)} %pops.5, f32[10240,128]{1,0:T(8,128)S(1)} %get-tuple-element.26.own_in), custom_call_target="tpu_custom_call", output_to_operand_aliasing={{}: (3, {})} | custom-call | tf_op jit(solution)/shard_map/pack_own/pallas_call | solution.py:812
  22.2 3.2 %collective-permute-done.3.zup = f32[108,128]{1,0:T(8,128)S(1)} collective-permute-done((f32[108,128]{1,0:T(8,128)S(1)}, f32[108,128]{1,0:T(8,128)S(1)}, u32[]{:S(2)}, u32[]{:S(2)}) %collective-permute-start.3) | collective-permute-done | bytes 55328 | tf_op jit(solution)/shard_map/ppermute | solution.py:809
  25.4 2.7 %collective-permute-done.4.zdown = f32[108,128]{1,0:T(8,128)S(1)} collective-permute-done((f32[108,128]{1,0:T(8,128)S(1)}, f32[108,128]{1,0:T(8,128)S(1)}, u32[]{:S(2)}, u32[]{:S(2)}) %collective-permute-start.4) | collective-permute-done | bytes 55328 | tf_op jit(solution)/shard_map/ppermute | solution.py:810
  28.1 0.0 collective-permute-done.2.zin
  28.1 0.0 collective-permute-done.up
  28.1 0.8 %collective-permute-done.1.down = f32[1480,128]{1,0:T(8,128)S(1)} collective-permute-done((f32[1480,128]{1,0:T(8,128)S(1)}, f32[1480,128]{1,0:T(8,128)S(1)}, u32[]{:S(2)}, u32[]{:S(2)}) %collective-permute-start.1) | collective-permute-done | bytes 757792 | tf_op jit(solution)/shard_map/ppermute | solution.py:789
  29.0 2.9 %settle_rim.1 = (f32[10240,128]{1,0:T(8,128)S(1)}, f32[608,128]{1,0:T(8,128)S(1)}, f32[384,128]{1,0:T(8,128)S(1)}, f32[24,128]{1,0:T(8,128)S(1)}, f32[472,128]{1,0:T(8,128)S(1)}, /*index=5*/f32[472,128]{1,0:T(8,128)S(1)}) custom-call(s32[3,12]{1,0:T(4,128)} %bitcast.4, f32[1480,128]{1,0:T(8,128)S(1)} %collective-permute-done.up, ...), custom_call_target="tpu_custom_call", output_to_operand_aliasing={{0}: (6, {})} | custom-call | tf_op jit(solution)/shard_map/settle_rim/pallas_call | solution.py:828
  31.9 3.4 %collective-permute-start.5 = (f32[472,128]{1,0:T(8,128)S(1)}, f32[472,128]{1,0:T(8,128)S(1)}, u32[]{:S(2)}, u32[]{:S(2)}) collective-permute-start(f32[472,128]{1,0:T(8,128)S(1)} %get-tuple-element.27), channel_id=1, source_target_pairs={{0,2},{2,4},{4,6},{1,3},{3,5},{5,7},{8,10},{10,12},{12,14},{9,11},... | collective-permute-start | bytes 725000 | tf_op jit(solution)/shard_map/ppermute | solution.py:852
  35.3 1.3 %collective-permute-start.6 = (f32[472,128]{1,0:T(8,128)S(1)}, f32[472,128]{1,0:T(8,128)S(1)}, u32[]{:S(2)}, u32[]{:S(2)}) collective-permute-start(f32[472,128]{1,0:T(8,128)S(1)} %get-tuple-element.28), channel_id=1, source_target_pairs={{2,0},{4,2},{6,4},{3,1},{5,3},{7,5},{10,8},{12,10},{14,12},{11,9},... | collective-permute-start | bytes 725000 | tf_op jit(solution)/shard_map/ppermute | solution.py:853
  36.6 26.9 %settle_all.1 = (f32[16720,128]{1,0:T(8,128)S(1)}, f32[9728,128]{1,0:T(8,128)S(1)}, f32[16720,128]{1,0:T(8,128)S(1)}) custom-call(f32[10240,128]{1,0:T(8,128)S(1)} %get-tuple-element.29.own, f32[608,128]{1,0:T(8,128)S(1)} %get-tuple-element.30.edge, f32[384,128]{1,0:T(8,128)S(1)} %get-tuple-element.31.zall, f32[24,128]{1,0:T(8,128)S(1)} %get-tuple-element.32.zedge), custom_call_target="tpu_custom_call" | custom-call | tf_op jit(solution)/shard_map/settle_all/pallas_call | solution.py:855
  63.5 0.0 collective-permute-done.5.rim_low
  63.5 0.0 collective-permute-done.6.rim_high
  63.5 5.4 %finish.1 = (f32[19,32,16,64]{3,2,1,0:T(8,128)}, f32[16720,128]{1,0:T(8,128)S(1)}) custom-call(f32[472,128]{1,0:T(8,128)S(1)} %collective-permute-done.5.rim_low, f32[472,128]{1,0:T(8,128)S(1)} %collective-permute-done.6.rim_high, f32[16720,128]{1,0:T(8,128)S(1)} %get-tuple-element.33.field, ...), custom_call_target="tpu_custom_call", output_to_operand_aliasing={{1}: (4, {})} | custom-call | tf_op jit(solution)/shard_map/finish/pallas_call | solution.py:864
Async XLA Ops:
  3.1 25.0 %collective-permute-start = (f32[1480,128]{1,0:T(8,128)S(1)}, f32[1480,128]{1,0:T(8,128)S(1)}, u32[]{:S(2)}, u32[]{:S(2)}) collective-permute-start(f32[1480,128]{1,0:T(8,128)S(1)} %get-tuple-element.21), channel_id=1, source_target_pairs={{0,8},{8,16},{16,24},{1,9},{9,17},{17,25},{2,10},{10,18},{18,26},{... | collective-permute-start | bytes 2273288 | tf_op jit(solution)/shard_map/ppermute | solution.py:788
  8.1 20.9 %collective-permute-start.1 = (f32[1480,128]{1,0:T(8,128)S(1)}, f32[1480,128]{1,0:T(8,128)S(1)}, u32[]{:S(2)}, u32[]{:S(2)}) collective-permute-start(f32[1480,128]{1,0:T(8,128)S(1)} %get-tuple-element.22), channel_id=1, source_target_pairs={{8,0},{16,8},{24,16},{9,1},{17,9},{25,17},{10,2},{18,10},{26,18},{... | collective-permute-start | bytes 2273288 | tf_op jit(solution)/shard_map/ppermute | solution.py:789
  13.1 15.1 %collective-permute-start.2 = (f32[392,128]{1,0:T(8,128)S(1)}, f32[392,128]{1,0:T(8,128)S(1)}, u32[]{:S(2)}, u32[]{:S(2)}) collective-permute-start(f32[392,128]{1,0:T(8,128)S(1)} %get-tuple-element.23), channel_id=1, source_target_pairs={{0,1},{1,0},{2,3},{3,2},{4,5},{5,4},{6,7},{7,6},{8,9},{9,8},{10,11... | collective-permute-start | bytes 602120 | tf_op jit(solution)/shard_map/ppermute | solution.py:806
  13.1 12.3 %collective-permute-start.3 = (f32[108,128]{1,0:T(8,128)S(1)}, f32[108,128]{1,0:T(8,128)S(1)}, u32[]{:S(2)}, u32[]{:S(2)}) collective-permute-start(f32[108,128]{1,0:T(8,128)S(1)} %get-tuple-element.24), channel_id=1, source_target_pairs={{0,9},{1,8},{8,17},{9,16},{16,25},{17,24},{2,11},{3,10},{10,19},{1... | collective-permute-start | bytes 165896 | tf_op jit(solution)/shard_map/ppermute | solution.py:809
  16.6 11.5 %collective-permute-start.4 = (f32[108,128]{1,0:T(8,128)S(1)}, f32[108,128]{1,0:T(8,128)S(1)}, u32[]{:S(2)}, u32[]{:S(2)}) collective-permute-start(f32[108,128]{1,0:T(8,128)S(1)} %get-tuple-element.25), channel_id=1, source_target_pairs={{8,1},{9,0},{16,9},{17,8},{24,17},{25,16},{10,3},{11,2},{18,11},{1... | collective-permute-start | bytes 165896 | tf_op jit(solution)/shard_map/ppermute | solution.py:810
  31.9 31.6 %collective-permute-start.5 = (f32[472,128]{1,0:T(8,128)S(1)}, f32[472,128]{1,0:T(8,128)S(1)}, u32[]{:S(2)}, u32[]{:S(2)}) collective-permute-start(f32[472,128]{1,0:T(8,128)S(1)} %get-tuple-element.27), channel_id=1, source_target_pairs={{0,2},{2,4},{4,6},{1,3},{3,5},{5,7},{8,10},{10,12},{12,14},{9,11},... | collective-permute-start | bytes 725000 | tf_op jit(solution)/shard_map/ppermute | solution.py:852
  35.3 28.2 %collective-permute-start.6 = (f32[472,128]{1,0:T(8,128)S(1)}, f32[472,128]{1,0:T(8,128)S(1)}, u32[]{:S(2)}, u32[]{:S(2)}) collective-permute-start(f32[472,128]{1,0:T(8,128)S(1)} %get-tuple-element.28), channel_id=1, source_target_pairs={{2,0},{4,2},{6,4},{3,1},{5,3},{7,5},{10,8},{12,10},{14,12},{11,9},... | collective-permute-start | bytes 725000 | tf_op jit(solution)/shard_map/ppermute | solution.py:853

commit v5 on v4

--- a/solution.py
+++ b/solution.py
@@ -57,9 +57,11 @@
 SPAN_X = BXD * EDGE
 SPAN_Y = BYD * EDGE
 SPAN_Z = BZD * EDGE
-PITCH = SPAN_Y + 8
-FIRST = 8
-FIELD = (SPAN_X + 4) * PITCH + 16
+PITCH = SPAN_X + 8
+STEP = PITCH // 8
+FIRST = 96
+FIELD = FIRST + (SPAN_Y + 1) * PITCH + 48
+TURN = 9
 EXT_X = SPAN_X + 4
 EXT_Z = SPAN_Z + 2
 RIM_UP = tuple(i for i in range(POPS) if VELOCITIES[i][1] == 1)
@@ -595,21 +597,32 @@
     return drift_y, spin, (total_y - 1) / 2.0
 
 
-def drifts_by_half(columns, depth):
+def first_step(columns, depth, field, later, begin, end):
     _, column_y, _ = place()
     drift_y, spin, centre_y = drifts_of(columns, depth)
     sublane = lax.broadcasted_iota(jnp.int32, (8, LANE), 0)
-    halves = []
-    for half in range(SPAN_Y // 8):
-        here_y = sublane + (column_y * SPAN_Y + 8 * half)
-        halves.append(spin * (here_y.astype(jnp.float32) - centre_y))
-    return drift_y, halves
+
+    def tile(n, carry):
+        base = pl.multiple_of(8 * n, 8)
+        line = (n - FIRST // 8 + 2 * STEP) // STEP
+        next_row = (sublane >= 6) & (n - FIRST // 8 + 2 * STEP - line * STEP == STEP - 1)
+        here_y = jnp.where(next_row, line + 1, line) + (column_y * SPAN_Y - 2)
+        drift_z = spin * (here_y.astype(jnp.float32) - centre_y)
+        old = [field[pl.ds(i * FIELD + base, 8), :] for i in range(POPS)]
+        values = streamed(pull_from(field, base), old, drift_y, drift_z)
+        post, _ = collide(values)
+        wall = old[0] < WALL_BELOW
+        for i in range(POPS):
+            later[pl.ds(i * FIELD + base, 8), :] = jnp.where(wall, old[0], post[i])
+        return carry
+
+    lax.fori_loop(FIRST // 8 + begin, FIRST // 8 + end, tile, 0)
 
 
 def pull_from(field, base):
     def pull(i):
         step_x, step_y, step_z = VELOCITIES[i]
-        return turned(field[pl.ds(i * FIELD + base - step_x * PITCH - step_y, 8), :], step_z)
+        return turned(field[pl.ds(i * FIELD + base - step_y * PITCH - step_x, 8), :], step_z)
 
     return pull
 
@@ -617,65 +630,58 @@
 def settle_all(layers, columns, depth, own, edge, zall, zedge, field, start, later):
     layer, _, column_z = place()
 
-    def flags_of(mark, inside):
-        return [jnp.where(inside, jnp.where(value > 0.5, ROTOR, 0.0), OUTSIDE) for value in mark]
+    def caps_of(mark, inside):
+        return [jnp.where(inside, jnp.where(value > 0.5, ROTOR, -ROTOR), OUTSIDE) for value in mark]
 
     def halves(yhi, carry):
         def rows_of_plane(chunk, plane):
             parts, zvalue = plane_parts(own, edge, zall, zedge, chunk, yhi, plane)
             return gathered_rows(parts, zvalue, plane % 8, column_z)
 
+        top = yhi * YLO * PITCH + FIRST
+
         def chunks(chunk, carry):
-            flags = flags_of(rows_of_plane(chunk, POPS), inside_lanes(8, column_z))
+            caps = caps_of(rows_of_plane(chunk, POPS), inside_lanes(8, column_z))
 
             def leave(i, values):
                 for ylo in range(YLO):
-                    row = i * FIELD + (8 * chunk + 2) * PITCH + FIRST + YLO * yhi + ylo
-                    value = jnp.where(flags[ylo] < WALL_BELOW, flags[ylo], values[ylo])
-                    field[pl.ds(row, 8, stride=PITCH), :] = value
-                    target = (i * SPAN_X + 8 * chunk) * SPAN_Y + YLO * yhi + ylo
-                    start[pl.ds(target, 8, stride=SPAN_Y), :] = values[ylo]
-
-            ahead(range(POPS), lambda i: rows_of_plane(chunk, i), leave, 3)
+                    row = pl.multiple_of(i * FIELD + top + ylo * PITCH + 8 * chunk, 8)
+                    field[pl.ds(row, 8), :] = jnp.minimum(values[ylo], caps[ylo])
+                    row = pl.multiple_of((i * SPAN_Y + YLO * yhi + ylo) * SPAN_X + 8 * chunk, 8)
+                    start[pl.ds(row, 8), :] = values[ylo]
+
+            ahead(range(POPS), lambda i: rows_of_plane(chunk, i), leave, 1)
             return carry
 
         lax.fori_loop(0, SPAN_X // 8, chunks, 0)
         inside = inside_lanes(4, column_z) & halo_x_inside(layer, layers)
-        flags = flags_of(rows_of_plane(None, POPS), inside)
+        caps = caps_of(rows_of_plane(None, POPS), inside)
 
         def leave(i, values):
             for ylo in range(YLO):
-                value = jnp.where(flags[ylo] < WALL_BELOW, flags[ylo], values[ylo])
-                for first, side in ((0, 0), (EXT_X - 2, 2)):
-                    row = i * FIELD + first * PITCH + FIRST + YLO * yhi + ylo
-                    field[pl.ds(row, 2, stride=PITCH), :] = value[side : side + 2]
-
-        ahead(range(POPS), lambda i: rows_of_plane(None, i), leave, 3)
+                value = jnp.minimum(values[ylo], caps[ylo])
+                row = i * FIELD + top + ylo * PITCH
+                field[pl.ds(row - 2, 2), :] = value[:2]
+                field[pl.ds(row + SPAN_X, 2), :] = value[2:]
+
+        ahead(range(POPS), lambda i: rows_of_plane(None, i), leave, 1)
         return carry
 
     lax.fori_loop(0, SPAN_Y // YLO, halves, 0)
-    drift_y, drifts = drifts_by_half(columns, depth)
-
-    def first_step(x, carry):
-        for half in range(SPAN_Y // 8):
-            base = pl.multiple_of(x * PITCH + FIRST + 8 * half, 8)
-            old = [field[pl.ds(i * FIELD + base, 8), :] for i in range(POPS)]
-            values = streamed(pull_from(field, base), old, drift_y, drifts[half])
-            post, _ = collide(values)
-            wall = old[0] < WALL_BELOW
-            for i in range(POPS):
-                later[pl.ds(i * FIELD + base, 8), :] = jnp.where(wall, old[0], post[i])
-        return carry
-
-    lax.fori_loop(1, EXT_X - 1, first_step, 0)
-
-
-def finish(columns, depth, rim_low, rim_high, field, start, later_in, out, later, low, high, result, sems):
-    del later_in
+    first_step(columns, depth, field, later, STEP, (SPAN_Y - 1) * STEP)
+
+
+def finish(columns, depth, rim_low, rim_high, field_in, start, later_in, out, field, later, turn, result, sems):
+    del field_in, later_in
     _, column_y, column_z = place()
     flat = (lanes() + 2 * column_z) % LANE
-    for source, target, there in ((rim_low, low, column_y > 0), (rim_high, high, column_y < columns - 1)):
+    sides = (
+        (rim_low, -1, -2, RIM_UP, column_y > 0),
+        (rim_high, SPAN_Y, SPAN_Y + 1, RIM_DOWN, column_y < columns - 1),
+    )
+    for source, near, far, rim, there in sides:
         for chunk in range(5):
+            size = min(8, EXT_X - 8 * chunk)
             blocks = [source[pl.ds(block * EXT_X + 8 * chunk, 8), :] for block in range(RIM_BLOCKS)]
             for plane in range(RIM):
                 block, begin = divmod(plane * EXT_Z, LANE)
@@ -684,60 +690,41 @@
                 if begin + EXT_Z > LANE:
                     value = jnp.where(flat < LANE - begin, value, pltpu.roll(blocks[block + 1], shift, 1))
                 value = jnp.where((flat < EXT_Z) & there, value, OUTSIDE)
-                target[pl.ds(plane * GRID_X + 8 * chunk, 8), :] = value
+                i, y = (plane, near) if plane < POPS else (rim[plane - POPS], far)
+                row = i * FIELD + FIRST + y * PITCH - 2 + 8 * chunk
+                field[pl.ds(row, size), :] = value[:size]
+
+    first_step(columns, depth, field, later, -STEP - 1, STEP)
+    first_step(columns, depth, field, later, (SPAN_Y - 1) * STEP - 1, (SPAN_Y + 1) * STEP)
 
     drift_y, spin, centre_y = drifts_of(columns, depth)
-    for source, face, rim in ((low, 0, RIM_UP), (high, SPAN_Y - 1, RIM_DOWN)):
-        outer = {i: POPS + n for n, i in enumerate(rim)}
-        toward = VELOCITIES[rim[0]][1]
-        for y in (face - toward, face):
-            drift_z = spin * ((column_y * SPAN_Y + y).astype(jnp.float32) - centre_y)
-            for chunk in range(5):
-                first = 1 + 8 * chunk
-                size = min(8, EXT_X - 1 - first)
-
-                def value_at(i, x, y):
-                    if y == face - 2 * toward:
-                        return source[pl.ds(outer[i] * GRID_X + x, size), :]
-                    if y == face - toward:
-                        return source[pl.ds(i * GRID_X + x, size), :]
-                    return field[pl.ds(i * FIELD + x * PITCH + FIRST + y, size, stride=PITCH), :]
-
-                def pull(i):
-                    step_x, step_y, step_z = VELOCITIES[i]
-                    return turned(value_at(i, first - step_x, y - step_y), step_z)
-
-                old = [value_at(i, first, y) for i in range(POPS)]
-                values = streamed(pull, old, drift_y[:size], drift_z)
-                post, _ = collide(values)
+
+    def leave(n):
+        part = pl.ds(n * 8, 8)
+        return pltpu.make_async_copy(result.at[:, part], out.at[:, part], sems.at[n])
+
+    def second_step(chunk, carry):
+        for half in range(SPAN_Y // 8):
+            for k in range(8):
+                y = 8 * half + k
+                base = pl.multiple_of(FIRST + y * PITCH + 8 * chunk, 8)
+                drift_z = spin * ((column_y * SPAN_Y + y).astype(jnp.float32) - centre_y)
+                old = [later[pl.ds(i * FIELD + base, 8), :] for i in range(POPS)]
+                values = streamed(pull_from(later, base), old, drift_y, drift_z)
                 wall = old[0] < WALL_BELOW
-                for i in range(POPS) if y == face else rim:
-                    row = i * FIELD + first * PITCH + FIRST + y
-                    later[pl.ds(row, size, stride=PITCH), :] = jnp.where(wall, old[0], post[i])
-
-    drift_y, drifts = drifts_by_half(columns, depth)
-    quarter = SPAN_X // 4
-
-    def leave(n):
-        part = pl.ds(n * quarter, quarter)
-        return pltpu.make_async_copy(result.at[:, part], out.at[:, part], sems.at[n])
-
-    def second_step(x, carry):
-        for half in range(SPAN_Y // 8):
-            base = pl.multiple_of((x + 2) * PITCH + FIRST + 8 * half, 8)
-            old = [later[pl.ds(i * FIELD + base, 8), :] for i in range(POPS)]
-            values = streamed(pull_from(later, base), old, drift_y, drifts[half])
-            wall = old[0] < WALL_BELOW
-            for i in range(POPS):
-                first = pl.multiple_of((i * SPAN_X + x) * SPAN_Y + 8 * half, 8)
-                value = jnp.where(wall, start[pl.ds(first, 8), :], values[i])
-                result[i, x, pl.ds(8 * half, 8), :] = value[:, :SPAN_Z]
+                for i in range(POPS):
+                    first = pl.multiple_of((i * SPAN_Y + y) * SPAN_X + 8 * chunk, 8)
+                    value = jnp.where(wall, start[pl.ds(first, 8), :], values[i])
+                    turn[pl.ds(i * 8 * TURN + k * TURN, 8), :] = value
+            for k in range(8):
+                values = [turn[pl.ds(i * 8 * TURN + k, 8, stride=TURN), :] for i in range(POPS)]
+                for i in range(POPS):
+                    result[i, 8 * chunk + k, 8 * half : 8 * half + 8, :] = values[i][:, :SPAN_Z]
+        leave(chunk).start()
         return carry
 
-    for n in range(4):
-        lax.fori_loop(n * quarter, (n + 1) * quarter, second_step, 0)
-        leave(n).start()
-    for n in range(4):
+    lax.fori_loop(0, SPAN_X // 8, second_step, 0)
+    for n in range(SPAN_X // 8):
         leave(n).wait()
 
 
@@ -861,21 +848,21 @@
         name="settle_all",
     )(own, edge, zall, zedge)
 
-    out, _ = pl.pallas_call(
+    out, _, _ = pl.pallas_call(
         functools.partial(finish, columns, depth),
         out_shape=(
             jax.ShapeDtypeStruct((POPS, SPAN_X, SPAN_Y, SPAN_Z), jnp.float32),
             kept(POPS * FIELD),
+            kept(POPS * FIELD),
         ),
         in_specs=[vmem] * 5,
-        out_specs=(hbm, vmem),
+        out_specs=(hbm, vmem, vmem),
         scratch_shapes=[
-            VMEM((RIM * GRID_X, LANE), jnp.float32),
-            VMEM((RIM * GRID_X, LANE), jnp.float32),
+            VMEM((POPS * 8 * TURN, LANE), jnp.float32),
             VMEM((POPS, SPAN_X, SPAN_Y, SPAN_Z), jnp.float32),
-            pltpu.SemaphoreType.DMA((4,)),
+            pltpu.SemaphoreType.DMA((SPAN_X // 8,)),
         ],
-        input_output_aliases={4: 1},
+        input_output_aliases={2: 1, 4: 2},
         compiler_params=params(16),
         name="finish",
     )(rim_low, rim_high, field, start, later)

time: 69.9 us -> 72.6 us (1.039)
  Pallas kernels: 46.3 us -> 48.6 us
    pallas_call x1, Pallas kernels: 26.9 us -> 28.9 us  [shards(): pl.pallas_call(functools.partial(settle_all, layers, columns, depth), out...]
where the time goes in v5:
time: 72.6 us; the launch traced here: 71.6 us
  Pallas kernels  48.6 us (67%)
  starting transfers between devices  16.5 us (23%)
  waiting for transfers between devices  6.34 us (9%)
    pallas_call x1, Pallas kernels, shards(): pl.pallas_call(functools.partial(settle_all, layers, columns, depth), out...  28.9 us
    pallas_call x1, Pallas kernels, shards(): pl.pallas_call(functools.partial(finish, columns, depth), out_shape=(jax....  5.97 us
    ppermute x1, starting transfers between devices, shards(): from_low = lax.ppermute(send_up, 'stream', up)  4.98 us
    pallas_call x1, Pallas kernels, shards(): pl.pallas_call(pack_own, out_shape=kept(LAYERS * BZD * BLOCK), in_specs=[...  4.65 us
    ppermute x1, starting transfers between devices, shards(): z_low = lax.ppermute(zsend_up, ('stream', 'cz'), zup_pairs)  3.99 us
    ppermute x1, starting transfers between devices, shards(): rim_low = lax.ppermute(rim_up, 'cy', cy_up)  3.41 us
    pallas_call x1, Pallas kernels, shards(): pl.pallas_call(pack_stream, out_shape=(kept(SENT_ROWS), kept(SENT_ROWS)),...  3.08 us
    pallas_call x1, Pallas kernels, shards(): pl.pallas_call(pack_edge, out_shape=(kept(LAYERS * BZD * BLOCK), kept(ZME...  3.05 us
  transfers between devices with their start and end apart: 7, of which 3 were waited for; matrix products, arithmetic and copies ran while one was open for 0% of the time, Pallas kernels for 51%

profile of v5, /device:TPU:0, one launch (start us, length us, event | category | flops | bytes accessed | tf_op | source)
XLA Modules:
  0.0 71.6 jit_solution(4003410028999120180)
XLA Ops:
  0.0 3.1 %pack_stream.1 = (f32[1480,128]{1,0:T(8,128)S(1)}, f32[1480,128]{1,0:T(8,128)S(1)}) custom-call(s32[3,12]{1,0:T(4,128)} %bitcast.1, s32[12,4096]{1,0:T(8,128)} %marks_in.5, f32[12,19,4096]{2,1,0:T(8,128)} %pops.5), custom_call_target="tpu_custom_call" | custom-call | tf_op jit(solution)/shard_map/pack_stream/pallas_call | solution.py:759
  3.1 5.0 %collective-permute-start = (f32[1480,128]{1,0:T(8,128)S(1)}, f32[1480,128]{1,0:T(8,128)S(1)}, u32[]{:S(2)}, u32[]{:S(2)}) collective-permute-start(f32[1480,128]{1,0:T(8,128)S(1)} %get-tuple-element.21), channel_id=1, source_target_pairs={{0,8},{8,16},{16,24},{1,9},{9,17},{17,25},{2,10},{10,18},{18,26},{... | collective-permute-start | bytes 2273288 | tf_op jit(solution)/shard_map/ppermute | solution.py:775
  8.1 1.3 %collective-permute-start.1 = (f32[1480,128]{1,0:T(8,128)S(1)}, f32[1480,128]{1,0:T(8,128)S(1)}, u32[]{:S(2)}, u32[]{:S(2)}) collective-permute-start(f32[1480,128]{1,0:T(8,128)S(1)} %get-tuple-element.22), channel_id=1, source_target_pairs={{8,0},{16,8},{24,16},{9,1},{17,9},{25,17},{10,2},{18,10},{26,18},{... | collective-permute-start | bytes 2273288 | tf_op jit(solution)/shard_map/ppermute | solution.py:776
  9.4 3.0 %pack_edge.1 = (f32[10240,128]{1,0:T(8,128)S(1)}, f32[392,128]{1,0:T(8,128)S(1)}, f32[108,128]{1,0:T(8,128)S(1)}, f32[108,128]{1,0:T(8,128)S(1)}) custom-call(s32[3,12]{1,0:T(4,128)} %bitcast.2, s32[12,4096]{1,0:T(8,128)} %marks_in.5, f32[12,19,4096]{2,1,0:T(8,128)} %pops.5), custom_call_target="tpu_custom_call" | custom-call | tf_op jit(solution)/shard_map/pack_edge/pallas_call | solution.py:778
  12.4 0.2 collective-permute-start.2
  12.7 4.0 %collective-permute-start.3 = (f32[108,128]{1,0:T(8,128)S(1)}, f32[108,128]{1,0:T(8,128)S(1)}, u32[]{:S(2)}, u32[]{:S(2)}) collective-permute-start(f32[108,128]{1,0:T(8,128)S(1)} %get-tuple-element.24), channel_id=1, source_target_pairs={{0,9},{1,8},{8,17},{9,16},{16,25},{17,24},{2,11},{3,10},{10,19},{1... | collective-permute-start | bytes 165896 | tf_op jit(solution)/shard_map/ppermute | solution.py:796
  16.7 1.3 %collective-permute-start.4 = (f32[108,128]{1,0:T(8,128)S(1)}, f32[108,128]{1,0:T(8,128)S(1)}, u32[]{:S(2)}, u32[]{:S(2)}) collective-permute-start(f32[108,128]{1,0:T(8,128)S(1)} %get-tuple-element.25), channel_id=1, source_target_pairs={{8,1},{9,0},{16,9},{17,8},{24,17},{25,16},{10,3},{11,2},{18,11},{1... | collective-permute-start | bytes 165896 | tf_op jit(solution)/shard_map/ppermute | solution.py:797
  18.0 4.6 %pack_own.1.own_in = f32[10240,128]{1,0:T(8,128)S(1)} custom-call(s32[3,12]{1,0:T(4,128)} %bitcast.3, s32[12,4096]{1,0:T(8,128)} %marks_in.5, f32[12,19,4096]{2,1,0:T(8,128)} %pops.5, f32[10240,128]{1,0:T(8,128)S(1)} %get-tuple-element.26.own_in), custom_call_target="tpu_custom_call", output_to_operand_aliasing={{}: (3, {})} | custom-call | tf_op jit(solution)/shard_map/pack_own/pallas_call | solution.py:799
  22.6 2.8 %collective-permute-done.3.zup = f32[108,128]{1,0:T(8,128)S(1)} collective-permute-done((f32[108,128]{1,0:T(8,128)S(1)}, f32[108,128]{1,0:T(8,128)S(1)}, u32[]{:S(2)}, u32[]{:S(2)}) %collective-permute-start.3) | collective-permute-done | bytes 55328 | tf_op jit(solution)/shard_map/ppermute | solution.py:796
  25.4 2.7 %collective-permute-done.4.zdown = f32[108,128]{1,0:T(8,128)S(1)} collective-permute-done((f32[108,128]{1,0:T(8,128)S(1)}, f32[108,128]{1,0:T(8,128)S(1)}, u32[]{:S(2)}, u32[]{:S(2)}) %collective-permute-start.4) | collective-permute-done | bytes 55328 | tf_op jit(solution)/shard_map/ppermute | solution.py:797
  28.1 0.0 collective-permute-done.2.zin
  28.1 0.0 collective-permute-done.up
  28.1 0.8 %collective-permute-done.1.down = f32[1480,128]{1,0:T(8,128)S(1)} collective-permute-done((f32[1480,128]{1,0:T(8,128)S(1)}, f32[1480,128]{1,0:T(8,128)S(1)}, u32[]{:S(2)}, u32[]{:S(2)}) %collective-permute-start.1) | collective-permute-done | bytes 757792 | tf_op jit(solution)/shard_map/ppermute | solution.py:776
  29.0 2.9 %settle_rim.1 = (f32[10240,128]{1,0:T(8,128)S(1)}, f32[608,128]{1,0:T(8,128)S(1)}, f32[384,128]{1,0:T(8,128)S(1)}, f32[24,128]{1,0:T(8,128)S(1)}, f32[472,128]{1,0:T(8,128)S(1)}, /*index=5*/f32[472,128]{1,0:T(8,128)S(1)}) custom-call(s32[3,12]{1,0:T(4,128)} %bitcast.4, f32[1480,128]{1,0:T(8,128)S(1)} %collective-permute-done.up, ...), custom_call_target="tpu_custom_call", output_to_operand_aliasing={{0}: (6, {})} | custom-call | tf_op jit(solution)/shard_map/settle_rim/pallas_call | solution.py:815
  31.9 3.4 %collective-permute-start.5 = (f32[472,128]{1,0:T(8,128)S(1)}, f32[472,128]{1,0:T(8,128)S(1)}, u32[]{:S(2)}, u32[]{:S(2)}) collective-permute-start(f32[472,128]{1,0:T(8,128)S(1)} %get-tuple-element.27), channel_id=1, source_target_pairs={{0,2},{2,4},{4,6},{1,3},{3,5},{5,7},{8,10},{10,12},{12,14},{9,11},... | collective-permute-start | bytes 725000 | tf_op jit(solution)/shard_map/ppermute | solution.py:839
  35.3 1.3 %collective-permute-start.6 = (f32[472,128]{1,0:T(8,128)S(1)}, f32[472,128]{1,0:T(8,128)S(1)}, u32[]{:S(2)}, u32[]{:S(2)}) collective-permute-start(f32[472,128]{1,0:T(8,128)S(1)} %get-tuple-element.28), channel_id=1, source_target_pairs={{2,0},{4,2},{6,4},{3,1},{5,3},{7,5},{10,8},{12,10},{14,12},{11,9},... | collective-permute-start | bytes 725000 | tf_op jit(solution)/shard_map/ppermute | solution.py:840
  36.6 28.9 %settle_all.1 = (f32[15656,128]{1,0:T(8,128)S(1)}, f32[9728,128]{1,0:T(8,128)S(1)}, f32[15656,128]{1,0:T(8,128)S(1)}) custom-call(f32[10240,128]{1,0:T(8,128)S(1)} %get-tuple-element.29.own, f32[608,128]{1,0:T(8,128)S(1)} %get-tuple-element.30.edge, f32[384,128]{1,0:T(8,128)S(1)} %get-tuple-element.31.zall, f32[24,128]{1,0:T(8,128)S(1)} %get-tuple-element.32.zedge), custom_call_target="tpu_custom_call" | custom-call | tf_op jit(solution)/shard_map/settle_all/pallas_call | solution.py:842
  65.6 0.0 collective-permute-done.5.rim_low
  65.6 0.0 collective-permute-done.6.rim_high
  65.6 6.0 %finish.1 = (f32[19,32,16,64]{3,2,1,0:T(8,128)}, f32[15656,128]{1,0:T(8,128)S(1)}, f32[15656,128]{1,0:T(8,128)S(1)}) custom-call(f32[472,128]{1,0:T(8,128)S(1)} %collective-permute-done.5.rim_low, f32[472,128]{1,0:T(8,128)S(1)} %collective-permute-done.6.rim_high, ...), custom_call_target="tpu_custom_call", output_to_operand_aliasing={{1}: (2, {}), {2}: (4, {})} | custom-call | tf_op jit(solution)/shard_map/finish/pallas_call | solution.py:851
Async XLA Ops:
  3.1 25.0 %collective-permute-start = (f32[1480,128]{1,0:T(8,128)S(1)}, f32[1480,128]{1,0:T(8,128)S(1)}, u32[]{:S(2)}, u32[]{:S(2)}) collective-permute-start(f32[1480,128]{1,0:T(8,128)S(1)} %get-tuple-element.21), channel_id=1, source_target_pairs={{0,8},{8,16},{16,24},{1,9},{9,17},{17,25},{2,10},{10,18},{18,26},{... | collective-permute-start | bytes 2273288 | tf_op jit(solution)/shard_map/ppermute | solution.py:775
  8.1 20.9 %collective-permute-start.1 = (f32[1480,128]{1,0:T(8,128)S(1)}, f32[1480,128]{1,0:T(8,128)S(1)}, u32[]{:S(2)}, u32[]{:S(2)}) collective-permute-start(f32[1480,128]{1,0:T(8,128)S(1)} %get-tuple-element.22), channel_id=1, source_target_pairs={{8,0},{16,8},{24,16},{9,1},{17,9},{25,17},{10,2},{18,10},{26,18},{... | collective-permute-start | bytes 2273288 | tf_op jit(solution)/shard_map/ppermute | solution.py:776
  12.4 15.7 %collective-permute-start.2 = (f32[392,128]{1,0:T(8,128)S(1)}, f32[392,128]{1,0:T(8,128)S(1)}, u32[]{:S(2)}, u32[]{:S(2)}) collective-permute-start(f32[392,128]{1,0:T(8,128)S(1)} %get-tuple-element.23), channel_id=1, source_target_pairs={{0,1},{1,0},{2,3},{3,2},{4,5},{5,4},{6,7},{7,6},{8,9},{9,8},{10,11... | collective-permute-start | bytes 602120 | tf_op jit(solution)/shard_map/ppermute | solution.py:793
  12.7 12.7 %collective-permute-start.3 = (f32[108,128]{1,0:T(8,128)S(1)}, f32[108,128]{1,0:T(8,128)S(1)}, u32[]{:S(2)}, u32[]{:S(2)}) collective-permute-start(f32[108,128]{1,0:T(8,128)S(1)} %get-tuple-element.24), channel_id=1, source_target_pairs={{0,9},{1,8},{8,17},{9,16},{16,25},{17,24},{2,11},{3,10},{10,19},{1... | collective-permute-start | bytes 165896 | tf_op jit(solution)/shard_map/ppermute | solution.py:796
  16.7 11.4 %collective-permute-start.4 = (f32[108,128]{1,0:T(8,128)S(1)}, f32[108,128]{1,0:T(8,128)S(1)}, u32[]{:S(2)}, u32[]{:S(2)}) collective-permute-start(f32[108,128]{1,0:T(8,128)S(1)} %get-tuple-element.25), channel_id=1, source_target_pairs={{8,1},{9,0},{16,9},{17,8},{24,17},{25,16},{10,3},{11,2},{18,11},{1... | collective-permute-start | bytes 165896 | tf_op jit(solution)/shard_map/ppermute | solution.py:797
  31.9 33.7 %collective-permute-start.5 = (f32[472,128]{1,0:T(8,128)S(1)}, f32[472,128]{1,0:T(8,128)S(1)}, u32[]{:S(2)}, u32[]{:S(2)}) collective-permute-start(f32[472,128]{1,0:T(8,128)S(1)} %get-tuple-element.27), channel_id=1, source_target_pairs={{0,2},{2,4},{4,6},{1,3},{3,5},{5,7},{8,10},{10,12},{12,14},{9,11},... | collective-permute-start | bytes 725000 | tf_op jit(solution)/shard_map/ppermute | solution.py:839
  35.3 30.3 %collective-permute-start.6 = (f32[472,128]{1,0:T(8,128)S(1)}, f32[472,128]{1,0:T(8,128)S(1)}, u32[]{:S(2)}, u32[]{:S(2)}) collective-permute-start(f32[472,128]{1,0:T(8,128)S(1)} %get-tuple-element.28), channel_id=1, source_target_pairs={{2,0},{4,2},{6,4},{3,1},{5,3},{7,5},{10,8},{12,10},{14,12},{11,9},... | collective-permute-start | bytes 725000 | tf_op jit(solution)/shard_map/ppermute | solution.py:840

commit v6 on v5

--- a/solution.py
+++ b/solution.py
@@ -332,7 +332,7 @@
         copies[held].start()
     mark_copy.wait()
     spread_marks(marks, dense)
-    spot = (lanes() % EDGE) // 2
+    spot = (lanes() & (EDGE - 1)) >> 1
     sublane = lax.broadcasted_iota(jnp.int32, (8, LANE), 0)
     flags = jnp.zeros((8, LANE), jnp.int32)
     for held in range(LAYERS):
@@ -348,7 +348,7 @@
                     total = jnp.zeros((8, LANE), jnp.float32)
                     for k in range(min(8, PLANES - group * 8)):
                         value = own[pl.ds(base + (group * 8 + k) * TILES + part * 8, 8), :]
-                        value = pltpu.roll(value, (2 * k - first_c + LANE) % LANE, 1)
+                        value = pltpu.roll(value, (2 * k - first_c + LANE) & (LANE - 1), 1)
                         total = jnp.where(spot == k, value, total)
                     totals.append((held * ZROWS + group * TILES + part * 8, total))
             for row, total in totals:
@@ -393,31 +393,38 @@
     lax.fori_loop(0, rows, settle, 0)
 
 
-def gathered(parts, zvalue, spot, ylo, column_z):
-    lane = lanes()
+class Lanes:
+    def __init__(self, column_z):
+        lane = lanes()
+        self.from_bz = [lane >= bz * EDGE for bz in range(BZD)]
+        self.main = lane < SPAN_Z
+        self.single = (lane & EDGE) != 0
+        self.double = (lane & (2 * EDGE)) != 0
+        self.goal = jnp.where(column_z == 0, SPAN_Z, LANE - 2)
+
+    def to_halo(self, ylo, spot):
+        return (self.goal - (ylo * EDGE + 2 * spot) + LANE) & (LANE - 1)
+
+
+def gathered(parts, zvalue, spot, ylo, masks):
     rows = parts[0].shape[0]
-    lane = lane[:rows]
     total = None
     for bz in range(BZD):
         shift = (bz * EDGE - ylo * EDGE) % LANE
         value = pltpu.roll(parts[bz], shift, 1) if shift else parts[bz]
-        total = value if total is None else jnp.where(lane // EDGE == bz, value, total)
-    goal = jnp.where(column_z == 0, SPAN_Z, LANE - 2)
-    zvalue = pltpu.roll(zvalue, (goal - (ylo * EDGE + 2 * spot) + LANE) % LANE, 1)
-    return jnp.where(lane >= SPAN_Z, zvalue, total)
-
-
-def gathered_rows(parts, zvalue, spot, column_z):
-    lane = lanes()[: parts[0].shape[0]]
-    single = (lane // EDGE) % 2 == 1
-    double = (lane // (2 * EDGE)) % 2 == 1
-    main = lane < SPAN_Z
+        total = value if total is None else jnp.where(masks.from_bz[bz][:rows], value, total)
+    beyond = pltpu.roll(zvalue, masks.to_halo(ylo, spot), 1)
+    return jnp.where(masks.main[:rows], total, beyond)
+
+
+def gathered_rows(parts, zvalue, spot, masks):
+    rows = parts[0].shape[0]
+    single, double, main = masks.single[:rows], masks.double[:rows], masks.main[:rows]
     pairs = []
     for n in (0, 2):
         even = jnp.where(single, pltpu.roll(parts[n + 1], EDGE, 1), parts[n])
         odd = jnp.where(single, parts[n + 1], pltpu.roll(parts[n], LANE - EDGE, 1))
         pairs.append((even, odd))
-    goal = jnp.where(column_z == 0, SPAN_Z, LANE - 2)
     out = [None] * YLO
     for r in range(4):
         low, high = pairs[0][r % 2], pairs[1][r % 2]
@@ -425,7 +432,7 @@
             both = jnp.where(double, pltpu.roll(high, 2 * EDGE, 1), low)
         else:
             both = jnp.where(double, high, pltpu.roll(low, LANE - 2 * EDGE, 1))
-        beyond = pltpu.roll(zvalue, (goal - (r * EDGE + 2 * spot) + LANE) % LANE, 1)
+        beyond = pltpu.roll(zvalue, masks.to_halo(r, spot), 1)
         out[r] = jnp.where(main, both, beyond)
         out[r + 4] = pltpu.roll(jnp.where(main, beyond, both), SPAN_Z, 1)
     return out
@@ -452,19 +459,18 @@
         else:
             parts = [edge[pl.ds(plane * 4 * FACE + 2 * bz + yhi, 4, stride=FACE), :] for bz in range(BZD)]
         return parts, zedge[pl.ds(group * 8 + yhi, 4, stride=2), :]
-    held, half = 1 + chunk // 2, chunk % 2
-    parts = []
-    for bz in range(BZD):
-        base = (held * BZD + bz) * BLOCK + plane * TILES + half * EDGE + yhi
-        parts.append(own[pl.ds(base, 8, stride=2), :])
-    return parts, zall[pl.ds(held * ZROWS + group * TILES + half * EDGE + yhi, 8, stride=2), :]
-
-
-def chunk_values(own, edge, zall, zedge, chunk, yhi, ylo, column_z):
+    held, half = 1 + (chunk >> 1), chunk & 1
+    first = held * (BZD * BLOCK) + half * EDGE + yhi
+    parts = [own[pl.ds(first + bz * BLOCK + plane * TILES, 8, stride=2), :] for bz in range(BZD)]
+    first = held * ZROWS + half * EDGE + yhi
+    return parts, zall[pl.ds(first + group * TILES, 8, stride=2), :]
+
+
+def chunk_values(own, edge, zall, zedge, chunk, yhi, ylo, masks):
     out = []
     for plane in range(PLANES):
         parts, zvalue = plane_parts(own, edge, zall, zedge, chunk, yhi, plane)
-        out.append(gathered(parts, zvalue, plane % 8, ylo, column_z))
+        out.append(gathered(parts, zvalue, plane % 8, ylo, masks))
     return out
 
 
@@ -542,12 +548,13 @@
                 moves.append((zedge, pl.ds(group * 8 + side * SLAB, SLAB), jnp.where(flag, mine, other)))
     for target, rows, value in moves:
         target[rows, :] = value
+    masks = Lanes(column_z)
+    inside_box = inside_lanes(8, column_z)
+    inside_halo = inside_lanes(4, column_z) & halo_x_inside(layer, layers)
     for chunk in (0, 1, 2, 3, None):
         for y in (0, 1, SPAN_Y - 2, SPAN_Y - 1):
-            values = chunk_values(own, edge, zall, zedge, chunk, y // YLO, y % YLO, column_z)
-            inside = inside_lanes(values[0].shape[0], column_z)
-            if chunk is None:
-                inside = inside & halo_x_inside(layer, layers)
+            values = chunk_values(own, edge, zall, zedge, chunk, y // YLO, y % YLO, masks)
+            inside = inside_halo if chunk is None else inside_box
             post = marked(values[:POPS], values[POPS], inside)
             target = post_down if y < 2 else post_up
             rim = RIM_DOWN if y < 2 else RIM_UP
@@ -568,7 +575,7 @@
             values = []
             for plane in range(RIM):
                 value = source[pl.ds(plane * GRID_X + 8 * chunk, 8), :]
-                values.append(pltpu.roll(value, (plane * EXT_Z + 2 * column_z) % LANE, 1))
+                values.append(pltpu.roll(value, (plane * EXT_Z + 2 * column_z) & (LANE - 1), 1))
             totals = []
             for block in range(RIM_BLOCKS):
                 total = jnp.zeros((8, LANE), jnp.float32)
@@ -629,6 +636,9 @@
 
 def settle_all(layers, columns, depth, own, edge, zall, zedge, field, start, later):
     layer, _, column_z = place()
+    masks = Lanes(column_z)
+    inside_box = inside_lanes(8, column_z)
+    inside_halo = inside_lanes(4, column_z) & halo_x_inside(layer, layers)
 
     def caps_of(mark, inside):
         return [jnp.where(inside, jnp.where(value > 0.5, ROTOR, -ROTOR), OUTSIDE) for value in mark]
@@ -636,12 +646,12 @@
     def halves(yhi, carry):
         def rows_of_plane(chunk, plane):
             parts, zvalue = plane_parts(own, edge, zall, zedge, chunk, yhi, plane)
-            return gathered_rows(parts, zvalue, plane % 8, column_z)
+            return gathered_rows(parts, zvalue, plane % 8, masks)
 
         top = yhi * YLO * PITCH + FIRST
 
         def chunks(chunk, carry):
-            caps = caps_of(rows_of_plane(chunk, POPS), inside_lanes(8, column_z))
+            caps = caps_of(rows_of_plane(chunk, POPS), inside_box)
 
             def leave(i, values):
                 for ylo in range(YLO):
@@ -654,8 +664,7 @@
             return carry
 
         lax.fori_loop(0, SPAN_X // 8, chunks, 0)
-        inside = inside_lanes(4, column_z) & halo_x_inside(layer, layers)
-        caps = caps_of(rows_of_plane(None, POPS), inside)
+        caps = caps_of(rows_of_plane(None, POPS), inside_halo)
 
         def leave(i, values):
             for ylo in range(YLO):
@@ -674,7 +683,7 @@
 def finish(columns, depth, rim_low, rim_high, field_in, start, later_in, out, field, later, turn, result, sems):
     del field_in, later_in
     _, column_y, column_z = place()
-    flat = (lanes() + 2 * column_z) % LANE
+    flat = (lanes() + 2 * column_z) & (LANE - 1)
     sides = (
         (rim_low, -1, -2, RIM_UP, column_y > 0),
         (rim_high, SPAN_Y, SPAN_Y + 1, RIM_DOWN, column_y < columns - 1),
@@ -685,7 +694,7 @@
             blocks = [source[pl.ds(block * EXT_X + 8 * chunk, 8), :] for block in range(RIM_BLOCKS)]
             for plane in range(RIM):
                 block, begin = divmod(plane * EXT_Z, LANE)
-                shift = (2 * LANE - begin - 2 * column_z) % LANE
+                shift = (2 * LANE - begin - 2 * column_z) & (LANE - 1)
                 value = pltpu.roll(blocks[block], shift, 1)
                 if begin + EXT_Z > LANE:
                     value = jnp.where(flat < LANE - begin, value, pltpu.roll(blocks[block + 1], shift, 1))

time: 72.6 us -> 74.1 us (1.021)
  Pallas kernels: 48.6 us -> 50.2 us
    pallas_call x1, Pallas kernels: 28.9 us -> 30.4 us  [shards(): pl.pallas_call(functools.partial(settle_all, layers, columns, depth), out...]
  transfers between devices with their start and end apart: 7 -> 7, of which waited for: 3 -> 3; matrix products, arithmetic and copies ran while one was open for 0% -> 0% of each run, Pallas kernels for 51% -> 52%
where the time goes in v6:
time: 74.1 us; the launch traced here: 73.1 us
  Pallas kernels  50.2 us (68%)
  starting transfers between devices  15.9 us (21%)
  waiting for transfers between devices  6.83 us (9%)
    pallas_call x1, Pallas kernels, shards(): pl.pallas_call(functools.partial(settle_all, layers, columns, depth), out...  30.4 us
    pallas_call x1, Pallas kernels, shards(): pl.pallas_call(functools.partial(finish, columns, depth), out_shape=(jax....  5.96 us
    ppermute x1, starting transfers between devices, shards(): from_low = lax.ppermute(send_up, 'stream', up)  4.98 us
    pallas_call x1, Pallas kernels, shards(): pl.pallas_call(pack_own, out_shape=kept(LAYERS * BZD * BLOCK), in_specs=[...  4.25 us
    ppermute x1, starting transfers between devices, shards(): z_low = lax.ppermute(zsend_up, ('stream', 'cz'), zup_pairs)  3.58 us
    pallas_call x1, Pallas kernels, shards(): pl.pallas_call(pack_edge, out_shape=(kept(LAYERS * BZD * BLOCK), kept(ZME...  3.54 us
    ppermute x1, starting transfers between devices, shards(): rim_low = lax.ppermute(rim_up, 'cy', cy_up)  3.41 us
    ppermute x1, waiting for transfers between devices, shards(): z_low = lax.ppermute(zsend_up, ('stream', 'cz'), zup_pairs)  3.28 us
  transfers between devices with their start and end apart: 7, of which 3 were waited for; matrix products, arithmetic and copies ran while one was open for 0% of the time, Pallas kernels for 52%

profile of v6, /device:TPU:0, one launch (start us, length us, event | category | flops | bytes accessed | tf_op | source)
XLA Modules:
  0.0 73.1 jit_solution(7222442170919801410)
XLA Ops:
  0.0 3.1 %pack_stream.1 = (f32[1480,128]{1,0:T(8,128)S(1)}, f32[1480,128]{1,0:T(8,128)S(1)}) custom-call(s32[3,12]{1,0:T(4,128)} %bitcast.1, s32[12,4096]{1,0:T(8,128)} %marks_in.5, f32[12,19,4096]{2,1,0:T(8,128)} %pops.5), custom_call_target="tpu_custom_call" | custom-call | tf_op jit(solution)/shard_map/pack_stream/pallas_call | solution.py:768
  3.1 5.0 %collective-permute-start = (f32[1480,128]{1,0:T(8,128)S(1)}, f32[1480,128]{1,0:T(8,128)S(1)}, u32[]{:S(2)}, u32[]{:S(2)}) collective-permute-start(f32[1480,128]{1,0:T(8,128)S(1)} %get-tuple-element.21), channel_id=1, source_target_pairs={{0,8},{8,16},{16,24},{1,9},{9,17},{17,25},{2,10},{10,18},{18,26},{... | collective-permute-start | bytes 2273288 | tf_op jit(solution)/shard_map/ppermute | solution.py:784
  8.1 1.3 %collective-permute-start.1 = (f32[1480,128]{1,0:T(8,128)S(1)}, f32[1480,128]{1,0:T(8,128)S(1)}, u32[]{:S(2)}, u32[]{:S(2)}) collective-permute-start(f32[1480,128]{1,0:T(8,128)S(1)} %get-tuple-element.22), channel_id=1, source_target_pairs={{8,0},{16,8},{24,16},{9,1},{17,9},{25,17},{10,2},{18,10},{26,18},{... | collective-permute-start | bytes 2273288 | tf_op jit(solution)/shard_map/ppermute | solution.py:785
  9.4 3.5 %pack_edge.1 = (f32[10240,128]{1,0:T(8,128)S(1)}, f32[392,128]{1,0:T(8,128)S(1)}, f32[108,128]{1,0:T(8,128)S(1)}, f32[108,128]{1,0:T(8,128)S(1)}) custom-call(s32[3,12]{1,0:T(4,128)} %bitcast.2, s32[12,4096]{1,0:T(8,128)} %marks_in.5, f32[12,19,4096]{2,1,0:T(8,128)} %pops.5), custom_call_target="tpu_custom_call" | custom-call | tf_op jit(solution)/shard_map/pack_edge/pallas_call | solution.py:787
  12.9 0.1 collective-permute-start.2
  13.0 3.6 %collective-permute-start.3 = (f32[108,128]{1,0:T(8,128)S(1)}, f32[108,128]{1,0:T(8,128)S(1)}, u32[]{:S(2)}, u32[]{:S(2)}) collective-permute-start(f32[108,128]{1,0:T(8,128)S(1)} %get-tuple-element.24), channel_id=1, source_target_pairs={{0,9},{1,8},{8,17},{9,16},{16,25},{17,24},{2,11},{3,10},{10,19},{1... | collective-permute-start | bytes 165896 | tf_op jit(solution)/shard_map/ppermute | solution.py:805
  16.6 1.3 %collective-permute-start.4 = (f32[108,128]{1,0:T(8,128)S(1)}, f32[108,128]{1,0:T(8,128)S(1)}, u32[]{:S(2)}, u32[]{:S(2)}) collective-permute-start(f32[108,128]{1,0:T(8,128)S(1)} %get-tuple-element.25), channel_id=1, source_target_pairs={{8,1},{9,0},{16,9},{17,8},{24,17},{25,16},{10,3},{11,2},{18,11},{1... | collective-permute-start | bytes 165896 | tf_op jit(solution)/shard_map/ppermute | solution.py:806
  17.9 4.3 %pack_own.1.own_in = f32[10240,128]{1,0:T(8,128)S(1)} custom-call(s32[3,12]{1,0:T(4,128)} %bitcast.3, s32[12,4096]{1,0:T(8,128)} %marks_in.5, f32[12,19,4096]{2,1,0:T(8,128)} %pops.5, f32[10240,128]{1,0:T(8,128)S(1)} %get-tuple-element.26.own_in), custom_call_target="tpu_custom_call", output_to_operand_aliasing={{}: (3, {})} | custom-call | tf_op jit(solution)/shard_map/pack_own/pallas_call | solution.py:808
  22.1 3.3 %collective-permute-done.3.zup = f32[108,128]{1,0:T(8,128)S(1)} collective-permute-done((f32[108,128]{1,0:T(8,128)S(1)}, f32[108,128]{1,0:T(8,128)S(1)}, u32[]{:S(2)}, u32[]{:S(2)}) %collective-permute-start.3) | collective-permute-done | bytes 55328 | tf_op jit(solution)/shard_map/ppermute | solution.py:805
  25.4 2.7 %collective-permute-done.4.zdown = f32[108,128]{1,0:T(8,128)S(1)} collective-permute-done((f32[108,128]{1,0:T(8,128)S(1)}, f32[108,128]{1,0:T(8,128)S(1)}, u32[]{:S(2)}, u32[]{:S(2)}) %collective-permute-start.4) | collective-permute-done | bytes 55328 | tf_op jit(solution)/shard_map/ppermute | solution.py:806
  28.1 0.0 collective-permute-done.2.zin
  28.1 0.0 collective-permute-done.up
  28.1 0.8 %collective-permute-done.1.down = f32[1480,128]{1,0:T(8,128)S(1)} collective-permute-done((f32[1480,128]{1,0:T(8,128)S(1)}, f32[1480,128]{1,0:T(8,128)S(1)}, u32[]{:S(2)}, u32[]{:S(2)}) %collective-permute-start.1) | collective-permute-done | bytes 757792 | tf_op jit(solution)/shard_map/ppermute | solution.py:785
  29.0 3.0 %settle_rim.1 = (f32[10240,128]{1,0:T(8,128)S(1)}, f32[608,128]{1,0:T(8,128)S(1)}, f32[384,128]{1,0:T(8,128)S(1)}, f32[24,128]{1,0:T(8,128)S(1)}, f32[472,128]{1,0:T(8,128)S(1)}, /*index=5*/f32[472,128]{1,0:T(8,128)S(1)}) custom-call(s32[3,12]{1,0:T(4,128)} %bitcast.4, f32[1480,128]{1,0:T(8,128)S(1)} %collective-permute-done.up, ...), custom_call_target="tpu_custom_call", output_to_operand_aliasing={{0}: (6, {})} | custom-call | tf_op jit(solution)/shard_map/settle_rim/pallas_call | solution.py:824
  31.9 3.4 %collective-permute-start.5 = (f32[472,128]{1,0:T(8,128)S(1)}, f32[472,128]{1,0:T(8,128)S(1)}, u32[]{:S(2)}, u32[]{:S(2)}) collective-permute-start(f32[472,128]{1,0:T(8,128)S(1)} %get-tuple-element.27), channel_id=1, source_target_pairs={{0,2},{2,4},{4,6},{1,3},{3,5},{5,7},{8,10},{10,12},{12,14},{9,11},... | collective-permute-start | bytes 725000 | tf_op jit(solution)/shard_map/ppermute | solution.py:848
  35.3 1.3 %collective-permute-start.6 = (f32[472,128]{1,0:T(8,128)S(1)}, f32[472,128]{1,0:T(8,128)S(1)}, u32[]{:S(2)}, u32[]{:S(2)}) collective-permute-start(f32[472,128]{1,0:T(8,128)S(1)} %get-tuple-element.28), channel_id=1, source_target_pairs={{2,0},{4,2},{6,4},{3,1},{5,3},{7,5},{10,8},{12,10},{14,12},{11,9},... | collective-permute-start | bytes 725000 | tf_op jit(solution)/shard_map/ppermute | solution.py:849
  36.6 30.4 %settle_all.1 = (f32[15656,128]{1,0:T(8,128)S(1)}, f32[9728,128]{1,0:T(8,128)S(1)}, f32[15656,128]{1,0:T(8,128)S(1)}) custom-call(f32[10240,128]{1,0:T(8,128)S(1)} %get-tuple-element.29.own, f32[608,128]{1,0:T(8,128)S(1)} %get-tuple-element.30.edge, f32[384,128]{1,0:T(8,128)S(1)} %get-tuple-element.31.zall, f32[24,128]{1,0:T(8,128)S(1)} %get-tuple-element.32.zedge), custom_call_target="tpu_custom_call" | custom-call | tf_op jit(solution)/shard_map/settle_all/pallas_call | solution.py:851
  67.1 0.0 collective-permute-done.5.rim_low
  67.1 0.0 collective-permute-done.6.rim_high
  67.1 6.0 %finish.1 = (f32[19,32,16,64]{3,2,1,0:T(8,128)}, f32[15656,128]{1,0:T(8,128)S(1)}, f32[15656,128]{1,0:T(8,128)S(1)}) custom-call(f32[472,128]{1,0:T(8,128)S(1)} %collective-permute-done.5.rim_low, f32[472,128]{1,0:T(8,128)S(1)} %collective-permute-done.6.rim_high, ...), custom_call_target="tpu_custom_call", output_to_operand_aliasing={{1}: (2, {}), {2}: (4, {})} | custom-call | tf_op jit(solution)/shard_map/finish/pallas_call | solution.py:860
Async XLA Ops:
  3.1 25.0 %collective-permute-start = (f32[1480,128]{1,0:T(8,128)S(1)}, f32[1480,128]{1,0:T(8,128)S(1)}, u32[]{:S(2)}, u32[]{:S(2)}) collective-permute-start(f32[1480,128]{1,0:T(8,128)S(1)} %get-tuple-element.21), channel_id=1, source_target_pairs={{0,8},{8,16},{16,24},{1,9},{9,17},{17,25},{2,10},{10,18},{18,26},{... | collective-permute-start | bytes 2273288 | tf_op jit(solution)/shard_map/ppermute | solution.py:784
  8.1 20.9 %collective-permute-start.1 = (f32[1480,128]{1,0:T(8,128)S(1)}, f32[1480,128]{1,0:T(8,128)S(1)}, u32[]{:S(2)}, u32[]{:S(2)}) collective-permute-start(f32[1480,128]{1,0:T(8,128)S(1)} %get-tuple-element.22), channel_id=1, source_target_pairs={{8,0},{16,8},{24,16},{9,1},{17,9},{25,17},{10,2},{18,10},{26,18},{... | collective-permute-start | bytes 2273288 | tf_op jit(solution)/shard_map/ppermute | solution.py:785
  12.9 15.2 %collective-permute-start.2 = (f32[392,128]{1,0:T(8,128)S(1)}, f32[392,128]{1,0:T(8,128)S(1)}, u32[]{:S(2)}, u32[]{:S(2)}) collective-permute-start(f32[392,128]{1,0:T(8,128)S(1)} %get-tuple-element.23), channel_id=1, source_target_pairs={{0,1},{1,0},{2,3},{3,2},{4,5},{5,4},{6,7},{7,6},{8,9},{9,8},{10,11... | collective-permute-start | bytes 602120 | tf_op jit(solution)/shard_map/ppermute | solution.py:802
  13.0 12.4 %collective-permute-start.3 = (f32[108,128]{1,0:T(8,128)S(1)}, f32[108,128]{1,0:T(8,128)S(1)}, u32[]{:S(2)}, u32[]{:S(2)}) collective-permute-start(f32[108,128]{1,0:T(8,128)S(1)} %get-tuple-element.24), channel_id=1, source_target_pairs={{0,9},{1,8},{8,17},{9,16},{16,25},{17,24},{2,11},{3,10},{10,19},{1... | collective-permute-start | bytes 165896 | tf_op jit(solution)/shard_map/ppermute | solution.py:805
  16.6 11.5 %collective-permute-start.4 = (f32[108,128]{1,0:T(8,128)S(1)}, f32[108,128]{1,0:T(8,128)S(1)}, u32[]{:S(2)}, u32[]{:S(2)}) collective-permute-start(f32[108,128]{1,0:T(8,128)S(1)} %get-tuple-element.25), channel_id=1, source_target_pairs={{8,1},{9,0},{16,9},{17,8},{24,17},{25,16},{10,3},{11,2},{18,11},{1... | collective-permute-start | bytes 165896 | tf_op jit(solution)/shard_map/ppermute | solution.py:806
  31.9 35.2 %collective-permute-start.5 = (f32[472,128]{1,0:T(8,128)S(1)}, f32[472,128]{1,0:T(8,128)S(1)}, u32[]{:S(2)}, u32[]{:S(2)}) collective-permute-start(f32[472,128]{1,0:T(8,128)S(1)} %get-tuple-element.27), channel_id=1, source_target_pairs={{0,2},{2,4},{4,6},{1,3},{3,5},{5,7},{8,10},{10,12},{12,14},{9,11},... | collective-permute-start | bytes 725000 | tf_op jit(solution)/shard_map/ppermute | solution.py:848
  35.3 31.8 %collective-permute-start.6 = (f32[472,128]{1,0:T(8,128)S(1)}, f32[472,128]{1,0:T(8,128)S(1)}, u32[]{:S(2)}, u32[]{:S(2)}) collective-permute-start(f32[472,128]{1,0:T(8,128)S(1)} %get-tuple-element.28), channel_id=1, source_target_pairs={{2,0},{4,2},{6,4},{3,1},{5,3},{7,5},{10,8},{12,10},{14,12},{11,9},... | collective-permute-start | bytes 725000 | tf_op jit(solution)/shard_map/ppermute | solution.py:849

commit v7 on v6

--- a/solution.py
+++ b/solution.py
@@ -41,6 +41,7 @@
 
 POPS = 19
 PLANES = 20
+QUAD = 4
 LANE = 128
 TILES = EDGE**3 // LANE
 BLOCK = PLANES * TILES
@@ -452,12 +453,10 @@
 
 
 def plane_parts(own, edge, zall, zedge, chunk, yhi, plane):
-    group = plane // 8
+    group = plane >> 3
     if chunk is None:
-        if plane == POPS:
-            parts = [jnp.zeros((4, LANE), jnp.float32)] * BZD
-        else:
-            parts = [edge[pl.ds(plane * 4 * FACE + 2 * bz + yhi, 4, stride=FACE), :] for bz in range(BZD)]
+        first = plane * 4 * FACE + yhi
+        parts = [edge[pl.ds(first + 2 * bz, 4, stride=FACE), :] for bz in range(BZD)]
         return parts, zedge[pl.ds(group * 8 + yhi, 4, stride=2), :]
     held, half = 1 + (chunk >> 1), chunk & 1
     first = held * (BZD * BLOCK) + half * EDGE + yhi
@@ -508,6 +507,8 @@
         inner, outer = (1, 0) if side == 0 else (2, 3)
         pairs = [(i, i, inner) for i in range(POPS)]
         pairs += [(POPS + n, i, outer) for n, i in enumerate(AHEAD if side == 0 else BACK)]
+        for x in (2 * side, 2 * side + 1):
+            edge[pl.ds((POPS * 4 + x) * FACE, FACE), :] = jnp.zeros((FACE, LANE), jnp.float32)
         values = [arrived[pl.ds(SENT_SLABS + plane * FACE, FACE), :] for plane, _, _ in pairs]
         for (_, i, x), value in zip(pairs, values):
             edge[pl.ds((i * 4 + x) * FACE, FACE), :] = value
@@ -644,36 +645,43 @@
         return [jnp.where(inside, jnp.where(value > 0.5, ROTOR, -ROTOR), OUTSIDE) for value in mark]
 
     def halves(yhi, carry):
+        top = yhi * YLO * PITCH + FIRST
+
         def rows_of_plane(chunk, plane):
             parts, zvalue = plane_parts(own, edge, zall, zedge, chunk, yhi, plane)
-            return gathered_rows(parts, zvalue, plane % 8, masks)
-
-        top = yhi * YLO * PITCH + FIRST
+            return gathered_rows(parts, zvalue, plane & 7, masks)
 
         def chunks(chunk, carry):
             caps = caps_of(rows_of_plane(chunk, POPS), inside_box)
 
-            def leave(i, values):
-                for ylo in range(YLO):
-                    row = pl.multiple_of(i * FIELD + top + ylo * PITCH + 8 * chunk, 8)
-                    field[pl.ds(row, 8), :] = jnp.minimum(values[ylo], caps[ylo])
-                    row = pl.multiple_of((i * SPAN_Y + YLO * yhi + ylo) * SPAN_X + 8 * chunk, 8)
-                    start[pl.ds(row, 8), :] = values[ylo]
-
-            ahead(range(POPS), lambda i: rows_of_plane(chunk, i), leave, 1)
+            def planes(quad, carry):
+                taken = [rows_of_plane(chunk, quad * QUAD + k) for k in range(QUAD)]
+                for k, values in enumerate(taken):
+                    i = quad * QUAD + k
+                    for ylo in range(YLO):
+                        row = pl.multiple_of(i * FIELD + top + ylo * PITCH + 8 * chunk, 8)
+                        field[pl.ds(row, 8), :] = jnp.minimum(values[ylo], caps[ylo])
+                        row = pl.multiple_of((i * SPAN_Y + YLO * yhi + ylo) * SPAN_X + 8 * chunk, 8)
+                        start[pl.ds(row, 8), :] = values[ylo]
+                return carry
+
+            lax.fori_loop(0, PLANES // QUAD, planes, 0)
             return carry
 
         lax.fori_loop(0, SPAN_X // 8, chunks, 0)
         caps = caps_of(rows_of_plane(None, POPS), inside_halo)
 
-        def leave(i, values):
-            for ylo in range(YLO):
-                value = jnp.minimum(values[ylo], caps[ylo])
-                row = i * FIELD + top + ylo * PITCH
-                field[pl.ds(row - 2, 2), :] = value[:2]
-                field[pl.ds(row + SPAN_X, 2), :] = value[2:]
-
-        ahead(range(POPS), lambda i: rows_of_plane(None, i), leave, 1)
+        def planes(quad, carry):
+            taken = [rows_of_plane(None, quad * QUAD + k) for k in range(QUAD)]
+            for k, values in enumerate(taken):
+                for ylo in range(YLO):
+                    value = jnp.minimum(values[ylo], caps[ylo])
+                    row = (quad * QUAD + k) * FIELD + top + ylo * PITCH
+                    field[pl.ds(row - 2, 2), :] = value[:2]
+                    field[pl.ds(row + SPAN_X, 2), :] = value[2:]
+            return carry
+
+        lax.fori_loop(0, PLANES // QUAD, planes, 0)
         return carry
 
     lax.fori_loop(0, SPAN_Y // YLO, halves, 0)
@@ -825,7 +833,7 @@
         functools.partial(settle_rim, layers),
         out_shape=(
             kept(LAYERS * BZD * BLOCK),
-            kept(POPS * 4 * FACE),
+            kept(PLANES * 4 * FACE),
             kept(LAYERS * ZROWS),
             kept(ZGROUPS * 8),
             kept(RIM_ROWS),
@@ -850,7 +858,7 @@
 
     field, start, later = pl.pallas_call(
         functools.partial(settle_all, layers, columns, depth),
-        out_shape=(kept(POPS * FIELD), kept(POPS * SPAN_X * SPAN_Y), kept(POPS * FIELD)),
+        out_shape=(kept(PLANES * FIELD), kept(PLANES * SPAN_X * SPAN_Y), kept(POPS * FIELD)),
         in_specs=[vmem] * 4,
         out_specs=(vmem,) * 3,
         compiler_params=params(16),
@@ -861,7 +869,7 @@
         functools.partial(finish, columns, depth),
         out_shape=(
             jax.ShapeDtypeStruct((POPS, SPAN_X, SPAN_Y, SPAN_Z), jnp.float32),
-            kept(POPS * FIELD),
+            kept(PLANES * FIELD),
             kept(POPS * FIELD),
         ),
         in_specs=[vmem] * 5,

time: 74.1 us -> 64.3 us (0.87)
  Pallas kernels: 50.2 us -> 40.3 us
  starting transfers between devices: 15.9 us -> 17 us
  waiting for transfers between devices: 6.83 us -> 5.85 us
    pallas_call x1, Pallas kernels: 30.4 us -> 20.8 us  [shards(): pl.pallas_call(functools.partial(settle_all, layers, columns, depth), out...]
    ppermute x1, starting transfers between devices: 3.58 us -> 4.69 us  [shards(): z_low = lax.ppermute(zsend_up, ('stream', 'cz'), zup_pairs)]
    ppermute x1, waiting for transfers between devices: 3.28 us -> 2.3 us  [shards(): z_low = lax.ppermute(zsend_up, ('stream', 'cz'), zup_pairs)]
  transfers between devices with their start and end apart: 7 -> 7, of which waited for: 3 -> 3; matrix products, arithmetic and copies ran while one was open for 0% -> 0% of each run, Pallas kernels for 52% -> 45%
where the time goes in v7:
time: 64.3 us; the launch traced here: 63.3 us
  Pallas kernels  40.3 us (63%)
  starting transfers between devices  17 us (26%)
  waiting for transfers between devices  5.85 us (9%)
    pallas_call x1, Pallas kernels, shards(): pl.pallas_call(functools.partial(settle_all, layers, columns, depth), out...  20.8 us
    pallas_call x1, Pallas kernels, shards(): pl.pallas_call(functools.partial(finish, columns, depth), out_shape=(jax....  5.82 us
    ppermute x1, starting transfers between devices, shards(): from_low = lax.ppermute(send_up, 'stream', up)  4.98 us
    ppermute x1, starting transfers between devices, shards(): z_low = lax.ppermute(zsend_up, ('stream', 'cz'), zup_pairs)  4.69 us
    pallas_call x1, Pallas kernels, shards(): pl.pallas_call(pack_own, out_shape=kept(LAYERS * BZD * BLOCK), in_specs=[...  4.62 us
    ppermute x1, starting transfers between devices, shards(): rim_low = lax.ppermute(rim_up, 'cy', cy_up)  3.41 us
    pallas_call x1, Pallas kernels, shards(): pl.pallas_call(pack_stream, out_shape=(kept(SENT_ROWS), kept(SENT_ROWS)),...  3.09 us
    pallas_call x1, Pallas kernels, shards(): pl.pallas_call(pack_edge, out_shape=(kept(LAYERS * BZD * BLOCK), kept(ZME...  3.03 us
  transfers between devices with their start and end apart: 7, of which 3 were waited for; matrix products, arithmetic and copies ran while one was open for 0% of the time, Pallas kernels for 45%

profile of v7, /device:TPU:0, one launch (start us, length us, event | category | flops | bytes accessed | tf_op | source)
XLA Modules:
  0.0 63.3 jit_solution(7148077330082531422)
XLA Ops:
  0.0 3.1 %pack_stream.1 = (f32[1480,128]{1,0:T(8,128)S(1)}, f32[1480,128]{1,0:T(8,128)S(1)}) custom-call(s32[3,12]{1,0:T(4,128)} %bitcast.1, s32[12,4096]{1,0:T(8,128)} %marks_in.5, f32[12,19,4096]{2,1,0:T(8,128)} %pops.5), custom_call_target="tpu_custom_call" | custom-call | tf_op jit(solution)/shard_map/pack_stream/pallas_call | solution.py:776
  3.1 5.0 %collective-permute-start = (f32[1480,128]{1,0:T(8,128)S(1)}, f32[1480,128]{1,0:T(8,128)S(1)}, u32[]{:S(2)}, u32[]{:S(2)}) collective-permute-start(f32[1480,128]{1,0:T(8,128)S(1)} %get-tuple-element.21), channel_id=1, source_target_pairs={{0,8},{8,16},{16,24},{1,9},{9,17},{17,25},{2,10},{10,18},{18,26},{... | collective-permute-start | bytes 2273288 | tf_op jit(solution)/shard_map/ppermute | solution.py:792
  8.1 1.3 %collective-permute-start.1 = (f32[1480,128]{1,0:T(8,128)S(1)}, f32[1480,128]{1,0:T(8,128)S(1)}, u32[]{:S(2)}, u32[]{:S(2)}) collective-permute-start(f32[1480,128]{1,0:T(8,128)S(1)} %get-tuple-element.22), channel_id=1, source_target_pairs={{8,0},{16,8},{24,16},{9,1},{17,9},{25,17},{10,2},{18,10},{26,18},{... | collective-permute-start | bytes 2273288 | tf_op jit(solution)/shard_map/ppermute | solution.py:793
  9.4 3.0 %pack_edge.1 = (f32[10240,128]{1,0:T(8,128)S(1)}, f32[392,128]{1,0:T(8,128)S(1)}, f32[108,128]{1,0:T(8,128)S(1)}, f32[108,128]{1,0:T(8,128)S(1)}) custom-call(s32[3,12]{1,0:T(4,128)} %bitcast.2, s32[12,4096]{1,0:T(8,128)} %marks_in.5, f32[12,19,4096]{2,1,0:T(8,128)} %pops.5), custom_call_target="tpu_custom_call" | custom-call | tf_op jit(solution)/shard_map/pack_edge/pallas_call | solution.py:795
  12.4 0.1 collective-permute-start.2
  12.5 4.7 %collective-permute-start.3 = (f32[108,128]{1,0:T(8,128)S(1)}, f32[108,128]{1,0:T(8,128)S(1)}, u32[]{:S(2)}, u32[]{:S(2)}) collective-permute-start(f32[108,128]{1,0:T(8,128)S(1)} %get-tuple-element.24), channel_id=1, source_target_pairs={{0,9},{1,8},{8,17},{9,16},{16,25},{17,24},{2,11},{3,10},{10,19},{1... | collective-permute-start | bytes 165896 | tf_op jit(solution)/shard_map/ppermute | solution.py:813
  17.2 1.3 %collective-permute-start.4 = (f32[108,128]{1,0:T(8,128)S(1)}, f32[108,128]{1,0:T(8,128)S(1)}, u32[]{:S(2)}, u32[]{:S(2)}) collective-permute-start(f32[108,128]{1,0:T(8,128)S(1)} %get-tuple-element.25), channel_id=1, source_target_pairs={{8,1},{9,0},{16,9},{17,8},{24,17},{25,16},{10,3},{11,2},{18,11},{1... | collective-permute-start | bytes 165896 | tf_op jit(solution)/shard_map/ppermute | solution.py:814
  18.5 4.6 %pack_own.1.own_in = f32[10240,128]{1,0:T(8,128)S(1)} custom-call(s32[3,12]{1,0:T(4,128)} %bitcast.3, s32[12,4096]{1,0:T(8,128)} %marks_in.5, f32[12,19,4096]{2,1,0:T(8,128)} %pops.5, f32[10240,128]{1,0:T(8,128)S(1)} %get-tuple-element.26.own_in), custom_call_target="tpu_custom_call", output_to_operand_aliasing={{}: (3, {})} | custom-call | tf_op jit(solution)/shard_map/pack_own/pallas_call | solution.py:816
  23.1 2.3 %collective-permute-done.3.zup = f32[108,128]{1,0:T(8,128)S(1)} collective-permute-done((f32[108,128]{1,0:T(8,128)S(1)}, f32[108,128]{1,0:T(8,128)S(1)}, u32[]{:S(2)}, u32[]{:S(2)}) %collective-permute-start.3) | collective-permute-done | bytes 55328 | tf_op jit(solution)/shard_map/ppermute | solution.py:813
  25.4 2.7 %collective-permute-done.4.zdown = f32[108,128]{1,0:T(8,128)S(1)} collective-permute-done((f32[108,128]{1,0:T(8,128)S(1)}, f32[108,128]{1,0:T(8,128)S(1)}, u32[]{:S(2)}, u32[]{:S(2)}) %collective-permute-start.4) | collective-permute-done | bytes 55328 | tf_op jit(solution)/shard_map/ppermute | solution.py:814
  28.1 0.0 collective-permute-done.2.zin
  28.1 0.0 collective-permute-done.up
  28.1 0.8 %collective-permute-done.1.down = f32[1480,128]{1,0:T(8,128)S(1)} collective-permute-done((f32[1480,128]{1,0:T(8,128)S(1)}, f32[1480,128]{1,0:T(8,128)S(1)}, u32[]{:S(2)}, u32[]{:S(2)}) %collective-permute-start.1) | collective-permute-done | bytes 757792 | tf_op jit(solution)/shard_map/ppermute | solution.py:793
  29.0 2.9 %settle_rim.1 = (f32[10240,128]{1,0:T(8,128)S(1)}, f32[640,128]{1,0:T(8,128)S(1)}, f32[384,128]{1,0:T(8,128)S(1)}, f32[24,128]{1,0:T(8,128)S(1)}, f32[472,128]{1,0:T(8,128)S(1)}, /*index=5*/f32[472,128]{1,0:T(8,128)S(1)}) custom-call(s32[3,12]{1,0:T(4,128)} %bitcast.4, f32[1480,128]{1,0:T(8,128)S(1)} %collective-permute-done.up, ...), custom_call_target="tpu_custom_call", output_to_operand_aliasing={{0}: (6, {})} | custom-call | tf_op jit(solution)/shard_map/settle_rim/pallas_call | solution.py:832
  31.9 3.4 %collective-permute-start.5 = (f32[472,128]{1,0:T(8,128)S(1)}, f32[472,128]{1,0:T(8,128)S(1)}, u32[]{:S(2)}, u32[]{:S(2)}) collective-permute-start(f32[472,128]{1,0:T(8,128)S(1)} %get-tuple-element.27), channel_id=1, source_target_pairs={{0,2},{2,4},{4,6},{1,3},{3,5},{5,7},{8,10},{10,12},{12,14},{9,11},... | collective-permute-start | bytes 725000 | tf_op jit(solution)/shard_map/ppermute | solution.py:856
  35.3 1.3 %collective-permute-start.6 = (f32[472,128]{1,0:T(8,128)S(1)}, f32[472,128]{1,0:T(8,128)S(1)}, u32[]{:S(2)}, u32[]{:S(2)}) collective-permute-start(f32[472,128]{1,0:T(8,128)S(1)} %get-tuple-element.28), channel_id=1, source_target_pairs={{2,0},{4,2},{6,4},{3,1},{5,3},{7,5},{10,8},{12,10},{14,12},{11,9},... | collective-permute-start | bytes 725000 | tf_op jit(solution)/shard_map/ppermute | solution.py:857
  36.6 20.8 %settle_all.1 = (f32[16480,128]{1,0:T(8,128)S(1)}, f32[10240,128]{1,0:T(8,128)S(1)}, f32[15656,128]{1,0:T(8,128)S(1)}) custom-call(f32[10240,128]{1,0:T(8,128)S(1)} %get-tuple-element.29.own, f32[640,128]{1,0:T(8,128)S(1)} %get-tuple-element.30.edge, f32[384,128]{1,0:T(8,128)S(1)} %get-tuple-element.31.zall, f32[24,128]{1,0:T(8,128)S(1)} %get-tuple-element.32.zedge), custom_call_target="tpu_custom_call" | custom-call | tf_op jit(solution)/shard_map/settle_all/pallas_call | solution.py:859
  57.5 0.0 collective-permute-done.5.rim_low
  57.5 0.0 collective-permute-done.6.rim_high
  57.5 5.8 %finish.1 = (f32[19,32,16,64]{3,2,1,0:T(8,128)}, f32[16480,128]{1,0:T(8,128)S(1)}, f32[15656,128]{1,0:T(8,128)S(1)}) custom-call(f32[472,128]{1,0:T(8,128)S(1)} %collective-permute-done.5.rim_low, f32[472,128]{1,0:T(8,128)S(1)} %collective-permute-done.6.rim_high, ...), custom_call_target="tpu_custom_call", output_to_operand_aliasing={{1}: (2, {}), {2}: (4, {})} | custom-call | tf_op jit(solution)/shard_map/finish/pallas_call | solution.py:868
Async XLA Ops:
  3.1 25.0 %collective-permute-start = (f32[1480,128]{1,0:T(8,128)S(1)}, f32[1480,128]{1,0:T(8,128)S(1)}, u32[]{:S(2)}, u32[]{:S(2)}) collective-permute-start(f32[1480,128]{1,0:T(8,128)S(1)} %get-tuple-element.21), channel_id=1, source_target_pairs={{0,8},{8,16},{16,24},{1,9},{9,17},{17,25},{2,10},{10,18},{18,26},{... | collective-permute-start | bytes 2273288 | tf_op jit(solution)/shard_map/ppermute | solution.py:792
  8.1 20.9 %collective-permute-start.1 = (f32[1480,128]{1,0:T(8,128)S(1)}, f32[1480,128]{1,0:T(8,128)S(1)}, u32[]{:S(2)}, u32[]{:S(2)}) collective-permute-start(f32[1480,128]{1,0:T(8,128)S(1)} %get-tuple-element.22), channel_id=1, source_target_pairs={{8,0},{16,8},{24,16},{9,1},{17,9},{25,17},{10,2},{18,10},{26,18},{... | collective-permute-start | bytes 2273288 | tf_op jit(solution)/shard_map/ppermute | solution.py:793
  12.4 15.7 %collective-permute-start.2 = (f32[392,128]{1,0:T(8,128)S(1)}, f32[392,128]{1,0:T(8,128)S(1)}, u32[]{:S(2)}, u32[]{:S(2)}) collective-permute-start(f32[392,128]{1,0:T(8,128)S(1)} %get-tuple-element.23), channel_id=1, source_target_pairs={{0,1},{1,0},{2,3},{3,2},{4,5},{5,4},{6,7},{7,6},{8,9},{9,8},{10,11... | collective-permute-start | bytes 602120 | tf_op jit(solution)/shard_map/ppermute | solution.py:810
  12.5 12.9 %collective-permute-start.3 = (f32[108,128]{1,0:T(8,128)S(1)}, f32[108,128]{1,0:T(8,128)S(1)}, u32[]{:S(2)}, u32[]{:S(2)}) collective-permute-start(f32[108,128]{1,0:T(8,128)S(1)} %get-tuple-element.24), channel_id=1, source_target_pairs={{0,9},{1,8},{8,17},{9,16},{16,25},{17,24},{2,11},{3,10},{10,19},{1... | collective-permute-start | bytes 165896 | tf_op jit(solution)/shard_map/ppermute | solution.py:813
  17.2 10.9 %collective-permute-start.4 = (f32[108,128]{1,0:T(8,128)S(1)}, f32[108,128]{1,0:T(8,128)S(1)}, u32[]{:S(2)}, u32[]{:S(2)}) collective-permute-start(f32[108,128]{1,0:T(8,128)S(1)} %get-tuple-element.25), channel_id=1, source_target_pairs={{8,1},{9,0},{16,9},{17,8},{24,17},{25,16},{10,3},{11,2},{18,11},{1... | collective-permute-start | bytes 165896 | tf_op jit(solution)/shard_map/ppermute | solution.py:814
  31.9 25.5 %collective-permute-start.5 = (f32[472,128]{1,0:T(8,128)S(1)}, f32[472,128]{1,0:T(8,128)S(1)}, u32[]{:S(2)}, u32[]{:S(2)}) collective-permute-start(f32[472,128]{1,0:T(8,128)S(1)} %get-tuple-element.27), channel_id=1, source_target_pairs={{0,2},{2,4},{4,6},{1,3},{3,5},{5,7},{8,10},{10,12},{12,14},{9,11},... | collective-permute-start | bytes 725000 | tf_op jit(solution)/shard_map/ppermute | solution.py:856
  35.3 22.1 %collective-permute-start.6 = (f32[472,128]{1,0:T(8,128)S(1)}, f32[472,128]{1,0:T(8,128)S(1)}, u32[]{:S(2)}, u32[]{:S(2)}) collective-permute-start(f32[472,128]{1,0:T(8,128)S(1)} %get-tuple-element.28), channel_id=1, source_target_pairs={{2,0},{4,2},{6,4},{3,1},{5,3},{7,5},{10,8},{12,10},{14,12},{11,9},... | collective-permute-start | bytes 725000 | tf_op jit(solution)/shard_map/ppermute | solution.py:857

commit v8 on v6

--- a/solution.py
+++ b/solution.py
@@ -66,7 +66,7 @@
 EXT_Z = SPAN_Z + 2
 RIM_UP = tuple(i for i in range(POPS) if VELOCITIES[i][1] == 1)
 RIM_DOWN = tuple(i for i in range(POPS) if VELOCITIES[i][1] == -1)
-RIM = POPS + len(RIM_UP)
+RIM = PLANES + len(RIM_UP) + 1
 AHEAD = tuple(i for i in range(POPS) if VELOCITIES[i][0] == 1)
 BACK = tuple(i for i in range(POPS) if VELOCITIES[i][0] == -1)
 FACE = 2 * BZD
@@ -76,10 +76,10 @@
 RIM_ROWS = RIM_BLOCKS * EXT_X + 4
 GRID_X = 48
 
-ROTOR = -1.0e30
-OUTSIDE = -2.0e30
-WALL_BELOW = -1.0e20
-OUT_BELOW = -1.5e30
+ROTOR = -(2.0**100)
+OUTSIDE = -(2.0**110)
+WALL_BELOW = -(2.0**80)
+OUT_BELOW = -(2.0**105)
 
 VMEM = pltpu.VMEM
 SMEM = pltpu.SMEM
@@ -308,10 +308,14 @@
             post, _ = collide(old)
             if x == inner:
                 pairs = [(i, i) for i in range(POPS)]
+                marks_at = POPS
             else:
-                pairs = [(POPS + n, i) for n, i in enumerate(AHEAD if side == 0 else BACK)]
+                pairs = [(PLANES + n, i) for n, i in enumerate(AHEAD if side == 0 else BACK)]
+                marks_at = RIM - 1
             for plane, i in pairs:
-                out[pl.ds(SENT_SLABS + plane * FACE, FACE), :] = jnp.where(mark, ROTOR, post[i])
+                out[pl.ds(SENT_SLABS + plane * FACE, FACE), :] = jnp.where(mark, old[i], post[i])
+            marks_of = strip[pl.ds(POPS * 2 * FACE + x * FACE, FACE), :]
+            out[pl.ds(SENT_SLABS + marks_at * FACE, FACE), :] = marks_of
 
 
 def pack_edge(places, marks_in, pops, own, zpack, zup, zdown, pos, table, marks, dense, stage, sems):
@@ -398,8 +402,6 @@
         lane = lanes()
         self.from_bz = [lane >= bz * EDGE for bz in range(BZD)]
         self.main = lane < SPAN_Z
-        self.single = (lane & EDGE) != 0
-        self.double = (lane & (2 * EDGE)) != 0
         self.goal = jnp.where(column_z == 0, SPAN_Z, LANE - 2)
 
     def to_halo(self, ylo, spot):
@@ -417,27 +419,6 @@
     return jnp.where(masks.main[:rows], total, beyond)
 
 
-def gathered_rows(parts, zvalue, spot, masks):
-    rows = parts[0].shape[0]
-    single, double, main = masks.single[:rows], masks.double[:rows], masks.main[:rows]
-    pairs = []
-    for n in (0, 2):
-        even = jnp.where(single, pltpu.roll(parts[n + 1], EDGE, 1), parts[n])
-        odd = jnp.where(single, parts[n + 1], pltpu.roll(parts[n], LANE - EDGE, 1))
-        pairs.append((even, odd))
-    out = [None] * YLO
-    for r in range(4):
-        low, high = pairs[0][r % 2], pairs[1][r % 2]
-        if r < 2:
-            both = jnp.where(double, pltpu.roll(high, 2 * EDGE, 1), low)
-        else:
-            both = jnp.where(double, high, pltpu.roll(low, LANE - 2 * EDGE, 1))
-        beyond = pltpu.roll(zvalue, masks.to_halo(r, spot), 1)
-        out[r] = jnp.where(main, both, beyond)
-        out[r + 4] = pltpu.roll(jnp.where(main, beyond, both), SPAN_Z, 1)
-    return out
-
-
 def inside_lanes(rows, column_z):
     lane = lanes()[:rows]
     low = (column_z == 0) & (lane >= SPAN_Z) & (lane < SPAN_Z + 2)
@@ -445,19 +426,17 @@
     return (lane < SPAN_Z) | low | high
 
 
-def marked(post, mark, inside):
-    flag = jnp.where(inside, jnp.where(mark > 0.5, ROTOR, 0.0), OUTSIDE)
-    wall = flag < WALL_BELOW
-    return [jnp.where(wall, flag, value) for value in post]
+def walled(values, mark, inside):
+    factor = jnp.where(mark > 0.5, ROTOR, 1.0)
+    cap = jnp.where(inside, -OUTSIDE, OUTSIDE)
+    return [jnp.minimum(value * factor, cap) for value in values]
 
 
 def plane_parts(own, edge, zall, zedge, chunk, yhi, plane):
-    group = plane // 8
+    group = plane >> 3
     if chunk is None:
-        if plane == POPS:
-            parts = [jnp.zeros((4, LANE), jnp.float32)] * BZD
-        else:
-            parts = [edge[pl.ds(plane * 4 * FACE + 2 * bz + yhi, 4, stride=FACE), :] for bz in range(BZD)]
+        first = plane * 4 * FACE + yhi
+        parts = [edge[pl.ds(first + 2 * bz, 4, stride=FACE), :] for bz in range(BZD)]
         return parts, zedge[pl.ds(group * 8 + yhi, 4, stride=2), :]
     held, half = 1 + (chunk >> 1), chunk & 1
     first = held * (BZD * BLOCK) + half * EDGE + yhi
@@ -466,9 +445,9 @@
     return parts, zall[pl.ds(first + group * TILES, 8, stride=2), :]
 
 
-def chunk_values(own, edge, zall, zedge, chunk, yhi, ylo, masks):
+def chunk_values(own, edge, zall, zedge, chunk, yhi, ylo, masks, planes=tuple(range(PLANES))):
     out = []
-    for plane in range(PLANES):
+    for plane in planes:
         parts, zvalue = plane_parts(own, edge, zall, zedge, chunk, yhi, plane)
         out.append(gathered(parts, zvalue, plane % 8, ylo, masks))
     return out
@@ -506,8 +485,8 @@
     place_copy.wait()
     for side, arrived in enumerate((up, down)):
         inner, outer = (1, 0) if side == 0 else (2, 3)
-        pairs = [(i, i, inner) for i in range(POPS)]
-        pairs += [(POPS + n, i, outer) for n, i in enumerate(AHEAD if side == 0 else BACK)]
+        pairs = [(i, i, inner) for i in range(PLANES)]
+        pairs += [(PLANES + n, i, outer) for n, i in enumerate((AHEAD if side == 0 else BACK) + (POPS,))]
         values = [arrived[pl.ds(SENT_SLABS + plane * FACE, FACE), :] for plane, _, _ in pairs]
         for (_, i, x), value in zip(pairs, values):
             edge[pl.ds((i * 4 + x) * FACE, FACE), :] = value
@@ -524,8 +503,7 @@
                 values = []
                 for _, i, x in pairs:
                     shift = 2 * (x if side == 0 else x - 2)
-                    mark = own[pl.ds(first + POPS * TILES + shift, 2), :] > 0.5
-                    values.append(jnp.where(mark, ROTOR, own[pl.ds(first + i * TILES + shift, 2), :]))
+                    values.append(own[pl.ds(first + i * TILES + shift, 2), :])
                 for (_, i, x), value in zip(pairs, values):
                     edge[pl.ds((i * 4 + x) * FACE + 2 * bz, 2), :] = value
 
@@ -549,25 +527,19 @@
     for target, rows, value in moves:
         target[rows, :] = value
     masks = Lanes(column_z)
-    inside_box = inside_lanes(8, column_z)
-    inside_halo = inside_lanes(4, column_z) & halo_x_inside(layer, layers)
     for chunk in (0, 1, 2, 3, None):
         for y in (0, 1, SPAN_Y - 2, SPAN_Y - 1):
-            values = chunk_values(own, edge, zall, zedge, chunk, y // YLO, y % YLO, masks)
-            inside = inside_halo if chunk is None else inside_box
-            post = marked(values[:POPS], values[POPS], inside)
-            target = post_down if y < 2 else post_up
-            rim = RIM_DOWN if y < 2 else RIM_UP
-            if y in (0, SPAN_Y - 1):
-                pairs = [(i, i) for i in range(POPS)]
-            else:
-                pairs = [(POPS + n, i) for n, i in enumerate(rim)]
-            for plane, i in pairs:
+            target, rim = (post_down, RIM_DOWN) if y < 2 else (post_up, RIM_UP)
+            near = y in (0, SPAN_Y - 1)
+            planes = tuple(range(PLANES)) if near else rim + (POPS,)
+            values = chunk_values(own, edge, zall, zedge, chunk, y // YLO, y % YLO, masks, planes)
+            for n, value in enumerate(values):
+                row = (n if near else PLANES + n) * GRID_X
                 if chunk is None:
-                    target[pl.ds(plane * GRID_X, 2), :] = post[i][:2]
-                    target[pl.ds(plane * GRID_X + EXT_X - 2, 2), :] = post[i][2:]
+                    target[pl.ds(row, 2), :] = value[:2]
+                    target[pl.ds(row + EXT_X - 2, 2), :] = value[2:]
                 else:
-                    target[pl.ds(plane * GRID_X + 2 + 8 * chunk, 8), :] = post[i]
+                    target[pl.ds(row + 2 + 8 * chunk, 8), :] = value
     lane = lanes()
     for source, target in ((post_up, rim_up), (post_down, rim_down)):
         for chunk in range(5):
@@ -620,7 +592,7 @@
         post, _ = collide(values)
         wall = old[0] < WALL_BELOW
         for i in range(POPS):
-            later[pl.ds(i * FIELD + base, 8), :] = jnp.where(wall, old[0], post[i])
+            later[pl.ds(i * FIELD + base, 8), :] = jnp.where(wall, old[i], post[i])
         return carry
 
     lax.fori_loop(FIRST // 8 + begin, FIRST // 8 + end, tile, 0)
@@ -634,74 +606,69 @@
     return pull
 
 
-def settle_all(layers, columns, depth, own, edge, zall, zedge, field, start, later):
+def settle_all(layers, columns, depth, own, edge, zall, zedge, field, later):
     layer, _, column_z = place()
     masks = Lanes(column_z)
     inside_box = inside_lanes(8, column_z)
     inside_halo = inside_lanes(4, column_z) & halo_x_inside(layer, layers)
 
-    def caps_of(mark, inside):
-        return [jnp.where(inside, jnp.where(value > 0.5, ROTOR, -ROTOR), OUTSIDE) for value in mark]
-
     def halves(yhi, carry):
-        def rows_of_plane(chunk, plane):
-            parts, zvalue = plane_parts(own, edge, zall, zedge, chunk, yhi, plane)
-            return gathered_rows(parts, zvalue, plane % 8, masks)
-
-        top = yhi * YLO * PITCH + FIRST
-
         def chunks(chunk, carry):
-            caps = caps_of(rows_of_plane(chunk, POPS), inside_box)
-
-            def leave(i, values):
-                for ylo in range(YLO):
-                    row = pl.multiple_of(i * FIELD + top + ylo * PITCH + 8 * chunk, 8)
-                    field[pl.ds(row, 8), :] = jnp.minimum(values[ylo], caps[ylo])
-                    row = pl.multiple_of((i * SPAN_Y + YLO * yhi + ylo) * SPAN_X + 8 * chunk, 8)
-                    start[pl.ds(row, 8), :] = values[ylo]
-
-            ahead(range(POPS), lambda i: rows_of_plane(chunk, i), leave, 1)
+            for ylo in range(YLO):
+                values = chunk_values(own, edge, zall, zedge, chunk, yhi, ylo, masks)
+                values = walled(values[:POPS], values[POPS], inside_box)
+                row = pl.multiple_of(FIRST + (YLO * yhi + ylo) * PITCH + 8 * chunk, 8)
+                for i in range(POPS):
+                    field[pl.ds(i * FIELD + row, 8), :] = values[i]
             return carry
 
         lax.fori_loop(0, SPAN_X // 8, chunks, 0)
-        caps = caps_of(rows_of_plane(None, POPS), inside_halo)
-
-        def leave(i, values):
-            for ylo in range(YLO):
-                value = jnp.minimum(values[ylo], caps[ylo])
-                row = i * FIELD + top + ylo * PITCH
-                field[pl.ds(row - 2, 2), :] = value[:2]
-                field[pl.ds(row + SPAN_X, 2), :] = value[2:]
-
-        ahead(range(POPS), lambda i: rows_of_plane(None, i), leave, 1)
+        for ylo in range(YLO):
+            values = chunk_values(own, edge, zall, zedge, None, yhi, ylo, masks)
+            values = walled(values[:POPS], values[POPS], inside_halo)
+            row = FIRST + (YLO * yhi + ylo) * PITCH
+            for i in range(POPS):
+                field[pl.ds(i * FIELD + row - 2, 2), :] = values[i][:2]
+                field[pl.ds(i * FIELD + row + SPAN_X, 2), :] = values[i][2:]
         return carry
 
     lax.fori_loop(0, SPAN_Y // YLO, halves, 0)
     first_step(columns, depth, field, later, STEP, (SPAN_Y - 1) * STEP)
 
 
-def finish(columns, depth, rim_low, rim_high, field_in, start, later_in, out, field, later, turn, result, sems):
+def finish(layers, columns, depth, rim_low, rim_high, field_in, later_in, out, field, later, turn, result, sems):
     del field_in, later_in
-    _, column_y, column_z = place()
+    layer, column_y, column_z = place()
     flat = (lanes() + 2 * column_z) & (LANE - 1)
     sides = (
         (rim_low, -1, -2, RIM_UP, column_y > 0),
         (rim_high, SPAN_Y, SPAN_Y + 1, RIM_DOWN, column_y < columns - 1),
     )
+    sublane = lax.broadcasted_iota(jnp.int32, (8, LANE), 0)
     for source, near, far, rim, there in sides:
         for chunk in range(5):
             size = min(8, EXT_X - 8 * chunk)
             blocks = [source[pl.ds(block * EXT_X + 8 * chunk, 8), :] for block in range(RIM_BLOCKS)]
-            for plane in range(RIM):
+
+            def plane_of(plane, blocks=blocks):
                 block, begin = divmod(plane * EXT_Z, LANE)
                 shift = (2 * LANE - begin - 2 * column_z) & (LANE - 1)
                 value = pltpu.roll(blocks[block], shift, 1)
                 if begin + EXT_Z > LANE:
                     value = jnp.where(flat < LANE - begin, value, pltpu.roll(blocks[block + 1], shift, 1))
-                value = jnp.where((flat < EXT_Z) & there, value, OUTSIDE)
-                i, y = (plane, near) if plane < POPS else (rim[plane - POPS], far)
-                row = i * FIELD + FIRST + y * PITCH - 2 + 8 * chunk
-                field[pl.ds(row, size), :] = value[:size]
+                return value
+
+            inside = (flat < EXT_Z) & there
+            if chunk == 0:
+                inside = inside & ((sublane >= 2) | (layer > 0))
+            if chunk == 4:
+                inside = inside & ((sublane < 2) | (layer < layers - 1))
+            for first, count, y, order in ((0, POPS, near, range(POPS)), (PLANES, len(rim), far, rim)):
+                mark = plane_of(POPS if y == near else RIM - 1)
+                values = walled([plane_of(first + n) for n in range(count)], mark, inside)
+                for i, value in zip(order, values):
+                    row = i * FIELD + FIRST + y * PITCH - 2 + 8 * chunk
+                    field[pl.ds(row, size), :] = value[:size]
 
     first_step(columns, depth, field, later, -STEP - 1, STEP)
     first_step(columns, depth, field, later, (SPAN_Y - 1) * STEP - 1, (SPAN_Y + 1) * STEP)
@@ -722,8 +689,7 @@
                 values = streamed(pull_from(later, base), old, drift_y, drift_z)
                 wall = old[0] < WALL_BELOW
                 for i in range(POPS):
-                    first = pl.multiple_of((i * SPAN_Y + y) * SPAN_X + 8 * chunk, 8)
-                    value = jnp.where(wall, start[pl.ds(first, 8), :], values[i])
+                    value = jnp.where(wall, old[i] * (1.0 / ROTOR), values[i])
                     turn[pl.ds(i * 8 * TURN + k * TURN, 8), :] = value
             for k in range(8):
                 values = [turn[pl.ds(i * 8 * TURN + k, 8, stride=TURN), :] for i in range(POPS)]
@@ -825,7 +791,7 @@
         functools.partial(settle_rim, layers),
         out_shape=(
             kept(LAYERS * BZD * BLOCK),
-            kept(POPS * 4 * FACE),
+            kept(PLANES * 4 * FACE),
             kept(LAYERS * ZROWS),
             kept(ZGROUPS * 8),
             kept(RIM_ROWS),
@@ -848,33 +814,33 @@
     rim_low = lax.ppermute(rim_up, "cy", cy_up)
     rim_high = lax.ppermute(rim_down, "cy", cy_down)
 
-    field, start, later = pl.pallas_call(
+    field, later = pl.pallas_call(
         functools.partial(settle_all, layers, columns, depth),
-        out_shape=(kept(POPS * FIELD), kept(POPS * SPAN_X * SPAN_Y), kept(POPS * FIELD)),
+        out_shape=(kept(POPS * FIELD), kept(POPS * FIELD)),
         in_specs=[vmem] * 4,
-        out_specs=(vmem,) * 3,
+        out_specs=(vmem,) * 2,
         compiler_params=params(16),
         name="settle_all",
     )(own, edge, zall, zedge)
 
     out, _, _ = pl.pallas_call(
-        functools.partial(finish, columns, depth),
+        functools.partial(finish, layers, columns, depth),
         out_shape=(
             jax.ShapeDtypeStruct((POPS, SPAN_X, SPAN_Y, SPAN_Z), jnp.float32),
             kept(POPS * FIELD),
             kept(POPS * FIELD),
         ),
-        in_specs=[vmem] * 5,
+        in_specs=[vmem] * 4,
         out_specs=(hbm, vmem, vmem),
         scratch_shapes=[
             VMEM((POPS * 8 * TURN, LANE), jnp.float32),
             VMEM((POPS, SPAN_X, SPAN_Y, SPAN_Z), jnp.float32),
             pltpu.SemaphoreType.DMA((SPAN_X // 8,)),
         ],
-        input_output_aliases={2: 1, 4: 2},
+        input_output_aliases={2: 1, 3: 2},
         compiler_params=params(16),
         name="finish",
-    )(rim_low, rim_high, field, start, later)
+    )(rim_low, rim_high, field, later)
     return out
 
 

time: 74.1 us -> 59.7 us (0.81)
  Pallas kernels: 50.2 us -> 35.7 us
    pallas_call x1, Pallas kernels: 30.4 us -> 15.9 us  [shards(): pl.pallas_call(functools.partial(settle_all, layers, columns, depth), out...]
  transfers between devices with their start and end apart: 7 -> 7, of which waited for: 3 -> 3; matrix products, arithmetic and copies ran while one was open for 0% -> 0% of each run, Pallas kernels for 52% -> 40%
where the time goes in v8:
time: 59.7 us; the launch traced here: 58.7 us
  Pallas kernels  35.7 us (60%)
  starting transfers between devices  15.9 us (27%)
  waiting for transfers between devices  7 us (12%)
    pallas_call x1, Pallas kernels, shards(): pl.pallas_call(functools.partial(settle_all, layers, columns, depth), out...  15.9 us
    pallas_call x1, Pallas kernels, shards(): pl.pallas_call(functools.partial(finish, layers, columns, depth), out_sha...  5.88 us
    ppermute x1, starting transfers between devices, shards(): from_low = lax.ppermute(send_up, 'stream', up)  4.98 us
    pallas_call x1, Pallas kernels, shards(): pl.pallas_call(pack_own, out_shape=kept(LAYERS * BZD * BLOCK), in_specs=[...  4.26 us
    ppermute x1, starting transfers between devices, shards(): z_low = lax.ppermute(zsend_up, ('stream', 'cz'), zup_pairs)  3.58 us
    pallas_call x1, Pallas kernels, shards(): pl.pallas_call(pack_edge, out_shape=(kept(LAYERS * BZD * BLOCK), kept(ZME...  3.54 us
    ppermute x1, waiting for transfers between devices, shards(): z_low = lax.ppermute(zsend_up, ('stream', 'cz'), zup_pairs)  3.45 us
    ppermute x1, starting transfers between devices, shards(): rim_low = lax.ppermute(rim_up, 'cy', cy_up)  3.41 us
  transfers between devices with their start and end apart: 7, of which 3 were waited for; matrix products, arithmetic and copies ran while one was open for 0% of the time, Pallas kernels for 40%

profile of v8, /device:TPU:0, one launch (start us, length us, event | category | flops | bytes accessed | tf_op | source)
XLA Modules:
  0.0 58.7 jit_solution(8527532874344940628)
XLA Ops:
  0.0 3.1 %pack_stream.1 = (f32[1496,128]{1,0:T(8,128)S(1)}, f32[1496,128]{1,0:T(8,128)S(1)}) custom-call(s32[3,12]{1,0:T(4,128)} %bitcast.1, s32[12,4096]{1,0:T(8,128)} %marks_in.5, f32[12,19,4096]{2,1,0:T(8,128)} %pops.5), custom_call_target="tpu_custom_call" | custom-call | tf_op jit(solution)/shard_map/pack_stream/pallas_call | solution.py:734
  3.1 5.0 %collective-permute-start = (f32[1496,128]{1,0:T(8,128)S(1)}, f32[1496,128]{1,0:T(8,128)S(1)}, u32[]{:S(2)}, u32[]{:S(2)}) collective-permute-start(f32[1496,128]{1,0:T(8,128)S(1)} %get-tuple-element.20), channel_id=1, source_target_pairs={{0,8},{8,16},{16,24},{1,9},{9,17},{17,25},{2,10},{10,18},{18,26},{... | collective-permute-start | bytes 2297864 | tf_op jit(solution)/shard_map/ppermute | solution.py:750
  8.1 1.3 %collective-permute-start.1 = (f32[1496,128]{1,0:T(8,128)S(1)}, f32[1496,128]{1,0:T(8,128)S(1)}, u32[]{:S(2)}, u32[]{:S(2)}) collective-permute-start(f32[1496,128]{1,0:T(8,128)S(1)} %get-tuple-element.21), channel_id=1, source_target_pairs={{8,0},{16,8},{24,16},{9,1},{17,9},{25,17},{10,2},{18,10},{26,18},{... | collective-permute-start | bytes 2297864 | tf_op jit(solution)/shard_map/ppermute | solution.py:751
  9.4 3.5 %pack_edge.1 = (f32[10240,128]{1,0:T(8,128)S(1)}, f32[392,128]{1,0:T(8,128)S(1)}, f32[108,128]{1,0:T(8,128)S(1)}, f32[108,128]{1,0:T(8,128)S(1)}) custom-call(s32[3,12]{1,0:T(4,128)} %bitcast.2, s32[12,4096]{1,0:T(8,128)} %marks_in.5, f32[12,19,4096]{2,1,0:T(8,128)} %pops.5), custom_call_target="tpu_custom_call" | custom-call | tf_op jit(solution)/shard_map/pack_edge/pallas_call | solution.py:753
  12.9 0.1 collective-permute-start.2
  13.0 3.6 %collective-permute-start.3 = (f32[108,128]{1,0:T(8,128)S(1)}, f32[108,128]{1,0:T(8,128)S(1)}, u32[]{:S(2)}, u32[]{:S(2)}) collective-permute-start(f32[108,128]{1,0:T(8,128)S(1)} %get-tuple-element.23), channel_id=1, source_target_pairs={{0,9},{1,8},{8,17},{9,16},{16,25},{17,24},{2,11},{3,10},{10,19},{1... | collective-permute-start | bytes 165896 | tf_op jit(solution)/shard_map/ppermute | solution.py:771
  16.6 1.3 %collective-permute-start.4 = (f32[108,128]{1,0:T(8,128)S(1)}, f32[108,128]{1,0:T(8,128)S(1)}, u32[]{:S(2)}, u32[]{:S(2)}) collective-permute-start(f32[108,128]{1,0:T(8,128)S(1)} %get-tuple-element.24), channel_id=1, source_target_pairs={{8,1},{9,0},{16,9},{17,8},{24,17},{25,16},{10,3},{11,2},{18,11},{1... | collective-permute-start | bytes 165896 | tf_op jit(solution)/shard_map/ppermute | solution.py:772
  17.9 4.3 %pack_own.1.own_in = f32[10240,128]{1,0:T(8,128)S(1)} custom-call(s32[3,12]{1,0:T(4,128)} %bitcast.3, s32[12,4096]{1,0:T(8,128)} %marks_in.5, f32[12,19,4096]{2,1,0:T(8,128)} %pops.5, f32[10240,128]{1,0:T(8,128)S(1)} %get-tuple-element.25.own_in), custom_call_target="tpu_custom_call", output_to_operand_aliasing={{}: (3, {})} | custom-call | tf_op jit(solution)/shard_map/pack_own/pallas_call | solution.py:774
  22.2 3.4 %collective-permute-done.3.zup = f32[108,128]{1,0:T(8,128)S(1)} collective-permute-done((f32[108,128]{1,0:T(8,128)S(1)}, f32[108,128]{1,0:T(8,128)S(1)}, u32[]{:S(2)}, u32[]{:S(2)}) %collective-permute-start.3) | collective-permute-done | bytes 55328 | tf_op jit(solution)/shard_map/ppermute | solution.py:771
  25.6 2.7 %collective-permute-done.4.zdown = f32[108,128]{1,0:T(8,128)S(1)} collective-permute-done((f32[108,128]{1,0:T(8,128)S(1)}, f32[108,128]{1,0:T(8,128)S(1)}, u32[]{:S(2)}, u32[]{:S(2)}) %collective-permute-start.4) | collective-permute-done | bytes 55328 | tf_op jit(solution)/shard_map/ppermute | solution.py:772
  28.3 0.0 collective-permute-done.2.zin
  28.3 0.0 collective-permute-done.up
  28.3 0.8 %collective-permute-done.1.down = f32[1496,128]{1,0:T(8,128)S(1)} collective-permute-done((f32[1496,128]{1,0:T(8,128)S(1)}, f32[1496,128]{1,0:T(8,128)S(1)}, u32[]{:S(2)}, u32[]{:S(2)}) %collective-permute-start.1) | collective-permute-done | bytes 765984 | tf_op jit(solution)/shard_map/ppermute | solution.py:751
  29.2 2.9 %settle_rim.1 = (f32[10240,128]{1,0:T(8,128)S(1)}, f32[640,128]{1,0:T(8,128)S(1)}, f32[384,128]{1,0:T(8,128)S(1)}, f32[24,128]{1,0:T(8,128)S(1)}, f32[508,128]{1,0:T(8,128)S(1)}, /*index=5*/f32[508,128]{1,0:T(8,128)S(1)}) custom-call(s32[3,12]{1,0:T(4,128)} %bitcast.4, f32[1496,128]{1,0:T(8,128)S(1)} %collective-permute-done.up, ...), custom_call_target="tpu_custom_call", output_to_operand_aliasing={{0}: (6, {})} | custom-call | tf_op jit(solution)/shard_map/settle_rim/pallas_call | solution.py:790
  32.1 3.4 %collective-permute-start.5 = (f32[508,128]{1,0:T(8,128)S(1)}, f32[508,128]{1,0:T(8,128)S(1)}, u32[]{:S(2)}, u32[]{:S(2)}) collective-permute-start(f32[508,128]{1,0:T(8,128)S(1)} %get-tuple-element.26), channel_id=1, source_target_pairs={{0,2},{2,4},{4,6},{1,3},{3,5},{5,7},{8,10},{10,12},{12,14},{9,11},... | collective-permute-start | bytes 780296 | tf_op jit(solution)/shard_map/ppermute | solution.py:814
  35.5 1.3 %collective-permute-start.6 = (f32[508,128]{1,0:T(8,128)S(1)}, f32[508,128]{1,0:T(8,128)S(1)}, u32[]{:S(2)}, u32[]{:S(2)}) collective-permute-start(f32[508,128]{1,0:T(8,128)S(1)} %get-tuple-element.27), channel_id=1, source_target_pairs={{2,0},{4,2},{6,4},{3,1},{5,3},{7,5},{10,8},{12,10},{14,12},{11,9},... | collective-permute-start | bytes 780296 | tf_op jit(solution)/shard_map/ppermute | solution.py:815
  36.8 15.9 %settle_all.1 = (f32[15656,128]{1,0:T(8,128)S(1)}, f32[15656,128]{1,0:T(8,128)S(1)}) custom-call(f32[10240,128]{1,0:T(8,128)S(1)} %get-tuple-element.28.own, f32[640,128]{1,0:T(8,128)S(1)} %get-tuple-element.29.edge, f32[384,128]{1,0:T(8,128)S(1)} %get-tuple-element.30.zall, f32[24,128]{1,0:T(8,128)S(1)} %get-tuple-element.31.zedge), custom_call_target="tpu_custom_call" | custom-call | tf_op jit(solution)/shard_map/settle_all/pallas_call | solution.py:817
  52.8 0.0 collective-permute-done.5.rim_low
  52.8 0.0 collective-permute-done.6.rim_high
  52.8 5.9 %finish.1 = (f32[19,32,16,64]{3,2,1,0:T(8,128)}, f32[15656,128]{1,0:T(8,128)S(1)}, f32[15656,128]{1,0:T(8,128)S(1)}) custom-call(f32[508,128]{1,0:T(8,128)S(1)} %collective-permute-done.5.rim_low, f32[508,128]{1,0:T(8,128)S(1)} %collective-permute-done.6.rim_high, ...), custom_call_target="tpu_custom_call", output_to_operand_aliasing={{1}: (2, {}), {2}: (3, {})} | custom-call | tf_op jit(solution)/shard_map/finish/pallas_call | solution.py:826
Async XLA Ops:
  3.1 25.2 %collective-permute-start = (f32[1496,128]{1,0:T(8,128)S(1)}, f32[1496,128]{1,0:T(8,128)S(1)}, u32[]{:S(2)}, u32[]{:S(2)}) collective-permute-start(f32[1496,128]{1,0:T(8,128)S(1)} %get-tuple-element.20), channel_id=1, source_target_pairs={{0,8},{8,16},{16,24},{1,9},{9,17},{17,25},{2,10},{10,18},{18,26},{... | collective-permute-start | bytes 2297864 | tf_op jit(solution)/shard_map/ppermute | solution.py:750
  8.1 21.1 %collective-permute-start.1 = (f32[1496,128]{1,0:T(8,128)S(1)}, f32[1496,128]{1,0:T(8,128)S(1)}, u32[]{:S(2)}, u32[]{:S(2)}) collective-permute-start(f32[1496,128]{1,0:T(8,128)S(1)} %get-tuple-element.21), channel_id=1, source_target_pairs={{8,0},{16,8},{24,16},{9,1},{17,9},{25,17},{10,2},{18,10},{26,18},{... | collective-permute-start | bytes 2297864 | tf_op jit(solution)/shard_map/ppermute | solution.py:751
  12.9 15.4 %collective-permute-start.2 = (f32[392,128]{1,0:T(8,128)S(1)}, f32[392,128]{1,0:T(8,128)S(1)}, u32[]{:S(2)}, u32[]{:S(2)}) collective-permute-start(f32[392,128]{1,0:T(8,128)S(1)} %get-tuple-element.22), channel_id=1, source_target_pairs={{0,1},{1,0},{2,3},{3,2},{4,5},{5,4},{6,7},{7,6},{8,9},{9,8},{10,11... | collective-permute-start | bytes 602120 | tf_op jit(solution)/shard_map/ppermute | solution.py:768
  13.0 12.6 %collective-permute-start.3 = (f32[108,128]{1,0:T(8,128)S(1)}, f32[108,128]{1,0:T(8,128)S(1)}, u32[]{:S(2)}, u32[]{:S(2)}) collective-permute-start(f32[108,128]{1,0:T(8,128)S(1)} %get-tuple-element.23), channel_id=1, source_target_pairs={{0,9},{1,8},{8,17},{9,16},{16,25},{17,24},{2,11},{3,10},{10,19},{1... | collective-permute-start | bytes 165896 | tf_op jit(solution)/shard_map/ppermute | solution.py:771
  16.6 11.7 %collective-permute-start.4 = (f32[108,128]{1,0:T(8,128)S(1)}, f32[108,128]{1,0:T(8,128)S(1)}, u32[]{:S(2)}, u32[]{:S(2)}) collective-permute-start(f32[108,128]{1,0:T(8,128)S(1)} %get-tuple-element.24), channel_id=1, source_target_pairs={{8,1},{9,0},{16,9},{17,8},{24,17},{25,16},{10,3},{11,2},{18,11},{1... | collective-permute-start | bytes 165896 | tf_op jit(solution)/shard_map/ppermute | solution.py:772
  32.1 20.7 %collective-permute-start.5 = (f32[508,128]{1,0:T(8,128)S(1)}, f32[508,128]{1,0:T(8,128)S(1)}, u32[]{:S(2)}, u32[]{:S(2)}) collective-permute-start(f32[508,128]{1,0:T(8,128)S(1)} %get-tuple-element.26), channel_id=1, source_target_pairs={{0,2},{2,4},{4,6},{1,3},{3,5},{5,7},{8,10},{10,12},{12,14},{9,11},... | collective-permute-start | bytes 780296 | tf_op jit(solution)/shard_map/ppermute | solution.py:814
  35.5 17.3 %collective-permute-start.6 = (f32[508,128]{1,0:T(8,128)S(1)}, f32[508,128]{1,0:T(8,128)S(1)}, u32[]{:S(2)}, u32[]{:S(2)}) collective-permute-start(f32[508,128]{1,0:T(8,128)S(1)} %get-tuple-element.27), channel_id=1, source_target_pairs={{2,0},{4,2},{6,4},{3,1},{5,3},{7,5},{10,8},{12,10},{14,12},{11,9},... | collective-permute-start | bytes 780296 | tf_op jit(solution)/shard_map/ppermute | solution.py:815

commit v9 on v8

--- a/solution.py
+++ b/solution.py
@@ -219,12 +219,16 @@
 
 
 def collide_block(ref, base):
-    for part in range(TILES // 8):
-        old = [ref[pl.ds(base + i * TILES + 8 * part, 8), :] for i in range(POPS)]
-        mark = ref[pl.ds(base + POPS * TILES + 8 * part, 8), :] > 0.5
-        post, _ = collide(old)
-        for i in range(POPS):
-            ref[pl.ds(base + i * TILES + 8 * part, 8), :] = jnp.where(mark, old[i], post[i])
+    for first in range(0, TILES // 8, 2):
+        moves = []
+        for part in (first, first + 1):
+            old = [ref[pl.ds(base + i * TILES + 8 * part, 8), :] for i in range(POPS)]
+            mark = ref[pl.ds(base + POPS * TILES + 8 * part, 8), :] > 0.5
+            post, _ = collide(old)
+            for i in range(POPS):
+                moves.append((base + i * TILES + 8 * part, jnp.where(mark, old[i], post[i])))
+        for row, value in moves:
+            ref[pl.ds(row, 8), :] = value
 
 
 def pack_block(out, base, stage, dense, row):
@@ -445,11 +449,14 @@
     return parts, zall[pl.ds(first + group * TILES, 8, stride=2), :]
 
 
-def chunk_values(own, edge, zall, zedge, chunk, yhi, ylo, masks, planes=tuple(range(PLANES))):
-    out = []
-    for plane in planes:
-        parts, zvalue = plane_parts(own, edge, zall, zedge, chunk, yhi, plane)
-        out.append(gathered(parts, zvalue, plane % 8, ylo, masks))
+def chunk_values(own, edge, zall, zedge, chunk, yhi, rows, masks):
+    out = [[] for _ in rows]
+    for plane in range(PLANES):
+        taken = [n for n, (_, planes) in enumerate(rows) if plane in planes]
+        if taken:
+            parts, zvalue = plane_parts(own, edge, zall, zedge, chunk, yhi, plane)
+        for n in taken:
+            out[n].append(gathered(parts, zvalue, plane % 8, rows[n][0], masks))
     return out
 
 
@@ -528,13 +535,11 @@
         target[rows, :] = value
     masks = Lanes(column_z)
     for chunk in (0, 1, 2, 3, None):
-        for y in (0, 1, SPAN_Y - 2, SPAN_Y - 1):
-            target, rim = (post_down, RIM_DOWN) if y < 2 else (post_up, RIM_UP)
-            near = y in (0, SPAN_Y - 1)
-            planes = tuple(range(PLANES)) if near else rim + (POPS,)
-            values = chunk_values(own, edge, zall, zedge, chunk, y // YLO, y % YLO, masks, planes)
-            for n, value in enumerate(values):
-                row = (n if near else PLANES + n) * GRID_X
+        for near, far, rim, target in ((0, 1, RIM_DOWN, post_down), (SPAN_Y - 1, SPAN_Y - 2, RIM_UP, post_up)):
+            rows = ((near % YLO, range(PLANES)), (far % YLO, rim + (POPS,)))
+            first, second = chunk_values(own, edge, zall, zedge, chunk, near // YLO, rows, masks)
+            for plane, value in enumerate(first + second):
+                row = plane * GRID_X
                 if chunk is None:
                     target[pl.ds(row, 2), :] = value[:2]
                     target[pl.ds(row + EXT_X - 2, 2), :] = value[2:]
@@ -576,26 +581,36 @@
     return drift_y, spin, (total_y - 1) / 2.0
 
 
-def first_step(columns, depth, field, later, begin, end):
+def first_step(columns, depth, field, later, begin, end, last):
     _, column_y, _ = place()
     drift_y, spin, centre_y = drifts_of(columns, depth)
     sublane = lax.broadcasted_iota(jnp.int32, (8, LANE), 0)
 
-    def tile(n, carry):
-        base = pl.multiple_of(8 * n, 8)
-        line = (n - FIRST // 8 + 2 * STEP) // STEP
-        next_row = (sublane >= 6) & (n - FIRST // 8 + 2 * STEP - line * STEP == STEP - 1)
-        here_y = jnp.where(next_row, line + 1, line) + (column_y * SPAN_Y - 2)
-        drift_z = spin * (here_y.astype(jnp.float32) - centre_y)
+    def tile(base, drift_z):
         old = [field[pl.ds(i * FIELD + base, 8), :] for i in range(POPS)]
         values = streamed(pull_from(field, base), old, drift_y, drift_z)
         post, _ = collide(values)
         wall = old[0] < WALL_BELOW
         for i in range(POPS):
             later[pl.ds(i * FIELD + base, 8), :] = jnp.where(wall, old[i], post[i])
+
+    def drift_at(y):
+        return spin * ((y + column_y * SPAN_Y).astype(jnp.float32) - centre_y)
+
+    def between(y):
+        return jnp.where(sublane < 6, drift_at(y - 1), drift_at(y))
+
+    def row(line, carry):
+        y = line - 2
+        base = pl.multiple_of(line * PITCH + (FIRST - 2 * PITCH), 8)
+        tile(base - 8, between(y))
+        for xc in range(STEP - 1):
+            tile(base + 8 * xc, drift_at(y))
         return carry
 
-    lax.fori_loop(FIRST // 8 + begin, FIRST // 8 + end, tile, 0)
+    lax.fori_loop(begin + 2, end + 2, row, 0)
+    if last:
+        tile(FIRST + end * PITCH - 8, between(jnp.int32(end)))
 
 
 def pull_from(field, base):
@@ -614,26 +629,30 @@
 
     def halves(yhi, carry):
         def chunks(chunk, carry):
-            for ylo in range(YLO):
-                values = chunk_values(own, edge, zall, zedge, chunk, yhi, ylo, masks)
-                values = walled(values[:POPS], values[POPS], inside_box)
-                row = pl.multiple_of(FIRST + (YLO * yhi + ylo) * PITCH + 8 * chunk, 8)
+            for ylo in range(0, YLO, 2):
+                rows = [(ylo + n, range(PLANES)) for n in range(2)]
+                pair = chunk_values(own, edge, zall, zedge, chunk, yhi, rows, masks)
+                pair = [walled(values[:POPS], values[POPS], inside_box) for values in pair]
+                for n, values in enumerate(pair):
+                    row = pl.multiple_of(FIRST + (YLO * yhi + ylo + n) * PITCH + 8 * chunk, 8)
+                    for i in range(POPS):
+                        field[pl.ds(i * FIELD + row, 8), :] = values[i]
+            return carry
+
+        lax.fori_loop(0, SPAN_X // 8, chunks, 0)
+        for ylo in range(0, YLO, 2):
+            rows = [(ylo + n, range(PLANES)) for n in range(2)]
+            pair = chunk_values(own, edge, zall, zedge, None, yhi, rows, masks)
+            pair = [walled(values[:POPS], values[POPS], inside_halo) for values in pair]
+            for n, values in enumerate(pair):
+                row = FIRST + (YLO * yhi + ylo + n) * PITCH
                 for i in range(POPS):
-                    field[pl.ds(i * FIELD + row, 8), :] = values[i]
-            return carry
-
-        lax.fori_loop(0, SPAN_X // 8, chunks, 0)
-        for ylo in range(YLO):
-            values = chunk_values(own, edge, zall, zedge, None, yhi, ylo, masks)
-            values = walled(values[:POPS], values[POPS], inside_halo)
-            row = FIRST + (YLO * yhi + ylo) * PITCH
-            for i in range(POPS):
-                field[pl.ds(i * FIELD + row - 2, 2), :] = values[i][:2]
-                field[pl.ds(i * FIELD + row + SPAN_X, 2), :] = values[i][2:]
+                    field[pl.ds(i * FIELD + row - 2, 2), :] = values[i][:2]
+                    field[pl.ds(i * FIELD + row + SPAN_X, 2), :] = values[i][2:]
         return carry
 
     lax.fori_loop(0, SPAN_Y // YLO, halves, 0)
-    first_step(columns, depth, field, later, STEP, (SPAN_Y - 1) * STEP)
+    first_step(columns, depth, field, later, 1, SPAN_Y - 1, False)
 
 
 def finish(layers, columns, depth, rim_low, rim_high, field_in, later_in, out, field, later, turn, result, sems):
@@ -670,8 +689,8 @@
                     row = i * FIELD + FIRST + y * PITCH - 2 + 8 * chunk
                     field[pl.ds(row, size), :] = value[:size]
 
-    first_step(columns, depth, field, later, -STEP - 1, STEP)
-    first_step(columns, depth, field, later, (SPAN_Y - 1) * STEP - 1, (SPAN_Y + 1) * STEP)
+    first_step(columns, depth, field, later, -1, 1, True)
+    first_step(columns, depth, field, later, SPAN_Y - 1, SPAN_Y + 1, True)
 
     drift_y, spin, centre_y = drifts_of(columns, depth)
 

time: 59.7 us -> 54.4 us (0.911)
  Pallas kernels: 35.7 us -> 30.4 us
    pallas_call x1, Pallas kernels: 15.9 us -> 11.9 us  [shards(): pl.pallas_call(functools.partial(settle_all, layers, columns, depth), out...]
    pallas_call x1, Pallas kernels: 5.88 us -> 4.7 us  [shards(): pl.pallas_call(functools.partial(finish, layers, columns, depth), out_sha...]
  transfers between devices with their start and end apart: 7 -> 7, of which waited for: 3 -> 4; matrix products, arithmetic and copies ran while one was open for 0% -> 0% of each run, Pallas kernels for 40% -> 37%
where the time goes in v9:
time: 54.4 us; the launch traced here: 53.9 us
  Pallas kernels  30.4 us (56%)
  starting transfers between devices  15.9 us (29%)
  waiting for transfers between devices  7.49 us (14%)
    pallas_call x1, Pallas kernels, shards(): pl.pallas_call(functools.partial(settle_all, layers, columns, depth), out...  11.9 us
    ppermute x1, starting transfers between devices, shards(): from_low = lax.ppermute(send_up, 'stream', up)  4.98 us
    pallas_call x1, Pallas kernels, shards(): pl.pallas_call(functools.partial(finish, layers, columns, depth), out_sha...  4.7 us
    pallas_call x1, Pallas kernels, shards(): pl.pallas_call(pack_own, out_shape=kept(LAYERS * BZD * BLOCK), in_specs=[...  4.26 us
    ppermute x1, starting transfers between devices, shards(): z_low = lax.ppermute(zsend_up, ('stream', 'cz'), zup_pairs)  3.58 us
    pallas_call x1, Pallas kernels, shards(): pl.pallas_call(pack_edge, out_shape=(kept(LAYERS * BZD * BLOCK), kept(ZME...  3.54 us
    ppermute x1, waiting for transfers between devices, shards(): z_low = lax.ppermute(zsend_up, ('stream', 'cz'), zup_pairs)  3.44 us
    ppermute x1, starting transfers between devices, shards(): rim_low = lax.ppermute(rim_up, 'cy', cy_up)  3.41 us
  transfers between devices with their start and end apart: 7, of which 4 were waited for; matrix products, arithmetic and copies ran while one was open for 0% of the time, Pallas kernels for 37%

profile of v9, /device:TPU:0, one launch (start us, length us, event | category | flops | bytes accessed | tf_op | source)
XLA Modules:
  0.0 53.9 jit_solution(145313754368221910)
XLA Ops:
  0.0 3.1 %pack_stream.1 = (f32[1496,128]{1,0:T(8,128)S(1)}, f32[1496,128]{1,0:T(8,128)S(1)}) custom-call(s32[3,12]{1,0:T(4,128)} %bitcast.1, s32[12,4096]{1,0:T(8,128)} %marks_in.5, f32[12,19,4096]{2,1,0:T(8,128)} %pops.5), custom_call_target="tpu_custom_call" | custom-call | tf_op jit(solution)/shard_map/pack_stream/pallas_call | solution.py:753
  3.1 5.0 %collective-permute-start = (f32[1496,128]{1,0:T(8,128)S(1)}, f32[1496,128]{1,0:T(8,128)S(1)}, u32[]{:S(2)}, u32[]{:S(2)}) collective-permute-start(f32[1496,128]{1,0:T(8,128)S(1)} %get-tuple-element.20), channel_id=1, source_target_pairs={{0,8},{8,16},{16,24},{1,9},{9,17},{17,25},{2,10},{10,18},{18,26},{... | collective-permute-start | bytes 2297864 | tf_op jit(solution)/shard_map/ppermute | solution.py:769
  8.1 1.3 %collective-permute-start.1 = (f32[1496,128]{1,0:T(8,128)S(1)}, f32[1496,128]{1,0:T(8,128)S(1)}, u32[]{:S(2)}, u32[]{:S(2)}) collective-permute-start(f32[1496,128]{1,0:T(8,128)S(1)} %get-tuple-element.21), channel_id=1, source_target_pairs={{8,0},{16,8},{24,16},{9,1},{17,9},{25,17},{10,2},{18,10},{26,18},{... | collective-permute-start | bytes 2297864 | tf_op jit(solution)/shard_map/ppermute | solution.py:770
  9.4 3.5 %pack_edge.1 = (f32[10240,128]{1,0:T(8,128)S(1)}, f32[392,128]{1,0:T(8,128)S(1)}, f32[108,128]{1,0:T(8,128)S(1)}, f32[108,128]{1,0:T(8,128)S(1)}) custom-call(s32[3,12]{1,0:T(4,128)} %bitcast.2, s32[12,4096]{1,0:T(8,128)} %marks_in.5, f32[12,19,4096]{2,1,0:T(8,128)} %pops.5), custom_call_target="tpu_custom_call" | custom-call | tf_op jit(solution)/shard_map/pack_edge/pallas_call | solution.py:772
  12.9 0.1 collective-permute-start.2
  13.0 3.6 %collective-permute-start.3 = (f32[108,128]{1,0:T(8,128)S(1)}, f32[108,128]{1,0:T(8,128)S(1)}, u32[]{:S(2)}, u32[]{:S(2)}) collective-permute-start(f32[108,128]{1,0:T(8,128)S(1)} %get-tuple-element.23), channel_id=1, source_target_pairs={{0,9},{1,8},{8,17},{9,16},{16,25},{17,24},{2,11},{3,10},{10,19},{1... | collective-permute-start | bytes 165896 | tf_op jit(solution)/shard_map/ppermute | solution.py:790
  16.6 1.3 %collective-permute-start.4 = (f32[108,128]{1,0:T(8,128)S(1)}, f32[108,128]{1,0:T(8,128)S(1)}, u32[]{:S(2)}, u32[]{:S(2)}) collective-permute-start(f32[108,128]{1,0:T(8,128)S(1)} %get-tuple-element.24), channel_id=1, source_target_pairs={{8,1},{9,0},{16,9},{17,8},{24,17},{25,16},{10,3},{11,2},{18,11},{1... | collective-permute-start | bytes 165896 | tf_op jit(solution)/shard_map/ppermute | solution.py:791
  17.9 4.3 %pack_own.1.own_in = f32[10240,128]{1,0:T(8,128)S(1)} custom-call(s32[3,12]{1,0:T(4,128)} %bitcast.3, s32[12,4096]{1,0:T(8,128)} %marks_in.5, f32[12,19,4096]{2,1,0:T(8,128)} %pops.5, f32[10240,128]{1,0:T(8,128)S(1)} %get-tuple-element.25.own_in), custom_call_target="tpu_custom_call", output_to_operand_aliasing={{}: (3, {})} | custom-call | tf_op jit(solution)/shard_map/pack_own/pallas_call | solution.py:793
  22.2 3.4 %collective-permute-done.3.zup = f32[108,128]{1,0:T(8,128)S(1)} collective-permute-done((f32[108,128]{1,0:T(8,128)S(1)}, f32[108,128]{1,0:T(8,128)S(1)}, u32[]{:S(2)}, u32[]{:S(2)}) %collective-permute-start.3) | collective-permute-done | bytes 55328 | tf_op jit(solution)/shard_map/ppermute | solution.py:790
  25.6 2.7 %collective-permute-done.4.zdown = f32[108,128]{1,0:T(8,128)S(1)} collective-permute-done((f32[108,128]{1,0:T(8,128)S(1)}, f32[108,128]{1,0:T(8,128)S(1)}, u32[]{:S(2)}, u32[]{:S(2)}) %collective-permute-start.4) | collective-permute-done | bytes 55328 | tf_op jit(solution)/shard_map/ppermute | solution.py:791
  28.3 0.0 collective-permute-done.2.zin
  28.3 0.0 collective-permute-done.up
  28.3 0.8 %collective-permute-done.1.down = f32[1496,128]{1,0:T(8,128)S(1)} collective-permute-done((f32[1496,128]{1,0:T(8,128)S(1)}, f32[1496,128]{1,0:T(8,128)S(1)}, u32[]{:S(2)}, u32[]{:S(2)}) %collective-permute-start.1) | collective-permute-done | bytes 765984 | tf_op jit(solution)/shard_map/ppermute | solution.py:770
  29.1 2.9 %settle_rim.1 = (f32[10240,128]{1,0:T(8,128)S(1)}, f32[640,128]{1,0:T(8,128)S(1)}, f32[384,128]{1,0:T(8,128)S(1)}, f32[24,128]{1,0:T(8,128)S(1)}, f32[508,128]{1,0:T(8,128)S(1)}, /*index=5*/f32[508,128]{1,0:T(8,128)S(1)}) custom-call(s32[3,12]{1,0:T(4,128)} %bitcast.4, f32[1496,128]{1,0:T(8,128)S(1)} %collective-permute-done.up, ...), custom_call_target="tpu_custom_call", output_to_operand_aliasing={{0}: (6, {})} | custom-call | tf_op jit(solution)/shard_map/settle_rim/pallas_call | solution.py:809
  32.1 3.4 %collective-permute-start.5 = (f32[508,128]{1,0:T(8,128)S(1)}, f32[508,128]{1,0:T(8,128)S(1)}, u32[]{:S(2)}, u32[]{:S(2)}) collective-permute-start(f32[508,128]{1,0:T(8,128)S(1)} %get-tuple-element.26), channel_id=1, source_target_pairs={{0,2},{2,4},{4,6},{1,3},{3,5},{5,7},{8,10},{10,12},{12,14},{9,11},... | collective-permute-start | bytes 780296 | tf_op jit(solution)/shard_map/ppermute | solution.py:833
  35.5 1.3 %collective-permute-start.6 = (f32[508,128]{1,0:T(8,128)S(1)}, f32[508,128]{1,0:T(8,128)S(1)}, u32[]{:S(2)}, u32[]{:S(2)}) collective-permute-start(f32[508,128]{1,0:T(8,128)S(1)} %get-tuple-element.27), channel_id=1, source_target_pairs={{2,0},{4,2},{6,4},{3,1},{5,3},{7,5},{10,8},{12,10},{14,12},{11,9},... | collective-permute-start | bytes 780296 | tf_op jit(solution)/shard_map/ppermute | solution.py:834
  36.8 11.9 %settle_all.1 = (f32[15656,128]{1,0:T(8,128)S(1)}, f32[15656,128]{1,0:T(8,128)S(1)}) custom-call(f32[10240,128]{1,0:T(8,128)S(1)} %get-tuple-element.28.own, f32[640,128]{1,0:T(8,128)S(1)} %get-tuple-element.29.edge, f32[384,128]{1,0:T(8,128)S(1)} %get-tuple-element.30.zall, f32[24,128]{1,0:T(8,128)S(1)} %get-tuple-element.31.zedge), custom_call_target="tpu_custom_call" | custom-call | tf_op jit(solution)/shard_map/settle_all/pallas_call | solution.py:836
  48.7 0.0 collective-permute-done.5.rim_low
  48.7 0.5 collective-permute-done.6.rim_high
  49.2 4.7 %finish.1 = (f32[19,32,16,64]{3,2,1,0:T(8,128)}, f32[15656,128]{1,0:T(8,128)S(1)}, f32[15656,128]{1,0:T(8,128)S(1)}) custom-call(f32[508,128]{1,0:T(8,128)S(1)} %collective-permute-done.5.rim_low, f32[508,128]{1,0:T(8,128)S(1)} %collective-permute-done.6.rim_high, ...), custom_call_target="tpu_custom_call", output_to_operand_aliasing={{1}: (2, {}), {2}: (3, {})} | custom-call | tf_op jit(solution)/shard_map/finish/pallas_call | solution.py:845
Async XLA Ops:
  3.1 25.2 %collective-permute-start = (f32[1496,128]{1,0:T(8,128)S(1)}, f32[1496,128]{1,0:T(8,128)S(1)}, u32[]{:S(2)}, u32[]{:S(2)}) collective-permute-start(f32[1496,128]{1,0:T(8,128)S(1)} %get-tuple-element.20), channel_id=1, source_target_pairs={{0,8},{8,16},{16,24},{1,9},{9,17},{17,25},{2,10},{10,18},{18,26},{... | collective-permute-start | bytes 2297864 | tf_op jit(solution)/shard_map/ppermute | solution.py:769
  8.1 21.1 %collective-permute-start.1 = (f32[1496,128]{1,0:T(8,128)S(1)}, f32[1496,128]{1,0:T(8,128)S(1)}, u32[]{:S(2)}, u32[]{:S(2)}) collective-permute-start(f32[1496,128]{1,0:T(8,128)S(1)} %get-tuple-element.21), channel_id=1, source_target_pairs={{8,0},{16,8},{24,16},{9,1},{17,9},{25,17},{10,2},{18,10},{26,18},{... | collective-permute-start | bytes 2297864 | tf_op jit(solution)/shard_map/ppermute | solution.py:770
  12.9 15.4 %collective-permute-start.2 = (f32[392,128]{1,0:T(8,128)S(1)}, f32[392,128]{1,0:T(8,128)S(1)}, u32[]{:S(2)}, u32[]{:S(2)}) collective-permute-start(f32[392,128]{1,0:T(8,128)S(1)} %get-tuple-element.22), channel_id=1, source_target_pairs={{0,1},{1,0},{2,3},{3,2},{4,5},{5,4},{6,7},{7,6},{8,9},{9,8},{10,11... | collective-permute-start | bytes 602120 | tf_op jit(solution)/shard_map/ppermute | solution.py:787
  13.0 12.6 %collective-permute-start.3 = (f32[108,128]{1,0:T(8,128)S(1)}, f32[108,128]{1,0:T(8,128)S(1)}, u32[]{:S(2)}, u32[]{:S(2)}) collective-permute-start(f32[108,128]{1,0:T(8,128)S(1)} %get-tuple-element.23), channel_id=1, source_target_pairs={{0,9},{1,8},{8,17},{9,16},{16,25},{17,24},{2,11},{3,10},{10,19},{1... | collective-permute-start | bytes 165896 | tf_op jit(solution)/shard_map/ppermute | solution.py:790
  16.6 11.7 %collective-permute-start.4 = (f32[108,128]{1,0:T(8,128)S(1)}, f32[108,128]{1,0:T(8,128)S(1)}, u32[]{:S(2)}, u32[]{:S(2)}) collective-permute-start(f32[108,128]{1,0:T(8,128)S(1)} %get-tuple-element.24), channel_id=1, source_target_pairs={{8,1},{9,0},{16,9},{17,8},{24,17},{25,16},{10,3},{11,2},{18,11},{1... | collective-permute-start | bytes 165896 | tf_op jit(solution)/shard_map/ppermute | solution.py:791
  32.1 16.6 %collective-permute-start.5 = (f32[508,128]{1,0:T(8,128)S(1)}, f32[508,128]{1,0:T(8,128)S(1)}, u32[]{:S(2)}, u32[]{:S(2)}) collective-permute-start(f32[508,128]{1,0:T(8,128)S(1)} %get-tuple-element.26), channel_id=1, source_target_pairs={{0,2},{2,4},{4,6},{1,3},{3,5},{5,7},{8,10},{10,12},{12,14},{9,11},... | collective-permute-start | bytes 780296 | tf_op jit(solution)/shard_map/ppermute | solution.py:833
  35.5 13.7 %collective-permute-start.6 = (f32[508,128]{1,0:T(8,128)S(1)}, f32[508,128]{1,0:T(8,128)S(1)}, u32[]{:S(2)}, u32[]{:S(2)}) collective-permute-start(f32[508,128]{1,0:T(8,128)S(1)} %get-tuple-element.27), channel_id=1, source_target_pairs={{2,0},{4,2},{6,4},{3,1},{5,3},{7,5},{10,8},{12,10},{14,12},{11,9},... | collective-permute-start | bytes 780296 | tf_op jit(solution)/shard_map/ppermute | solution.py:834

commit v10 on v9

--- a/solution.py
+++ b/solution.py
@@ -372,7 +372,7 @@
         zdown[target, :] = zpack[pl.ds(ZROWS + group * TILES, SLAB), :]
 
 
-def pack_own(places, marks_in, pops, own_in, own, pos, marks, dense, stage, sems):
+def pack_own(places, marks_in, pops, own_in, own, edge, flags, pos, table, marks, dense, stage, sems):
     del own_in
     layer, _, column_z = place()
     edge_bz = jnp.where(column_z == 0, BZD - 1, 0)
@@ -399,6 +399,32 @@
         return carry
 
     lax.fori_loop(0, rows, settle, 0)
+    fill_table(pos, table)
+    line = lax.broadcasted_iota(jnp.int32, (FACE, LANE), 0) >> 1
+    for side in range(2):
+        here = jnp.zeros((FACE, LANE), jnp.int32)
+        for bz in range(BZD):
+            goal = (0 if side == 0 else LAYERS - 1) * BZD + bz
+            present = table[goal] >= 0
+            here = jnp.where((line == bz) & present, 1, here)
+
+            @pl.when(present)
+            def _(side=side, goal=goal, bz=bz):
+                first = goal * BLOCK + (TILES - SLAB if side == 0 else 0)
+                values = []
+                for _, i, x in slab_planes(side):
+                    shift = 2 * (x if side == 0 else x - 2)
+                    values.append(own[pl.ds(first + i * TILES + shift, 2), :])
+                for (_, i, x), value in zip(slab_planes(side), values):
+                    edge[pl.ds((i * 4 + x) * FACE + 2 * bz, 2), :] = value
+
+        flags[pl.ds(side * FACE, FACE), :] = here.astype(jnp.float32)
+
+
+def slab_planes(side):
+    inner, outer = (1, 0) if side == 0 else (2, 3)
+    pairs = [(i, i, inner) for i in range(PLANES)]
+    return pairs + [(PLANES + n, i, outer) for n, i in enumerate((AHEAD if side == 0 else BACK) + (POPS,))]
 
 
 class Lanes:
@@ -467,53 +493,37 @@
     return low | high
 
 
-def settle_rim(layers, places, up, down, zin, zup, zdown, own_in, own, edge, zall, zedge, rim_up, rim_down, pos, post_up, post_down, sem):
+def settle_rim(layers, up, down, zin, zup, zdown, edge_own, flags, own_in, own, edge, zall, zedge, rim_up, rim_down, post_up, post_down):
     del own_in
     layer, _, column_z = place()
-    place_copy = pltpu.make_async_copy(places, pos, sem)
-    place_copy.start()
+    codes = []
     for arrived in (up, down):
+        first = layer == 0 if arrived is up else layer == layers - 1
         for j in range(MOVE_CAP):
             bx = arrived[pl.ds(SENT_META + 2 * j, 1), :].astype(jnp.int32)
             bz = arrived[pl.ds(SENT_META + 2 * j + 1, 1), :].astype(jnp.int32)
             code = (bx - layer * BXD) * BZD + (bz - column_z * BZD)
-            mine = (bx >= layer * BXD) & (bx < (layer + 1) * BXD)
-            first = layer == 0 if arrived is up else layer == layers - 1
-            code = jnp.max(jnp.where(mine, code, -1))
-
-            @pl.when((code >= 0) & jnp.logical_not(first))
-            def _(arrived=arrived, j=j, code=code):
-                base = pl.multiple_of((jnp.clip(code, 0, BXD * BZD - 1) + BZD) * BLOCK, 8)
-                for k in range(0, BLOCK, 128):
-                    values = [arrived[pl.ds(j * BLOCK + k + 8 * n, 8), :] for n in range(16)]
-                    for n, value in enumerate(values):
-                        own[pl.ds(base + k + 8 * n, 8), :] = value
-
-    place_copy.wait()
+            mine = (bx >= layer * BXD) & (bx < (layer + 1) * BXD) & jnp.logical_not(first)
+            codes.append((arrived, j, jnp.max(jnp.where(mine, code, -1))))
+    for arrived, j, code in codes:
+
+        @pl.when(code >= 0)
+        def _(arrived=arrived, j=j, code=code):
+            base = pl.multiple_of((jnp.clip(code, 0, BXD * BZD - 1) + BZD) * BLOCK, 8)
+            for k in range(0, BLOCK, 128):
+                values = [arrived[pl.ds(j * BLOCK + k + 8 * n, 8), :] for n in range(16)]
+                for n, value in enumerate(values):
+                    own[pl.ds(base + k + 8 * n, 8), :] = value
+
     for side, arrived in enumerate((up, down)):
-        inner, outer = (1, 0) if side == 0 else (2, 3)
-        pairs = [(i, i, inner) for i in range(PLANES)]
-        pairs += [(PLANES + n, i, outer) for n, i in enumerate((AHEAD if side == 0 else BACK) + (POPS,))]
-        values = [arrived[pl.ds(SENT_SLABS + plane * FACE, FACE), :] for plane, _, _ in pairs]
-        for (_, i, x), value in zip(pairs, values):
-            edge[pl.ds((i * 4 + x) * FACE, FACE), :] = value
-        for bz in range(BZD):
-            here = jnp.int32(0)
-            goal = (0 if side == 0 else LAYERS - 1) * BZD + bz
-            for row in range(pos.shape[1]):
-                hit = (pos[0, row] >= 0) & (slot_of(pos, row, layer, column_z) == goal)
-                here = jnp.where(hit, 1, here)
-
-            @pl.when(here == 1)
-            def _(side=side, pairs=pairs, goal=goal, bz=bz):
-                first = goal * BLOCK + (TILES - SLAB if side == 0 else 0)
-                values = []
-                for _, i, x in pairs:
-                    shift = 2 * (x if side == 0 else x - 2)
-                    values.append(own[pl.ds(first + i * TILES + shift, 2), :])
-                for (_, i, x), value in zip(pairs, values):
-                    edge[pl.ds((i * 4 + x) * FACE + 2 * bz, 2), :] = value
-
+        here = flags[pl.ds(side * FACE, FACE), :] > 0.5
+        values = []
+        for plane, i, x in slab_planes(side):
+            row = (i * 4 + x) * FACE
+            other = arrived[pl.ds(SENT_SLABS + plane * FACE, FACE), :]
+            values.append((row, jnp.where(here, edge_own[pl.ds(row, FACE), :], other)))
+        for row, value in values:
+            edge[pl.ds(row, FACE), :] = value
     moves = []
     for held in range(LAYERS):
         flag = zin[pl.ds(ZMETA + held, 1), :] > 0.5
@@ -621,34 +631,53 @@
     return pull
 
 
-def settle_all(layers, columns, depth, own, edge, zall, zedge, field, later):
+def settle_all(layers, columns, depth, own, edge, zall, zedge, field, later, turn):
     layer, _, column_z = place()
     masks = Lanes(column_z)
+    lane = lanes()
+    group_of = [((lane >> 4) & (BZD - 1)) == bz for bz in range(BZD)]
     inside_box = inside_lanes(8, column_z)
     inside_halo = inside_lanes(4, column_z) & halo_x_inside(layer, layers)
 
+    def relay(chunk, yhi, inside, leave):
+        for plane in range(PLANES):
+            parts, zvalue = plane_parts(own, edge, zall, zedge, chunk, yhi, plane)
+            size = zvalue.shape[0]
+            main = masks.main[:size]
+            for r in range(4):
+                both = None
+                for bz in range(BZD):
+                    shift = (bz - r) * EDGE % LANE
+                    value = pltpu.roll(parts[bz], shift, 1) if shift else parts[bz]
+                    both = value if both is None else jnp.where(group_of[bz][:size], value, both)
+                beyond = pltpu.roll(zvalue, masks.to_halo(r, plane % 8), 1)
+                turn[pl.ds((plane * YLO + r) * 8, size), :] = jnp.where(main, both, beyond)
+                turn[pl.ds((plane * YLO + r + 4) * 8, size), :] = jnp.where(main, beyond, both)
+        for ylo in range(YLO):
+            values = [turn[pl.ds((plane * YLO + ylo) * 8, size), :] for plane in range(PLANES)]
+            if ylo >= 4:
+                values = [pltpu.roll(value, SPAN_Z, 1) for value in values]
+            leave(ylo, walled(values[:POPS], values[POPS], inside))
+
     def halves(yhi, carry):
         def chunks(chunk, carry):
-            for ylo in range(0, YLO, 2):
-                rows = [(ylo + n, range(PLANES)) for n in range(2)]
-                pair = chunk_values(own, edge, zall, zedge, chunk, yhi, rows, masks)
-                pair = [walled(values[:POPS], values[POPS], inside_box) for values in pair]
-                for n, values in enumerate(pair):
-                    row = pl.multiple_of(FIRST + (YLO * yhi + ylo + n) * PITCH + 8 * chunk, 8)
-                    for i in range(POPS):
-                        field[pl.ds(i * FIELD + row, 8), :] = values[i]
+            def leave(ylo, values):
+                row = pl.multiple_of(FIRST + (YLO * yhi + ylo) * PITCH + 8 * chunk, 8)
+                for i in range(POPS):
+                    field[pl.ds(i * FIELD + row, 8), :] = values[i]
+
+            relay(chunk, yhi, inside_box, leave)
             return carry
 
         lax.fori_loop(0, SPAN_X // 8, chunks, 0)
-        for ylo in range(0, YLO, 2):
-            rows = [(ylo + n, range(PLANES)) for n in range(2)]
-            pair = chunk_values(own, edge, zall, zedge, None, yhi, rows, masks)
-            pair = [walled(values[:POPS], values[POPS], inside_halo) for values in pair]
-            for n, values in enumerate(pair):
-                row = FIRST + (YLO * yhi + ylo + n) * PITCH
-                for i in range(POPS):
-                    field[pl.ds(i * FIELD + row - 2, 2), :] = values[i][:2]
-                    field[pl.ds(i * FIELD + row + SPAN_X, 2), :] = values[i][2:]
+
+        def leave(ylo, values):
+            row = FIRST + (YLO * yhi + ylo) * PITCH
+            for i in range(POPS):
+                field[pl.ds(i * FIELD + row - 2, 2), :] = values[i][:2]
+                field[pl.ds(i * FIELD + row + SPAN_X, 2), :] = values[i][2:]
+
+        relay(None, yhi, inside_halo, leave)
         return carry
 
     lax.fori_loop(0, SPAN_Y // YLO, halves, 0)
@@ -694,9 +723,9 @@
 
     drift_y, spin, centre_y = drifts_of(columns, depth)
 
-    def leave(n):
-        part = pl.ds(n * 8, 8)
-        return pltpu.make_async_copy(result.at[:, part], out.at[:, part], sems.at[n])
+    def leave(chunk, half):
+        part = (slice(None), pl.ds(chunk * 8, 8), pl.ds(half * 8, 8))
+        return pltpu.make_async_copy(result.at[part], out.at[part], sems.at[chunk, half])
 
     def second_step(chunk, carry):
         for half in range(SPAN_Y // 8):
@@ -714,12 +743,13 @@
                 values = [turn[pl.ds(i * 8 * TURN + k, 8, stride=TURN), :] for i in range(POPS)]
                 for i in range(POPS):
                     result[i, 8 * chunk + k, 8 * half : 8 * half + 8, :] = values[i][:, :SPAN_Z]
-        leave(chunk).start()
+            leave(chunk, half).start()
         return carry
 
     lax.fori_loop(0, SPAN_X // 8, second_step, 0)
-    for n in range(SPAN_X // 8):
-        leave(n).wait()
+    for chunk in range(SPAN_X // 8):
+        for half in range(SPAN_Y // 8):
+            leave(chunk, half).wait()
 
 
 def rows_of(count):
@@ -790,12 +820,12 @@
     z_low = lax.ppermute(zsend_up, ("stream", "cz"), zup_pairs)
     z_high = lax.ppermute(zsend_down, ("stream", "cz"), zdown_pairs)
 
-    own = pl.pallas_call(
+    own, edge_own, flags = pl.pallas_call(
         pack_own,
-        out_shape=kept(LAYERS * BZD * BLOCK),
+        out_shape=(kept(LAYERS * BZD * BLOCK), kept(PLANES * 4 * FACE), kept(2 * FACE)),
         in_specs=[hbm, hbm, hbm, vmem],
-        out_specs=vmem,
-        scratch_shapes=[place_scratch]
+        out_specs=(vmem,) * 3,
+        scratch_shapes=[place_scratch, table_scratch]
         + mark_scratch
         + [
             VMEM((rows, POPS, EDGE**3), jnp.float32),
@@ -816,18 +846,16 @@
             kept(RIM_ROWS),
             kept(RIM_ROWS),
         ),
-        in_specs=[hbm] + [vmem] * 6,
+        in_specs=[vmem] * 8,
         out_specs=(vmem,) * 6,
         scratch_shapes=[
-            place_scratch,
             VMEM((RIM * GRID_X, LANE), jnp.float32),
             VMEM((RIM * GRID_X, LANE), jnp.float32),
-            pltpu.SemaphoreType.DMA,
         ],
-        input_output_aliases={6: 0},
+        input_output_aliases={7: 0},
         compiler_params=params(16),
         name="settle_rim",
-    )(places, from_low, from_high, zin, z_low, z_high, own)
+    )(from_low, from_high, zin, z_low, z_high, edge_own, flags, own)
     cy_up = [(i, i + 1) for i in range(columns - 1)]
     cy_down = [(i + 1, i) for i in range(columns - 1)]
     rim_low = lax.ppermute(rim_up, "cy", cy_up)
@@ -838,6 +866,7 @@
         out_shape=(kept(POPS * FIELD), kept(POPS * FIELD)),
         in_specs=[vmem] * 4,
         out_specs=(vmem,) * 2,
+        scratch_shapes=[VMEM((PLANES * YLO * 8, LANE), jnp.float32)],
         compiler_params=params(16),
         name="settle_all",
     )(own, edge, zall, zedge)
@@ -854,7 +883,7 @@
         scratch_shapes=[
             VMEM((POPS * 8 * TURN, LANE), jnp.float32),
             VMEM((POPS, SPAN_X, SPAN_Y, SPAN_Z), jnp.float32),
-            pltpu.SemaphoreType.DMA((SPAN_X // 8,)),
+            pltpu.SemaphoreType.DMA((SPAN_X // 8, SPAN_Y // 8)),
         ],
         input_output_aliases={2: 1, 3: 2},
         compiler_params=params(16),

time: 54.4 us -> 53.2 us (0.978)
  Pallas kernels: 30.4 us -> 26.2 us
  waiting for transfers between devices: 7.49 us -> 10.1 us
  starting transfers between devices: 15.9 us -> 16.5 us
    pallas_call x1, Pallas kernels: 11.9 us -> 8.7 us  [shards(): pl.pallas_call(functools.partial(settle_all, layers, columns, depth), out...]
    ppermute x1, waiting for transfers between devices: 0.5 us -> 3.7 us  [shards(): rim_high = lax.ppermute(rim_down, 'cy', cy_down)]
    pallas_call x1, Pallas kernels: 2.93 us -> 1.88 us  [shards(): pl.pallas_call(functools.partial(settle_rim, layers), out_shape=(kept(LAY...]
    ppermute x1, waiting for transfers between devices: 3.44 us -> 2.82 us  [shards(): z_low = lax.ppermute(zsend_up, ('stream', 'cz'), zup_pairs)]
  transfers between devices with their start and end apart: 7 -> 7, of which waited for: 4 -> 4; matrix products, arithmetic and copies ran while one was open for 0% -> 0% of each run, Pallas kernels for 37% -> 31%
where the time goes in v10:
time: 53.2 us; the launch traced here: 52.9 us
  Pallas kernels  26.2 us (49%)
  starting transfers between devices  16.5 us (31%)
  waiting for transfers between devices  10.1 us (19%)
    pallas_call x1, Pallas kernels, shards(): pl.pallas_call(functools.partial(settle_all, layers, columns, depth), out...  8.7 us
    ppermute x1, starting transfers between devices, shards(): from_low = lax.ppermute(send_up, 'stream', up)  4.98 us
    pallas_call x1, Pallas kernels, shards(): pl.pallas_call(pack_own, out_shape=(kept(LAYERS * BZD * BLOCK), kept(PLAN...  4.79 us
    pallas_call x1, Pallas kernels, shards(): pl.pallas_call(functools.partial(finish, layers, columns, depth), out_sha...  4.71 us
    ppermute x1, starting transfers between devices, shards(): z_low = lax.ppermute(zsend_up, ('stream', 'cz'), zup_pairs)  3.98 us
    ppermute x1, waiting for transfers between devices, shards(): rim_high = lax.ppermute(rim_down, 'cy', cy_down)  3.7 us
    ppermute x1, starting transfers between devices, shards(): rim_low = lax.ppermute(rim_up, 'cy', cy_up)  3.41 us
    pallas_call x1, Pallas kernels, shards(): pl.pallas_call(pack_stream, out_shape=(kept(SENT_ROWS), kept(SENT_ROWS)),...  3.09 us
  transfers between devices with their start and end apart: 7, of which 4 were waited for; matrix products, arithmetic and copies ran while one was open for 0% of the time, Pallas kernels for 31%

profile of v10, /device:TPU:0, one launch (start us, length us, event | category | flops | bytes accessed | tf_op | source)
XLA Modules:
  0.0 52.9 jit_solution(9813982691313899076)
XLA Ops:
  0.0 3.1 %pack_stream.1 = (f32[1496,128]{1,0:T(8,128)S(1)}, f32[1496,128]{1,0:T(8,128)S(1)}) custom-call(s32[3,12]{1,0:T(4,128)} %bitcast.1, s32[12,4096]{1,0:T(8,128)} %marks_in.5, f32[12,19,4096]{2,1,0:T(8,128)} %pops.5), custom_call_target="tpu_custom_call" | custom-call | tf_op jit(solution)/shard_map/pack_stream/pallas_call | solution.py:783
  3.1 5.0 %collective-permute-start = (f32[1496,128]{1,0:T(8,128)S(1)}, f32[1496,128]{1,0:T(8,128)S(1)}, u32[]{:S(2)}, u32[]{:S(2)}) collective-permute-start(f32[1496,128]{1,0:T(8,128)S(1)} %get-tuple-element.23), channel_id=1, source_target_pairs={{0,8},{8,16},{16,24},{1,9},{9,17},{17,25},{2,10},{10,18},{18,26},{... | collective-permute-start | bytes 2297864 | tf_op jit(solution)/shard_map/ppermute | solution.py:799
  8.1 1.3 %collective-permute-start.1 = (f32[1496,128]{1,0:T(8,128)S(1)}, f32[1496,128]{1,0:T(8,128)S(1)}, u32[]{:S(2)}, u32[]{:S(2)}) collective-permute-start(f32[1496,128]{1,0:T(8,128)S(1)} %get-tuple-element.24), channel_id=1, source_target_pairs={{8,0},{16,8},{24,16},{9,1},{17,9},{25,17},{10,2},{18,10},{26,18},{... | collective-permute-start | bytes 2297864 | tf_op jit(solution)/shard_map/ppermute | solution.py:800
  9.4 3.1 %pack_edge.1 = (f32[10240,128]{1,0:T(8,128)S(1)}, f32[392,128]{1,0:T(8,128)S(1)}, f32[108,128]{1,0:T(8,128)S(1)}, f32[108,128]{1,0:T(8,128)S(1)}) custom-call(s32[3,12]{1,0:T(4,128)} %bitcast.2, s32[12,4096]{1,0:T(8,128)} %marks_in.5, f32[12,19,4096]{2,1,0:T(8,128)} %pops.5), custom_call_target="tpu_custom_call" | custom-call | tf_op jit(solution)/shard_map/pack_edge/pallas_call | solution.py:802
  12.4 0.3 collective-permute-start.2
  12.7 4.0 %collective-permute-start.3 = (f32[108,128]{1,0:T(8,128)S(1)}, f32[108,128]{1,0:T(8,128)S(1)}, u32[]{:S(2)}, u32[]{:S(2)}) collective-permute-start(f32[108,128]{1,0:T(8,128)S(1)} %get-tuple-element.26), channel_id=1, source_target_pairs={{0,9},{1,8},{8,17},{9,16},{16,25},{17,24},{2,11},{3,10},{10,19},{1... | collective-permute-start | bytes 165896 | tf_op jit(solution)/shard_map/ppermute | solution.py:820
  16.7 1.3 %collective-permute-start.4 = (f32[108,128]{1,0:T(8,128)S(1)}, f32[108,128]{1,0:T(8,128)S(1)}, u32[]{:S(2)}, u32[]{:S(2)}) collective-permute-start(f32[108,128]{1,0:T(8,128)S(1)} %get-tuple-element.27), channel_id=1, source_target_pairs={{8,1},{9,0},{16,9},{17,8},{24,17},{25,16},{10,3},{11,2},{18,11},{1... | collective-permute-start | bytes 165896 | tf_op jit(solution)/shard_map/ppermute | solution.py:821
  18.0 4.8 %pack_own.1 = (f32[10240,128]{1,0:T(8,128)S(1)}, f32[640,128]{1,0:T(8,128)S(1)}, f32[16,128]{1,0:T(8,128)S(1)}) custom-call(s32[3,12]{1,0:T(4,128)} %bitcast.3, s32[12,4096]{1,0:T(8,128)} %marks_in.5, f32[12,19,4096]{2,1,0:T(8,128)} %pops.5, f32[10240,128]{1,0:T(8,128)S(1)} %get-tuple-element.28.own_in), custom_call_target="tpu_custom_call", output_to_operand_aliasing={{0}: (3, {})} | custom-call | tf_op jit(solution)/shard_map/pack_own/pallas_call | solution.py:823
  22.8 2.8 %collective-permute-done.3.zup = f32[108,128]{1,0:T(8,128)S(1)} collective-permute-done((f32[108,128]{1,0:T(8,128)S(1)}, f32[108,128]{1,0:T(8,128)S(1)}, u32[]{:S(2)}, u32[]{:S(2)}) %collective-permute-start.3) | collective-permute-done | bytes 55328 | tf_op jit(solution)/shard_map/ppermute | solution.py:820
  25.6 2.7 %collective-permute-done.4.zdown = f32[108,128]{1,0:T(8,128)S(1)} collective-permute-done((f32[108,128]{1,0:T(8,128)S(1)}, f32[108,128]{1,0:T(8,128)S(1)}, u32[]{:S(2)}, u32[]{:S(2)}) %collective-permute-start.4) | collective-permute-done | bytes 55328 | tf_op jit(solution)/shard_map/ppermute | solution.py:821
  28.3 0.0 collective-permute-done.2.zin
  28.3 0.0 collective-permute-done.up
  28.3 0.8 %collective-permute-done.1.down = f32[1496,128]{1,0:T(8,128)S(1)} collective-permute-done((f32[1496,128]{1,0:T(8,128)S(1)}, f32[1496,128]{1,0:T(8,128)S(1)}, u32[]{:S(2)}, u32[]{:S(2)}) %collective-permute-start.1) | collective-permute-done | bytes 765984 | tf_op jit(solution)/shard_map/ppermute | solution.py:800
  29.2 1.9 %settle_rim.1 = (f32[10240,128]{1,0:T(8,128)S(1)}, f32[640,128]{1,0:T(8,128)S(1)}, f32[384,128]{1,0:T(8,128)S(1)}, f32[24,128]{1,0:T(8,128)S(1)}, f32[508,128]{1,0:T(8,128)S(1)}, /*index=5*/f32[508,128]{1,0:T(8,128)S(1)}) custom-call(f32[1496,128]{1,0:T(8,128)S(1)} %collective-permute-done.up, ...), custom_call_target="tpu_custom_call", output_to_operand_aliasing={{0}: (7, {})} | custom-call | tf_op jit(solution)/shard_map/settle_rim/pallas_call | solution.py:839
  31.0 3.4 %collective-permute-start.5 = (f32[508,128]{1,0:T(8,128)S(1)}, f32[508,128]{1,0:T(8,128)S(1)}, u32[]{:S(2)}, u32[]{:S(2)}) collective-permute-start(f32[508,128]{1,0:T(8,128)S(1)} %get-tuple-element.32), channel_id=1, source_target_pairs={{0,2},{2,4},{4,6},{1,3},{3,5},{5,7},{8,10},{10,12},{12,14},{9,11},... | collective-permute-start | bytes 780296 | tf_op jit(solution)/shard_map/ppermute | solution.py:861
  34.5 1.3 %collective-permute-start.6 = (f32[508,128]{1,0:T(8,128)S(1)}, f32[508,128]{1,0:T(8,128)S(1)}, u32[]{:S(2)}, u32[]{:S(2)}) collective-permute-start(f32[508,128]{1,0:T(8,128)S(1)} %get-tuple-element.33), channel_id=1, source_target_pairs={{2,0},{4,2},{6,4},{3,1},{5,3},{7,5},{10,8},{12,10},{14,12},{11,9},... | collective-permute-start | bytes 780296 | tf_op jit(solution)/shard_map/ppermute | solution.py:862
  35.8 8.7 %settle_all.1 = (f32[15656,128]{1,0:T(8,128)S(1)}, f32[15656,128]{1,0:T(8,128)S(1)}) custom-call(f32[10240,128]{1,0:T(8,128)S(1)} %get-tuple-element.34.own, f32[640,128]{1,0:T(8,128)S(1)} %get-tuple-element.35.edge, f32[384,128]{1,0:T(8,128)S(1)} %get-tuple-element.36.zall, f32[24,128]{1,0:T(8,128)S(1)} %get-tuple-element.37.zedge), custom_call_target="tpu_custom_call" | custom-call | tf_op jit(solution)/shard_map/settle_all/pallas_call | solution.py:864
  44.5 0.0 collective-permute-done.5.rim_low
  44.5 3.7 %collective-permute-done.6.rim_high = f32[508,128]{1,0:T(8,128)S(1)} collective-permute-done((f32[508,128]{1,0:T(8,128)S(1)}, f32[508,128]{1,0:T(8,128)S(1)}, u32[]{:S(2)}, u32[]{:S(2)}) %collective-permute-start.6) | collective-permute-done | bytes 260128 | tf_op jit(solution)/shard_map/ppermute | solution.py:862
  48.2 4.7 %finish.1 = (f32[19,32,16,64]{3,2,1,0:T(8,128)}, f32[15656,128]{1,0:T(8,128)S(1)}, f32[15656,128]{1,0:T(8,128)S(1)}) custom-call(f32[508,128]{1,0:T(8,128)S(1)} %collective-permute-done.5.rim_low, f32[508,128]{1,0:T(8,128)S(1)} %collective-permute-done.6.rim_high, ...), custom_call_target="tpu_custom_call", output_to_operand_aliasing={{1}: (2, {}), {2}: (3, {})} | custom-call | tf_op jit(solution)/shard_map/finish/pallas_call | solution.py:874
Async XLA Ops:
  3.1 25.2 %collective-permute-start = (f32[1496,128]{1,0:T(8,128)S(1)}, f32[1496,128]{1,0:T(8,128)S(1)}, u32[]{:S(2)}, u32[]{:S(2)}) collective-permute-start(f32[1496,128]{1,0:T(8,128)S(1)} %get-tuple-element.23), channel_id=1, source_target_pairs={{0,8},{8,16},{16,24},{1,9},{9,17},{17,25},{2,10},{10,18},{18,26},{... | collective-permute-start | bytes 2297864 | tf_op jit(solution)/shard_map/ppermute | solution.py:799
  8.1 21.1 %collective-permute-start.1 = (f32[1496,128]{1,0:T(8,128)S(1)}, f32[1496,128]{1,0:T(8,128)S(1)}, u32[]{:S(2)}, u32[]{:S(2)}) collective-permute-start(f32[1496,128]{1,0:T(8,128)S(1)} %get-tuple-element.24), channel_id=1, source_target_pairs={{8,0},{16,8},{24,16},{9,1},{17,9},{25,17},{10,2},{18,10},{26,18},{... | collective-permute-start | bytes 2297864 | tf_op jit(solution)/shard_map/ppermute | solution.py:800
  12.4 15.9 %collective-permute-start.2 = (f32[392,128]{1,0:T(8,128)S(1)}, f32[392,128]{1,0:T(8,128)S(1)}, u32[]{:S(2)}, u32[]{:S(2)}) collective-permute-start(f32[392,128]{1,0:T(8,128)S(1)} %get-tuple-element.25), channel_id=1, source_target_pairs={{0,1},{1,0},{2,3},{3,2},{4,5},{5,4},{6,7},{7,6},{8,9},{9,8},{10,11... | collective-permute-start | bytes 602120 | tf_op jit(solution)/shard_map/ppermute | solution.py:817
  12.7 12.9 %collective-permute-start.3 = (f32[108,128]{1,0:T(8,128)S(1)}, f32[108,128]{1,0:T(8,128)S(1)}, u32[]{:S(2)}, u32[]{:S(2)}) collective-permute-start(f32[108,128]{1,0:T(8,128)S(1)} %get-tuple-element.26), channel_id=1, source_target_pairs={{0,9},{1,8},{8,17},{9,16},{16,25},{17,24},{2,11},{3,10},{10,19},{1... | collective-permute-start | bytes 165896 | tf_op jit(solution)/shard_map/ppermute | solution.py:820
  16.7 11.6 %collective-permute-start.4 = (f32[108,128]{1,0:T(8,128)S(1)}, f32[108,128]{1,0:T(8,128)S(1)}, u32[]{:S(2)}, u32[]{:S(2)}) collective-permute-start(f32[108,128]{1,0:T(8,128)S(1)} %get-tuple-element.27), channel_id=1, source_target_pairs={{8,1},{9,0},{16,9},{17,8},{24,17},{25,16},{10,3},{11,2},{18,11},{1... | collective-permute-start | bytes 165896 | tf_op jit(solution)/shard_map/ppermute | solution.py:821
  31.0 13.4 %collective-permute-start.5 = (f32[508,128]{1,0:T(8,128)S(1)}, f32[508,128]{1,0:T(8,128)S(1)}, u32[]{:S(2)}, u32[]{:S(2)}) collective-permute-start(f32[508,128]{1,0:T(8,128)S(1)} %get-tuple-element.32), channel_id=1, source_target_pairs={{0,2},{2,4},{4,6},{1,3},{3,5},{5,7},{8,10},{10,12},{12,14},{9,11},... | collective-permute-start | bytes 780296 | tf_op jit(solution)/shard_map/ppermute | solution.py:861
  34.5 13.7 %collective-permute-start.6 = (f32[508,128]{1,0:T(8,128)S(1)}, f32[508,128]{1,0:T(8,128)S(1)}, u32[]{:S(2)}, u32[]{:S(2)}) collective-permute-start(f32[508,128]{1,0:T(8,128)S(1)} %get-tuple-element.33), channel_id=1, source_target_pairs={{2,0},{4,2},{6,4},{3,1},{5,3},{7,5},{10,8},{12,10},{14,12},{11,9},... | collective-permute-start | bytes 780296 | tf_op jit(solution)/shard_map/ppermute | solution.py:862

commit v11 on v10

--- a/solution.py
+++ b/solution.py
@@ -66,11 +66,15 @@
 EXT_Z = SPAN_Z + 2
 RIM_UP = tuple(i for i in range(POPS) if VELOCITIES[i][1] == 1)
 RIM_DOWN = tuple(i for i in range(POPS) if VELOCITIES[i][1] == -1)
-RIM = PLANES + len(RIM_UP) + 1
+TOWARD = len(RIM_UP)
+SLAB_PLANES = PLANES + TOWARD + 1
+STREAMED = POPS - TOWARD
+RIM = STREAMED + 1 + TOWARD + 1
+KEPT = POPS + TOWARD
 AHEAD = tuple(i for i in range(POPS) if VELOCITIES[i][0] == 1)
 BACK = tuple(i for i in range(POPS) if VELOCITIES[i][0] == -1)
 FACE = 2 * BZD
-SENT_META = SENT_SLABS + RIM * FACE
+SENT_META = SENT_SLABS + SLAB_PLANES * FACE
 SENT_ROWS = SENT_META + 8
 RIM_BLOCKS = -(-RIM * EXT_Z // LANE)
 RIM_ROWS = RIM_BLOCKS * EXT_X + 4
@@ -165,27 +169,20 @@
     return parts[0]
 
 
-def streamed(pull, own, drift_y, drift_z):
-    push = pushes(total_of(own), drift_y, drift_z)
-    out = [own[0]]
-    for i in range(1, POPS):
+def streamed(pull, own, density, drift_y, drift_z, wanted=range(POPS)):
+    push = pushes(density, drift_y, drift_z)
+    out = {}
+    for i in wanted:
+        if i == 0:
+            out[i] = own[0]
+            continue
         pulled = pull(i)
         bounced = own[OPPOSITE[i]]
         blocked = pulled < WALL_BELOW
         if push[i] is not None:
             bounced = jnp.where(pulled < OUT_BELOW, bounced, bounced + push[i])
-        out.append(jnp.where(blocked, bounced, pulled))
+        out[i] = jnp.where(blocked, bounced, pulled)
     return out
-
-
-def ahead(items, take, leave, depth):
-    waiting = []
-    for n in items:
-        waiting.append((n, take(n)))
-        if len(waiting) > depth:
-            leave(*waiting.pop(0))
-    for pair in waiting:
-        leave(*pair)
 
 
 def place():
@@ -315,7 +312,7 @@
                 marks_at = POPS
             else:
                 pairs = [(PLANES + n, i) for n, i in enumerate(AHEAD if side == 0 else BACK)]
-                marks_at = RIM - 1
+                marks_at = SLAB_PLANES - 1
             for plane, i in pairs:
                 out[pl.ds(SENT_SLABS + plane * FACE, FACE), :] = jnp.where(mark, old[i], post[i])
             marks_of = strip[pl.ds(POPS * 2 * FACE + x * FACE, FACE), :]
@@ -493,9 +490,9 @@
     return low | high
 
 
-def settle_rim(layers, up, down, zin, zup, zdown, edge_own, flags, own_in, own, edge, zall, zedge, rim_up, rim_down, post_up, post_down):
+def settle_rim(layers, columns, depth, up, down, zin, zup, zdown, edge_own, flags, own_in, own, edge, zall, zedge, rim_up, rim_down, post_up, post_down):
     del own_in
-    layer, _, column_z = place()
+    layer, column_y, column_z = place()
     codes = []
     for arrived in (up, down):
         first = layer == 0 if arrived is up else layer == layers - 1
@@ -544,24 +541,50 @@
     for target, rows, value in moves:
         target[rows, :] = value
     masks = Lanes(column_z)
+    inside_box = inside_lanes(8, column_z)
+    inside_halo = inside_lanes(4, column_z) & halo_x_inside(layer, layers)
+    sides = ((0, 1, RIM_DOWN, RIM_UP, post_down), (SPAN_Y - 1, SPAN_Y - 2, RIM_UP, RIM_DOWN, post_up))
     for chunk in (0, 1, 2, 3, None):
-        for near, far, rim, target in ((0, 1, RIM_DOWN, post_down), (SPAN_Y - 1, SPAN_Y - 2, RIM_UP, post_up)):
+        inside = inside_halo if chunk is None else inside_box
+        for near, far, rim, _, target in sides:
             rows = ((near % YLO, range(PLANES)), (far % YLO, rim + (POPS,)))
             first, second = chunk_values(own, edge, zall, zedge, chunk, near // YLO, rows, masks)
-            for plane, value in enumerate(first + second):
+            planes = walled(first[:POPS], first[POPS], inside)
+            planes += walled(second[:TOWARD], second[TOWARD], inside)
+            sent = [first[i] for i in rim] + [first[POPS]]
+            spots = list(range(KEPT)) + [KEPT + STREAMED + 1 + n for n in range(len(sent))]
+            for plane, value in zip(spots, planes + sent):
                 row = plane * GRID_X
                 if chunk is None:
                     target[pl.ds(row, 2), :] = value[:2]
                     target[pl.ds(row + EXT_X - 2, 2), :] = value[2:]
                 else:
                     target[pl.ds(row + 2 + 8 * chunk, 8), :] = value
+    drift_y, spin, centre_y = drifts_of(columns, depth)
+    for near, _, rim, away, target in sides:
+        drift_z = spin * ((column_y * SPAN_Y + near).astype(jnp.float32) - centre_y)
+        wanted = [i for i in range(POPS) if i not in away]
+        plane_of = {i: POPS + rim.index(i) if i in rim else i for i in wanted}
+        for chunk in range(5):
+            first = 1 + 8 * chunk
+
+            def pull(i):
+                step_x, _, step_z = VELOCITIES[i]
+                return turned(target[pl.ds(plane_of[i] * GRID_X + first - step_x, 8), :], step_z)
+
+            old = [target[pl.ds(i * GRID_X + first, 8), :] for i in range(POPS)]
+            rho = total_of(old)
+            values = streamed(pull, old, rho, drift_y, drift_z, wanted)
+            size = min(8, EXT_X - 1 - first)
+            for n, value in enumerate([values[i] for i in wanted] + [rho]):
+                target[pl.ds((KEPT + n) * GRID_X + first, size), :] = value[:size]
     lane = lanes()
     for source, target in ((post_up, rim_up), (post_down, rim_down)):
         for chunk in range(5):
             size = min(8, EXT_X - 8 * chunk)
             values = []
             for plane in range(RIM):
-                value = source[pl.ds(plane * GRID_X + 8 * chunk, 8), :]
+                value = source[pl.ds((KEPT + plane) * GRID_X + 8 * chunk, 8), :]
                 values.append(pltpu.roll(value, (plane * EXT_Z + 2 * column_z) & (LANE - 1), 1))
             totals = []
             for block in range(RIM_BLOCKS):
@@ -598,7 +621,7 @@
 
     def tile(base, drift_z):
         old = [field[pl.ds(i * FIELD + base, 8), :] for i in range(POPS)]
-        values = streamed(pull_from(field, base), old, drift_y, drift_z)
+        values = streamed(pull_from(field, base), old, total_of(old), drift_y, drift_z)
         post, _ = collide(values)
         wall = old[0] < WALL_BELOW
         for i in range(POPS):
@@ -684,42 +707,55 @@
     first_step(columns, depth, field, later, 1, SPAN_Y - 1, False)
 
 
-def finish(layers, columns, depth, rim_low, rim_high, field_in, later_in, out, field, later, turn, result, sems):
+def finish(layers, columns, depth, rim_low, rim_high, field_in, later_in, out, field, later, low, high, turn, result, sems):
     del field_in, later_in
     layer, column_y, column_z = place()
     flat = (lanes() + 2 * column_z) & (LANE - 1)
     sides = (
-        (rim_low, -1, -2, RIM_UP, column_y > 0),
-        (rim_high, SPAN_Y, SPAN_Y + 1, RIM_DOWN, column_y < columns - 1),
+        (rim_low, low, -1, RIM_UP, RIM_DOWN, column_y > 0),
+        (rim_high, high, SPAN_Y, RIM_DOWN, RIM_UP, column_y < columns - 1),
     )
     sublane = lax.broadcasted_iota(jnp.int32, (8, LANE), 0)
-    for source, near, far, rim, there in sides:
+    for source, ready, y, rim, _, there in sides:
         for chunk in range(5):
             size = min(8, EXT_X - 8 * chunk)
             blocks = [source[pl.ds(block * EXT_X + 8 * chunk, 8), :] for block in range(RIM_BLOCKS)]
-
-            def plane_of(plane, blocks=blocks):
+            values = []
+            for plane in range(RIM):
                 block, begin = divmod(plane * EXT_Z, LANE)
                 shift = (2 * LANE - begin - 2 * column_z) & (LANE - 1)
                 value = pltpu.roll(blocks[block], shift, 1)
                 if begin + EXT_Z > LANE:
                     value = jnp.where(flat < LANE - begin, value, pltpu.roll(blocks[block + 1], shift, 1))
-                return value
-
+                values.append(value)
             inside = (flat < EXT_Z) & there
             if chunk == 0:
                 inside = inside & ((sublane >= 2) | (layer > 0))
             if chunk == 4:
                 inside = inside & ((sublane < 2) | (layer < layers - 1))
-            for first, count, y, order in ((0, POPS, near, range(POPS)), (PLANES, len(rim), far, rim)):
-                mark = plane_of(POPS if y == near else RIM - 1)
-                values = walled([plane_of(first + n) for n in range(count)], mark, inside)
-                for i, value in zip(order, values):
-                    row = i * FIELD + FIRST + y * PITCH - 2 + 8 * chunk
-                    field[pl.ds(row, size), :] = value[:size]
-
-    first_step(columns, depth, field, later, -1, 1, True)
-    first_step(columns, depth, field, later, SPAN_Y - 1, SPAN_Y + 1, True)
+            for n in range(STREAMED + 1):
+                ready[pl.ds(n * GRID_X + 8 * chunk, 8), :] = values[n]
+            for i, value in zip(rim, walled(values[STREAMED + 1 : RIM - 1], values[RIM - 1], inside)):
+                field[pl.ds(i * FIELD + FIRST + y * PITCH - 2 + 8 * chunk, size), :] = value[:size]
+
+    first_step(columns, depth, field, later, 0, 1, True)
+    first_step(columns, depth, field, later, SPAN_Y - 1, SPAN_Y, True)
+    drift_y, spin, centre_y = drifts_of(columns, depth)
+    for _, ready, y, rim, away, _ in sides:
+        drift_z = spin * ((column_y * SPAN_Y + y).astype(jnp.float32) - centre_y)
+        for chunk in range(5):
+            first = 1 + 8 * chunk
+            base = FIRST + y * PITCH - 2 + first
+            old = {i: field[pl.ds(i * FIELD + base, 8), :] for i in rim}
+            rho = ready[pl.ds(STREAMED * GRID_X + first, 8), :]
+            values = streamed(pull_from(field, base), old, rho, drift_y, drift_z, away)
+            for n, i in enumerate([i for i in range(POPS) if i not in away]):
+                values[i] = ready[pl.ds(n * GRID_X + first, 8), :]
+            post, _ = collide(values)
+            wall = old[rim[0]] < WALL_BELOW
+            size = min(8, EXT_X - 1 - first)
+            for i in rim:
+                later[pl.ds(i * FIELD + base, size), :] = jnp.where(wall, old[i], post[i])[:size]
 
     drift_y, spin, centre_y = drifts_of(columns, depth)
 
@@ -734,7 +770,7 @@
                 base = pl.multiple_of(FIRST + y * PITCH + 8 * chunk, 8)
                 drift_z = spin * ((column_y * SPAN_Y + y).astype(jnp.float32) - centre_y)
                 old = [later[pl.ds(i * FIELD + base, 8), :] for i in range(POPS)]
-                values = streamed(pull_from(later, base), old, drift_y, drift_z)
+                values = streamed(pull_from(later, base), old, total_of(old), drift_y, drift_z)
                 wall = old[0] < WALL_BELOW
                 for i in range(POPS):
                     value = jnp.where(wall, old[i] * (1.0 / ROTOR), values[i])
@@ -837,7 +873,7 @@
     )(places, solid_cells, populations, own)
 
     own, edge, zall, zedge, rim_up, rim_down = pl.pallas_call(
-        functools.partial(settle_rim, layers),
+        functools.partial(settle_rim, layers, columns, depth),
         out_shape=(
             kept(LAYERS * BZD * BLOCK),
             kept(PLANES * 4 * FACE),
@@ -849,8 +885,8 @@
         in_specs=[vmem] * 8,
         out_specs=(vmem,) * 6,
         scratch_shapes=[
-            VMEM((RIM * GRID_X, LANE), jnp.float32),
-            VMEM((RIM * GRID_X, LANE), jnp.float32),
+            VMEM(((KEPT + RIM) * GRID_X, LANE), jnp.float32),
+            VMEM(((KEPT + RIM) * GRID_X, LANE), jnp.float32),
         ],
         input_output_aliases={7: 0},
         compiler_params=params(16),
@@ -881,6 +917,8 @@
         in_specs=[vmem] * 4,
         out_specs=(hbm, vmem, vmem),
         scratch_shapes=[
+            VMEM(((STREAMED + 1) * GRID_X, LANE), jnp.float32),
+            VMEM(((STREAMED + 1) * GRID_X, LANE), jnp.float32),
             VMEM((POPS * 8 * TURN, LANE), jnp.float32),
             VMEM((POPS, SPAN_X, SPAN_Y, SPAN_Z), jnp.float32),
             pltpu.SemaphoreType.DMA((SPAN_X // 8, SPAN_Y // 8)),

time: 53.2 us -> 50.2 us (0.944)
  waiting for transfers between devices: 10.1 us -> 7.82 us
    ppermute x1, waiting for transfers between devices: 3.7 us -> 1.24 us  [shards(): rim_high = lax.ppermute(rim_down, 'cy', cy_down)]
    pallas_call x1, Pallas kernels: 3.05 us -> 3.69 us  [shards(): pl.pallas_call(pack_edge, out_shape=(kept(LAYERS * BZD * BLOCK), kept(ZME...]
    pallas_call x1, Pallas kernels: 4.71 us -> 4.12 us  [shards(): pl.pallas_call(functools.partial(finish, layers, columns, depth), out_sha...]
  transfers between devices with their start and end apart: 7 -> 7, of which waited for: 4 -> 4; matrix products, arithmetic and copies ran while one was open for 0% -> 0% of each run, Pallas kernels for 31% -> 34%
where the time goes in v11:
time: 50.2 us; the launch traced here: 49.9 us
  Pallas kernels  26 us (52%)
  starting transfers between devices  16 us (32%)
  waiting for transfers between devices  7.82 us (16%)
    pallas_call x1, Pallas kernels, shards(): pl.pallas_call(functools.partial(settle_all, layers, columns, depth), out...  8.7 us
    ppermute x1, starting transfers between devices, shards(): from_low = lax.ppermute(send_up, 'stream', up)  4.98 us
    pallas_call x1, Pallas kernels, shards(): pl.pallas_call(pack_own, out_shape=(kept(LAYERS * BZD * BLOCK), kept(PLAN...  4.48 us
    pallas_call x1, Pallas kernels, shards(): pl.pallas_call(functools.partial(finish, layers, columns, depth), out_sha...  4.12 us
    pallas_call x1, Pallas kernels, shards(): pl.pallas_call(pack_edge, out_shape=(kept(LAYERS * BZD * BLOCK), kept(ZME...  3.69 us
    ppermute x1, starting transfers between devices, shards(): z_low = lax.ppermute(zsend_up, ('stream', 'cz'), zup_pairs)  3.63 us
    ppermute x1, starting transfers between devices, shards(): rim_low = lax.ppermute(rim_up, 'cy', cy_up)  3.41 us
    pallas_call x1, Pallas kernels, shards(): pl.pallas_call(pack_stream, out_shape=(kept(SENT_ROWS), kept(SENT_ROWS)),...  3.09 us
  transfers between devices with their start and end apart: 7, of which 4 were waited for; matrix products, arithmetic and copies ran while one was open for 0% of the time, Pallas kernels for 34%

profile of v11, /device:TPU:0, one launch (start us, length us, event | category | flops | bytes accessed | tf_op | source)
XLA Modules:
  0.0 49.9 jit_solution(6082642255731309279)
XLA Ops:
  0.0 3.1 %pack_stream.1 = (f32[1496,128]{1,0:T(8,128)S(1)}, f32[1496,128]{1,0:T(8,128)S(1)}) custom-call(s32[3,12]{1,0:T(4,128)} %bitcast.1, s32[12,4096]{1,0:T(8,128)} %marks_in.5, f32[12,19,4096]{2,1,0:T(8,128)} %pops.5), custom_call_target="tpu_custom_call" | custom-call | tf_op jit(solution)/shard_map/pack_stream/pallas_call | solution.py:819
  3.1 5.0 %collective-permute-start = (f32[1496,128]{1,0:T(8,128)S(1)}, f32[1496,128]{1,0:T(8,128)S(1)}, u32[]{:S(2)}, u32[]{:S(2)}) collective-permute-start(f32[1496,128]{1,0:T(8,128)S(1)} %get-tuple-element.23), channel_id=1, source_target_pairs={{0,8},{8,16},{16,24},{1,9},{9,17},{17,25},{2,10},{10,18},{18,26},{... | collective-permute-start | bytes 2297864 | tf_op jit(solution)/shard_map/ppermute | solution.py:835
  8.1 1.3 %collective-permute-start.1 = (f32[1496,128]{1,0:T(8,128)S(1)}, f32[1496,128]{1,0:T(8,128)S(1)}, u32[]{:S(2)}, u32[]{:S(2)}) collective-permute-start(f32[1496,128]{1,0:T(8,128)S(1)} %get-tuple-element.24), channel_id=1, source_target_pairs={{8,0},{16,8},{24,16},{9,1},{17,9},{25,17},{10,2},{18,10},{26,18},{... | collective-permute-start | bytes 2297864 | tf_op jit(solution)/shard_map/ppermute | solution.py:836
  9.4 3.7 %pack_edge.1 = (f32[10240,128]{1,0:T(8,128)S(1)}, f32[392,128]{1,0:T(8,128)S(1)}, f32[108,128]{1,0:T(8,128)S(1)}, f32[108,128]{1,0:T(8,128)S(1)}) custom-call(s32[3,12]{1,0:T(4,128)} %bitcast.2, s32[12,4096]{1,0:T(8,128)} %marks_in.5, f32[12,19,4096]{2,1,0:T(8,128)} %pops.5), custom_call_target="tpu_custom_call" | custom-call | tf_op jit(solution)/shard_map/pack_edge/pallas_call | solution.py:838
  13.1 0.1 collective-permute-start.2
  13.2 3.6 %collective-permute-start.3 = (f32[108,128]{1,0:T(8,128)S(1)}, f32[108,128]{1,0:T(8,128)S(1)}, u32[]{:S(2)}, u32[]{:S(2)}) collective-permute-start(f32[108,128]{1,0:T(8,128)S(1)} %get-tuple-element.26), channel_id=1, source_target_pairs={{0,9},{1,8},{8,17},{9,16},{16,25},{17,24},{2,11},{3,10},{10,19},{1... | collective-permute-start | bytes 165896 | tf_op jit(solution)/shard_map/ppermute | solution.py:856
  16.8 1.3 %collective-permute-start.4 = (f32[108,128]{1,0:T(8,128)S(1)}, f32[108,128]{1,0:T(8,128)S(1)}, u32[]{:S(2)}, u32[]{:S(2)}) collective-permute-start(f32[108,128]{1,0:T(8,128)S(1)} %get-tuple-element.27), channel_id=1, source_target_pairs={{8,1},{9,0},{16,9},{17,8},{24,17},{25,16},{10,3},{11,2},{18,11},{1... | collective-permute-start | bytes 165896 | tf_op jit(solution)/shard_map/ppermute | solution.py:857
  18.1 4.5 %pack_own.1 = (f32[10240,128]{1,0:T(8,128)S(1)}, f32[640,128]{1,0:T(8,128)S(1)}, f32[16,128]{1,0:T(8,128)S(1)}) custom-call(s32[3,12]{1,0:T(4,128)} %bitcast.3, s32[12,4096]{1,0:T(8,128)} %marks_in.5, f32[12,19,4096]{2,1,0:T(8,128)} %pops.5, f32[10240,128]{1,0:T(8,128)S(1)} %get-tuple-element.28.own_in), custom_call_target="tpu_custom_call", output_to_operand_aliasing={{0}: (3, {})} | custom-call | tf_op jit(solution)/shard_map/pack_own/pallas_call | solution.py:859
  22.6 3.0 %collective-permute-done.3.zup = f32[108,128]{1,0:T(8,128)S(1)} collective-permute-done((f32[108,128]{1,0:T(8,128)S(1)}, f32[108,128]{1,0:T(8,128)S(1)}, u32[]{:S(2)}, u32[]{:S(2)}) %collective-permute-start.3) | collective-permute-done | bytes 55328 | tf_op jit(solution)/shard_map/ppermute | solution.py:856
  25.6 2.7 %collective-permute-done.4.zdown = f32[108,128]{1,0:T(8,128)S(1)} collective-permute-done((f32[108,128]{1,0:T(8,128)S(1)}, f32[108,128]{1,0:T(8,128)S(1)}, u32[]{:S(2)}, u32[]{:S(2)}) %collective-permute-start.4) | collective-permute-done | bytes 55328 | tf_op jit(solution)/shard_map/ppermute | solution.py:857
  28.3 0.0 collective-permute-done.2.zin
  28.3 0.0 collective-permute-done.up
  28.3 0.8 %collective-permute-done.1.down = f32[1496,128]{1,0:T(8,128)S(1)} collective-permute-done((f32[1496,128]{1,0:T(8,128)S(1)}, f32[1496,128]{1,0:T(8,128)S(1)}, u32[]{:S(2)}, u32[]{:S(2)}) %collective-permute-start.1) | collective-permute-done | bytes 765984 | tf_op jit(solution)/shard_map/ppermute | solution.py:836
  29.2 2.0 %settle_rim.1 = (f32[10240,128]{1,0:T(8,128)S(1)}, f32[640,128]{1,0:T(8,128)S(1)}, f32[384,128]{1,0:T(8,128)S(1)}, f32[24,128]{1,0:T(8,128)S(1)}, f32[400,128]{1,0:T(8,128)S(1)}, /*index=5*/f32[400,128]{1,0:T(8,128)S(1)}) custom-call(f32[1496,128]{1,0:T(8,128)S(1)} %collective-permute-done.up, ...), custom_call_target="tpu_custom_call", output_to_operand_aliasing={{0}: (7, {})} | custom-call | tf_op jit(solution)/shard_map/settle_rim/pallas_call | solution.py:875
  31.1 3.4 %collective-permute-start.5 = (f32[400,128]{1,0:T(8,128)S(1)}, f32[400,128]{1,0:T(8,128)S(1)}, u32[]{:S(2)}, u32[]{:S(2)}) collective-permute-start(f32[400,128]{1,0:T(8,128)S(1)} %get-tuple-element.32), channel_id=1, source_target_pairs={{0,2},{2,4},{4,6},{1,3},{3,5},{5,7},{8,10},{10,12},{12,14},{9,11},... | collective-permute-start | bytes 614408 | tf_op jit(solution)/shard_map/ppermute | solution.py:897
  34.5 1.3 %collective-permute-start.6 = (f32[400,128]{1,0:T(8,128)S(1)}, f32[400,128]{1,0:T(8,128)S(1)}, u32[]{:S(2)}, u32[]{:S(2)}) collective-permute-start(f32[400,128]{1,0:T(8,128)S(1)} %get-tuple-element.33), channel_id=1, source_target_pairs={{2,0},{4,2},{6,4},{3,1},{5,3},{7,5},{10,8},{12,10},{14,12},{11,9},... | collective-permute-start | bytes 614408 | tf_op jit(solution)/shard_map/ppermute | solution.py:898
  35.8 8.7 %settle_all.1 = (f32[15656,128]{1,0:T(8,128)S(1)}, f32[15656,128]{1,0:T(8,128)S(1)}) custom-call(f32[10240,128]{1,0:T(8,128)S(1)} %get-tuple-element.34.own, f32[640,128]{1,0:T(8,128)S(1)} %get-tuple-element.35.edge, f32[384,128]{1,0:T(8,128)S(1)} %get-tuple-element.36.zall, f32[24,128]{1,0:T(8,128)S(1)} %get-tuple-element.37.zedge), custom_call_target="tpu_custom_call" | custom-call | tf_op jit(solution)/shard_map/settle_all/pallas_call | solution.py:900
  44.6 0.0 collective-permute-done.5.rim_low
  44.6 1.2 %collective-permute-done.6.rim_high = f32[400,128]{1,0:T(8,128)S(1)} collective-permute-done((f32[400,128]{1,0:T(8,128)S(1)}, f32[400,128]{1,0:T(8,128)S(1)}, u32[]{:S(2)}, u32[]{:S(2)}) %collective-permute-start.6) | collective-permute-done | bytes 204832 | tf_op jit(solution)/shard_map/ppermute | solution.py:898
  45.8 4.1 %finish.1 = (f32[19,32,16,64]{3,2,1,0:T(8,128)}, f32[15656,128]{1,0:T(8,128)S(1)}, f32[15656,128]{1,0:T(8,128)S(1)}) custom-call(f32[400,128]{1,0:T(8,128)S(1)} %collective-permute-done.5.rim_low, f32[400,128]{1,0:T(8,128)S(1)} %collective-permute-done.6.rim_high, ...), custom_call_target="tpu_custom_call", output_to_operand_aliasing={{1}: (2, {}), {2}: (3, {})} | custom-call | tf_op jit(solution)/shard_map/finish/pallas_call | solution.py:910
Async XLA Ops:
  3.1 25.2 %collective-permute-start = (f32[1496,128]{1,0:T(8,128)S(1)}, f32[1496,128]{1,0:T(8,128)S(1)}, u32[]{:S(2)}, u32[]{:S(2)}) collective-permute-start(f32[1496,128]{1,0:T(8,128)S(1)} %get-tuple-element.23), channel_id=1, source_target_pairs={{0,8},{8,16},{16,24},{1,9},{9,17},{17,25},{2,10},{10,18},{18,26},{... | collective-permute-start | bytes 2297864 | tf_op jit(solution)/shard_map/ppermute | solution.py:835
  8.1 21.1 %collective-permute-start.1 = (f32[1496,128]{1,0:T(8,128)S(1)}, f32[1496,128]{1,0:T(8,128)S(1)}, u32[]{:S(2)}, u32[]{:S(2)}) collective-permute-start(f32[1496,128]{1,0:T(8,128)S(1)} %get-tuple-element.24), channel_id=1, source_target_pairs={{8,0},{16,8},{24,16},{9,1},{17,9},{25,17},{10,2},{18,10},{26,18},{... | collective-permute-start | bytes 2297864 | tf_op jit(solution)/shard_map/ppermute | solution.py:836
  13.1 15.2 %collective-permute-start.2 = (f32[392,128]{1,0:T(8,128)S(1)}, f32[392,128]{1,0:T(8,128)S(1)}, u32[]{:S(2)}, u32[]{:S(2)}) collective-permute-start(f32[392,128]{1,0:T(8,128)S(1)} %get-tuple-element.25), channel_id=1, source_target_pairs={{0,1},{1,0},{2,3},{3,2},{4,5},{5,4},{6,7},{7,6},{8,9},{9,8},{10,11... | collective-permute-start | bytes 602120 | tf_op jit(solution)/shard_map/ppermute | solution.py:853
  13.2 12.5 %collective-permute-start.3 = (f32[108,128]{1,0:T(8,128)S(1)}, f32[108,128]{1,0:T(8,128)S(1)}, u32[]{:S(2)}, u32[]{:S(2)}) collective-permute-start(f32[108,128]{1,0:T(8,128)S(1)} %get-tuple-element.26), channel_id=1, source_target_pairs={{0,9},{1,8},{8,17},{9,16},{16,25},{17,24},{2,11},{3,10},{10,19},{1... | collective-permute-start | bytes 165896 | tf_op jit(solution)/shard_map/ppermute | solution.py:856
  16.8 11.5 %collective-permute-start.4 = (f32[108,128]{1,0:T(8,128)S(1)}, f32[108,128]{1,0:T(8,128)S(1)}, u32[]{:S(2)}, u32[]{:S(2)}) collective-permute-start(f32[108,128]{1,0:T(8,128)S(1)} %get-tuple-element.27), channel_id=1, source_target_pairs={{8,1},{9,0},{16,9},{17,8},{24,17},{25,16},{10,3},{11,2},{18,11},{1... | collective-permute-start | bytes 165896 | tf_op jit(solution)/shard_map/ppermute | solution.py:857
  31.1 13.4 %collective-permute-start.5 = (f32[400,128]{1,0:T(8,128)S(1)}, f32[400,128]{1,0:T(8,128)S(1)}, u32[]{:S(2)}, u32[]{:S(2)}) collective-permute-start(f32[400,128]{1,0:T(8,128)S(1)} %get-tuple-element.32), channel_id=1, source_target_pairs={{0,2},{2,4},{4,6},{1,3},{3,5},{5,7},{8,10},{10,12},{12,14},{9,11},... | collective-permute-start | bytes 614408 | tf_op jit(solution)/shard_map/ppermute | solution.py:897
  34.5 11.3 %collective-permute-start.6 = (f32[400,128]{1,0:T(8,128)S(1)}, f32[400,128]{1,0:T(8,128)S(1)}, u32[]{:S(2)}, u32[]{:S(2)}) collective-permute-start(f32[400,128]{1,0:T(8,128)S(1)} %get-tuple-element.33), channel_id=1, source_target_pairs={{2,0},{4,2},{6,4},{3,1},{5,3},{7,5},{10,8},{12,10},{14,12},{11,9},... | collective-permute-start | bytes 614408 | tf_op jit(solution)/shard_map/ppermute | solution.py:898

commit v12 on v11

--- a/solution.py
+++ b/solution.py
@@ -46,6 +46,8 @@
 BLOCK = PLANES * TILES
 YLO = LANE // EDGE
 SLAB = 4
+ODD = TILES + 1
+STRIP = 2 * 2 * BZD + 1
 GROUPS = ((0, 8), (8, 8), (16, 3))
 SENT_SLABS = MOVE_CAP * BLOCK
 LAYERS = BXD + 2
@@ -212,36 +214,28 @@
         for begin in range(0, TILES, 8):
             values = [marks[first : first + size, t * LANE : (t + 1) * LANE] for t in range(begin, begin + 8)]
             for k, value in enumerate(values):
-                dense[pl.ds(first * TILES + begin + k, size, stride=TILES), :] = value.astype(jnp.float32)
-
-
-def collide_block(ref, base):
-    for first in range(0, TILES // 8, 2):
-        moves = []
-        for part in (first, first + 1):
-            old = [ref[pl.ds(base + i * TILES + 8 * part, 8), :] for i in range(POPS)]
-            mark = ref[pl.ds(base + POPS * TILES + 8 * part, 8), :] > 0.5
-            post, _ = collide(old)
-            for i in range(POPS):
-                moves.append((base + i * TILES + 8 * part, jnp.where(mark, old[i], post[i])))
-        for row, value in moves:
-            ref[pl.ds(row, 8), :] = value
-
-
-def pack_block(out, base, stage, dense, row):
-    out[pl.ds(base + POPS * TILES, TILES), :] = dense[pl.ds(pl.multiple_of(row * TILES, 8), TILES), :]
+                dense[pl.ds(first * ODD + begin + k, size, stride=ODD), :] = value.astype(jnp.float32)
+
+
+def pack_block(out, base, stage, dense, row, raw):
     for first in range(0, TILES, 4):
         moves = []
         for tile in range(first, first + 4):
             for group, size in GROUPS:
                 value = stage[group : group + size, tile * LANE : (tile + 1) * LANE]
-                moves.append((pl.ds(base + group * TILES + tile, size, stride=TILES), value))
+                moves.append((pl.ds(group * ODD + tile, size, stride=ODD), value))
         for target, value in moves:
-            out[target, :] = value
-    collide_block(out, base)
-
-
-def pack_stream(places, marks_in, pops, up, down, pos, table, marks, dense, blocks, slabs, strip, sems):
+            raw[target, :] = value
+    for part in range(TILES // 8):
+        old = [raw[pl.ds(i * ODD + 8 * part, 8), :] for i in range(POPS)]
+        mark = dense[pl.ds(row * ODD + 8 * part, 8), :]
+        post, _ = collide(old)
+        for i in range(POPS):
+            out[pl.ds(base + i * TILES + 8 * part, 8), :] = jnp.where(mark > 0.5, old[i], post[i])
+        out[pl.ds(base + POPS * TILES + 8 * part, 8), :] = mark
+
+
+def pack_stream(places, marks_in, pops, up, down, pos, table, marks, dense, raw, blocks, slabs, strip, sems):
     mark_copy = pltpu.make_async_copy(marks_in, marks, sems.at[0])
     mark_copy.start()
     place_copy = pltpu.make_async_copy(places, pos, sems.at[1])
@@ -284,11 +278,11 @@
                 out[pl.ds(SENT_META + 2 * j + k, 1), :] = value
             n = side * MOVE_CAP + j
             copies[n].wait()
-            pack_block(out, j * BLOCK, blocks.at[n], dense, row)
+            pack_block(out, j * BLOCK, blocks.at[n], dense, row, raw)
     for side, out in enumerate((up, down)):
         for bz in range(BZD):
             n = side * BZD + bz
-            first = slab_rows[n] * TILES + (TILES - SLAB if side == 0 else 0)
+            first = slab_rows[n] * ODD + (TILES - SLAB if side == 0 else 0)
             slab_copies[n].wait()
             moves = []
             for x in range(2):
@@ -297,15 +291,15 @@
                     row = x * FACE + 2 * bz + yhi
                     for group, size in GROUPS:
                         value = slabs[n, group : group + size, q * LANE : (q + 1) * LANE]
-                        moves.append((pl.ds(group * 2 * FACE + row, size, stride=2 * FACE), value))
-                row = POPS * 2 * FACE + x * FACE + 2 * bz
+                        moves.append((pl.ds(group * STRIP + row, size, stride=STRIP), value))
+                row = POPS * STRIP + x * FACE + 2 * bz
                 moves.append((pl.ds(row, 2), dense[pl.ds(first + 2 * x, 2), :]))
             for target, value in moves:
                 strip[target, :] = value
         inner = 1 if side == 0 else 0
         for x in range(2):
-            old = [strip[pl.ds(i * 2 * FACE + x * FACE, FACE), :] for i in range(POPS)]
-            mark = strip[pl.ds(POPS * 2 * FACE + x * FACE, FACE), :] > 0.5
+            old = [strip[pl.ds(i * STRIP + x * FACE, FACE), :] for i in range(POPS)]
+            mark = strip[pl.ds(POPS * STRIP + x * FACE, FACE), :] > 0.5
             post, _ = collide(old)
             if x == inner:
                 pairs = [(i, i) for i in range(POPS)]
@@ -315,11 +309,11 @@
                 marks_at = SLAB_PLANES - 1
             for plane, i in pairs:
                 out[pl.ds(SENT_SLABS + plane * FACE, FACE), :] = jnp.where(mark, old[i], post[i])
-            marks_of = strip[pl.ds(POPS * 2 * FACE + x * FACE, FACE), :]
+            marks_of = strip[pl.ds(POPS * STRIP + x * FACE, FACE), :]
             out[pl.ds(SENT_SLABS + marks_at * FACE, FACE), :] = marks_of
 
 
-def pack_edge(places, marks_in, pops, own, zpack, zup, zdown, pos, table, marks, dense, stage, sems):
+def pack_edge(places, marks_in, pops, own, zpack, zup, zdown, pos, table, marks, dense, raw, stage, sems):
     column_z = lax.axis_index("cz")
     mark_copy = pltpu.make_async_copy(marks_in, marks, sems.at[LAYERS])
     mark_copy.start()
@@ -346,7 +340,7 @@
 
         @pl.when(found[held] >= 0)
         def _(held=held, base=base):
-            pack_block(own, base, stage.at[held], dense, row_of[held])
+            pack_block(own, base, stage.at[held], dense, row_of[held], raw)
             totals = []
             for group in range(ZGROUPS):
                 for part in range(TILES // 8):
@@ -369,7 +363,7 @@
         zdown[target, :] = zpack[pl.ds(ZROWS + group * TILES, SLAB), :]
 
 
-def pack_own(places, marks_in, pops, own_in, own, edge, flags, pos, table, marks, dense, stage, sems):
+def pack_own(places, marks_in, pops, own_in, own, edge, flags, pos, table, marks, dense, raw, stage, sems):
     del own_in
     layer, _, column_z = place()
     edge_bz = jnp.where(column_z == 0, BZD - 1, 0)
@@ -391,7 +385,7 @@
 
         @pl.when((pos[0, row] >= 0) & (slot % BZD != edge_bz))
         def _():
-            pack_block(own, pl.multiple_of(slot * BLOCK, 8), stage.at[row], dense, row)
+            pack_block(own, pl.multiple_of(slot * BLOCK, 8), stage.at[row], dense, row, raw)
 
         return carry
 
@@ -812,7 +806,11 @@
     places = pltpu.with_memory_space_constraint(block_pos.T, pltpu.HBM)
     place_scratch = SMEM((3, rows), jnp.int32)
     table_scratch = SMEM((LAYERS * BZD,), jnp.int32)
-    mark_scratch = [VMEM((rows, EDGE**3), jnp.int32), VMEM((rows * TILES, LANE), jnp.float32)]
+    mark_scratch = [
+        VMEM((rows, EDGE**3), jnp.int32),
+        VMEM((rows * ODD, LANE), jnp.float32),
+        VMEM((POPS * ODD, LANE), jnp.float32),
+    ]
 
     up = [(i, i + 1) for i in range(layers - 1)]
     down = [(i + 1, i) for i in range(layers - 1)]
@@ -826,7 +824,7 @@
         + [
             VMEM((2 * MOVE_CAP, POPS, EDGE**3), jnp.float32),
             VMEM((2 * BZD, POPS, SLAB * LANE), jnp.float32),
-            VMEM((PLANES * 2 * FACE, LANE), jnp.float32),
+            VMEM((PLANES * STRIP, LANE), jnp.float32),
             pltpu.SemaphoreType.DMA((2 + 2 * MOVE_CAP + 2 * BZD,)),
         ],
         compiler_params=params(16),

time: 50.2 us -> 49.7 us (0.990)
  Pallas kernels: 26 us -> 22.7 us
  waiting for transfers between devices: 7.82 us -> 9.79 us
  starting transfers between devices: 16 us -> 16.8 us
    ppermute x1, waiting for transfers between devices: 3.02 us -> 5 us  [shards(): z_low = lax.ppermute(zsend_up, ('stream', 'cz'), zup_pairs)]
    pallas_call x1, Pallas kernels: 4.48 us -> 2.82 us  [shards(): pl.pallas_call(pack_own, out_shape=(kept(LAYERS * BZD * BLOCK), kept(PLAN...]
    pallas_call x1, Pallas kernels: 3.69 us -> 2.57 us  [shards(): pl.pallas_call(pack_edge, out_shape=(kept(LAYERS * BZD * BLOCK), kept(ZME...]
    ppermute x1, starting transfers between devices: 3.63 us -> 4.43 us  [shards(): z_low = lax.ppermute(zsend_up, ('stream', 'cz'), zup_pairs)]
    pallas_call x1, Pallas kernels: 3.09 us -> 2.52 us  [shards(): pl.pallas_call(pack_stream, out_shape=(kept(SENT_ROWS), kept(SENT_ROWS)),...]
  transfers between devices with their start and end apart: 7 -> 7, of which waited for: 4 -> 4; matrix products, arithmetic and copies ran while one was open for 0% -> 0% of each run, Pallas kernels for 34% -> 29%
where the time goes in v12:
time: 49.7 us; the launch traced here: 49.4 us
  Pallas kernels  22.7 us (46%)
  starting transfers between devices  16.8 us (34%)
  waiting for transfers between devices  9.79 us (20%)
    pallas_call x1, Pallas kernels, shards(): pl.pallas_call(functools.partial(settle_all, layers, columns, depth), out...  8.7 us
    ppermute x1, waiting for transfers between devices, shards(): z_low = lax.ppermute(zsend_up, ('stream', 'cz'), zup_pairs)  5 us
    ppermute x1, starting transfers between devices, shards(): from_low = lax.ppermute(send_up, 'stream', up)  4.97 us
    ppermute x1, starting transfers between devices, shards(): z_low = lax.ppermute(zsend_up, ('stream', 'cz'), zup_pairs)  4.43 us
    pallas_call x1, Pallas kernels, shards(): pl.pallas_call(functools.partial(finish, layers, columns, depth), out_sha...  4.12 us
    ppermute x1, starting transfers between devices, shards(): rim_low = lax.ppermute(rim_up, 'cy', cy_up)  3.41 us
    pallas_call x1, Pallas kernels, shards(): pl.pallas_call(pack_own, out_shape=(kept(LAYERS * BZD * BLOCK), kept(PLAN...  2.82 us
    ppermute x1, waiting for transfers between devices, shards(): z_high = lax.ppermute(zsend_down, ('stream', 'cz'), zdown_pairs)  2.69 us
  transfers between devices with their start and end apart: 7, of which 4 were waited for; matrix products, arithmetic and copies ran while one was open for 0% of the time, Pallas kernels for 29%

profile of v12, /device:TPU:0, one launch (start us, length us, event | category | flops | bytes accessed | tf_op | source)
XLA Modules:
  0.0 49.4 jit_solution(4555792912492840508)
XLA Ops:
  0.0 2.5 %pack_stream.1 = (f32[1496,128]{1,0:T(8,128)S(1)}, f32[1496,128]{1,0:T(8,128)S(1)}) custom-call(s32[3,12]{1,0:T(4,128)} %bitcast.1, s32[12,4096]{1,0:T(8,128)} %marks_in.5, f32[12,19,4096]{2,1,0:T(8,128)} %pops.5), custom_call_target="tpu_custom_call" | custom-call | tf_op jit(solution)/shard_map/pack_stream/pallas_call | solution.py:817
  2.5 5.0 %collective-permute-start = (f32[1496,128]{1,0:T(8,128)S(1)}, f32[1496,128]{1,0:T(8,128)S(1)}, u32[]{:S(2)}, u32[]{:S(2)}) collective-permute-start(f32[1496,128]{1,0:T(8,128)S(1)} %get-tuple-element.23), channel_id=1, source_target_pairs={{0,8},{8,16},{16,24},{1,9},{9,17},{17,25},{2,10},{10,18},{18,26},{... | collective-permute-start | bytes 2297864 | tf_op jit(solution)/shard_map/ppermute | solution.py:833
  7.5 1.3 %collective-permute-start.1 = (f32[1496,128]{1,0:T(8,128)S(1)}, f32[1496,128]{1,0:T(8,128)S(1)}, u32[]{:S(2)}, u32[]{:S(2)}) collective-permute-start(f32[1496,128]{1,0:T(8,128)S(1)} %get-tuple-element.24), channel_id=1, source_target_pairs={{8,0},{16,8},{24,16},{9,1},{17,9},{25,17},{10,2},{18,10},{26,18},{... | collective-permute-start | bytes 2297864 | tf_op jit(solution)/shard_map/ppermute | solution.py:834
  8.8 2.6 %pack_edge.1 = (f32[10240,128]{1,0:T(8,128)S(1)}, f32[392,128]{1,0:T(8,128)S(1)}, f32[108,128]{1,0:T(8,128)S(1)}, f32[108,128]{1,0:T(8,128)S(1)}) custom-call(s32[3,12]{1,0:T(4,128)} %bitcast.2, s32[12,4096]{1,0:T(8,128)} %marks_in.5, f32[12,19,4096]{2,1,0:T(8,128)} %pops.5), custom_call_target="tpu_custom_call" | custom-call | tf_op jit(solution)/shard_map/pack_edge/pallas_call | solution.py:836
  11.4 0.1 collective-permute-start.2
  11.5 4.4 %collective-permute-start.3 = (f32[108,128]{1,0:T(8,128)S(1)}, f32[108,128]{1,0:T(8,128)S(1)}, u32[]{:S(2)}, u32[]{:S(2)}) collective-permute-start(f32[108,128]{1,0:T(8,128)S(1)} %get-tuple-element.26), channel_id=1, source_target_pairs={{0,9},{1,8},{8,17},{9,16},{16,25},{17,24},{2,11},{3,10},{10,19},{1... | collective-permute-start | bytes 165896 | tf_op jit(solution)/shard_map/ppermute | solution.py:854
  15.9 1.3 %collective-permute-start.4 = (f32[108,128]{1,0:T(8,128)S(1)}, f32[108,128]{1,0:T(8,128)S(1)}, u32[]{:S(2)}, u32[]{:S(2)}) collective-permute-start(f32[108,128]{1,0:T(8,128)S(1)} %get-tuple-element.27), channel_id=1, source_target_pairs={{8,1},{9,0},{16,9},{17,8},{24,17},{25,16},{10,3},{11,2},{18,11},{1... | collective-permute-start | bytes 165896 | tf_op jit(solution)/shard_map/ppermute | solution.py:855
  17.2 2.8 %pack_own.1 = (f32[10240,128]{1,0:T(8,128)S(1)}, f32[640,128]{1,0:T(8,128)S(1)}, f32[16,128]{1,0:T(8,128)S(1)}) custom-call(s32[3,12]{1,0:T(4,128)} %bitcast.3, s32[12,4096]{1,0:T(8,128)} %marks_in.5, f32[12,19,4096]{2,1,0:T(8,128)} %pops.5, f32[10240,128]{1,0:T(8,128)S(1)} %get-tuple-element.28.own_in), custom_call_target="tpu_custom_call", output_to_operand_aliasing={{0}: (3, {})} | custom-call | tf_op jit(solution)/shard_map/pack_own/pallas_call | solution.py:857
  20.0 5.0 %collective-permute-done.3.zup = f32[108,128]{1,0:T(8,128)S(1)} collective-permute-done((f32[108,128]{1,0:T(8,128)S(1)}, f32[108,128]{1,0:T(8,128)S(1)}, u32[]{:S(2)}, u32[]{:S(2)}) %collective-permute-start.3) | collective-permute-done | bytes 55328 | tf_op jit(solution)/shard_map/ppermute | solution.py:854
  25.0 2.7 %collective-permute-done.4.zdown = f32[108,128]{1,0:T(8,128)S(1)} collective-permute-done((f32[108,128]{1,0:T(8,128)S(1)}, f32[108,128]{1,0:T(8,128)S(1)}, u32[]{:S(2)}, u32[]{:S(2)}) %collective-permute-start.4) | collective-permute-done | bytes 55328 | tf_op jit(solution)/shard_map/ppermute | solution.py:855
  27.7 0.0 collective-permute-done.2.zin
  27.7 0.0 collective-permute-done.up
  27.7 0.8 %collective-permute-done.1.down = f32[1496,128]{1,0:T(8,128)S(1)} collective-permute-done((f32[1496,128]{1,0:T(8,128)S(1)}, f32[1496,128]{1,0:T(8,128)S(1)}, u32[]{:S(2)}, u32[]{:S(2)}) %collective-permute-start.1) | collective-permute-done | bytes 765984 | tf_op jit(solution)/shard_map/ppermute | solution.py:834
  28.6 2.0 %settle_rim.1 = (f32[10240,128]{1,0:T(8,128)S(1)}, f32[640,128]{1,0:T(8,128)S(1)}, f32[384,128]{1,0:T(8,128)S(1)}, f32[24,128]{1,0:T(8,128)S(1)}, f32[400,128]{1,0:T(8,128)S(1)}, /*index=5*/f32[400,128]{1,0:T(8,128)S(1)}) custom-call(f32[1496,128]{1,0:T(8,128)S(1)} %collective-permute-done.up, ...), custom_call_target="tpu_custom_call", output_to_operand_aliasing={{0}: (7, {})} | custom-call | tf_op jit(solution)/shard_map/settle_rim/pallas_call | solution.py:873
  30.6 3.4 %collective-permute-start.5 = (f32[400,128]{1,0:T(8,128)S(1)}, f32[400,128]{1,0:T(8,128)S(1)}, u32[]{:S(2)}, u32[]{:S(2)}) collective-permute-start(f32[400,128]{1,0:T(8,128)S(1)} %get-tuple-element.32), channel_id=1, source_target_pairs={{0,2},{2,4},{4,6},{1,3},{3,5},{5,7},{8,10},{10,12},{12,14},{9,11},... | collective-permute-start | bytes 614408 | tf_op jit(solution)/shard_map/ppermute | solution.py:895
  34.0 1.3 %collective-permute-start.6 = (f32[400,128]{1,0:T(8,128)S(1)}, f32[400,128]{1,0:T(8,128)S(1)}, u32[]{:S(2)}, u32[]{:S(2)}) collective-permute-start(f32[400,128]{1,0:T(8,128)S(1)} %get-tuple-element.33), channel_id=1, source_target_pairs={{2,0},{4,2},{6,4},{3,1},{5,3},{7,5},{10,8},{12,10},{14,12},{11,9},... | collective-permute-start | bytes 614408 | tf_op jit(solution)/shard_map/ppermute | solution.py:896
  35.3 8.7 %settle_all.1 = (f32[15656,128]{1,0:T(8,128)S(1)}, f32[15656,128]{1,0:T(8,128)S(1)}) custom-call(f32[10240,128]{1,0:T(8,128)S(1)} %get-tuple-element.34.own, f32[640,128]{1,0:T(8,128)S(1)} %get-tuple-element.35.edge, f32[384,128]{1,0:T(8,128)S(1)} %get-tuple-element.36.zall, f32[24,128]{1,0:T(8,128)S(1)} %get-tuple-element.37.zedge), custom_call_target="tpu_custom_call" | custom-call | tf_op jit(solution)/shard_map/settle_all/pallas_call | solution.py:898
  44.0 0.0 collective-permute-done.5.rim_low
  44.0 1.2 %collective-permute-done.6.rim_high = f32[400,128]{1,0:T(8,128)S(1)} collective-permute-done((f32[400,128]{1,0:T(8,128)S(1)}, f32[400,128]{1,0:T(8,128)S(1)}, u32[]{:S(2)}, u32[]{:S(2)}) %collective-permute-start.6) | collective-permute-done | bytes 204832 | tf_op jit(solution)/shard_map/ppermute | solution.py:896
  45.2 4.1 %finish.1 = (f32[19,32,16,64]{3,2,1,0:T(8,128)}, f32[15656,128]{1,0:T(8,128)S(1)}, f32[15656,128]{1,0:T(8,128)S(1)}) custom-call(f32[400,128]{1,0:T(8,128)S(1)} %collective-permute-done.5.rim_low, f32[400,128]{1,0:T(8,128)S(1)} %collective-permute-done.6.rim_high, ...), custom_call_target="tpu_custom_call", output_to_operand_aliasing={{1}: (2, {}), {2}: (3, {})} | custom-call | tf_op jit(solution)/shard_map/finish/pallas_call | solution.py:908
Async XLA Ops:
  2.5 25.2 %collective-permute-start = (f32[1496,128]{1,0:T(8,128)S(1)}, f32[1496,128]{1,0:T(8,128)S(1)}, u32[]{:S(2)}, u32[]{:S(2)}) collective-permute-start(f32[1496,128]{1,0:T(8,128)S(1)} %get-tuple-element.23), channel_id=1, source_target_pairs={{0,8},{8,16},{16,24},{1,9},{9,17},{17,25},{2,10},{10,18},{18,26},{... | collective-permute-start | bytes 2297864 | tf_op jit(solution)/shard_map/ppermute | solution.py:833
  7.5 21.1 %collective-permute-start.1 = (f32[1496,128]{1,0:T(8,128)S(1)}, f32[1496,128]{1,0:T(8,128)S(1)}, u32[]{:S(2)}, u32[]{:S(2)}) collective-permute-start(f32[1496,128]{1,0:T(8,128)S(1)} %get-tuple-element.24), channel_id=1, source_target_pairs={{8,0},{16,8},{24,16},{9,1},{17,9},{25,17},{10,2},{18,10},{26,18},{... | collective-permute-start | bytes 2297864 | tf_op jit(solution)/shard_map/ppermute | solution.py:834
  11.4 16.3 %collective-permute-start.2 = (f32[392,128]{1,0:T(8,128)S(1)}, f32[392,128]{1,0:T(8,128)S(1)}, u32[]{:S(2)}, u32[]{:S(2)}) collective-permute-start(f32[392,128]{1,0:T(8,128)S(1)} %get-tuple-element.25), channel_id=1, source_target_pairs={{0,1},{1,0},{2,3},{3,2},{4,5},{5,4},{6,7},{7,6},{8,9},{9,8},{10,11... | collective-permute-start | bytes 602120 | tf_op jit(solution)/shard_map/ppermute | solution.py:851
  11.5 13.6 %collective-permute-start.3 = (f32[108,128]{1,0:T(8,128)S(1)}, f32[108,128]{1,0:T(8,128)S(1)}, u32[]{:S(2)}, u32[]{:S(2)}) collective-permute-start(f32[108,128]{1,0:T(8,128)S(1)} %get-tuple-element.26), channel_id=1, source_target_pairs={{0,9},{1,8},{8,17},{9,16},{16,25},{17,24},{2,11},{3,10},{10,19},{1... | collective-permute-start | bytes 165896 | tf_op jit(solution)/shard_map/ppermute | solution.py:854
  15.9 11.8 %collective-permute-start.4 = (f32[108,128]{1,0:T(8,128)S(1)}, f32[108,128]{1,0:T(8,128)S(1)}, u32[]{:S(2)}, u32[]{:S(2)}) collective-permute-start(f32[108,128]{1,0:T(8,128)S(1)} %get-tuple-element.27), channel_id=1, source_target_pairs={{8,1},{9,0},{16,9},{17,8},{24,17},{25,16},{10,3},{11,2},{18,11},{1... | collective-permute-start | bytes 165896 | tf_op jit(solution)/shard_map/ppermute | solution.py:855
  30.6 13.4 %collective-permute-start.5 = (f32[400,128]{1,0:T(8,128)S(1)}, f32[400,128]{1,0:T(8,128)S(1)}, u32[]{:S(2)}, u32[]{:S(2)}) collective-permute-start(f32[400,128]{1,0:T(8,128)S(1)} %get-tuple-element.32), channel_id=1, source_target_pairs={{0,2},{2,4},{4,6},{1,3},{3,5},{5,7},{8,10},{10,12},{12,14},{9,11},... | collective-permute-start | bytes 614408 | tf_op jit(solution)/shard_map/ppermute | solution.py:895
  34.0 11.3 %collective-permute-start.6 = (f32[400,128]{1,0:T(8,128)S(1)}, f32[400,128]{1,0:T(8,128)S(1)}, u32[]{:S(2)}, u32[]{:S(2)}) collective-permute-start(f32[400,128]{1,0:T(8,128)S(1)} %get-tuple-element.33), channel_id=1, source_target_pairs={{2,0},{4,2},{6,4},{3,1},{5,3},{7,5},{10,8},{12,10},{14,12},{11,9},... | collective-permute-start | bytes 614408 | tf_op jit(solution)/shard_map/ppermute | solution.py:896

commit v13 on v12

--- a/solution.py
+++ b/solution.py
@@ -648,11 +648,12 @@
     return pull
 
 
-def settle_all(layers, columns, depth, own, edge, zall, zedge, field, later, turn):
+def settle_all(layers, columns, depth, own, edge, zall, zedge, field, later, half, turn):
     layer, _, column_z = place()
     masks = Lanes(column_z)
     lane = lanes()
-    group_of = [((lane >> 4) & (BZD - 1)) == bz for bz in range(BZD)]
+    single = (lane & EDGE) != 0
+    double = (lane & (2 * EDGE)) != 0
     inside_box = inside_lanes(8, column_z)
     inside_halo = inside_lanes(4, column_z) & halo_x_inside(layer, layers)
 
@@ -660,13 +661,21 @@
         for plane in range(PLANES):
             parts, zvalue = plane_parts(own, edge, zall, zedge, chunk, yhi, plane)
             size = zvalue.shape[0]
-            main = masks.main[:size]
+            for n in range(0, BZD, 2):
+                even = jnp.where(single[:size], pltpu.roll(parts[n + 1], EDGE, 1), parts[n])
+                odd = jnp.where(single[:size], parts[n + 1], pltpu.roll(parts[n], LANE - EDGE, 1))
+                half[pl.ds((plane * 4 + n) * 8, size), :] = even
+                half[pl.ds((plane * 4 + n + 1) * 8, size), :] = odd
+        main = masks.main[:size]
+        for plane in range(PLANES):
+            _, zvalue = plane_parts(own, edge, zall, zedge, chunk, yhi, plane)
             for r in range(4):
-                both = None
-                for bz in range(BZD):
-                    shift = (bz - r) * EDGE % LANE
-                    value = pltpu.roll(parts[bz], shift, 1) if shift else parts[bz]
-                    both = value if both is None else jnp.where(group_of[bz][:size], value, both)
+                low = half[pl.ds((plane * 4 + r % 2) * 8, size), :]
+                high = half[pl.ds((plane * 4 + 2 + r % 2) * 8, size), :]
+                if r < 2:
+                    both = jnp.where(double[:size], pltpu.roll(high, 2 * EDGE, 1), low)
+                else:
+                    both = jnp.where(double[:size], high, pltpu.roll(low, LANE - 2 * EDGE, 1))
                 beyond = pltpu.roll(zvalue, masks.to_halo(r, plane % 8), 1)
                 turn[pl.ds((plane * YLO + r) * 8, size), :] = jnp.where(main, both, beyond)
                 turn[pl.ds((plane * YLO + r + 4) * 8, size), :] = jnp.where(main, beyond, both)
@@ -900,7 +909,10 @@
         out_shape=(kept(POPS * FIELD), kept(POPS * FIELD)),
         in_specs=[vmem] * 4,
         out_specs=(vmem,) * 2,
-        scratch_shapes=[VMEM((PLANES * YLO * 8, LANE), jnp.float32)],
+        scratch_shapes=[
+            VMEM((PLANES * 4 * 8, LANE), jnp.float32),
+            VMEM((PLANES * YLO * 8, LANE), jnp.float32),
+        ],
         compiler_params=params(16),
         name="settle_all",
     )(own, edge, zall, zedge)

time: 49.7 us -> 49.7 us (level)
  waiting for transfers between devices: 9.79 us -> 10.6 us
  Pallas kernels: 22.7 us -> 22 us
    ppermute x1, waiting for transfers between devices: 1.24 us -> 2.03 us  [shards(): rim_high = lax.ppermute(rim_down, 'cy', cy_down)]
    pallas_call x1, Pallas kernels: 8.7 us -> 7.91 us  [shards(): pl.pallas_call(functools.partial(settle_all, layers, columns, depth), out...]
  transfers between devices with their start and end apart: 7 -> 7, of which waited for: 4 -> 4; matrix products, arithmetic and copies ran while one was open for 0% -> 0% of each run, Pallas kernels for 29% -> 27%
where the time goes in v13:
time: 49.7 us; the launch traced here: 49.4 us
  Pallas kernels  22 us (44%)
  starting transfers between devices  16.6 us (33%)
  waiting for transfers between devices  10.6 us (21%)
    pallas_call x1, Pallas kernels, shards(): pl.pallas_call(functools.partial(settle_all, layers, columns, depth), out...  7.91 us
    ppermute x1, waiting for transfers between devices, shards(): z_low = lax.ppermute(zsend_up, ('stream', 'cz'), zup_pairs)  5 us
    ppermute x1, starting transfers between devices, shards(): from_low = lax.ppermute(send_up, 'stream', up)  4.97 us
    ppermute x1, starting transfers between devices, shards(): z_low = lax.ppermute(zsend_up, ('stream', 'cz'), zup_pairs)  4.31 us
    pallas_call x1, Pallas kernels, shards(): pl.pallas_call(functools.partial(finish, layers, columns, depth), out_sha...  4.12 us
    ppermute x1, starting transfers between devices, shards(): rim_low = lax.ppermute(rim_up, 'cy', cy_up)  3.41 us
    pallas_call x1, Pallas kernels, shards(): pl.pallas_call(pack_edge, out_shape=(kept(LAYERS * BZD * BLOCK), kept(ZME...  2.8 us
    pallas_call x1, Pallas kernels, shards(): pl.pallas_call(pack_own, out_shape=(kept(LAYERS * BZD * BLOCK), kept(PLAN...  2.71 us
  transfers between devices with their start and end apart: 7, of which 4 were waited for; matrix products, arithmetic and copies ran while one was open for 0% of the time, Pallas kernels for 27%

profile of v13, /device:TPU:0, one launch (start us, length us, event | category | flops | bytes accessed | tf_op | source)
XLA Modules:
  0.0 49.4 jit_solution(2836356927023952773)
XLA Ops:
  0.0 2.5 %pack_stream.1 = (f32[1496,128]{1,0:T(8,128)S(1)}, f32[1496,128]{1,0:T(8,128)S(1)}) custom-call(s32[3,12]{1,0:T(4,128)} %bitcast.1, s32[12,4096]{1,0:T(8,128)} %marks_in.5, f32[12,19,4096]{2,1,0:T(8,128)} %pops.5), custom_call_target="tpu_custom_call" | custom-call | tf_op jit(solution)/shard_map/pack_stream/pallas_call | solution.py:826
  2.5 5.0 %collective-permute-start = (f32[1496,128]{1,0:T(8,128)S(1)}, f32[1496,128]{1,0:T(8,128)S(1)}, u32[]{:S(2)}, u32[]{:S(2)}) collective-permute-start(f32[1496,128]{1,0:T(8,128)S(1)} %get-tuple-element.23), channel_id=1, source_target_pairs={{0,8},{8,16},{16,24},{1,9},{9,17},{17,25},{2,10},{10,18},{18,26},{... | collective-permute-start | bytes 2297864 | tf_op jit(solution)/shard_map/ppermute | solution.py:842
  7.5 1.3 %collective-permute-start.1 = (f32[1496,128]{1,0:T(8,128)S(1)}, f32[1496,128]{1,0:T(8,128)S(1)}, u32[]{:S(2)}, u32[]{:S(2)}) collective-permute-start(f32[1496,128]{1,0:T(8,128)S(1)} %get-tuple-element.24), channel_id=1, source_target_pairs={{8,0},{16,8},{24,16},{9,1},{17,9},{25,17},{10,2},{18,10},{26,18},{... | collective-permute-start | bytes 2297864 | tf_op jit(solution)/shard_map/ppermute | solution.py:843
  8.8 2.8 %pack_edge.1 = (f32[10240,128]{1,0:T(8,128)S(1)}, f32[392,128]{1,0:T(8,128)S(1)}, f32[108,128]{1,0:T(8,128)S(1)}, f32[108,128]{1,0:T(8,128)S(1)}) custom-call(s32[3,12]{1,0:T(4,128)} %bitcast.2, s32[12,4096]{1,0:T(8,128)} %marks_in.5, f32[12,19,4096]{2,1,0:T(8,128)} %pops.5), custom_call_target="tpu_custom_call" | custom-call | tf_op jit(solution)/shard_map/pack_edge/pallas_call | solution.py:845
  11.6 0.1 collective-permute-start.2
  11.7 4.3 %collective-permute-start.3 = (f32[108,128]{1,0:T(8,128)S(1)}, f32[108,128]{1,0:T(8,128)S(1)}, u32[]{:S(2)}, u32[]{:S(2)}) collective-permute-start(f32[108,128]{1,0:T(8,128)S(1)} %get-tuple-element.26), channel_id=1, source_target_pairs={{0,9},{1,8},{8,17},{9,16},{16,25},{17,24},{2,11},{3,10},{10,19},{1... | collective-permute-start | bytes 165896 | tf_op jit(solution)/shard_map/ppermute | solution.py:863
  16.0 1.3 %collective-permute-start.4 = (f32[108,128]{1,0:T(8,128)S(1)}, f32[108,128]{1,0:T(8,128)S(1)}, u32[]{:S(2)}, u32[]{:S(2)}) collective-permute-start(f32[108,128]{1,0:T(8,128)S(1)} %get-tuple-element.27), channel_id=1, source_target_pairs={{8,1},{9,0},{16,9},{17,8},{24,17},{25,16},{10,3},{11,2},{18,11},{1... | collective-permute-start | bytes 165896 | tf_op jit(solution)/shard_map/ppermute | solution.py:864
  17.3 2.7 %pack_own.1 = (f32[10240,128]{1,0:T(8,128)S(1)}, f32[640,128]{1,0:T(8,128)S(1)}, f32[16,128]{1,0:T(8,128)S(1)}) custom-call(s32[3,12]{1,0:T(4,128)} %bitcast.3, s32[12,4096]{1,0:T(8,128)} %marks_in.5, f32[12,19,4096]{2,1,0:T(8,128)} %pops.5, f32[10240,128]{1,0:T(8,128)S(1)} %get-tuple-element.28.own_in), custom_call_target="tpu_custom_call", output_to_operand_aliasing={{0}: (3, {})} | custom-call | tf_op jit(solution)/shard_map/pack_own/pallas_call | solution.py:866
  20.0 5.0 %collective-permute-done.3.zup = f32[108,128]{1,0:T(8,128)S(1)} collective-permute-done((f32[108,128]{1,0:T(8,128)S(1)}, f32[108,128]{1,0:T(8,128)S(1)}, u32[]{:S(2)}, u32[]{:S(2)}) %collective-permute-start.3) | collective-permute-done | bytes 55328 | tf_op jit(solution)/shard_map/ppermute | solution.py:863
  25.0 2.7 %collective-permute-done.4.zdown = f32[108,128]{1,0:T(8,128)S(1)} collective-permute-done((f32[108,128]{1,0:T(8,128)S(1)}, f32[108,128]{1,0:T(8,128)S(1)}, u32[]{:S(2)}, u32[]{:S(2)}) %collective-permute-start.4) | collective-permute-done | bytes 55328 | tf_op jit(solution)/shard_map/ppermute | solution.py:864
  27.7 0.0 collective-permute-done.2.zin
  27.7 0.0 collective-permute-done.up
  27.7 0.8 %collective-permute-done.1.down = f32[1496,128]{1,0:T(8,128)S(1)} collective-permute-done((f32[1496,128]{1,0:T(8,128)S(1)}, f32[1496,128]{1,0:T(8,128)S(1)}, u32[]{:S(2)}, u32[]{:S(2)}) %collective-permute-start.1) | collective-permute-done | bytes 765984 | tf_op jit(solution)/shard_map/ppermute | solution.py:843
  28.6 2.0 %settle_rim.1 = (f32[10240,128]{1,0:T(8,128)S(1)}, f32[640,128]{1,0:T(8,128)S(1)}, f32[384,128]{1,0:T(8,128)S(1)}, f32[24,128]{1,0:T(8,128)S(1)}, f32[400,128]{1,0:T(8,128)S(1)}, /*index=5*/f32[400,128]{1,0:T(8,128)S(1)}) custom-call(f32[1496,128]{1,0:T(8,128)S(1)} %collective-permute-done.up, ...), custom_call_target="tpu_custom_call", output_to_operand_aliasing={{0}: (7, {})} | custom-call | tf_op jit(solution)/shard_map/settle_rim/pallas_call | solution.py:882
  30.6 3.4 %collective-permute-start.5 = (f32[400,128]{1,0:T(8,128)S(1)}, f32[400,128]{1,0:T(8,128)S(1)}, u32[]{:S(2)}, u32[]{:S(2)}) collective-permute-start(f32[400,128]{1,0:T(8,128)S(1)} %get-tuple-element.32), channel_id=1, source_target_pairs={{0,2},{2,4},{4,6},{1,3},{3,5},{5,7},{8,10},{10,12},{12,14},{9,11},... | collective-permute-start | bytes 614408 | tf_op jit(solution)/shard_map/ppermute | solution.py:904
  34.0 1.3 %collective-permute-start.6 = (f32[400,128]{1,0:T(8,128)S(1)}, f32[400,128]{1,0:T(8,128)S(1)}, u32[]{:S(2)}, u32[]{:S(2)}) collective-permute-start(f32[400,128]{1,0:T(8,128)S(1)} %get-tuple-element.33), channel_id=1, source_target_pairs={{2,0},{4,2},{6,4},{3,1},{5,3},{7,5},{10,8},{12,10},{14,12},{11,9},... | collective-permute-start | bytes 614408 | tf_op jit(solution)/shard_map/ppermute | solution.py:905
  35.3 7.9 %settle_all.1 = (f32[15656,128]{1,0:T(8,128)S(1)}, f32[15656,128]{1,0:T(8,128)S(1)}) custom-call(f32[10240,128]{1,0:T(8,128)S(1)} %get-tuple-element.34.own, f32[640,128]{1,0:T(8,128)S(1)} %get-tuple-element.35.edge, f32[384,128]{1,0:T(8,128)S(1)} %get-tuple-element.36.zall, f32[24,128]{1,0:T(8,128)S(1)} %get-tuple-element.37.zedge), custom_call_target="tpu_custom_call" | custom-call | tf_op jit(solution)/shard_map/settle_all/pallas_call | solution.py:907
  43.2 0.0 collective-permute-done.5.rim_low
  43.2 2.0 %collective-permute-done.6.rim_high = f32[400,128]{1,0:T(8,128)S(1)} collective-permute-done((f32[400,128]{1,0:T(8,128)S(1)}, f32[400,128]{1,0:T(8,128)S(1)}, u32[]{:S(2)}, u32[]{:S(2)}) %collective-permute-start.6) | collective-permute-done | bytes 204832 | tf_op jit(solution)/shard_map/ppermute | solution.py:905
  45.2 4.1 %finish.1 = (f32[19,32,16,64]{3,2,1,0:T(8,128)}, f32[15656,128]{1,0:T(8,128)S(1)}, f32[15656,128]{1,0:T(8,128)S(1)}) custom-call(f32[400,128]{1,0:T(8,128)S(1)} %collective-permute-done.5.rim_low, f32[400,128]{1,0:T(8,128)S(1)} %collective-permute-done.6.rim_high, ...), custom_call_target="tpu_custom_call", output_to_operand_aliasing={{1}: (2, {}), {2}: (3, {})} | custom-call | tf_op jit(solution)/shard_map/finish/pallas_call | solution.py:920
Async XLA Ops:
  2.5 25.2 %collective-permute-start = (f32[1496,128]{1,0:T(8,128)S(1)}, f32[1496,128]{1,0:T(8,128)S(1)}, u32[]{:S(2)}, u32[]{:S(2)}) collective-permute-start(f32[1496,128]{1,0:T(8,128)S(1)} %get-tuple-element.23), channel_id=1, source_target_pairs={{0,8},{8,16},{16,24},{1,9},{9,17},{17,25},{2,10},{10,18},{18,26},{... | collective-permute-start | bytes 2297864 | tf_op jit(solution)/shard_map/ppermute | solution.py:842
  7.5 21.1 %collective-permute-start.1 = (f32[1496,128]{1,0:T(8,128)S(1)}, f32[1496,128]{1,0:T(8,128)S(1)}, u32[]{:S(2)}, u32[]{:S(2)}) collective-permute-start(f32[1496,128]{1,0:T(8,128)S(1)} %get-tuple-element.24), channel_id=1, source_target_pairs={{8,0},{16,8},{24,16},{9,1},{17,9},{25,17},{10,2},{18,10},{26,18},{... | collective-permute-start | bytes 2297864 | tf_op jit(solution)/shard_map/ppermute | solution.py:843
  11.6 16.1 %collective-permute-start.2 = (f32[392,128]{1,0:T(8,128)S(1)}, f32[392,128]{1,0:T(8,128)S(1)}, u32[]{:S(2)}, u32[]{:S(2)}) collective-permute-start(f32[392,128]{1,0:T(8,128)S(1)} %get-tuple-element.25), channel_id=1, source_target_pairs={{0,1},{1,0},{2,3},{3,2},{4,5},{5,4},{6,7},{7,6},{8,9},{9,8},{10,11... | collective-permute-start | bytes 602120 | tf_op jit(solution)/shard_map/ppermute | solution.py:860
  11.7 13.3 %collective-permute-start.3 = (f32[108,128]{1,0:T(8,128)S(1)}, f32[108,128]{1,0:T(8,128)S(1)}, u32[]{:S(2)}, u32[]{:S(2)}) collective-permute-start(f32[108,128]{1,0:T(8,128)S(1)} %get-tuple-element.26), channel_id=1, source_target_pairs={{0,9},{1,8},{8,17},{9,16},{16,25},{17,24},{2,11},{3,10},{10,19},{1... | collective-permute-start | bytes 165896 | tf_op jit(solution)/shard_map/ppermute | solution.py:863
  16.0 11.7 %collective-permute-start.4 = (f32[108,128]{1,0:T(8,128)S(1)}, f32[108,128]{1,0:T(8,128)S(1)}, u32[]{:S(2)}, u32[]{:S(2)}) collective-permute-start(f32[108,128]{1,0:T(8,128)S(1)} %get-tuple-element.27), channel_id=1, source_target_pairs={{8,1},{9,0},{16,9},{17,8},{24,17},{25,16},{10,3},{11,2},{18,11},{1... | collective-permute-start | bytes 165896 | tf_op jit(solution)/shard_map/ppermute | solution.py:864
  30.6 12.6 %collective-permute-start.5 = (f32[400,128]{1,0:T(8,128)S(1)}, f32[400,128]{1,0:T(8,128)S(1)}, u32[]{:S(2)}, u32[]{:S(2)}) collective-permute-start(f32[400,128]{1,0:T(8,128)S(1)} %get-tuple-element.32), channel_id=1, source_target_pairs={{0,2},{2,4},{4,6},{1,3},{3,5},{5,7},{8,10},{10,12},{12,14},{9,11},... | collective-permute-start | bytes 614408 | tf_op jit(solution)/shard_map/ppermute | solution.py:904
  34.0 11.3 %collective-permute-start.6 = (f32[400,128]{1,0:T(8,128)S(1)}, f32[400,128]{1,0:T(8,128)S(1)}, u32[]{:S(2)}, u32[]{:S(2)}) collective-permute-start(f32[400,128]{1,0:T(8,128)S(1)} %get-tuple-element.33), channel_id=1, source_target_pairs={{2,0},{4,2},{6,4},{3,1},{5,3},{7,5},{10,8},{12,10},{14,12},{11,9},... | collective-permute-start | bytes 614408 | tf_op jit(solution)/shard_map/ppermute | solution.py:905

commit v14 on v13

--- a/solution.py
+++ b/solution.py
@@ -767,22 +767,31 @@
         return pltpu.make_async_copy(result.at[part], out.at[part], sems.at[chunk, half])
 
     def second_step(chunk, carry):
-        for half in range(SPAN_Y // 8):
+        def tile(half, k):
+            y = 8 * half + k
+            base = pl.multiple_of(FIRST + y * PITCH + 8 * chunk, 8)
+            drift_z = spin * ((column_y * SPAN_Y + y).astype(jnp.float32) - centre_y)
+            old = [later[pl.ds(i * FIELD + base, 8), :] for i in range(POPS)]
+            values = streamed(pull_from(later, base), old, total_of(old), drift_y, drift_z)
+            wall = old[0] < WALL_BELOW
+            for i in range(POPS):
+                value = jnp.where(wall, old[i] * (1.0 / ROTOR), values[i])
+                turn[pl.ds(((half * POPS + i) * 8 + k) * TURN, 8), :] = value
+
+        def place_row(half, k):
+            values = [turn[pl.ds((half * POPS + i) * 8 * TURN + k, 8, stride=TURN), :] for i in range(POPS)]
+            for i in range(POPS):
+                result[i, 8 * chunk + k, 8 * half : 8 * half + 8, :] = values[i][:, :SPAN_Z]
+
+        halves = SPAN_Y // 8
+        for half in range(halves + 1):
             for k in range(8):
-                y = 8 * half + k
-                base = pl.multiple_of(FIRST + y * PITCH + 8 * chunk, 8)
-                drift_z = spin * ((column_y * SPAN_Y + y).astype(jnp.float32) - centre_y)
-                old = [later[pl.ds(i * FIELD + base, 8), :] for i in range(POPS)]
-                values = streamed(pull_from(later, base), old, total_of(old), drift_y, drift_z)
-                wall = old[0] < WALL_BELOW
-                for i in range(POPS):
-                    value = jnp.where(wall, old[i] * (1.0 / ROTOR), values[i])
-                    turn[pl.ds(i * 8 * TURN + k * TURN, 8), :] = value
-            for k in range(8):
-                values = [turn[pl.ds(i * 8 * TURN + k, 8, stride=TURN), :] for i in range(POPS)]
-                for i in range(POPS):
-                    result[i, 8 * chunk + k, 8 * half : 8 * half + 8, :] = values[i][:, :SPAN_Z]
-            leave(chunk, half).start()
+                if half < halves:
+                    tile(half, k)
+                if half > 0:
+                    place_row(half - 1, k)
+            if half > 0:
+                leave(chunk, half - 1).start()
         return carry
 
     lax.fori_loop(0, SPAN_X // 8, second_step, 0)
@@ -929,7 +938,7 @@
         scratch_shapes=[
             VMEM(((STREAMED + 1) * GRID_X, LANE), jnp.float32),
             VMEM(((STREAMED + 1) * GRID_X, LANE), jnp.float32),
-            VMEM((POPS * 8 * TURN, LANE), jnp.float32),
+            VMEM((SPAN_Y // 8 * POPS * 8 * TURN, LANE), jnp.float32),
             VMEM((POPS, SPAN_X, SPAN_Y, SPAN_Z), jnp.float32),
             pltpu.SemaphoreType.DMA((SPAN_X // 8, SPAN_Y // 8)),
         ],

time: 49.7 us -> 49.7 us (level)
  no operation moved by 1% of the time
where the time goes in v14:
time: 49.7 us; the launch traced here: 49.3 us
  Pallas kernels  22 us (44%)
  starting transfers between devices  16.6 us (33%)
  waiting for transfers between devices  10.6 us (21%)
    pallas_call x1, Pallas kernels, shards(): pl.pallas_call(functools.partial(settle_all, layers, columns, depth), out...  7.91 us
    ppermute x1, waiting for transfers between devices, shards(): z_low = lax.ppermute(zsend_up, ('stream', 'cz'), zup_pairs)  5.03 us
    ppermute x1, starting transfers between devices, shards(): from_low = lax.ppermute(send_up, 'stream', up)  4.97 us
    ppermute x1, starting transfers between devices, shards(): z_low = lax.ppermute(zsend_up, ('stream', 'cz'), zup_pairs)  4.31 us
    pallas_call x1, Pallas kernels, shards(): pl.pallas_call(functools.partial(finish, layers, columns, depth), out_sha...  4.09 us
    ppermute x1, starting transfers between devices, shards(): rim_low = lax.ppermute(rim_up, 'cy', cy_up)  3.41 us
    pallas_call x1, Pallas kernels, shards(): pl.pallas_call(pack_edge, out_shape=(kept(LAYERS * BZD * BLOCK), kept(ZME...  2.8 us
    ppermute x1, waiting for transfers between devices, shards(): z_high = lax.ppermute(zsend_down, ('stream', 'cz'), zdown_pairs)  2.69 us
  transfers between devices with their start and end apart: 7, of which 4 were waited for; matrix products, arithmetic and copies ran while one was open for 0% of the time, Pallas kernels for 27%

profile of v14, /device:TPU:0, one launch (start us, length us, event | category | flops | bytes accessed | tf_op | source)
XLA Modules:
  0.0 49.3 jit_solution(4084001700873359235)
XLA Ops:
  0.0 2.5 %pack_stream.1 = (f32[1496,128]{1,0:T(8,128)S(1)}, f32[1496,128]{1,0:T(8,128)S(1)}) custom-call(s32[3,12]{1,0:T(4,128)} %bitcast.1, s32[12,4096]{1,0:T(8,128)} %marks_in.5, f32[12,19,4096]{2,1,0:T(8,128)} %pops.5), custom_call_target="tpu_custom_call" | custom-call | tf_op jit(solution)/shard_map/pack_stream/pallas_call | solution.py:835
  2.5 5.0 %collective-permute-start = (f32[1496,128]{1,0:T(8,128)S(1)}, f32[1496,128]{1,0:T(8,128)S(1)}, u32[]{:S(2)}, u32[]{:S(2)}) collective-permute-start(f32[1496,128]{1,0:T(8,128)S(1)} %get-tuple-element.23), channel_id=1, source_target_pairs={{0,8},{8,16},{16,24},{1,9},{9,17},{17,25},{2,10},{10,18},{18,26},{... | collective-permute-start | bytes 2297864 | tf_op jit(solution)/shard_map/ppermute | solution.py:851
  7.5 1.3 %collective-permute-start.1 = (f32[1496,128]{1,0:T(8,128)S(1)}, f32[1496,128]{1,0:T(8,128)S(1)}, u32[]{:S(2)}, u32[]{:S(2)}) collective-permute-start(f32[1496,128]{1,0:T(8,128)S(1)} %get-tuple-element.24), channel_id=1, source_target_pairs={{8,0},{16,8},{24,16},{9,1},{17,9},{25,17},{10,2},{18,10},{26,18},{... | collective-permute-start | bytes 2297864 | tf_op jit(solution)/shard_map/ppermute | solution.py:852
  8.8 2.8 %pack_edge.1 = (f32[10240,128]{1,0:T(8,128)S(1)}, f32[392,128]{1,0:T(8,128)S(1)}, f32[108,128]{1,0:T(8,128)S(1)}, f32[108,128]{1,0:T(8,128)S(1)}) custom-call(s32[3,12]{1,0:T(4,128)} %bitcast.2, s32[12,4096]{1,0:T(8,128)} %marks_in.5, f32[12,19,4096]{2,1,0:T(8,128)} %pops.5), custom_call_target="tpu_custom_call" | custom-call | tf_op jit(solution)/shard_map/pack_edge/pallas_call | solution.py:854
  11.6 0.1 collective-permute-start.2
  11.7 4.3 %collective-permute-start.3 = (f32[108,128]{1,0:T(8,128)S(1)}, f32[108,128]{1,0:T(8,128)S(1)}, u32[]{:S(2)}, u32[]{:S(2)}) collective-permute-start(f32[108,128]{1,0:T(8,128)S(1)} %get-tuple-element.26), channel_id=1, source_target_pairs={{0,9},{1,8},{8,17},{9,16},{16,25},{17,24},{2,11},{3,10},{10,19},{1... | collective-permute-start | bytes 165896 | tf_op jit(solution)/shard_map/ppermute | solution.py:872
  16.0 1.3 %collective-permute-start.4 = (f32[108,128]{1,0:T(8,128)S(1)}, f32[108,128]{1,0:T(8,128)S(1)}, u32[]{:S(2)}, u32[]{:S(2)}) collective-permute-start(f32[108,128]{1,0:T(8,128)S(1)} %get-tuple-element.27), channel_id=1, source_target_pairs={{8,1},{9,0},{16,9},{17,8},{24,17},{25,16},{10,3},{11,2},{18,11},{1... | collective-permute-start | bytes 165896 | tf_op jit(solution)/shard_map/ppermute | solution.py:873
  17.3 2.7 %pack_own.1 = (f32[10240,128]{1,0:T(8,128)S(1)}, f32[640,128]{1,0:T(8,128)S(1)}, f32[16,128]{1,0:T(8,128)S(1)}) custom-call(s32[3,12]{1,0:T(4,128)} %bitcast.3, s32[12,4096]{1,0:T(8,128)} %marks_in.5, f32[12,19,4096]{2,1,0:T(8,128)} %pops.5, f32[10240,128]{1,0:T(8,128)S(1)} %get-tuple-element.28.own_in), custom_call_target="tpu_custom_call", output_to_operand_aliasing={{0}: (3, {})} | custom-call | tf_op jit(solution)/shard_map/pack_own/pallas_call | solution.py:875
  20.0 5.0 %collective-permute-done.3.zup = f32[108,128]{1,0:T(8,128)S(1)} collective-permute-done((f32[108,128]{1,0:T(8,128)S(1)}, f32[108,128]{1,0:T(8,128)S(1)}, u32[]{:S(2)}, u32[]{:S(2)}) %collective-permute-start.3) | collective-permute-done | bytes 55328 | tf_op jit(solution)/shard_map/ppermute | solution.py:872
  25.0 2.7 %collective-permute-done.4.zdown = f32[108,128]{1,0:T(8,128)S(1)} collective-permute-done((f32[108,128]{1,0:T(8,128)S(1)}, f32[108,128]{1,0:T(8,128)S(1)}, u32[]{:S(2)}, u32[]{:S(2)}) %collective-permute-start.4) | collective-permute-done | bytes 55328 | tf_op jit(solution)/shard_map/ppermute | solution.py:873
  27.7 0.0 collective-permute-done.2.zin
  27.7 0.0 collective-permute-done.up
  27.7 0.8 %collective-permute-done.1.down = f32[1496,128]{1,0:T(8,128)S(1)} collective-permute-done((f32[1496,128]{1,0:T(8,128)S(1)}, f32[1496,128]{1,0:T(8,128)S(1)}, u32[]{:S(2)}, u32[]{:S(2)}) %collective-permute-start.1) | collective-permute-done | bytes 765984 | tf_op jit(solution)/shard_map/ppermute | solution.py:852
  28.6 2.0 %settle_rim.1 = (f32[10240,128]{1,0:T(8,128)S(1)}, f32[640,128]{1,0:T(8,128)S(1)}, f32[384,128]{1,0:T(8,128)S(1)}, f32[24,128]{1,0:T(8,128)S(1)}, f32[400,128]{1,0:T(8,128)S(1)}, /*index=5*/f32[400,128]{1,0:T(8,128)S(1)}) custom-call(f32[1496,128]{1,0:T(8,128)S(1)} %collective-permute-done.up, ...), custom_call_target="tpu_custom_call", output_to_operand_aliasing={{0}: (7, {})} | custom-call | tf_op jit(solution)/shard_map/settle_rim/pallas_call | solution.py:891
  30.6 3.4 %collective-permute-start.5 = (f32[400,128]{1,0:T(8,128)S(1)}, f32[400,128]{1,0:T(8,128)S(1)}, u32[]{:S(2)}, u32[]{:S(2)}) collective-permute-start(f32[400,128]{1,0:T(8,128)S(1)} %get-tuple-element.32), channel_id=1, source_target_pairs={{0,2},{2,4},{4,6},{1,3},{3,5},{5,7},{8,10},{10,12},{12,14},{9,11},... | collective-permute-start | bytes 614408 | tf_op jit(solution)/shard_map/ppermute | solution.py:913
  34.0 1.3 %collective-permute-start.6 = (f32[400,128]{1,0:T(8,128)S(1)}, f32[400,128]{1,0:T(8,128)S(1)}, u32[]{:S(2)}, u32[]{:S(2)}) collective-permute-start(f32[400,128]{1,0:T(8,128)S(1)} %get-tuple-element.33), channel_id=1, source_target_pairs={{2,0},{4,2},{6,4},{3,1},{5,3},{7,5},{10,8},{12,10},{14,12},{11,9},... | collective-permute-start | bytes 614408 | tf_op jit(solution)/shard_map/ppermute | solution.py:914
  35.3 7.9 %settle_all.1 = (f32[15656,128]{1,0:T(8,128)S(1)}, f32[15656,128]{1,0:T(8,128)S(1)}) custom-call(f32[10240,128]{1,0:T(8,128)S(1)} %get-tuple-element.34.own, f32[640,128]{1,0:T(8,128)S(1)} %get-tuple-element.35.edge, f32[384,128]{1,0:T(8,128)S(1)} %get-tuple-element.36.zall, f32[24,128]{1,0:T(8,128)S(1)} %get-tuple-element.37.zedge), custom_call_target="tpu_custom_call" | custom-call | tf_op jit(solution)/shard_map/settle_all/pallas_call | solution.py:916
  43.2 0.0 collective-permute-done.5.rim_low
  43.2 2.0 %collective-permute-done.6.rim_high = f32[400,128]{1,0:T(8,128)S(1)} collective-permute-done((f32[400,128]{1,0:T(8,128)S(1)}, f32[400,128]{1,0:T(8,128)S(1)}, u32[]{:S(2)}, u32[]{:S(2)}) %collective-permute-start.6) | collective-permute-done | bytes 204832 | tf_op jit(solution)/shard_map/ppermute | solution.py:914
  45.2 4.1 %finish.1 = (f32[19,32,16,64]{3,2,1,0:T(8,128)}, f32[15656,128]{1,0:T(8,128)S(1)}, f32[15656,128]{1,0:T(8,128)S(1)}) custom-call(f32[400,128]{1,0:T(8,128)S(1)} %collective-permute-done.5.rim_low, f32[400,128]{1,0:T(8,128)S(1)} %collective-permute-done.6.rim_high, ...), custom_call_target="tpu_custom_call", output_to_operand_aliasing={{1}: (2, {}), {2}: (3, {})} | custom-call | tf_op jit(solution)/shard_map/finish/pallas_call | solution.py:929
Async XLA Ops:
  2.5 25.2 %collective-permute-start = (f32[1496,128]{1,0:T(8,128)S(1)}, f32[1496,128]{1,0:T(8,128)S(1)}, u32[]{:S(2)}, u32[]{:S(2)}) collective-permute-start(f32[1496,128]{1,0:T(8,128)S(1)} %get-tuple-element.23), channel_id=1, source_target_pairs={{0,8},{8,16},{16,24},{1,9},{9,17},{17,25},{2,10},{10,18},{18,26},{... | collective-permute-start | bytes 2297864 | tf_op jit(solution)/shard_map/ppermute | solution.py:851
  7.5 21.1 %collective-permute-start.1 = (f32[1496,128]{1,0:T(8,128)S(1)}, f32[1496,128]{1,0:T(8,128)S(1)}, u32[]{:S(2)}, u32[]{:S(2)}) collective-permute-start(f32[1496,128]{1,0:T(8,128)S(1)} %get-tuple-element.24), channel_id=1, source_target_pairs={{8,0},{16,8},{24,16},{9,1},{17,9},{25,17},{10,2},{18,10},{26,18},{... | collective-permute-start | bytes 2297864 | tf_op jit(solution)/shard_map/ppermute | solution.py:852
  11.6 16.1 %collective-permute-start.2 = (f32[392,128]{1,0:T(8,128)S(1)}, f32[392,128]{1,0:T(8,128)S(1)}, u32[]{:S(2)}, u32[]{:S(2)}) collective-permute-start(f32[392,128]{1,0:T(8,128)S(1)} %get-tuple-element.25), channel_id=1, source_target_pairs={{0,1},{1,0},{2,3},{3,2},{4,5},{5,4},{6,7},{7,6},{8,9},{9,8},{10,11... | collective-permute-start | bytes 602120 | tf_op jit(solution)/shard_map/ppermute | solution.py:869
  11.7 13.3 %collective-permute-start.3 = (f32[108,128]{1,0:T(8,128)S(1)}, f32[108,128]{1,0:T(8,128)S(1)}, u32[]{:S(2)}, u32[]{:S(2)}) collective-permute-start(f32[108,128]{1,0:T(8,128)S(1)} %get-tuple-element.26), channel_id=1, source_target_pairs={{0,9},{1,8},{8,17},{9,16},{16,25},{17,24},{2,11},{3,10},{10,19},{1... | collective-permute-start | bytes 165896 | tf_op jit(solution)/shard_map/ppermute | solution.py:872
  16.0 11.7 %collective-permute-start.4 = (f32[108,128]{1,0:T(8,128)S(1)}, f32[108,128]{1,0:T(8,128)S(1)}, u32[]{:S(2)}, u32[]{:S(2)}) collective-permute-start(f32[108,128]{1,0:T(8,128)S(1)} %get-tuple-element.27), channel_id=1, source_target_pairs={{8,1},{9,0},{16,9},{17,8},{24,17},{25,16},{10,3},{11,2},{18,11},{1... | collective-permute-start | bytes 165896 | tf_op jit(solution)/shard_map/ppermute | solution.py:873
  30.6 12.6 %collective-permute-start.5 = (f32[400,128]{1,0:T(8,128)S(1)}, f32[400,128]{1,0:T(8,128)S(1)}, u32[]{:S(2)}, u32[]{:S(2)}) collective-permute-start(f32[400,128]{1,0:T(8,128)S(1)} %get-tuple-element.32), channel_id=1, source_target_pairs={{0,2},{2,4},{4,6},{1,3},{3,5},{5,7},{8,10},{10,12},{12,14},{9,11},... | collective-permute-start | bytes 614408 | tf_op jit(solution)/shard_map/ppermute | solution.py:913
  34.0 11.3 %collective-permute-start.6 = (f32[400,128]{1,0:T(8,128)S(1)}, f32[400,128]{1,0:T(8,128)S(1)}, u32[]{:S(2)}, u32[]{:S(2)}) collective-permute-start(f32[400,128]{1,0:T(8,128)S(1)} %get-tuple-element.33), channel_id=1, source_target_pairs={{2,0},{4,2},{6,4},{3,1},{5,3},{7,5},{10,8},{12,10},{14,12},{11,9},... | collective-permute-start | bytes 614408 | tf_op jit(solution)/shard_map/ppermute | solution.py:914
